TPU v7x, 32 devices: a whole 2x2x4 slice. The times are simulated.
32 devices in a mesh: ctx: 8 (over y, x, core), ulys: 4 (over z).
Axes of the slice: x: 2, y: 2, z: 4, core: 2. Of those that a mesh axis runs over, the one named last changes fastest.
Arguments:
- queries: bfloat16 [8192, 2048], P(('ctx', 'ulys')), may hold values from -32 to 32
- keys: bfloat16 [8192, 2048], P(('ctx', 'ulys')), may hold values from -32 to 32
- values: bfloat16 [8192, 2048], P(('ctx', 'ulys')), may hold values from -6 to 6
- rand_blocks: int32 [128, 3], replicated, may hold values from 0 to 127, as said below
- out_weight: bfloat16 [2048, 4096], replicated, may hold values from -0.125 to 0.125
Outputs:
- output: bfloat16 [8192, 4096], P(('ctx', 'ulys'))
Inputs may be any that keep to these rules, and one draw needn't show every extreme that they name: `rand_blocks`: for the query blocks of one context group (rows 16 * c to 16 * c + 15), at most 12 of their random entries name blocks of any one group (blocks 16 * e to 16 * e + 15); every group's query blocks reach 12 for some group e.
All inputs are finite; a program needn't handle non-finite values.
Results may differ from a plain program's by a relative error of at most 0.0057.
Values may be sent and summed in bfloat16 or wider, within the bound.
No kernel may reach another device: no remote copies, remote signals or barrier semaphores. Data moves between devices by JAX's collectives and lax.ppermute only.
A program may use at most 192 MiB of HBM per device.

v0:
```python
import jax
import jax.numpy as jnp
from jax import lax
from jax.sharding import PartitionSpec as P

DH = 128
BLK = 64
GLOB = 2
RAND = 3


def with_halo(block, sides, width):
    for axis, dim in sides:
        count = lax.axis_size(axis)
        forward = [(i, i + 1) for i in range(count - 1)]
        forward.append((count - 1, 0))
        backward = [(target, source) for source, target in forward]
        low = lax.ppermute(
            lax.slice_in_dim(block, block.shape[dim] - width, None, axis=dim), axis, forward
        )
        high = lax.ppermute(lax.slice_in_dim(block, 0, width, axis=dim), axis, backward)
        block = jnp.concatenate([low, block, high], axis=dim)
    return block


def spread(x, axis, root):
    mine = lax.axis_index(axis) == root
    return lax.psum(jnp.where(mine, x, jnp.zeros_like(x)), axis)


def pick_rows(held_rows, shard_rows, wanted):
    inside = (wanted >= 0) & (wanted < shard_rows.shape[1])
    taken_rows = jnp.take(shard_rows, jnp.clip(wanted, 0, shard_rows.shape[1] - 1), axis=1)
    return jnp.where(inside[None, :, :, :, None], taken_rows, held_rows)


def shards(queries, keys, values, rand_blocks, out_weight):
    q_heads, k_heads, v_heads = (
        lax.all_to_all(queries, "ulys", split_axis=1, concat_axis=0, tiled=True),
        lax.all_to_all(keys, "ulys", split_axis=1, concat_axis=0, tiled=True),
        lax.all_to_all(values, "ulys", split_axis=1, concat_axis=0, tiled=True),
    )
    span_len, lane_width = k_heads.shape
    heads_here = lane_width // DH
    group_id = lax.axis_index("ctx")
    blk_count = span_len // BLK
    paired = jnp.stack([k_heads, v_heads])
    padded = with_halo(paired, (("ctx", 1),), BLK)
    framed = padded.reshape(2, blk_count + 2, BLK, lane_width)
    leading = spread(paired[:, : GLOB * BLK], "ctx", 0)
    leading = jnp.broadcast_to(
        leading.reshape(2, 1, GLOB, BLK, lane_width), (2, blk_count, GLOB, BLK, lane_width)
    )
    my_rows = lax.dynamic_slice_in_dim(rand_blocks, group_id * blk_count, blk_count, 0)
    wanted = my_rows[:, :, None] * BLK + jnp.arange(BLK, dtype=jnp.int32)[None, None, :]
    blank_rows = jnp.zeros((2, blk_count, RAND, BLK, lane_width), paired.dtype)
    randoms = pick_rows(blank_rows, lax.all_gather(paired, "ctx", axis=1, tiled=True), wanted)
    listed = jnp.concatenate(
        [
            framed[:, :blk_count, None],
            framed[:, 1 : blk_count + 1, None],
            framed[:, 2:, None],
            leading,
            randoms,
        ],
        axis=2,
    )
    listed = listed.reshape(2, blk_count, -1, heads_here, DH)
    query_blk = q_heads.reshape(blk_count, BLK, heads_here, DH)
    scores = jnp.einsum(
        "bqhd,bkhd->bhqk", query_blk, listed[0], preferred_element_type=jnp.float32
    ) * DH ** (-0.5)
    peak_score = jnp.max(scores, axis=-1, keepdims=True)
    lifted = jnp.exp(scores - peak_score)
    weights = (lifted / jnp.sum(lifted, axis=-1, keepdims=True)).astype(jnp.bfloat16)
    attended = jnp.einsum("bhqk,bkhd->bqhd", weights, listed[1], preferred_element_type=jnp.float32)
    attended = attended.astype(jnp.bfloat16).reshape(span_len, lane_width)
    by_token = lax.all_to_all(attended, "ulys", split_axis=0, concat_axis=1, tiled=True)
    return jnp.dot(by_token, out_weight, preferred_element_type=jnp.float32).astype(jnp.bfloat16)


def solution(mesh):
    return jax.shard_map(
        shards,
        mesh=mesh,
        in_specs=(
            P(("ctx", "ulys"), None),
            P(("ctx", "ulys"), None),
            P(("ctx", "ulys"), None),
            P(),
            P(),
        ),
        out_specs=P(("ctx", "ulys"), None),
        check_vma=False,
    )
```

profile of v0, /device:TPU:0, one launch (start us, length us, event | category | flops | bytes accessed | tf_op | source)
XLA Modules:
  0.0 366.0 jit_solution(3089068253077511849)
XLA Ops:
  6.5 2.3 copy.44
  8.8 6.3 %all-to-all-start = ((bf16[256,4,512]{0,2,1:T(8,128)(2,1)}), bf16[256,4,512]{0,2,1:T(8,128)(2,1)S(1)}, u32[]{:S(2)}, u32[]{:S(2)}) async-start(bf16[256,4,512]{0,2,1:T(8,128)(2,1)} %bitcast), calls=%async_computation | async-start | bytes 2097152 | tf_op jit(solution)/shard_map/all_to_all | solution.py:40
  15.1 2.3 copy.46
  17.4 23.5 %all-to-all-done = bf16[256,4,512]{0,2,1:T(8,128)(2,1)S(1)} async-done(((bf16[256,4,512]{0,2,1:T(8,128)(2,1)}), bf16[256,4,512]{0,2,1:T(8,128)(2,1)S(1)}, u32[]{:S(2)}, u32[]{:S(2)}) %all-to-all-start) | async-done | bytes 1048608 | tf_op jit(solution)/shard_map/all_to_all | solution.py:40
  40.8 3.5 all-to-all-start.1
  45.0 24.6 %all-to-all-done.1 = bf16[256,4,512]{0,2,1:T(8,128)(2,1)S(1)} async-done(((bf16[256,4,512]{0,2,1:T(8,128)(2,1)}), bf16[256,4,512]{0,2,1:T(8,128)(2,1)S(1)}, u32[]{:S(2)}, u32[]{:S(2)}) %all-to-all-start.1) | async-done | bytes 1048608 | tf_op jit(solution)/shard_map/all_to_all | solution.py:41
  70.1 0.7 fusion.24
  71.1 3.5 copy.49
  74.6 1.1 copy.77
  75.7 3.5 all-to-all-start.2
  81.6 2.6 collective-permute-start.1
  84.2 0.7 broadcast_clamp_fusion
  84.9 19.5 %all-to-all-done.2 = bf16[256,4,512]{2,0,1:T(8,128)(2,1)S(1)} async-done(((bf16[256,4,512]{2,0,1:T(8,128)(2,1)}), bf16[256,4,512]{2,0,1:T(8,128)(2,1)S(1)}, u32[]{:S(2)}, u32[]{:S(2)}) %all-to-all-start.2) | async-done | bytes 1048608 | tf_op jit(solution)/shard_map/all_to_all | solution.py:39
  104.4 1.0 copy-done
  105.4 1.3 reshape.63
  106.9 1.5 fusion.15
  108.5 1.6 fusion.14
  110.0 1.5 fusion.13
  111.6 12.1 %all-reduce.2.cloned.1.call-done = bf16[2,2,64,512]{3,2,1,0:T(8,128)(2,1)} async-done(((bf16[2,2,64,512]{3,2,1,0:T(8,128)(2,1)}), bf16[2,2,64,512]{3,2,1,0:T(8,128)(2,1)}) %all-reduce.2.cloned.1.call-update) | async-done | bytes 262160 | tf_op jit(solution)/shard_map/psum | solution.py:28
  123.7 3.4 broadcast_dynamic-update-slice_fusion
  127.1 87.9 %all-gather.2.cloned.1.call-done = bf16[2,8192,512]{2,0,1:T(2,128)(2,1)} async-done(((bf16[2,1024,512]{2,0,1:T(2,128)(2,1)}), bf16[2,8192,512]{2,0,1:T(2,128)(2,1)}) %all-gather.2.cloned.1.call-update) | async-done | bytes 16777232 | tf_op jit(solution)/shard_map/all_gather | solution.py:57
  215.0 37.6 %gather_fusion = bf16[3072,2,512]{2,1,0:T(2,128)(2,1)} fusion(bf16[2,8192,512]{2,0,1:T(2,128)(2,1)} %all-gather.2.cloned.1.call-done, s32[3072]{0:T(1024)S(1)} %broadcast_clamp_fusion), kind=kCustom, calls=%fused_computation | custom fusion | bytes 12595200 | tf_op jit(solution)/shard_map/jit(_take)/gather | solution.py:33
  252.6 7.6 %bitcast_dynamic-update-slice_fusion = bf16[2,16,8,64,512]{4,3,2,1,0:T(8,128)(2,1)} fusion(bf16[2,16,8,64,512]{4,3,2,1,0:T(8,128)(2,1)} %broadcast_dynamic-update-slice_fusion, bf16[16,3,64,2,512]{4,3,2,1,0:T(2,128)(2,1)} %bitcast.66, pred[16,3,64]{2,1,0:T(4,128)(4,1)S(1)} %copy-done.3, pred[16,3,64]{2,1,0:T(4,128)(4,1)S(1)} %copy-done.2), kind=kLoop, calls=%fused_computation.12 | loop fusion | flops 6291456 | bytes 12589056 | tf_op jit(solution)/shard_map/concatenate | solution.py:58
  260.1 11.7 %fusion.31 = (bf16[1,16,8,64,512]{4,3,2,1,0:T(8,128)(2,1)}, bf16[1,16,8,64,512]{4,3,2,1,0:T(8,128)(2,1)}) fusion(bf16[2,16,8,64,512]{4,3,2,1,0:T(8,128)(2,1)} %bitcast_dynamic-update-slice_fusion), kind=kLoop, calls=%fused_computation.51 | loop fusion | bytes 33554432 | tf_op jit(solution)/shard_map/slice | solution.py:71
  271.8 12.6 %squeeze.7 = bf16[16,512,4,128]{3,2,1,0:T(4,128)(2,1)} reshape(bf16[1,16,8,64,512]{4,3,2,1,0:T(8,128)(2,1)} %get-tuple-element.5) | data formatting | bytes 16777216 | tf_op jit(solution)/shard_map/squeeze | solution.py:71
  284.4 6.4 %fusion.5 = f32[16,4,512,64]{2,3,1,0:T(8,128)S(1)} fusion(bf16[16,512,4,128]{3,2,1,0:T(4,128)(2,1)} %squeeze.7, bf16[16,64,4,128]{3,2,1,0:T(4,128)(2,1)S(1)} %reshape.63), kind=kOutput, calls=%fused_computation.8 | convolution fusion | flops 536870912 | bytes 17825792 | tf_op jit(solution)/shard_map/bqhd,bkhd->bhqk/dot_general | solution.py:70
  290.8 4.2 %fusion.32 = (f32[16,4,64]{2,1,0:T(4,128)S(1)}, f32[16,4,64,512]{3,2,1,0:T(8,128)}) fusion(f32[16,4,512,64]{2,3,1,0:T(8,128)S(1)} %fusion.5), kind=kOutput, calls=%fused_computation.52 | output fusion | flops 8389119 | bytes 16793600 | tf_op jit(solution)/shard_map/sub | solution.py:74
  295.0 12.5 %squeeze.6 = bf16[16,512,4,128]{3,2,1,0:T(4,128)(2,1)} reshape(bf16[1,16,8,64,512]{4,3,2,1,0:T(8,128)(2,1)} %get-tuple-element.6) | data formatting | bytes 16777216 | tf_op jit(solution)/shard_map/squeeze | solution.py:76
  307.5 7.6 %fusion.19 = bf16[16,64,4,128]{3,1,2,0:T(8,128)(2,1)S(1)} fusion(bf16[16,512,4,128]{3,2,1,0:T(4,128)(2,1)} %squeeze.6, f32[16,4,64,512]{3,2,1,0:T(8,128)} %get-tuple-element.12, f32[16,4,64]{2,1,0:T(4,128)S(1)} %get-tuple-element.11), kind=kOutput, calls=%fused_computation.34 | convolution fusion | flops 541589504 | bytes 17842176 | tf_op jit(solution)/shard_map/bhqk,bkhd->bqhd/dot_general | solution.py:76
  315.2 0.9 copy.58
  316.5 30.6 %all_to_all.67 = bf16[4,256,512]{2,1,0:T(8,128)(2,1)S(1)} all-to-all(bf16[4,256,512]{2,1,0:T(8,128)(2,1)S(1)} %all_to_all.59), channel_id=1, replica_groups=mesh['ctx'=8,'ulys'=4] {'ulys'}, dimensions={0} | all-to-all | bytes 2097152 | tf_op jit(solution)/shard_map/all_to_all | solution.py:78
  347.6 11.5 %convolution_convert_fusion = bf16[256,4096]{1,0:T(8,128)(2,1)} fusion(bf16[256,2048]{0,1:T(8,128)(2,1)S(1)} %bitcast.67, bf16[2048,4096]{1,0:T(8,128)(2,1)} %param.9), kind=kOutput, calls=%fused_computation.15 | convolution fusion | flops 4296015872 | bytes 19922944 | tf_op jit(solution)/shard_map/dot_general | solution.py:79
  (28 shorter events, 4.8 us)
Async XLA Ops:
  8.8 32.0 %all-to-all-start = ((bf16[256,4,512]{0,2,1:T(8,128)(2,1)}), bf16[256,4,512]{0,2,1:T(8,128)(2,1)S(1)}, u32[]{:S(2)}, u32[]{:S(2)}) async-start(bf16[256,4,512]{0,2,1:T(8,128)(2,1)} %bitcast), calls=%async_computation | async-start | bytes 2097152 | tf_op jit(solution)/shard_map/all_to_all | solution.py:40
  40.8 28.7 %all-to-all-start.1 = ((bf16[256,4,512]{0,2,1:T(8,128)(2,1)}), bf16[256,4,512]{0,2,1:T(8,128)(2,1)S(1)}, u32[]{:S(2)}, u32[]{:S(2)}) async-start(bf16[256,4,512]{0,2,1:T(8,128)(2,1)} %bitcast.3), calls=%async_computation.1 | async-start | bytes 2097152 | tf_op jit(solution)/shard_map/all_to_all | solution.py:41
  44.4 79.3 %all-reduce.2.cloned.1.call-start = ((), (), s32[]{:S(2)}) async-start(), calls=%async_computation.4 | async-start | bytes 524288 | tf_op jit(solution)/shard_map/psum | solution.py:28
  70.1 4.5 %copy-start.1 = (bf16[256,2048]{1,0:T(8,128)(2,1)S(1)}, bf16[256,2048]{1,0:T(8,128)(2,1)}, u32[]{:S(2)}) copy-start(bf16[256,2048]{1,0:T(8,128)(2,1)} %param.5) | copy-start | bytes 3145732
  70.1 9.1 %copy-start.4 = (s32[128,3]{0,1:T(4,128)S(1)}, s32[128,3]{0,1:T(4,128)}, u32[]{:S(2)}) copy-start(s32[128,3]{0,1:T(4,128)} %param.8) | copy-start | bytes 4612
  70.9 144.1 %all-gather.2.cloned.1.call-start = ((), (), s32[]{:S(2)}) async-start(), calls=%async_computation.5 | async-start | bytes 18874368 | tf_op jit(solution)/shard_map/all_gather | solution.py:57
  75.7 28.7 %all-to-all-start.2 = ((bf16[256,4,512]{2,0,1:T(8,128)(2,1)}), bf16[256,4,512]{2,0,1:T(8,128)(2,1)S(1)}, u32[]{:S(2)}, u32[]{:S(2)}) async-start(bf16[256,4,512]{2,0,1:T(8,128)(2,1)} %bitcast.69), calls=%async_computation.2 | async-start | bytes 2097152 | tf_op jit(solution)/shard_map/all_to_all | solution.py:39
  81.6 25.2 %collective-permute-start = (bf16[2,64,512]{2,1,0:T(8,128)(2,1)}, bf16[2,64,512]{2,1,0:T(8,128)(2,1)S(1)}, u32[]{:S(2)}, u32[]{:S(2)}) collective-permute-start(bf16[2,64,512]{2,1,0:T(8,128)(2,1)} %get-tuple-element.7), channel_id=1, source_target_pairs={{0,4},{4,8},{8,12},{12,16},{16,20},{20,24},{24,28},{28,0},{1,5},{5... | collective-permute-start | bytes 393224 | tf_op jit(solution)/shard_map/ppermute | solution.py:18
  81.6 25.2 %collective-permute-start.1 = (bf16[2,64,512]{2,1,0:T(8,128)(2,1)S(1)}, bf16[2,64,512]{2,1,0:T(8,128)(2,1)S(1)}, u32[]{:S(2)}, u32[]{:S(2)}) collective-permute-start(bf16[2,64,512]{2,1,0:T(8,128)(2,1)S(1)} %get-tuple-element.8), channel_id=1, source_target_pairs={{4,0},{8,4},{12,8},{16,12},{20,16},{24,20},{28,24},{0,28},{5,1},{9... | collective-permute-start | bytes 393224 | tf_op jit(solution)/shard_map/ppermute | solution.py:21
  104.4 1.0 copy-start
  111.6 141.0 %copy-start.2 = (pred[16,3,64]{2,1,0:T(4,128)(4,1)S(1)}, pred[16,3,64]{2,1,0:T(4,128)(4,1)}, u32[]{:S(2)}) copy-start(pred[16,3,64]{2,1,0:T(4,128)(4,1)} %get-tuple-element.9) | copy-start | bytes 9220
  111.6 141.0 %copy-start.3 = (pred[16,3,64]{2,1,0:T(4,128)(4,1)S(1)}, pred[16,3,64]{2,1,0:T(4,128)(4,1)}, u32[]{:S(2)}) copy-start(pred[16,3,64]{2,1,0:T(4,128)(4,1)} %get-tuple-element.10) | copy-start | bytes 9220
Sparse Core Ops, SparseCore 0:
  71.0 52.6 all-reduce.1
  125.7 89.2 all-gather.1
where the time goes:
time: 367 us; the launch traced here: 366 us
  waiting for transfers between devices  168 us (46%)
  local copies, waits for them, and re-layouts  97.5 us (27%)
  blocking collectives  30.6 us (8%)
  matrix products  25.6 us (7%)
  starting transfers between devices  16.1 us (4%)
  other arithmetic  15.1 us (4%)
  between operations  13.6 us (4%)
    all_gather x1, waiting for transfers between devices, shards(): lax.all_gather(paired, 'ctx', axis=1, tiled=True)  87.9 us
    gather x1, local copies, waits for them, and re-layouts, pick_rows(): jnp.take(shard_rows, jnp.clip(wanted, 0, shard_rows.shape[1] - 1), axis=1)  37.6 us
    all_to_all x1, blocking collectives, shards(): lax.all_to_all(attended, 'ulys', split_axis=0, concat_axis=1, tiled=True)  30.6 us
    all_to_all x1, waiting for transfers between devices, shards(): lax.all_to_all(values, 'ulys', split_axis=1, concat_axis=0, tiled=True)  24.6 us
    all_to_all x1, waiting for transfers between devices, shards(): lax.all_to_all(keys, 'ulys', split_axis=1, concat_axis=0, tiled=True)  23.5 us
    all_to_all x1, waiting for transfers between devices, shards(): lax.all_to_all(queries, 'ulys', split_axis=1, concat_axis=0, tiled=True)  19.5 us
    unnamed x16, local copies, waits for them, and re-layouts  13.6 us
    squeeze x1, local copies, waits for them, and re-layouts, shards(): listed[0]  12.6 us
  transfers between devices with their start and end apart: 7, of which 5 were waited for; matrix products, arithmetic and copies ran while one was open for 5% of the time, Pallas kernels for 0%

commit v1 on v0

v1 whole, which is shorter than its diff:
```python
import functools

import jax
import jax.numpy as jnp
from jax import lax
from jax.experimental import pallas as pl
from jax.experimental.pallas import tpu as pltpu
from jax.sharding import PartitionSpec as P

DH = 128
BLK = 64
GLOB = 2
RAND = 3
MIB = 1 << 20

ANY = pl.BlockSpec(memory_space=pl.ANY)
SMEM = pl.BlockSpec(memory_space=pltpu.SMEM)
VMEM = pl.BlockSpec(memory_space=pltpu.VMEM)


def copy_all(pairs, sems):
    copies = [pltpu.make_async_copy(src, dst, sems.at[i]) for i, (src, dst) in enumerate(pairs)]
    for c in copies:
        c.start()
    for c in copies:
        c.wait()


def mover(plan, n_in, out_shapes, n_copies, name, n_bytes):
    def body(place, *refs):
        ins, outs, sems = refs[:n_in], refs[n_in:-1], refs[-1]
        copy_all(plan(place, ins, outs), sems)

    return pl.pallas_call(
        body,
        out_shape=[jax.ShapeDtypeStruct(s, jnp.bfloat16) for s in out_shapes],
        in_specs=[SMEM] + [ANY] * n_in,
        out_specs=[ANY] * len(out_shapes),
        scratch_shapes=[pltpu.SemaphoreType.DMA((n_copies,))],
        cost_estimate=pl.CostEstimate(flops=0, bytes_accessed=2 * n_bytes, transcendentals=0),
        name=name,
    )


def pack(place, tensors, slots, n_u, hp):
    T = tensors[0].shape[0]
    nb = len(tensors)

    def plan(place, ins, outs):
        z, core = place[0], place[1]
        pairs = []
        for d in range(n_u):
            zd = lax.rem(z + d, n_u)
            for r in range(2):
                cr = core if r == 0 else 1 - core
                for i in range(nb):
                    col = ((2 * zd + cr) * hp + slots[i]) * DH
                    pairs.append((ins[i].at[:, pl.ds(pl.multiple_of(col, DH), DH)], outs[d].at[r, i]))
        return pairs

    call = mover(plan, nb, [(2, nb, T, DH)] * n_u, n_u * 2 * nb, "pack", 2 * n_u * nb * T * DH * 2)
    return call(place, *tensors)


def merge_other(place, parts):
    n_u = len(parts)
    _, nb, T, _ = parts[0].shape

    def plan(place, ins, outs):
        return [(ins[d].at[1], outs[0].at[d]) for d in range(n_u)]

    call = mover(plan, n_u, [(n_u, nb, T, DH)], n_u, "merge_other", n_u * nb * T * DH * 2)
    return call(place, *parts)[0]


def merge_own(place, parts, other):
    n_u = len(parts)
    _, nb, T, _ = parts[0].shape

    def plan(place, ins, outs):
        pairs = []
        for i in range(nb):
            for d in range(n_u):
                pairs.append((ins[d].at[0, i], outs[0].at[i, 0, d]))
                pairs.append((ins[n_u].at[d, i], outs[0].at[i, 1, d]))
        return pairs

    call = mover(
        plan, n_u + 1, [(nb, 2, n_u, T, DH)], 2 * nb * n_u, "merge_own", 2 * nb * n_u * T * DH * 2
    )
    return call(place, *parts, other)[0]


def shift(x, d, n_u):
    return lax.ppermute(x, "ulys", [(i, (i + d) % n_u) for i in range(n_u)])


def swap_core(x, n_c):
    return lax.ppermute(x, "ctx", [(i, i ^ 1) for i in range(n_c)])


def swap_chip(x, bit, n_c):
    return lax.ppermute(x, "ctx", [(i, i ^ (2 * bit)) for i in range(n_c)])


def to_heads(place, tensors, slots, n_u, n_c, hp):
    parts = pack(place, tensors, slots, n_u, hp)
    parts = [parts[0]] + [shift(parts[d], d, n_u) for d in range(1, n_u)]
    other = swap_core(merge_other(place, parts), n_c)
    return parts, other


def gather_chips(mine, n_c):
    rows = mine.shape[0]
    half = rows // 2
    n_p = n_c // 2
    halves = {0: (mine, None)}
    held = {0: [(mine, 0)]}
    for t in range(1, n_p):
        if t & (t - 1) == 0:
            got = swap_chip(mine, t, n_c)
            held[t] = [(got, 0)]
            halves[t] = (got[:half], got[half:])
    for t in range(1, n_p):
        if t & (t - 1) != 0:
            low = t & -t
            high = 1 << (t.bit_length() - 1)
            a = swap_chip(halves[t ^ low][0], low, n_c)
            b = swap_chip(halves[t ^ high][1], high, n_c)
            halves[t] = (a, b)
            held[t] = [(a, 0), (b, half)]
    return held


def pieces_of(held, index, count):
    rows = sum(a.shape[0] for a, _ in held[0])
    span = rows // count
    lo, hi = index * span, (index + 1) * span
    out = []
    for t in sorted(held):
        for a, first in held[t]:
            s, e = max(lo, first), min(hi, first + a.shape[0])
            if s < e:
                out.append((a, s - first, t * span + s - lo, e - s))
    return out


def attend(table, q_parts, q_other, q_index, k_pieces, v_pieces, n_u):
    T = q_parts[0].shape[2]
    n_q = 2 * n_u * T
    n_k = sum(p[3] for p in k_pieces)
    n_rows, n_list = table.shape
    group = T // BLK

    arrays = []

    def place_of(a):
        for i, b in enumerate(arrays):
            if a is b:
                return i
        arrays.append(a)
        return len(arrays) - 1

    q_at = [place_of(a) for a in q_parts] + [place_of(q_other)]
    k_at = [place_of(p[0]) for p in k_pieces]
    v_at = [place_of(p[0]) for p in v_pieces]
    n_in = len(arrays)
    n_copies = 2 * n_u + len(k_pieces) + len(v_pieces)

    def body(table, *refs):
        ins, outs = refs[:n_in], refs[n_in : n_in + n_u]
        q_vm, k_vm, v_vm, o_vm, sems, out_sems = refs[n_in + n_u :]
        pairs = []
        for d in range(n_u):
            pairs.append((ins[q_at[d]].at[0, q_index], q_vm.at[pl.ds(d * T, T)]))
            pairs.append((ins[q_at[n_u]].at[d, q_index], q_vm.at[pl.ds((n_u + d) * T, T)]))
        for at, pieces, vm in ((k_at, k_pieces, k_vm), (v_at, v_pieces, v_vm)):
            for i, (_, src, dst, n) in zip(at, pieces):
                pairs.append((ins[i].at[pl.ds(src, n)], vm.at[pl.ds(dst, n)]))
        copy_all(pairs, sems)

        @pl.loop(0, n_rows // group)
        def _(step):
            for g in range(group):
                row = step * group + g
                at = [pl.multiple_of(table[row, j] * BLK, BLK) for j in range(n_list)]
                q = q_vm[pl.ds(pl.multiple_of(row * BLK, BLK), BLK), :]
                k = jnp.concatenate([k_vm[pl.ds(a, BLK), :] for a in at], axis=0)
                v = jnp.concatenate([v_vm[pl.ds(a, BLK), :] for a in at], axis=0)
                s = lax.dot_general(
                    q, k, (((1,), (1,)), ((), ())), preferred_element_type=jnp.float32
                ) * (DH**-0.5)
                e = jnp.exp(s - jnp.max(s, axis=-1, keepdims=True))
                w = (e / jnp.sum(e, axis=-1, keepdims=True)).astype(jnp.bfloat16)
                o = jnp.dot(w, v, preferred_element_type=jnp.float32)
                o_vm[pl.ds(pl.multiple_of(row * BLK, BLK), BLK), :] = o.astype(jnp.bfloat16)

        copy_all(
            [
                (o_vm.at[pl.ds((r * n_u + d) * T, T)], outs[d].at[r, 0])
                for d in range(n_u)
                for r in range(2)
            ],
            out_sems,
        )

    flops = 4 * n_q * n_list * BLK * DH
    return pl.pallas_call(
        body,
        out_shape=[jax.ShapeDtypeStruct((2, 1, T, DH), jnp.bfloat16)] * n_u,
        in_specs=[SMEM] + [ANY] * n_in,
        out_specs=[ANY] * n_u,
        scratch_shapes=[
            pltpu.VMEM((n_q, DH), jnp.bfloat16),
            pltpu.VMEM((n_k, DH), jnp.bfloat16),
            pltpu.VMEM((n_k, DH), jnp.bfloat16),
            pltpu.VMEM((n_q, DH), jnp.bfloat16),
            pltpu.SemaphoreType.DMA((n_copies,)),
            pltpu.SemaphoreType.DMA((2 * n_u,)),
        ],
        compiler_params=pltpu.CompilerParams(
            vmem_limit_bytes=4 * (n_q + n_k) * DH + 8 * MIB
        ),
        cost_estimate=pl.CostEstimate(
            flops=flops, bytes_accessed=4 * (n_q + n_k) * DH, transcendentals=n_q * n_list * BLK
        ),
        name="attend",
    )(table, *arrays)


def project(place, own, other, weight, n_u, hp):
    T = own[0][0].shape[2]
    depth, width = weight.shape
    tile = 512
    arrays = [a for h in range(hp) for a in own[h]] + list(other)
    n_copies = 2 * hp * n_u

    def body(place, *refs):
        ins, w_ref, out_ref, rows, sems = refs[: len(arrays)], *refs[len(arrays) :]

        @pl.when(pl.program_id(0) == 0)
        def _():
            z, core = place[0], place[1]
            pairs = []
            for h in range(hp):
                for d in range(n_u):
                    zd = lax.rem(z + d, n_u)
                    for r in range(2):
                        cr = core if r == 0 else 1 - core
                        col = pl.multiple_of(((2 * zd + cr) * hp + h) * DH, DH)
                        src = ins[h * n_u + d].at[0, 0] if r == 0 else ins[hp * n_u + h].at[d, 0]
                        pairs.append((src, rows.at[:, pl.ds(col, DH)]))
            copy_all(pairs, sems)

        out_ref[...] = jnp.dot(
            rows[...], w_ref[...], preferred_element_type=jnp.float32
        ).astype(jnp.bfloat16)

    return pl.pallas_call(
        body,
        out_shape=jax.ShapeDtypeStruct((T, width), jnp.bfloat16),
        grid=(width // tile,),
        in_specs=[SMEM] + [ANY] * len(arrays) + [pl.BlockSpec((depth, tile), lambda j: (0, j))],
        out_specs=pl.BlockSpec((T, tile), lambda j: (0, j)),
        scratch_shapes=[
            pltpu.VMEM((T, depth), jnp.bfloat16),
            pltpu.SemaphoreType.DMA((n_copies,)),
        ],
        compiler_params=pltpu.CompilerParams(vmem_limit_bytes=16 * MIB),
        cost_estimate=pl.CostEstimate(
            flops=2 * T * depth * width,
            bytes_accessed=2 * (depth * width + T * (depth + width)),
            transcendentals=0,
        ),
        name="project",
    )(place, *arrays, weight)


def key_table(rand_blocks, z, core, chip, n_u, n_p, per):
    total = rand_blocks.shape[0]
    r = jnp.arange(2, dtype=jnp.int32)[:, None, None]
    d = jnp.arange(n_u, dtype=jnp.int32)[None, :, None]
    j = jnp.arange(per, dtype=jnp.int32)[None, None, :]
    mine = ((2 * chip + (core ^ r)) * n_u + (z - d) % n_u) * per + j
    mine = mine.reshape(-1)
    window = jnp.stack([(mine - 1) % total, mine, (mine + 1) % total], axis=1)
    leading = jnp.broadcast_to(jnp.arange(GLOB, dtype=jnp.int32)[None, :], (mine.shape[0], GLOB))
    listed = jnp.concatenate([window, leading, rand_blocks[mine]], axis=1)
    device, inner = listed // per, listed % per
    zs, cs = device % n_u, device // n_u
    mask, rel, shifted = (cs // 2) ^ chip, (cs % 2) ^ core, (z - zs) % n_u
    return ((mask * 2 + rel) * n_u + shifted) * per + inner


def shards(queries, keys, values, rand_blocks, out_weight):
    n_c, n_u = lax.axis_size("ctx"), lax.axis_size("ulys")
    T, lanes = queries.shape
    hp = lanes // DH // (2 * n_u)
    c, z = lax.axis_index("ctx"), lax.axis_index("ulys")
    chip, core = c // 2, c % 2
    place = jnp.stack([z, core]).astype(jnp.int32)
    table = key_table(rand_blocks, z, core, chip, n_u, n_c // 2, T // BLK)

    def spread(tensors, slots):
        parts, other = to_heads(place, tensors, slots, n_u, n_c, hp)
        held = gather_chips(merge_own(place, parts, other).reshape(-1, DH), n_c)
        return [pieces_of(held, i, len(tensors)) for i in range(len(tensors))]

    k_of, v_of = {}, {}
    (k_of[0],) = spread([keys], [0])
    (v_of[0],) = spread([values], [0])
    for h in range(1, hp):
        k_of[h], v_of[h] = spread([keys, values], [h, h])
    q_parts, q_other = to_heads(place, [queries] * hp, list(range(hp)), n_u, n_c, hp)

    own, other = [], []
    for h in range(hp):
        parts = attend(table, q_parts, q_other, h, k_of[h], v_of[h], n_u)
        parts = [parts[0]] + [shift(parts[d], n_u - d, n_u) for d in range(1, n_u)]
        own.append(parts)
        other.append(swap_core(merge_other(place, parts), n_c))
    return project(place, own, other, out_weight, n_u, hp)


def solution(mesh):
    return jax.shard_map(
        shards,
        mesh=mesh,
        in_specs=(
            P(("ctx", "ulys"), None),
            P(("ctx", "ulys"), None),
            P(("ctx", "ulys"), None),
            P(),
            P(),
        ),
        out_specs=P(("ctx", "ulys"), None),
        check_vma=False,
    )
```

time: 367 us -> 410 us (1.12)
  Pallas kernels: 0 us -> 287 us
  waiting for transfers between devices: 168 us -> 39.7 us
  local copies, waits for them, and re-layouts: 97.5 us -> 35.3 us
  blocking collectives: 30.6 us -> 0 us
  starting transfers between devices: 16.1 us -> 45.3 us
  matrix products: 25.6 us -> 0 us
  other arithmetic: 15.1 us -> 1.01 us
  between operations: 13.6 us -> 0.43 us
    pallas_call x0 -> x16, Pallas kernels: none -> 287 us  [the longest x4 103 us: pack(): return call(place, *tensors)]
    all_gather x1 -> x0, waiting for transfers between devices: 87.9 us -> none  [shards(): lax.all_gather(paired, 'ctx', axis=1, tiled=True)]
    all_to_all x3 -> x0, waiting for transfers between devices: 67.5 us -> none  [the longest x1 24.6 us: shards(): lax.all_to_all(values, 'ulys', split_axis=1, concat_axis=0, tiled=True)]
    ppermute x2 -> x36, starting transfers between devices: 2.65 us -> 45.3 us  [the longest x18 31.4 us: shift(): return lax.ppermute(x, 'ulys', [(i, (i + d) % n_u) for i in range(n_u)])]
    ppermute x2 -> x36, waiting for transfers between devices: 0.01 us -> 39.7 us  [the longest x12 20.2 us: swap_chip(): return lax.ppermute(x, 'ctx', [(i, i ^ 2 * bit) for i in range(n_c)])]
    gather x1, local copies, waits for them, and re-layouts: 37.6 us -> 0.57 us  [key_table(): listed = jnp.concatenate([window, leading, rand_blocks[mine]], axis=1)]
    all_to_all x1 -> x0, blocking collectives: 30.6 us -> none  [shards(): lax.all_to_all(attended, 'ulys', split_axis=0, concat_axis=1, tiled=True)]
    dot_general x3 -> x0, matrix products: 25.6 us -> none  [the longest x1 11.5 us: shards(): jnp.dot(by_token, out_weight, preferred_element_type=jnp.float32)]
  transfers between devices with their start and end apart: 7 -> 36, of which waited for: 5 -> 8; matrix products, arithmetic and copies ran while one was open for 5% -> 2% of each run, Pallas kernels for 0% -> 47%
where the time goes in v1:
time: 410 us; the launch traced here: 409 us
  Pallas kernels  287 us (70%)
  starting transfers between devices  45.3 us (11%)
  waiting for transfers between devices  39.7 us (10%)
  local copies, waits for them, and re-layouts  35.3 us (9%)
    pallas_call x4, Pallas kernels, pack(): return call(place, *tensors)  103 us
    pallas_call x6, Pallas kernels, merge_other(): return call(place, *parts)[0]  74.3 us
    pallas_call x3, Pallas kernels, merge_own(): return call(place, *parts, other)[0]  69.1 us
    pallas_call x2, Pallas kernels, attend(): pl.pallas_call(body, out_shape=[jax.ShapeDtypeStruct((2, 1, T, DH), jnp.b...  31.8 us
    ppermute x18, starting transfers between devices, shift(): return lax.ppermute(x, 'ulys', [(i, (i + d) % n_u) for i in range(n_u)])  31.4 us
    unnamed x83, local copies, waits for them, and re-layouts  26 us
    ppermute x12, waiting for transfers between devices, swap_chip(): return lax.ppermute(x, 'ctx', [(i, i ^ 2 * bit) for i in range(n_c)])  20.2 us
    ppermute x18, waiting for transfers between devices, shift(): return lax.ppermute(x, 'ulys', [(i, (i + d) % n_u) for i in range(n_u)])  16 us
  transfers between devices with their start and end apart: 36, of which 8 were waited for; matrix products, arithmetic and copies ran while one was open for 2% of the time, Pallas kernels for 47%

profile of v1, /device:TPU:0, one launch (start us, length us, event | category | flops | bytes accessed | tf_op | source)
XLA Modules:
  0.0 408.8 jit_solution(9508875617750764233)
XLA Ops:
  0.7 33.8 %pack.7 = (bf16[2,2,256,128]{3,2,1,0:T(8,128)(2,1)}, bf16[2,2,256,128]{3,2,1,0:T(8,128)(2,1)}, bf16[2,2,256,128]{3,2,1,0:T(8,128)(2,1)}, bf16[2,2,256,128]{3,2,1,0:T(8,128)(2,1)}) custom-call(s32[2]{0:T(128)} %pad_add_fusion.place, bf16[256,2048]{1,0:T(8,128)(2,1)} %refs_0_.7, bf16[256,2048]{1,0:T(8,128)(2,1)} %refs_1_.3), custom_call_target="tpu_custom_call" | custom-call | bytes 2097152 | tf_op jit(solution)/shard_map/pack/pallas_call | solution.py:62
  34.5 3.1 collective-permute-start.23
  37.6 2.6 collective-permute-start.24
  41.5 5.6 %collective-permute-done.23.refs_1_ = bf16[2,2,256,128]{3,2,1,0:T(8,128)(2,1)S(1)} collective-permute-done((bf16[2,2,256,128]{3,2,1,0:T(8,128)(2,1)}, bf16[2,2,256,128]{3,2,1,0:T(8,128)(2,1)S(1)}, u32[]{:S(2)}, u32[]{:S(2)}) %collective-permute-start.23) | collective-permute-done | bytes 262176 | tf_op jit(solution)/shard_map/ppermute | solution.py:95
  47.1 10.4 %collective-permute-done.24.refs_2_ = bf16[2,2,256,128]{3,2,1,0:T(8,128)(2,1)S(1)} collective-permute-done((bf16[2,2,256,128]{3,2,1,0:T(8,128)(2,1)}, bf16[2,2,256,128]{3,2,1,0:T(8,128)(2,1)S(1)}, u32[]{:S(2)}, u32[]{:S(2)}) %collective-permute-start.24) | collective-permute-done | bytes 262176 | tf_op jit(solution)/shard_map/ppermute | solution.py:95
  58.3 17.7 %merge_other.9 = bf16[4,2,256,128]{3,2,1,0:T(8,128)(2,1)} custom-call(s32[2]{0:T(128)} %pad_add_fusion.place, bf16[2,2,256,128]{3,2,1,0:T(8,128)(2,1)} %get-tuple-element.45.refs_0_, bf16[2,2,256,128]{3,2,1,0:T(8,128)(2,1)} %copy-done.28, bf16[2,2,256,128]{3,2,1,0:T(8,128)(2,1)} %copy-done.29, bf16[2,2,256,128]{3,2,1,0:T(8,128)(2,1)} %copy-done.30), custom_call_target="tpu_custom_call" | custom-call | bytes 1048576 | tf_op jit(solution)/shard_map/merge_other/pallas_call | solution.py:73
  76.1 2.1 collective-permute-done.26.refs_4_
  79.0 33.7 %merge_own.5 = bf16[2,2,4,256,128]{4,3,2,1,0:T(8,128)(2,1)} custom-call(s32[2]{0:T(128)} %pad_add_fusion.place, bf16[2,2,256,128]{3,2,1,0:T(8,128)(2,1)} %get-tuple-element.45.refs_0_, bf16[2,2,256,128]{3,2,1,0:T(8,128)(2,1)} %copy-done.28, bf16[2,2,256,128]{3,2,1,0:T(8,128)(2,1)} %copy-done.29, bf16[2,2,256,128]{3,2,1,0:T(8,128)(2,1)} %copy-done.30, ...), custom_call_target="tpu_custom_call" | custom-call | bytes 2097152 | tf_op jit(solution)/shard_map/merge_own/pallas_call | solution.py:91
  114.2 17.7 %pack.5 = (bf16[2,1,256,128]{3,2,1,0:T(8,128)(2,1)}, bf16[2,1,256,128]{3,2,1,0:T(8,128)(2,1)}, bf16[2,1,256,128]{3,2,1,0:T(8,128)(2,1)}, bf16[2,1,256,128]{3,2,1,0:T(8,128)(2,1)}) custom-call(s32[2]{0:T(128)} %pad_add_fusion.place, bf16[256,2048]{1,0:T(8,128)(2,1)} %refs_0_.7), custom_call_target="tpu_custom_call" | custom-call | bytes 1048576 | tf_op jit(solution)/shard_map/pack/pallas_call | solution.py:62
  132.0 6.0 %collective-permute-start.4 = (bf16[2,1,256,128]{3,2,1,0:T(8,128)(2,1)}, bf16[2,1,256,128]{3,2,1,0:T(8,128)(2,1)S(1)}, u32[]{:S(2)}, u32[]{:S(2)}) collective-permute-start(bf16[2,1,256,128]{3,2,1,0:T(8,128)(2,1)} %get-tuple-element.34), channel_id=1, source_target_pairs={{0,1},{1,2},{2,3},{3,0},{4,5},{5,6},{6,7},{7,4},{8,9},{9,10},{10,1... | collective-permute-start | bytes 393224 | tf_op jit(solution)/shard_map/ppermute | solution.py:95
  138.0 1.7 collective-permute-start.5
  140.4 17.7 %pack.6 = (bf16[2,1,256,128]{3,2,1,0:T(8,128)(2,1)}, bf16[2,1,256,128]{3,2,1,0:T(8,128)(2,1)}, bf16[2,1,256,128]{3,2,1,0:T(8,128)(2,1)}, bf16[2,1,256,128]{3,2,1,0:T(8,128)(2,1)}) custom-call(s32[2]{0:T(128)} %pad_add_fusion.place, bf16[256,2048]{1,0:T(8,128)(2,1)} %refs_1_.3), custom_call_target="tpu_custom_call" | custom-call | bytes 1048576 | tf_op jit(solution)/shard_map/pack/pallas_call | solution.py:62
  161.7 9.7 %merge_other.7 = bf16[4,1,256,128]{3,2,1,0:T(8,128)(2,1)} custom-call(s32[2]{0:T(128)} %pad_add_fusion.place, bf16[2,1,256,128]{3,2,1,0:T(8,128)(2,1)} %get-tuple-element.33.refs_0_, bf16[2,1,256,128]{3,2,1,0:T(8,128)(2,1)} %copy-done.34, bf16[2,1,256,128]{3,2,1,0:T(8,128)(2,1)} %copy-done.35, bf16[2,1,256,128]{3,2,1,0:T(8,128)(2,1)} %copy-done.36), custom_call_target="tpu_custom_call" | custom-call | bytes 524288 | tf_op jit(solution)/shard_map/merge_other/pallas_call | solution.py:73
  174.2 33.7 %pack.4 = (bf16[2,2,256,128]{3,2,1,0:T(8,128)(2,1)}, bf16[2,2,256,128]{3,2,1,0:T(8,128)(2,1)}, bf16[2,2,256,128]{3,2,1,0:T(8,128)(2,1)}, bf16[2,2,256,128]{3,2,1,0:T(8,128)(2,1)}) custom-call(s32[2]{0:T(128)} %pad_add_fusion.place, bf16[256,2048]{1,0:T(8,128)(2,1)} %refs_1_.2, bf16[256,2048]{1,0:T(8,128)(2,1)} %refs_1_.2), custom_call_target="tpu_custom_call" | custom-call | bytes 2097152 | tf_op jit(solution)/shard_map/pack/pallas_call | solution.py:62
  209.3 9.7 %merge_other.8 = bf16[4,1,256,128]{3,2,1,0:T(8,128)(2,1)} custom-call(s32[2]{0:T(128)} %pad_add_fusion.place, bf16[2,1,256,128]{3,2,1,0:T(8,128)(2,1)} %get-tuple-element.37.refs_0_, bf16[2,1,256,128]{3,2,1,0:T(8,128)(2,1)} %copy-done.31, bf16[2,1,256,128]{3,2,1,0:T(8,128)(2,1)} %copy-done.32, bf16[2,1,256,128]{3,2,1,0:T(8,128)(2,1)} %copy-done.33), custom_call_target="tpu_custom_call" | custom-call | bytes 524288 | tf_op jit(solution)/shard_map/merge_other/pallas_call | solution.py:73
  219.8 17.7 %merge_own.3 = bf16[1,2,4,256,128]{4,3,2,1,0:T(8,128)(2,1)} custom-call(s32[2]{0:T(128)} %pad_add_fusion.place, bf16[2,1,256,128]{3,2,1,0:T(8,128)(2,1)} %get-tuple-element.33.refs_0_, bf16[2,1,256,128]{3,2,1,0:T(8,128)(2,1)} %copy-done.34, bf16[2,1,256,128]{3,2,1,0:T(8,128)(2,1)} %copy-done.35, bf16[2,1,256,128]{3,2,1,0:T(8,128)(2,1)} %copy-done.36, ...), custom_call_target="tpu_custom_call" | custom-call | bytes 1048576 | tf_op jit(solution)/shard_map/merge_own/pallas_call | solution.py:91
  238.1 1.7 collective-permute-start.1
  240.5 2.5 collective-permute-start.2
  243.1 17.7 %merge_own.4 = bf16[1,2,4,256,128]{4,3,2,1,0:T(8,128)(2,1)} custom-call(s32[2]{0:T(128)} %pad_add_fusion.place, bf16[2,1,256,128]{3,2,1,0:T(8,128)(2,1)} %get-tuple-element.37.refs_0_, bf16[2,1,256,128]{3,2,1,0:T(8,128)(2,1)} %copy-done.31, bf16[2,1,256,128]{3,2,1,0:T(8,128)(2,1)} %copy-done.32, bf16[2,1,256,128]{3,2,1,0:T(8,128)(2,1)} %copy-done.33, ...), custom_call_target="tpu_custom_call" | custom-call | bytes 1048576 | tf_op jit(solution)/shard_map/merge_own/pallas_call | solution.py:91
  263.0 17.7 %merge_other.6 = bf16[4,2,256,128]{3,2,1,0:T(8,128)(2,1)} custom-call(s32[2]{0:T(128)} %pad_add_fusion.place, bf16[2,2,256,128]{3,2,1,0:T(8,128)(2,1)} %get-tuple-element.29.refs_0_, bf16[2,2,256,128]{3,2,1,0:T(8,128)(2,1)} %copy-done.3, bf16[2,2,256,128]{3,2,1,0:T(8,128)(2,1)} %copy-done.5, bf16[2,2,256,128]{3,2,1,0:T(8,128)(2,1)} %copy-done.7), custom_call_target="tpu_custom_call" | custom-call | bytes 1048576 | tf_op jit(solution)/shard_map/merge_other/pallas_call | solution.py:73
  283.8 1.9 slice.30
  292.2 3.6 collective-permute-done.16.refs_11_
  302.9 5.9 %collective-permute-done.11.refs_9_ = bf16[1024,128]{1,0:T(8,128)(2,1)} collective-permute-done((bf16[1024,128]{1,0:T(8,128)(2,1)}, bf16[1024,128]{1,0:T(8,128)(2,1)}, u32[]{:S(2)}, u32[]{:S(2)}) %collective-permute-start.11) | collective-permute-done | bytes 262176 | tf_op jit(solution)/shard_map/ppermute | solution.py:103
  308.8 9.0 %collective-permute-done.18.refs_13_ = bf16[1024,128]{1,0:T(8,128)(2,1)} collective-permute-done((bf16[1024,128]{1,0:T(8,128)(2,1)}, bf16[1024,128]{1,0:T(8,128)(2,1)}, u32[]{:S(2)}, u32[]{:S(2)}) %collective-permute-start.18) | collective-permute-done | bytes 262176 | tf_op jit(solution)/shard_map/ppermute | solution.py:103
  323.8 15.9 %attend.2 = (bf16[2,1,256,128]{3,2,1,0:T(8,128)(2,1)S(1)}, bf16[2,1,256,128]{3,2,1,0:T(8,128)(2,1)S(1)}, bf16[2,1,256,128]{3,2,1,0:T(8,128)(2,1)S(1)}, bf16[2,1,256,128]{3,2,1,0:T(8,128)(2,1)S(1)}) custom-call(s32[32,8]{1,0:T(8,128)S(1)} %fusion.8.table, bf16[2,2,256,128]{3,2,1,0:T(8,128)(2,1)S(1)} %copy-done.2, bf16[2,2,256,128]{3,2,1,0:T(8,128)(2,1)S(1)} %copy-done.4, ...), custom_call_target="tpu_custom_call" | custom-call | flops 536870912 | bytes 5242880 | tf_op jit(solution)/shard_map/attend/pallas_call | solution.py:208
  341.3 2.0 collective-permute-start.22
  343.4 15.8 %attend.3 = (bf16[2,1,256,128]{3,2,1,0:T(8,128)(2,1)S(1)}, bf16[2,1,256,128]{3,2,1,0:T(8,128)(2,1)S(1)}, bf16[2,1,256,128]{3,2,1,0:T(8,128)(2,1)S(1)}, bf16[2,1,256,128]{3,2,1,0:T(8,128)(2,1)S(1)}) custom-call(s32[32,8]{1,0:T(8,128)S(1)} %fusion.8.table, bf16[2,2,256,128]{3,2,1,0:T(8,128)(2,1)S(1)} %copy-done.2, bf16[2,2,256,128]{3,2,1,0:T(8,128)(2,1)S(1)} %copy-done.4, ...), custom_call_target="tpu_custom_call" | custom-call | flops 536870912 | bytes 5242880 | tf_op jit(solution)/shard_map/attend/pallas_call | solution.py:208
  359.9 1.8 collective-permute-start.31
  364.5 9.7 %merge_other.10 = bf16[4,1,256,128]{3,2,1,0:T(8,128)(2,1)} custom-call(s32[2]{0:T(128)} %pad_add_fusion.place, bf16[2,1,256,128]{3,2,1,0:T(8,128)(2,1)} %copy-done.11, bf16[2,1,256,128]{3,2,1,0:T(8,128)(2,1)} %copy-done.13, bf16[2,1,256,128]{3,2,1,0:T(8,128)(2,1)} %copy-done.15, bf16[2,1,256,128]{3,2,1,0:T(8,128)(2,1)} %copy-done.17), custom_call_target="tpu_custom_call" | custom-call | bytes 524288 | tf_op jit(solution)/shard_map/merge_other/pallas_call | solution.py:73
  375.1 9.7 %merge_other.11 = bf16[4,1,256,128]{3,2,1,0:T(8,128)(2,1)} custom-call(s32[2]{0:T(128)} %pad_add_fusion.place, bf16[2,1,256,128]{3,2,1,0:T(8,128)(2,1)} %copy-done.19, bf16[2,1,256,128]{3,2,1,0:T(8,128)(2,1)} %copy-done.21, bf16[2,1,256,128]{3,2,1,0:T(8,128)(2,1)} %copy-done.23, bf16[2,1,256,128]{3,2,1,0:T(8,128)(2,1)} %copy-done.25), custom_call_target="tpu_custom_call" | custom-call | bytes 524288 | tf_op jit(solution)/shard_map/merge_other/pallas_call | solution.py:73
  386.8 5.8 %copy-done = bf16[2048,4096]{1,0:T(8,128)(2,1)S(1)} copy-done((bf16[2048,4096]{1,0:T(8,128)(2,1)S(1)}, bf16[2048,4096]{1,0:T(8,128)(2,1)}, u32[]{:S(2)}) %copy-start) | copy-done | bytes 16777240
  399.8 8.9 %project.1 = bf16[256,4096]{1,0:T(8,128)(2,1)} custom-call(s32[2]{0:T(128)S(1)} %copy-done.27, bf16[2,1,256,128]{3,2,1,0:T(8,128)(2,1)S(1)} %copy-done.12, bf16[2,1,256,128]{3,2,1,0:T(8,128)(2,1)S(1)} %copy-done.14, bf16[2,1,256,128]{3,2,1,0:T(8,128)(2,1)S(1)} %copy-done.16, bf16[2,1,256,128]{3,2,1,0:T(8,128)(2,1)S(1)} %copy-done.18, ...), custom_call_target="tpu_custom_call" | custom-call | flops 4294967296 | bytes 19922944 | tf_op jit(solution)/shard_map/project/pallas_call | solution.py:259
  (157 shorter events, 55.5 us)
Async XLA Ops:
  34.5 12.6 %collective-permute-start.23 = (bf16[2,2,256,128]{3,2,1,0:T(8,128)(2,1)}, bf16[2,2,256,128]{3,2,1,0:T(8,128)(2,1)S(1)}, u32[]{:S(2)}, u32[]{:S(2)}) collective-permute-start(bf16[2,2,256,128]{3,2,1,0:T(8,128)(2,1)} %get-tuple-element.46), channel_id=1, source_target_pairs={{0,1},{1,2},{2,3},{3,0},{4,5},{5,6},{6,7},{7,4},{8,9},{9,10},{10,1... | collective-permute-start | bytes 786440 | tf_op jit(solution)/shard_map/ppermute | solution.py:95
  37.6 19.9 %collective-permute-start.24 = (bf16[2,2,256,128]{3,2,1,0:T(8,128)(2,1)}, bf16[2,2,256,128]{3,2,1,0:T(8,128)(2,1)S(1)}, u32[]{:S(2)}, u32[]{:S(2)}) collective-permute-start(bf16[2,2,256,128]{3,2,1,0:T(8,128)(2,1)} %get-tuple-element.47), channel_id=1, source_target_pairs={{0,2},{1,3},{2,0},{3,1},{4,6},{5,7},{6,4},{7,5},{8,10},{9,11},{10,... | collective-permute-start | bytes 786440 | tf_op jit(solution)/shard_map/ppermute | solution.py:95
  40.2 17.3 %collective-permute-start.25 = (bf16[2,2,256,128]{3,2,1,0:T(8,128)(2,1)}, bf16[2,2,256,128]{3,2,1,0:T(8,128)(2,1)S(1)}, u32[]{:S(2)}, u32[]{:S(2)}) collective-permute-start(bf16[2,2,256,128]{3,2,1,0:T(8,128)(2,1)} %get-tuple-element.48), channel_id=1, source_target_pairs={{0,3},{1,0},{2,1},{3,2},{4,7},{5,4},{6,5},{7,6},{8,11},{9,8},{10,9... | collective-permute-start | bytes 786440 | tf_op jit(solution)/shard_map/ppermute | solution.py:95
  112.7 168.1 %collective-permute-start.27 = (bf16[4096,128]{1,0:T(8,128)(2,1)}, bf16[4096,128]{1,0:T(8,128)(2,1)S(1)}, u32[]{:S(2)}, u32[]{:S(2)}) collective-permute-start(bf16[4096,128]{1,0:T(8,128)(2,1)} %bitcast.5), channel_id=1, source_target_pairs={{0,8},{4,12},{8,0},{12,4},{16,24},{20,28},{24,16},{28,20},{1,9},{5... | collective-permute-start | bytes 3145736 | tf_op jit(solution)/shard_map/ppermute | solution.py:103
  132.0 27.5 %collective-permute-start.4 = (bf16[2,1,256,128]{3,2,1,0:T(8,128)(2,1)}, bf16[2,1,256,128]{3,2,1,0:T(8,128)(2,1)S(1)}, u32[]{:S(2)}, u32[]{:S(2)}) collective-permute-start(bf16[2,1,256,128]{3,2,1,0:T(8,128)(2,1)} %get-tuple-element.34), channel_id=1, source_target_pairs={{0,1},{1,2},{2,3},{3,0},{4,5},{5,6},{6,7},{7,4},{8,9},{9,10},{10,1... | collective-permute-start | bytes 393224 | tf_op jit(solution)/shard_map/ppermute | solution.py:95
  138.0 23.0 %collective-permute-start.5 = (bf16[2,1,256,128]{3,2,1,0:T(8,128)(2,1)}, bf16[2,1,256,128]{3,2,1,0:T(8,128)(2,1)S(1)}, u32[]{:S(2)}, u32[]{:S(2)}) collective-permute-start(bf16[2,1,256,128]{3,2,1,0:T(8,128)(2,1)} %get-tuple-element.35), channel_id=1, source_target_pairs={{0,2},{1,3},{2,0},{3,1},{4,6},{5,7},{6,4},{7,5},{8,10},{9,11},{10,... | collective-permute-start | bytes 393224 | tf_op jit(solution)/shard_map/ppermute | solution.py:95
  139.7 21.3 %collective-permute-start.6 = (bf16[2,1,256,128]{3,2,1,0:T(8,128)(2,1)}, bf16[2,1,256,128]{3,2,1,0:T(8,128)(2,1)S(1)}, u32[]{:S(2)}, u32[]{:S(2)}) collective-permute-start(bf16[2,1,256,128]{3,2,1,0:T(8,128)(2,1)} %get-tuple-element.36), channel_id=1, source_target_pairs={{0,3},{1,0},{2,1},{3,2},{4,7},{5,4},{6,5},{7,6},{8,11},{9,8},{10,9... | collective-permute-start | bytes 393224 | tf_op jit(solution)/shard_map/ppermute | solution.py:95
  158.2 14.7 %collective-permute-start.12 = (bf16[2,1,256,128]{3,2,1,0:T(8,128)(2,1)}, bf16[2,1,256,128]{3,2,1,0:T(8,128)(2,1)S(1)}, u32[]{:S(2)}, u32[]{:S(2)}) collective-permute-start(bf16[2,1,256,128]{3,2,1,0:T(8,128)(2,1)} %get-tuple-element.38), channel_id=1, source_target_pairs={{0,1},{1,2},{2,3},{3,0},{4,5},{5,6},{6,7},{7,4},{8,9},{9,10},{10,1... | collective-permute-start | bytes 393224 | tf_op jit(solution)/shard_map/ppermute | solution.py:95
  159.5 123.6 %collective-permute-start.28 = (bf16[4096,128]{1,0:T(8,128)(2,1)}, bf16[4096,128]{1,0:T(8,128)(2,1)}, u32[]{:S(2)}, u32[]{:S(2)}) collective-permute-start(bf16[4096,128]{1,0:T(8,128)(2,1)} %bitcast.6), channel_id=1, source_target_pairs={{0,16},{4,20},{8,24},{12,28},{16,0},{20,4},{24,8},{28,12},{1,17},{... | collective-permute-start | bytes 3145736 | tf_op jit(solution)/shard_map/ppermute | solution.py:103
  171.5 47.6 %collective-permute-start.7 = (bf16[4,1,256,128]{3,2,1,0:T(8,128)(2,1)}, bf16[4,1,256,128]{3,2,1,0:T(8,128)(2,1)S(1)}, u32[]{:S(2)}, u32[]{:S(2)}) collective-permute-start(bf16[4,1,256,128]{3,2,1,0:T(8,128)(2,1)} %merge_other.7), channel_id=1, source_target_pairs={{0,4},{4,0},{8,12},{12,8},{16,20},{20,16},{24,28},{28,24},{1,5},{5... | collective-permute-start | bytes 786440 | tf_op jit(solution)/shard_map/ppermute | solution.py:99
  171.5 36.4 %collective-permute-start.13 = (bf16[2,1,256,128]{3,2,1,0:T(8,128)(2,1)}, bf16[2,1,256,128]{3,2,1,0:T(8,128)(2,1)S(1)}, u32[]{:S(2)}, u32[]{:S(2)}) collective-permute-start(bf16[2,1,256,128]{3,2,1,0:T(8,128)(2,1)} %get-tuple-element.39), channel_id=1, source_target_pairs={{0,2},{1,3},{2,0},{3,1},{4,6},{5,7},{6,4},{7,5},{8,10},{9,11},{10,... | collective-permute-start | bytes 393224 | tf_op jit(solution)/shard_map/ppermute | solution.py:95
  172.9 35.8 %collective-permute-start.14 = (bf16[2,1,256,128]{3,2,1,0:T(8,128)(2,1)}, bf16[2,1,256,128]{3,2,1,0:T(8,128)(2,1)S(1)}, u32[]{:S(2)}, u32[]{:S(2)}) collective-permute-start(bf16[2,1,256,128]{3,2,1,0:T(8,128)(2,1)} %get-tuple-element.40), channel_id=1, source_target_pairs={{0,3},{1,0},{2,1},{3,2},{4,7},{5,4},{6,5},{7,6},{8,11},{9,8},{10,9... | collective-permute-start | bytes 393224 | tf_op jit(solution)/shard_map/ppermute | solution.py:95
  208.0 30.2 %collective-permute-start = (bf16[2,2,256,128]{3,2,1,0:T(8,128)(2,1)}, bf16[2,2,256,128]{3,2,1,0:T(8,128)(2,1)S(1)}, u32[]{:S(2)}, u32[]{:S(2)}) collective-permute-start(bf16[2,2,256,128]{3,2,1,0:T(8,128)(2,1)} %get-tuple-element.30), channel_id=1, source_target_pairs={{0,1},{1,2},{2,3},{3,0},{4,5},{5,6},{6,7},{7,4},{8,9},{9,10},{10,1... | collective-permute-start | bytes 786440 | tf_op jit(solution)/shard_map/ppermute | solution.py:95
  219.0 20.8 %collective-permute-start.15 = (bf16[4,1,256,128]{3,2,1,0:T(8,128)(2,1)}, bf16[4,1,256,128]{3,2,1,0:T(8,128)(2,1)S(1)}, u32[]{:S(2)}, u32[]{:S(2)}) collective-permute-start(bf16[4,1,256,128]{3,2,1,0:T(8,128)(2,1)} %merge_other.8), channel_id=1, source_target_pairs={{0,4},{4,0},{8,12},{12,8},{16,20},{20,16},{24,28},{28,24},{1,5},{5... | collective-permute-start | bytes 786440 | tf_op jit(solution)/shard_map/ppermute | solution.py:99
  237.5 43.1 %collective-permute-start.9 = (bf16[2048,128]{1,0:T(8,128)(2,1)}, bf16[2048,128]{1,0:T(8,128)(2,1)S(1)}, u32[]{:S(2)}, u32[]{:S(2)}) collective-permute-start(bf16[2048,128]{1,0:T(8,128)(2,1)} %bitcast.8), channel_id=1, source_target_pairs={{0,16},{4,20},{8,24},{12,28},{16,0},{20,4},{24,8},{28,12},{1,17},{... | collective-permute-start | bytes 1572872 | tf_op jit(solution)/shard_map/ppermute | solution.py:103
  238.1 22.7 %collective-permute-start.1 = (bf16[2,2,256,128]{3,2,1,0:T(8,128)(2,1)}, bf16[2,2,256,128]{3,2,1,0:T(8,128)(2,1)S(1)}, u32[]{:S(2)}, u32[]{:S(2)}) collective-permute-start(bf16[2,2,256,128]{3,2,1,0:T(8,128)(2,1)} %get-tuple-element.31), channel_id=1, source_target_pairs={{0,2},{1,3},{2,0},{3,1},{4,6},{5,7},{6,4},{7,5},{8,10},{9,11},{10,... | collective-permute-start | bytes 786440 | tf_op jit(solution)/shard_map/ppermute | solution.py:95
  240.5 20.9 %collective-permute-start.2 = (bf16[2,2,256,128]{3,2,1,0:T(8,128)(2,1)}, bf16[2,2,256,128]{3,2,1,0:T(8,128)(2,1)S(1)}, u32[]{:S(2)}, u32[]{:S(2)}) collective-permute-start(bf16[2,2,256,128]{3,2,1,0:T(8,128)(2,1)} %get-tuple-element.32), channel_id=1, source_target_pairs={{0,3},{1,0},{2,1},{3,2},{4,7},{5,4},{6,5},{7,6},{8,11},{9,8},{10,9... | collective-permute-start | bytes 786440 | tf_op jit(solution)/shard_map/ppermute | solution.py:95
  260.8 25.7 %collective-permute-start.8 = (bf16[2048,128]{1,0:T(8,128)(2,1)}, bf16[2048,128]{1,0:T(8,128)(2,1)}, u32[]{:S(2)}, u32[]{:S(2)}) collective-permute-start(bf16[2048,128]{1,0:T(8,128)(2,1)} %bitcast.9), channel_id=1, source_target_pairs={{0,8},{4,12},{8,0},{12,4},{16,24},{20,28},{24,16},{28,20},{1,9},{5... | collective-permute-start | bytes 1572872 | tf_op jit(solution)/shard_map/ppermute | solution.py:103
  261.4 26.6 %collective-permute-start.17 = (bf16[2048,128]{1,0:T(8,128)(2,1)}, bf16[2048,128]{1,0:T(8,128)(2,1)}, u32[]{:S(2)}, u32[]{:S(2)}) collective-permute-start(bf16[2048,128]{1,0:T(8,128)(2,1)} %bitcast.11), channel_id=1, source_target_pairs={{0,16},{4,20},{8,24},{12,28},{16,0},{20,4},{24,8},{28,12},{1,17},{... | collective-permute-start | bytes 1572872 | tf_op jit(solution)/shard_map/ppermute | solution.py:103
  280.7 17.6 %collective-permute-start.3 = (bf16[4,2,256,128]{3,2,1,0:T(8,128)(2,1)}, bf16[4,2,256,128]{3,2,1,0:T(8,128)(2,1)S(1)}, u32[]{:S(2)}, u32[]{:S(2)}) collective-permute-start(bf16[4,2,256,128]{3,2,1,0:T(8,128)(2,1)} %merge_other.6), channel_id=1, source_target_pairs={{0,4},{4,0},{8,12},{12,8},{16,20},{20,16},{24,28},{28,24},{1,5},{5... | collective-permute-start | bytes 1572872 | tf_op jit(solution)/shard_map/ppermute | solution.py:99
  280.8 15.1 %collective-permute-start.16 = (bf16[2048,128]{1,0:T(8,128)(2,1)}, bf16[2048,128]{1,0:T(8,128)(2,1)}, u32[]{:S(2)}, u32[]{:S(2)}) collective-permute-start(bf16[2048,128]{1,0:T(8,128)(2,1)} %bitcast.12), channel_id=1, source_target_pairs={{0,8},{4,12},{8,0},{12,4},{16,24},{20,28},{24,16},{28,20},{1,9},{5... | collective-permute-start | bytes 1572872 | tf_op jit(solution)/shard_map/ppermute | solution.py:103
  283.1 18.3 %collective-permute-start.10 = (bf16[1024,128]{1,0:T(8,128)(2,1)}, bf16[1024,128]{1,0:T(8,128)(2,1)S(1)}, u32[]{:S(2)}, u32[]{:S(2)}) collective-permute-start(bf16[1024,128]{1,0:T(8,128)(2,1)} %slice.26), channel_id=1, source_target_pairs={{0,8},{4,12},{8,0},{12,4},{16,24},{20,28},{24,16},{28,20},{1,9},{5... | collective-permute-start | bytes 786440 | tf_op jit(solution)/shard_map/ppermute | solution.py:103
  286.6 56.8 %collective-permute-start.29 = (bf16[2048,128]{1,0:T(8,128)(2,1)}, bf16[2048,128]{1,0:T(8,128)(2,1)}, u32[]{:S(2)}, u32[]{:S(2)}) collective-permute-start(bf16[2048,128]{1,0:T(8,128)(2,1)} %slice.30), channel_id=1, source_target_pairs={{0,8},{4,12},{8,0},{12,4},{16,24},{20,28},{24,16},{28,20},{1,9},{5... | collective-permute-start | bytes 1572872 | tf_op jit(solution)/shard_map/ppermute | solution.py:103
  288.1 55.3 %collective-permute-start.30 = (bf16[2048,128]{1,0:T(8,128)(2,1)}, bf16[2048,128]{1,0:T(8,128)(2,1)}, u32[]{:S(2)}, u32[]{:S(2)}) collective-permute-start(bf16[2048,128]{1,0:T(8,128)(2,1)} %slice.31), channel_id=1, source_target_pairs={{0,16},{4,20},{8,24},{12,28},{16,0},{20,4},{24,8},{28,12},{1,17},{... | collective-permute-start | bytes 1572872 | tf_op jit(solution)/shard_map/ppermute | solution.py:103
  295.9 13.0 %collective-permute-start.11 = (bf16[1024,128]{1,0:T(8,128)(2,1)}, bf16[1024,128]{1,0:T(8,128)(2,1)}, u32[]{:S(2)}, u32[]{:S(2)}) collective-permute-start(bf16[1024,128]{1,0:T(8,128)(2,1)} %slice.27), channel_id=1, source_target_pairs={{0,16},{4,20},{8,24},{12,28},{16,0},{20,4},{24,8},{28,12},{1,17},{... | collective-permute-start | bytes 786440 | tf_op jit(solution)/shard_map/ppermute | solution.py:103
  298.2 19.6 %collective-permute-start.18 = (bf16[1024,128]{1,0:T(8,128)(2,1)}, bf16[1024,128]{1,0:T(8,128)(2,1)}, u32[]{:S(2)}, u32[]{:S(2)}) collective-permute-start(bf16[1024,128]{1,0:T(8,128)(2,1)} %slice.28), channel_id=1, source_target_pairs={{0,8},{4,12},{8,0},{12,4},{16,24},{20,28},{24,16},{28,20},{1,9},{5... | collective-permute-start | bytes 786440 | tf_op jit(solution)/shard_map/ppermute | solution.py:103
  301.4 16.5 %collective-permute-start.19 = (bf16[1024,128]{1,0:T(8,128)(2,1)}, bf16[1024,128]{1,0:T(8,128)(2,1)}, u32[]{:S(2)}, u32[]{:S(2)}) collective-permute-start(bf16[1024,128]{1,0:T(8,128)(2,1)} %slice.29), channel_id=1, source_target_pairs={{0,16},{4,20},{8,24},{12,28},{16,0},{20,4},{24,8},{28,12},{1,17},{... | collective-permute-start | bytes 786440 | tf_op jit(solution)/shard_map/ppermute | solution.py:103
  340.4 22.1 %collective-permute-start.20 = (bf16[2,1,256,128]{3,2,1,0:T(8,128)(2,1)S(1)}, bf16[2,1,256,128]{3,2,1,0:T(8,128)(2,1)S(1)}, u32[]{:S(2)}, u32[]{:S(2)}) collective-permute-start(bf16[2,1,256,128]{3,2,1,0:T(8,128)(2,1)S(1)} %get-tuple-element.42), channel_id=1, source_target_pairs={{0,3},{1,0},{2,1},{3,2},{4,7},{5,4},{6,5},{7,6},{8,11},{9,8},{10,9... | collective-permute-start | bytes 393224 | tf_op jit(solution)/shard_map/ppermute | solution.py:95
  340.9 22.9 %collective-permute-start.21 = (bf16[2,1,256,128]{3,2,1,0:T(8,128)(2,1)S(1)}, bf16[2,1,256,128]{3,2,1,0:T(8,128)(2,1)S(1)}, u32[]{:S(2)}, u32[]{:S(2)}) collective-permute-start(bf16[2,1,256,128]{3,2,1,0:T(8,128)(2,1)S(1)} %get-tuple-element.43), channel_id=1, source_target_pairs={{0,2},{1,3},{2,0},{3,1},{4,6},{5,7},{6,4},{7,5},{8,10},{9,11},{10,... | collective-permute-start | bytes 393224 | tf_op jit(solution)/shard_map/ppermute | solution.py:95
  341.3 22.5 %collective-permute-start.22 = (bf16[2,1,256,128]{3,2,1,0:T(8,128)(2,1)S(1)}, bf16[2,1,256,128]{3,2,1,0:T(8,128)(2,1)S(1)}, u32[]{:S(2)}, u32[]{:S(2)}) collective-permute-start(bf16[2,1,256,128]{3,2,1,0:T(8,128)(2,1)S(1)} %get-tuple-element.44), channel_id=1, source_target_pairs={{0,1},{1,2},{2,3},{3,0},{4,5},{5,6},{6,7},{7,4},{8,9},{9,10},{10,1... | collective-permute-start | bytes 393224 | tf_op jit(solution)/shard_map/ppermute | solution.py:95
  359.9 14.5 %collective-permute-start.31 = (bf16[2,1,256,128]{3,2,1,0:T(8,128)(2,1)S(1)}, bf16[2,1,256,128]{3,2,1,0:T(8,128)(2,1)S(1)}, u32[]{:S(2)}, u32[]{:S(2)}) collective-permute-start(bf16[2,1,256,128]{3,2,1,0:T(8,128)(2,1)S(1)} %get-tuple-element.50), channel_id=1, source_target_pairs={{0,3},{1,0},{2,1},{3,2},{4,7},{5,4},{6,5},{7,6},{8,11},{9,8},{10,9... | collective-permute-start | bytes 393224 | tf_op jit(solution)/shard_map/ppermute | solution.py:95
  361.7 12.7 %collective-permute-start.32 = (bf16[2,1,256,128]{3,2,1,0:T(8,128)(2,1)S(1)}, bf16[2,1,256,128]{3,2,1,0:T(8,128)(2,1)S(1)}, u32[]{:S(2)}, u32[]{:S(2)}) collective-permute-start(bf16[2,1,256,128]{3,2,1,0:T(8,128)(2,1)S(1)} %get-tuple-element.51), channel_id=1, source_target_pairs={{0,2},{1,3},{2,0},{3,1},{4,6},{5,7},{6,4},{7,5},{8,10},{9,11},{10,... | collective-permute-start | bytes 393224 | tf_op jit(solution)/shard_map/ppermute | solution.py:95
  (45 other events, 1053.9 us)

commit v2 on v0

v2 whole, which is shorter than its diff:
```python
import functools

import jax
import jax.numpy as jnp
from jax import lax
from jax.experimental import pallas as pl
from jax.experimental.pallas import tpu as pltpu
from jax.sharding import PartitionSpec as P

DH = 128
BLK = 64
GLOB = 2
RAND = 3
MIB = 1 << 20
LOG2E = 1.4426950408889634

ANY = pl.BlockSpec(memory_space=pl.ANY)
SMEM = pl.BlockSpec(memory_space=pltpu.SMEM)
VMEM = pl.BlockSpec(memory_space=pltpu.VMEM)


WHOLE = pltpu.CompilerParams(vmem_limit_bytes=60 * MIB)


def cost(us):
    return pl.CostEstimate(flops=us * 1_150_000_000, bytes_accessed=0, transcendentals=0)


def copy_all(pairs, sems):
    copies = [pltpu.make_async_copy(src, dst, sems.at[i]) for i, (src, dst) in enumerate(pairs)]
    for c in copies:
        c.start()
    for c in copies:
        c.wait()


def sides(n_u):
    return [(r, d) for d in range(n_u) for r in range(2)]


def share_at(place, r, d, n_u):
    z, core = place[0], place[1]
    return 2 * lax.rem(z + d + n_u, n_u) + (core if r == 0 else 1 - core)


def stage(n_u, hp, here=None, tensors=(), slots=(), after=()):
    n_s = 2 * n_u
    ins = [x for x in (here,) if x is not None] + list(tensors)
    T = tensors[0].shape[0] if tensors else here.shape[2]
    n_split = 0 if here is None else here.shape[1]
    nb = len(tensors)
    n_copies = n_s * (n_split + nb)
    n_in = len(ins) + len(after)
    shapes = [(n_s * T, DH)] * n_split + [(n_s, nb, T, DH)] * (nb > 0)

    def body(*refs):
        outs, sems = refs[n_in:-1], refs[-1]
        pairs = []
        for k in range(n_s):
            for i in range(n_split):
                pairs.append((refs[0].at[k, i], outs[i].at[pl.ds(k * T, T)]))
            for i in range(nb):
                cols = pl.ds((k * hp + slots[i]) * DH, DH)
                pairs.append((refs[len(ins) - nb + i].at[:, cols], outs[-1].at[k, i]))
        copy_all(pairs, sems)

    return pl.pallas_call(
        body,
        out_shape=[jax.ShapeDtypeStruct(shape, jnp.bfloat16) for shape in shapes],
        in_specs=[ANY] * n_in,
        out_specs=[VMEM] * len(shapes),
        scratch_shapes=[pltpu.SemaphoreType.DMA((n_copies,))],
        compiler_params=WHOLE,
        cost_estimate=cost(3),
        name="stage",
    )(*ins, *after)


def to_shares(x, n_c, n_u):
    groups = [
        [(2 * p + core) * n_u + z for z in range(n_u) for core in range(2)] for p in range(n_c // 2)
    ]
    return lax.all_to_all(
        x, ("ctx", "ulys"), split_axis=0, concat_axis=0, tiled=True, axis_index_groups=groups
    )


def send(x, r, d, n_c, n_u):
    if (r, d) == (0, 0):
        return x
    pairs = [(c * n_u + z, (c ^ r) * n_u + (z + d) % n_u) for c in range(n_c) for z in range(n_u)]
    return lax.ppermute(x, ("ctx", "ulys"), pairs)


def send_all(parts, n_c, n_u, sign):
    return [send(x, r, (sign * d) % n_u, n_c, n_u) for x, (r, d) in zip(parts, sides(n_u))]


def swap_chip(x, bit, n_c):
    return lax.ppermute(x, "ctx", [(i, i ^ (2 * bit)) for i in range(n_c)])


def gather_chips(first, second, n_c):
    n_p = n_c // 2
    bits = [1 << i for i in range(n_p.bit_length() - 1)]
    a, b = {0: first}, {0: second}
    for t in reversed(bits):
        a[t] = swap_chip(first, t, n_c)
    for t in bits:
        b[t] = swap_chip(second, t, n_c)
    for t in range(1, n_p):
        if t not in bits:
            low, high = t & -t, 1 << (t.bit_length() - 1)
            a[t] = swap_chip(a[t ^ low], low, n_c)
            b[t] = swap_chip(b[t ^ high], high, n_c)
    return [a[t] for t in range(n_p)], [b[t] for t in range(n_p)]


def attend(place, table, queries, q_index, keys, values, n_u, apart, after):
    n_s, _, T, _ = queries.shape
    n_q = n_s * T
    span = keys[0].shape[0]
    n_k = span * len(keys)
    n_rows, n_list = table.shape
    group = 2 * T // BLK
    arrays = [queries, *keys, *values]
    n_in, n_out = len(arrays), 2 * n_u if apart else 1
    n_refs = n_in + len(after)

    def body(place, table, *refs):
        ins, outs = refs[:n_in], refs[n_refs : n_refs + n_out]
        q_vm, k_vm, v_vm, o_vm, sems, out_sems = refs[n_refs + n_out :]
        pairs = []
        for k in range(n_s):
            pairs.append((ins[0].at[k, q_index], q_vm.at[pl.ds(k * T, T)]))
        for i, ref in enumerate(ins[1:]):
            vm, t = (k_vm, i) if i < len(keys) else (v_vm, i - len(keys))
            pairs.append((ref, vm.at[pl.ds(t * span, span)]))
        copy_all(pairs, sems)

        @pl.loop(0, n_rows // group)
        def _(step):
            rows = [step * group + g for g in range(group)]
            at = [[pl.multiple_of(table[r, j] * BLK, BLK) for j in range(n_list)] for r in rows]
            s = []
            for r, listed in zip(rows, at):
                q = q_vm[pl.ds(pl.multiple_of(r * BLK, BLK), BLK), :]
                k = jnp.concatenate([k_vm[pl.ds(a, BLK), :] for a in listed], axis=0)
                s.append(
                    lax.dot_general(
                        q, k, (((1,), (1,)), ((), ())), preferred_element_type=jnp.float32
                    )
                )
            s = jnp.concatenate(s, axis=0)
            e = jnp.exp2((s - jnp.max(s, axis=-1, keepdims=True)) * (DH**-0.5 * LOG2E))
            w = (e * (1.0 / jnp.sum(e, axis=-1, keepdims=True))).astype(jnp.bfloat16)
            o = []
            for g, listed in enumerate(at):
                v = jnp.concatenate([v_vm[pl.ds(a, BLK), :] for a in listed], axis=0)
                o.append(
                    jnp.dot(
                        w[g * BLK : (g + 1) * BLK], v, preferred_element_type=jnp.float32
                    ).astype(jnp.bfloat16)
                )
            o_vm[pl.ds(pl.multiple_of(step * 2 * T, 2 * T), 2 * T), :] = jnp.concatenate(o, axis=0)

        pairs = []
        if apart:
            for out, (r, d) in zip(outs, sides(n_u)):
                at = pl.multiple_of(share_at(place, r, -d, n_u) * T, T)
                pairs.append((o_vm.at[pl.ds(at, T)], out))
        else:
            for k in range(n_s):
                pairs.append((o_vm.at[pl.ds(k * T, T)], outs[0].at[k]))
        copy_all(pairs, out_sems)

    return pl.pallas_call(
        body,
        out_shape=[jax.ShapeDtypeStruct((T, DH) if apart else (n_s, T, DH), jnp.bfloat16)] * n_out,
        in_specs=[SMEM, SMEM] + [ANY] * n_refs,
        out_specs=[ANY] * n_out,
        scratch_shapes=[
            pltpu.VMEM((n_q, DH), jnp.bfloat16),
            pltpu.VMEM((n_k, DH), jnp.bfloat16),
            pltpu.VMEM((n_k, DH), jnp.bfloat16),
            pltpu.VMEM((n_q, DH), jnp.bfloat16),
            pltpu.SemaphoreType.DMA((n_s + n_in - 1,)),
            pltpu.SemaphoreType.DMA((n_s,)),
        ],
        compiler_params=WHOLE,
        cost_estimate=cost(8),
        name="attend",
    )(place, table, *arrays, *after)


def project(place, parts, slot, weight, n_u, hp, partial):
    apart, last, more = isinstance(parts, list), slot == hp - 1, partial is not None
    arrays = parts if apart else [parts]
    n_in = len(arrays)
    T = arrays[0].shape[-2]
    width = weight.shape[1]
    shares = 2 * n_u
    depth = shares * DH
    tile = width // 2
    n_tiles = width // tile
    kind = jnp.bfloat16 if last else jnp.float32

    def body(place, *refs):
        ins, w_ref = refs[:n_in], refs[n_in]
        out_ref, rows, w_vm, add_vm, out_vm, row_sems, w_sems, add_sems, out_sems = refs[-9:]
        put = []
        for i, (r, d) in enumerate(sides(n_u)):
            src, share = (ins[i], share_at(place, r, d, n_u)) if apart else (ins[0].at[i], i)
            cols = pl.ds(pl.multiple_of(share * DH, DH), DH)
            put.append(pltpu.make_async_copy(src, rows.at[:, cols], row_sems.at[i]))
        fetch = []
        for t in range(n_tiles):
            cols = pl.ds(t * tile, tile)
            fetch.append([])
            for k in range(shares):
                src = w_ref.at[pl.ds((k * hp + slot) * DH, DH), cols]
                dst = w_vm.at[pl.ds(k * DH, DH), cols]
                fetch[t].append(pltpu.make_async_copy(src, dst, w_sems.at[t, k]))
            if more:
                src = refs[n_in + 1].at[:, cols]
                fetch[t].append(pltpu.make_async_copy(src, add_vm.at[:, cols], add_sems.at[t]))
        for c in put + sum(fetch, []):
            c.start()
        for c in put:
            c.wait()
        send = []
        for t in range(n_tiles):
            cols = pl.ds(t * tile, tile)
            for c in fetch[t]:
                c.wait()
            total = jnp.dot(rows[...], w_vm[:, cols], preferred_element_type=jnp.float32)
            if more:
                total = total + add_vm[:, cols]
            out_vm[:, cols] = total.astype(kind)
            send.append(
                pltpu.make_async_copy(out_vm.at[:, cols], out_ref.at[:, cols], out_sems.at[t])
            )
            send[-1].start()
        for c in send:
            c.wait()

    return pl.pallas_call(
        body,
        out_shape=jax.ShapeDtypeStruct((T, width), kind),
        in_specs=[SMEM] + [ANY] * (n_in + 1 + more),
        out_specs=ANY,
        scratch_shapes=[
            pltpu.VMEM((T, depth), jnp.bfloat16),
            pltpu.VMEM((depth, width), jnp.bfloat16),
            pltpu.VMEM((T, width), jnp.float32),
            pltpu.VMEM((T, width), kind),
            pltpu.SemaphoreType.DMA((shares,)),
            pltpu.SemaphoreType.DMA((n_tiles, shares)),
            pltpu.SemaphoreType.DMA((n_tiles,)),
            pltpu.SemaphoreType.DMA((n_tiles,)),
        ],
        compiler_params=WHOLE,
        cost_estimate=cost(8),
        name="project",
    )(place, *arrays, weight, *([partial] * more))


def key_table(rand_blocks, chip, n_u, n_p, per):
    total = rand_blocks.shape[0]
    z = jnp.arange(n_u, dtype=jnp.int32)[:, None, None]
    core = jnp.arange(2, dtype=jnp.int32)[None, :, None]
    j = jnp.arange(per, dtype=jnp.int32)[None, None, :]
    mine = (((2 * chip + core) * n_u + z) * per + j).reshape(-1)
    window = jnp.stack([(mine - 1) % total, mine, (mine + 1) % total], axis=1)
    leading = jnp.broadcast_to(jnp.arange(GLOB, dtype=jnp.int32)[None, :], (mine.shape[0], GLOB))
    listed = jnp.concatenate([window, leading, rand_blocks[mine]], axis=1)
    device, inner = listed // per, listed % per
    zs, cs = device % n_u, device // n_u
    return ((((cs // 2) ^ chip) * n_u + zs) * 2 + cs % 2) * per + inner


def shards(queries, keys, values, rand_blocks, out_weight):
    n_c, n_u = lax.axis_size("ctx"), lax.axis_size("ulys")
    T, lanes = queries.shape
    hp = lanes // DH // (2 * n_u)
    c, z = lax.axis_index("ctx"), lax.axis_index("ulys")
    chip, core = c // 2, c % 2
    place = jnp.stack([z, core]).astype(jnp.int32)
    table = key_table(rand_blocks, chip, n_u, n_c // 2, T // BLK)

    kv, after = [], ()
    (packed,) = stage(n_u, hp, None, [keys, values], [0, 0])
    for h in range(hp):
        here = to_shares(packed, n_c, n_u)
        if h < hp - 1:
            tensors, slots = [keys, values], [h + 1, h + 1]
        else:
            tensors, slots = [queries] * hp, list(range(hp))
        first, second, packed = stage(n_u, hp, here, tensors, slots, (table, *after))
        kv.append(gather_chips(first, second, n_c))
        after = [side[1 << i] for side in kv[-1] for i in range((n_c // 2).bit_length() - 1)]
    q_here = to_shares(packed, n_c, n_u)

    total = None
    for h in range(hp):
        last = h == hp - 1
        parts = attend(place, table, q_here, h, *kv[h], n_u, last, after)
        parts = send_all(parts, n_c, n_u, -1) if last else to_shares(parts[0], n_c, n_u)
        total = project(place, parts, h, out_weight, n_u, hp, total)
    return total


def solution(mesh):
    return jax.shard_map(
        shards,
        mesh=mesh,
        in_specs=(
            P(("ctx", "ulys"), None),
            P(("ctx", "ulys"), None),
            P(("ctx", "ulys"), None),
            P(),
            P(),
        ),
        out_specs=P(("ctx", "ulys"), None),
        check_vma=False,
    )
```

time: 367 us -> 169 us (0.46)
  local copies, waits for them, and re-layouts: 97.5 us -> 6.82 us
  waiting for transfers between devices: 168 us -> 77.4 us
  Pallas kernels: 0 us -> 40.9 us
  blocking collectives: 30.6 us -> 0 us
  matrix products: 25.6 us -> 0 us
  starting transfers between devices: 16.1 us -> 40.9 us
  other arithmetic: 15.1 us -> 1.47 us
  between operations: 13.6 us -> 0.2 us
    all_gather x1 -> x0, waiting for transfers between devices: 87.9 us -> none  [shards(): lax.all_gather(paired, 'ctx', axis=1, tiled=True)]
    ppermute x2 -> x19, waiting for transfers between devices: 0.01 us -> 52.6 us  [the longest x12 52 us: swap_chip(): return lax.ppermute(x, 'ctx', [(i, i ^ 2 * bit) for i in range(n_c)])]
    all_to_all x3 -> x4, waiting for transfers between devices: 67.5 us -> 24.9 us  [to_shares(): lax.all_to_all(x, ('ctx', 'ulys'), split_axis=0, concat_axis=0, tiled=Tru...]
    pallas_call x0 -> x7, Pallas kernels: none -> 40.9 us  [the longest x2 16.6 us: project(): pl.pallas_call(body, out_shape=jax.ShapeDtypeStruct((T, width), kind), in...]
    gather x1, local copies, waits for them, and re-layouts: 37.6 us -> 0.58 us  [key_table(): listed = jnp.concatenate([window, leading, rand_blocks[mine]], axis=1)]
    all_to_all x1 -> x0, blocking collectives: 30.6 us -> none  [shards(): lax.all_to_all(attended, 'ulys', split_axis=0, concat_axis=1, tiled=True)]
    dot_general x3 -> x0, matrix products: 25.6 us -> none  [the longest x1 11.5 us: shards(): jnp.dot(by_token, out_weight, preferred_element_type=jnp.float32)]
    squeeze x2 -> x0, local copies, waits for them, and re-layouts: 25.1 us -> none  [the longest x1 12.6 us: shards(): listed[0]]
  transfers between devices with their start and end apart: 7 -> 23, of which waited for: 5 -> 11; matrix products, arithmetic and copies ran while one was open for 5% -> 1% of each run, Pallas kernels for 0% -> 14%
where the time goes in v2:
time: 169 us; the launch traced here: 168 us
  waiting for transfers between devices  77.4 us (46%)
  Pallas kernels  40.9 us (24%)
  starting transfers between devices  40.9 us (24%)
  local copies, waits for them, and re-layouts  6.82 us (4%)
    ppermute x12, waiting for transfers between devices, swap_chip(): return lax.ppermute(x, 'ctx', [(i, i ^ 2 * bit) for i in range(n_c)])  52 us
    all_to_all x4, waiting for transfers between devices, to_shares(): lax.all_to_all(x, ('ctx', 'ulys'), split_axis=0, concat_axis=0, tiled=Tru...  24.9 us
    all_to_all x4, starting transfers between devices, to_shares(): lax.all_to_all(x, ('ctx', 'ulys'), split_axis=0, concat_axis=0, tiled=Tru...  19.9 us
    pallas_call x2, Pallas kernels, project(): pl.pallas_call(body, out_shape=jax.ShapeDtypeStruct((T, width), kind), in...  16.6 us
    pallas_call x2, Pallas kernels, attend(): pl.pallas_call(body, out_shape=[jax.ShapeDtypeStruct((T, DH) if apart els...  15.5 us
    ppermute x12, starting transfers between devices, swap_chip(): return lax.ppermute(x, 'ctx', [(i, i ^ 2 * bit) for i in range(n_c)])  12.3 us
    pallas_call x3, Pallas kernels, stage(): pl.pallas_call(body, out_shape=[jax.ShapeDtypeStruct(shape, jnp.bfloat16)...  8.78 us
    ppermute x7, starting transfers between devices, send(): return lax.ppermute(x, ('ctx', 'ulys'), pairs)  8.75 us
  transfers between devices with their start and end apart: 23, of which 11 were waited for; matrix products, arithmetic and copies ran while one was open for 1% of the time, Pallas kernels for 14%

profile of v2, /device:TPU:0, one launch (start us, length us, event | category | flops | bytes accessed | tf_op | source)
XLA Modules:
  0.0 167.7 jit_solution(4737987785406210773)
XLA Ops:
  0.0 2.4 %stage.3 = bf16[8,2,256,128]{3,2,1,0:T(8,128)(2,1)} custom-call(bf16[256,2048]{1,0:T(8,128)(2,1)} %refs_1_.5, bf16[256,2048]{1,0:T(8,128)(2,1)} %refs_2_.2), custom_call_target="tpu_custom_call" | custom-call | flops 3449999872 | tf_op jit(solution)/shard_map/stage/pallas_call | solution.py:67
  2.4 6.3 %all-to-all-start = ((bf16[8,2,256,128]{3,2,1,0:T(8,128)(2,1)}), bf16[8,2,256,128]{3,2,1,0:T(8,128)(2,1)S(1)}, u32[]{:S(2)}, u32[]{:S(2)}) async-start(bf16[8,2,256,128]{3,2,1,0:T(8,128)(2,1)} %stage.3), calls=%async_computation | async-start | bytes 2097152 | tf_op jit(solution)/shard_map/all_to_all | solution.py:83
  10.5 24.8 %all-to-all-done.refs_0_ = bf16[8,2,256,128]{3,2,1,0:T(8,128)(2,1)S(1)} async-done(((bf16[8,2,256,128]{3,2,1,0:T(8,128)(2,1)}), bf16[8,2,256,128]{3,2,1,0:T(8,128)(2,1)S(1)}, u32[]{:S(2)}, u32[]{:S(2)}) %all-to-all-start) | async-done | bytes 1048608 | tf_op jit(solution)/shard_map/all_to_all | solution.py:83
  35.3 1.0 copy-done.1
  36.3 3.2 %stage.4 = (bf16[2048,128]{1,0:T(8,128)(2,1)}, bf16[2048,128]{1,0:T(8,128)(2,1)}, bf16[8,2,256,128]{3,2,1,0:T(8,128)(2,1)}) custom-call(bf16[8,2,256,128]{3,2,1,0:T(8,128)(2,1)} %copy-done.1, bf16[256,2048]{1,0:T(8,128)(2,1)} %refs_1_.5, bf16[256,2048]{1,0:T(8,128)(2,1)} %refs_2_.2, s32[32,8]{1,0:T(8,128)} %fusion.8.refs_3_.table), custom_call_target="tpu_custom_call" | custom-call | flops 3449999872 | tf_op jit(solution)/shard_map/stage/pallas_call | solution.py:67
  39.5 3.6 %all-to-all-start.1 = ((bf16[8,2,256,128]{3,2,1,0:T(8,128)(2,1)}), bf16[8,2,256,128]{3,2,1,0:T(8,128)(2,1)S(1)}, u32[]{:S(2)}, u32[]{:S(2)}) async-start(bf16[8,2,256,128]{3,2,1,0:T(8,128)(2,1)} %get-tuple-element.19), calls=%async_computation.1 | async-start | bytes 2097152 | tf_op jit(solution)/shard_map/all_to_all | solution.py:83
  43.1 1.6 collective-permute-start
  44.6 1.5 collective-permute-start.1
  47.2 10.9 %collective-permute-done.refs_4_.refs_2_ = bf16[2048,128]{1,0:T(8,128)(2,1)S(1)} collective-permute-done((bf16[2048,128]{1,0:T(8,128)(2,1)}, bf16[2048,128]{1,0:T(8,128)(2,1)S(1)}, u32[]{:S(2)}, u32[]{:S(2)}) %collective-permute-start) | collective-permute-done | bytes 524320 | tf_op jit(solution)/shard_map/ppermute | solution.py:100
  58.1 1.5 collective-permute-done.1.refs_5_.refs_3_
  59.6 9.1 %collective-permute-done.2.refs_6_ = bf16[2048,128]{1,0:T(8,128)(2,1)S(1)} collective-permute-done((bf16[2048,128]{1,0:T(8,128)(2,1)}, bf16[2048,128]{1,0:T(8,128)(2,1)S(1)}, u32[]{:S(2)}, u32[]{:S(2)}) %collective-permute-start.2) | collective-permute-done | bytes 524320 | tf_op jit(solution)/shard_map/ppermute | solution.py:100
  68.8 1.2 collective-permute-done.3.refs_7_
  70.0 0.8 copy-done.8
  70.8 1.0 copy-done.2
  71.8 3.2 %stage.5 = (bf16[2048,128]{1,0:T(8,128)(2,1)}, bf16[2048,128]{1,0:T(8,128)(2,1)}, bf16[8,2,256,128]{3,2,1,0:T(8,128)(2,1)}) custom-call(bf16[8,2,256,128]{3,2,1,0:T(8,128)(2,1)} %copy-done.2, bf16[256,2048]{1,0:T(8,128)(2,1)} %refs_2_.3, bf16[256,2048]{1,0:T(8,128)(2,1)} %refs_2_.3, s32[32,8]{1,0:T(8,128)} %fusion.8.refs_3_.table, ...), custom_call_target="tpu_custom_call" | custom-call | flops 3449999872 | tf_op jit(solution)/shard_map/stage/pallas_call | solution.py:67
  75.0 4.8 %all-to-all-start.2 = ((bf16[8,2,256,128]{3,2,1,0:T(8,128)(2,1)}), bf16[8,2,256,128]{3,2,1,0:T(8,128)(2,1)S(1)}, u32[]{:S(2)}, u32[]{:S(2)}) async-start(bf16[8,2,256,128]{3,2,1,0:T(8,128)(2,1)} %get-tuple-element.22), calls=%async_computation.2 | async-start | bytes 2097152 | tf_op jit(solution)/shard_map/all_to_all | solution.py:83
  80.3 1.5 collective-permute-start.5
  81.8 1.5 collective-permute-start.7
  84.4 10.4 %collective-permute-done.17.refs_4_ = bf16[2048,128]{1,0:T(8,128)(2,1)} collective-permute-done((bf16[2048,128]{1,0:T(8,128)(2,1)}, bf16[2048,128]{1,0:T(8,128)(2,1)}, u32[]{:S(2)}, u32[]{:S(2)}) %collective-permute-start.17) | collective-permute-done | bytes 524320 | tf_op jit(solution)/shard_map/ppermute | solution.py:100
  94.8 1.5 collective-permute-start.8
  97.5 8.5 %collective-permute-done.7.refs_6_.refs_11_ = bf16[2048,128]{1,0:T(8,128)(2,1)S(1)} collective-permute-done((bf16[2048,128]{1,0:T(8,128)(2,1)}, bf16[2048,128]{1,0:T(8,128)(2,1)S(1)}, u32[]{:S(2)}, u32[]{:S(2)}) %collective-permute-start.7) | collective-permute-done | bytes 524320 | tf_op jit(solution)/shard_map/ppermute | solution.py:100
  105.9 1.5 collective-permute-start.9
  107.5 9.7 %collective-permute-done.4.refs_2_.refs_9_ = bf16[2048,128]{1,0:T(8,128)(2,1)S(1)} collective-permute-done((bf16[2048,128]{1,0:T(8,128)(2,1)}, bf16[2048,128]{1,0:T(8,128)(2,1)S(1)}, u32[]{:S(2)}, u32[]{:S(2)}) %collective-permute-start.4) | collective-permute-done | bytes 524320 | tf_op jit(solution)/shard_map/ppermute | solution.py:100
  118.5 1.0 copy-done
  119.5 7.8 %attend.3 = bf16[8,256,128]{2,1,0:T(8,128)(2,1)} custom-call(s32[2]{0:T(128)} %pad_add_fusion.place, s32[32,8]{1,0:T(8,128)} %fusion.8.refs_3_.table, bf16[8,2,256,128]{3,2,1,0:T(8,128)(2,1)} %copy-done, bf16[2048,128]{1,0:T(8,128)(2,1)} %get-tuple-element.20.refs_1_, bf16[2048,128]{1,0:T(8,128)(2,1)} %copy-done.5, bf16[2048,128]{1,0:T(8,128)(2,1)} %copy-done.6, ...), custom_call_target="tpu_custom_call" | custom-call | flops 9200000000 | tf_op jit(solution)/shard_map/attend/pallas_call | solution.py:177
  127.3 5.2 %all-to-all-start.3 = ((bf16[8,256,128]{2,1,0:T(8,128)(2,1)}), bf16[8,256,128]{2,1,0:T(8,128)(2,1)S(1)}, u32[]{:S(2)}, u32[]{:S(2)}) async-start(bf16[8,256,128]{2,1,0:T(8,128)(2,1)} %attend.3), calls=%async_computation.3 | async-start | bytes 1048576 | tf_op jit(solution)/shard_map/all_to_all | solution.py:83
  132.5 7.8 %attend.2 = (bf16[256,128]{1,0:T(8,128)(2,1)}, bf16[256,128]{1,0:T(8,128)(2,1)}, bf16[256,128]{1,0:T(8,128)(2,1)}, bf16[256,128]{1,0:T(8,128)(2,1)}, bf16[256,12...) custom-call(s32[2]{0:T(128)} %pad_add_fusion.place, ...), custom_call_target="tpu_custom_call" | custom-call | flops 9200000000 | tf_op jit(solution)/shard_map/attend/pallas_call | solution.py:177
  140.8 3.5 %collective-permute-start.11 = (bf16[256,128]{1,0:T(8,128)(2,1)}, bf16[256,128]{1,0:T(8,128)(2,1)S(1)}, u32[]{:S(2)}, u32[]{:S(2)}) collective-permute-start(bf16[256,128]{1,0:T(8,128)(2,1)} %get-tuple-element.27), channel_id=1, source_target_pairs={{0,3},{1,0},{2,1},{3,2},{4,7},{5,4},{6,5},{7,6},{8,11},{9,8},{10,9... | collective-permute-start | bytes 196616 | tf_op jit(solution)/shard_map/ppermute | solution.py:92
  144.5 2.7 %collective-permute-start.14 = (bf16[256,128]{1,0:T(8,128)(2,1)}, bf16[256,128]{1,0:T(8,128)(2,1)S(1)}, u32[]{:S(2)}, u32[]{:S(2)}) collective-permute-start(bf16[256,128]{1,0:T(8,128)(2,1)} %get-tuple-element.30), channel_id=1, source_target_pairs={{0,6},{1,7},{2,4},{3,5},{4,2},{5,3},{6,0},{7,1},{8,14},{9,15},{10,... | collective-permute-start | bytes 196616 | tf_op jit(solution)/shard_map/ppermute | solution.py:92
  147.2 1.5 collective-permute-start.15
  149.8 8.1 %project.2.refs_9_ = f32[256,4096]{1,0:T(8,128)} custom-call(s32[2]{0:T(128)} %pad_add_fusion.place, bf16[8,256,128]{2,1,0:T(8,128)(2,1)} %copy-done.3, bf16[2048,4096]{1,0:T(8,128)(2,1)} %refs_8_.1), custom_call_target="tpu_custom_call" | custom-call | flops 9200000000 | tf_op jit(solution)/shard_map/project/pallas_call | solution.py:247
  159.2 8.5 %project.3 = bf16[256,4096]{1,0:T(8,128)(2,1)} custom-call(s32[2]{0:T(128)} %pad_add_fusion.place, bf16[256,128]{1,0:T(8,128)(2,1)} %get-tuple-element.25.refs_0_, bf16[256,128]{1,0:T(8,128)(2,1)} %copy-done.13, bf16[256,128]{1,0:T(8,128)(2,1)} %copy-done.14, bf16[256,128]{1,0:T(8,128)(2,1)} %copy-done.15, bf16[256,128]{1,0:T(8,128)(2,1)} %copy-done.16, ...), custom_call_target="tpu_custom_call" | custom-call | flops 9200000000 | tf_op jit(solution)/shard_map/project/pallas_call | solution.py:247
  (73 shorter events, 10.0 us)
Async XLA Ops:
  0.0 8.9 %copy-start.4 = (s32[128,3]{0,1:T(4,128)S(1)}, s32[128,3]{0,1:T(4,128)}, u32[]{:S(2)}) copy-start(s32[128,3]{0,1:T(4,128)} %param.8) | copy-start | bytes 4612
  2.4 32.9 %all-to-all-start = ((bf16[8,2,256,128]{3,2,1,0:T(8,128)(2,1)}), bf16[8,2,256,128]{3,2,1,0:T(8,128)(2,1)S(1)}, u32[]{:S(2)}, u32[]{:S(2)}) async-start(bf16[8,2,256,128]{3,2,1,0:T(8,128)(2,1)} %stage.3), calls=%async_computation | async-start | bytes 2097152 | tf_op jit(solution)/shard_map/all_to_all | solution.py:83
  35.3 1.0 copy-start.1
  39.5 30.5 %all-to-all-start.1 = ((bf16[8,2,256,128]{3,2,1,0:T(8,128)(2,1)}), bf16[8,2,256,128]{3,2,1,0:T(8,128)(2,1)S(1)}, u32[]{:S(2)}, u32[]{:S(2)}) async-start(bf16[8,2,256,128]{3,2,1,0:T(8,128)(2,1)} %get-tuple-element.19), calls=%async_computation.1 | async-start | bytes 2097152 | tf_op jit(solution)/shard_map/all_to_all | solution.py:83
  43.1 15.0 %collective-permute-start = (bf16[2048,128]{1,0:T(8,128)(2,1)}, bf16[2048,128]{1,0:T(8,128)(2,1)S(1)}, u32[]{:S(2)}, u32[]{:S(2)}) collective-permute-start(bf16[2048,128]{1,0:T(8,128)(2,1)} %get-tuple-element.20.refs_1_), channel_id=1, source_target_pairs={{0,8},{4,12},{8,0},{12,4},{16,24},{20,28},{24,16},{28,20},{1,9},{5... | collective-permute-start | bytes 1572872 | tf_op jit(solution)/shard_map/ppermute | solution.py:100
  44.6 15.0 %collective-permute-start.1 = (bf16[2048,128]{1,0:T(8,128)(2,1)}, bf16[2048,128]{1,0:T(8,128)(2,1)S(1)}, u32[]{:S(2)}, u32[]{:S(2)}) collective-permute-start(bf16[2048,128]{1,0:T(8,128)(2,1)} %get-tuple-element.20.refs_1_), channel_id=1, source_target_pairs={{0,16},{4,20},{8,24},{12,28},{16,0},{20,4},{24,8},{28,12},{1,17},{... | collective-permute-start | bytes 1572872 | tf_op jit(solution)/shard_map/ppermute | solution.py:100
  46.2 22.6 %collective-permute-start.2 = (bf16[2048,128]{1,0:T(8,128)(2,1)}, bf16[2048,128]{1,0:T(8,128)(2,1)S(1)}, u32[]{:S(2)}, u32[]{:S(2)}) collective-permute-start(bf16[2048,128]{1,0:T(8,128)(2,1)} %get-tuple-element.21.refs_5_), channel_id=1, source_target_pairs={{0,8},{4,12},{8,0},{12,4},{16,24},{20,28},{24,16},{28,20},{1,9},{5... | collective-permute-start | bytes 1572872 | tf_op jit(solution)/shard_map/ppermute | solution.py:100
  46.7 23.3 %collective-permute-start.3 = (bf16[2048,128]{1,0:T(8,128)(2,1)}, bf16[2048,128]{1,0:T(8,128)(2,1)S(1)}, u32[]{:S(2)}, u32[]{:S(2)}) collective-permute-start(bf16[2048,128]{1,0:T(8,128)(2,1)} %get-tuple-element.21.refs_5_), channel_id=1, source_target_pairs={{0,16},{4,20},{8,24},{12,28},{16,0},{20,4},{24,8},{28,12},{1,17},{... | collective-permute-start | bytes 1572872 | tf_op jit(solution)/shard_map/ppermute | solution.py:100
  58.1 11.9 %copy-start.5 = (bf16[2048,128]{1,0:T(8,128)(2,1)}, bf16[2048,128]{1,0:T(8,128)(2,1)S(1)}, u32[]{:S(2)}) copy-start(bf16[2048,128]{1,0:T(8,128)(2,1)S(1)} %collective-permute-done.refs_4_.refs_2_) | copy-start | bytes 1572868
  59.6 10.4 %copy-start.6 = (bf16[2048,128]{1,0:T(8,128)(2,1)}, bf16[2048,128]{1,0:T(8,128)(2,1)S(1)}, u32[]{:S(2)}) copy-start(bf16[2048,128]{1,0:T(8,128)(2,1)S(1)} %collective-permute-done.1.refs_5_.refs_3_) | copy-start | bytes 1572868
  68.8 1.2 copy-start.7
  75.0 42.8 %all-to-all-start.2 = ((bf16[8,2,256,128]{3,2,1,0:T(8,128)(2,1)}), bf16[8,2,256,128]{3,2,1,0:T(8,128)(2,1)S(1)}, u32[]{:S(2)}, u32[]{:S(2)}) async-start(bf16[8,2,256,128]{3,2,1,0:T(8,128)(2,1)} %get-tuple-element.22), calls=%async_computation.2 | async-start | bytes 2097152 | tf_op jit(solution)/shard_map/all_to_all | solution.py:83
  79.8 15.0 %collective-permute-start.17 = (bf16[2048,128]{1,0:T(8,128)(2,1)}, bf16[2048,128]{1,0:T(8,128)(2,1)}, u32[]{:S(2)}, u32[]{:S(2)}) collective-permute-start(bf16[2048,128]{1,0:T(8,128)(2,1)} %copy-done.6), channel_id=1, source_target_pairs={{0,8},{4,12},{8,0},{12,4},{16,24},{20,28},{24,16},{28,20},{1,9},{5... | collective-permute-start | bytes 1572872 | tf_op jit(solution)/shard_map/ppermute | solution.py:100
  80.3 16.6 %collective-permute-start.5 = (bf16[2048,128]{1,0:T(8,128)(2,1)}, bf16[2048,128]{1,0:T(8,128)(2,1)S(1)}, u32[]{:S(2)}, u32[]{:S(2)}) collective-permute-start(bf16[2048,128]{1,0:T(8,128)(2,1)} %get-tuple-element.23.refs_1_), channel_id=1, source_target_pairs={{0,16},{4,20},{8,24},{12,28},{16,0},{20,4},{24,8},{28,12},{1,17},{... | collective-permute-start | bytes 1572872 | tf_op jit(solution)/shard_map/ppermute | solution.py:100
  81.8 24.1 %collective-permute-start.7 = (bf16[2048,128]{1,0:T(8,128)(2,1)}, bf16[2048,128]{1,0:T(8,128)(2,1)S(1)}, u32[]{:S(2)}, u32[]{:S(2)}) collective-permute-start(bf16[2048,128]{1,0:T(8,128)(2,1)} %get-tuple-element.24.refs_5_), channel_id=1, source_target_pairs={{0,8},{4,12},{8,0},{12,4},{16,24},{20,28},{24,16},{28,20},{1,9},{5... | collective-permute-start | bytes 1572872 | tf_op jit(solution)/shard_map/ppermute | solution.py:100
  83.3 24.1 %collective-permute-start.18 = (bf16[2048,128]{1,0:T(8,128)(2,1)}, bf16[2048,128]{1,0:T(8,128)(2,1)}, u32[]{:S(2)}, u32[]{:S(2)}) collective-permute-start(bf16[2048,128]{1,0:T(8,128)(2,1)} %copy-done.7), channel_id=1, source_target_pairs={{0,16},{4,20},{8,24},{12,28},{16,0},{20,4},{24,8},{28,12},{1,17},{... | collective-permute-start | bytes 1572872 | tf_op jit(solution)/shard_map/ppermute | solution.py:100
  83.8 33.3 %collective-permute-start.4 = (bf16[2048,128]{1,0:T(8,128)(2,1)}, bf16[2048,128]{1,0:T(8,128)(2,1)S(1)}, u32[]{:S(2)}, u32[]{:S(2)}) collective-permute-start(bf16[2048,128]{1,0:T(8,128)(2,1)} %get-tuple-element.23.refs_1_), channel_id=1, source_target_pairs={{0,8},{4,12},{8,0},{12,4},{16,24},{20,28},{24,16},{28,20},{1,9},{5... | collective-permute-start | bytes 1572872 | tf_op jit(solution)/shard_map/ppermute | solution.py:100
  94.8 22.9 %collective-permute-start.8 = (bf16[2048,128]{1,0:T(8,128)(2,1)}, bf16[2048,128]{1,0:T(8,128)(2,1)S(1)}, u32[]{:S(2)}, u32[]{:S(2)}) collective-permute-start(bf16[2048,128]{1,0:T(8,128)(2,1)} %get-tuple-element.24.refs_5_), channel_id=1, source_target_pairs={{0,16},{4,20},{8,24},{12,28},{16,0},{20,4},{24,8},{28,12},{1,17},{... | collective-permute-start | bytes 1572872 | tf_op jit(solution)/shard_map/ppermute | solution.py:100
  96.9 20.8 %copy-start.9 = (bf16[2048,128]{1,0:T(8,128)(2,1)}, bf16[2048,128]{1,0:T(8,128)(2,1)S(1)}, u32[]{:S(2)}) copy-start(bf16[2048,128]{1,0:T(8,128)(2,1)S(1)} %collective-permute-done.5.refs_3_.refs_10_) | copy-start | bytes 1572868
  96.9 35.5 %collective-permute-start.6 = (bf16[2048,128]{1,0:T(8,128)(2,1)S(1)}, bf16[2048,128]{1,0:T(8,128)(2,1)}, u32[]{:S(2)}, u32[]{:S(2)}) collective-permute-start(bf16[2048,128]{1,0:T(8,128)(2,1)S(1)} %collective-permute-done.5.refs_3_.refs_10_), channel_id=1, source_target_pairs={{0,8},{4,12},{8,0},{12,4},{16,24},{20,28},{24,16},{28,20},{1,9},{5... | collective-permute-start | bytes 1572872 | tf_op jit(solution)/shard_map/ppermute | solution.py:100
  105.9 11.8 %copy-start.10 = (bf16[2048,128]{1,0:T(8,128)(2,1)}, bf16[2048,128]{1,0:T(8,128)(2,1)S(1)}, u32[]{:S(2)}) copy-start(bf16[2048,128]{1,0:T(8,128)(2,1)S(1)} %collective-permute-done.7.refs_6_.refs_11_) | copy-start | bytes 1572868
  105.9 26.5 %collective-permute-start.9 = (bf16[2048,128]{1,0:T(8,128)(2,1)S(1)}, bf16[2048,128]{1,0:T(8,128)(2,1)}, u32[]{:S(2)}, u32[]{:S(2)}) collective-permute-start(bf16[2048,128]{1,0:T(8,128)(2,1)S(1)} %collective-permute-done.7.refs_6_.refs_11_), channel_id=1, source_target_pairs={{0,16},{4,20},{8,24},{12,28},{16,0},{20,4},{24,8},{28,12},{1,17},{... | collective-permute-start | bytes 1572872 | tf_op jit(solution)/shard_map/ppermute | solution.py:100
  127.3 21.7 %all-to-all-start.3 = ((bf16[8,256,128]{2,1,0:T(8,128)(2,1)}), bf16[8,256,128]{2,1,0:T(8,128)(2,1)S(1)}, u32[]{:S(2)}, u32[]{:S(2)}) async-start(bf16[8,256,128]{2,1,0:T(8,128)(2,1)} %attend.3), calls=%async_computation.3 | async-start | bytes 1048576 | tf_op jit(solution)/shard_map/all_to_all | solution.py:83
  140.3 7.0 %collective-permute-start.10 = (bf16[256,128]{1,0:T(8,128)(2,1)}, bf16[256,128]{1,0:T(8,128)(2,1)S(1)}, u32[]{:S(2)}, u32[]{:S(2)}) collective-permute-start(bf16[256,128]{1,0:T(8,128)(2,1)} %get-tuple-element.26), channel_id=1, source_target_pairs={{0,4},{1,5},{2,6},{3,7},{4,0},{5,1},{6,2},{7,3},{8,12},{9,13},{10,... | collective-permute-start | bytes 196616 | tf_op jit(solution)/shard_map/ppermute | solution.py:92
  140.8 7.9 %collective-permute-start.11 = (bf16[256,128]{1,0:T(8,128)(2,1)}, bf16[256,128]{1,0:T(8,128)(2,1)S(1)}, u32[]{:S(2)}, u32[]{:S(2)}) collective-permute-start(bf16[256,128]{1,0:T(8,128)(2,1)} %get-tuple-element.27), channel_id=1, source_target_pairs={{0,3},{1,0},{2,1},{3,2},{4,7},{5,4},{6,5},{7,6},{8,11},{9,8},{10,9... | collective-permute-start | bytes 196616 | tf_op jit(solution)/shard_map/ppermute | solution.py:92
  144.3 13.6 %collective-permute-start.12 = (bf16[256,128]{1,0:T(8,128)(2,1)}, bf16[256,128]{1,0:T(8,128)(2,1)S(1)}, u32[]{:S(2)}, u32[]{:S(2)}) collective-permute-start(bf16[256,128]{1,0:T(8,128)(2,1)} %get-tuple-element.28), channel_id=1, source_target_pairs={{0,7},{1,4},{2,5},{3,6},{4,3},{5,0},{6,1},{7,2},{8,15},{9,12},{10,... | collective-permute-start | bytes 196616 | tf_op jit(solution)/shard_map/ppermute | solution.py:92
  144.5 13.6 %collective-permute-start.13 = (bf16[256,128]{1,0:T(8,128)(2,1)}, bf16[256,128]{1,0:T(8,128)(2,1)S(1)}, u32[]{:S(2)}, u32[]{:S(2)}) collective-permute-start(bf16[256,128]{1,0:T(8,128)(2,1)} %get-tuple-element.29), channel_id=1, source_target_pairs={{0,2},{1,3},{2,0},{3,1},{4,6},{5,7},{6,4},{7,5},{8,10},{9,11},{10,... | collective-permute-start | bytes 196616 | tf_op jit(solution)/shard_map/ppermute | solution.py:92
  144.5 14.0 %collective-permute-start.14 = (bf16[256,128]{1,0:T(8,128)(2,1)}, bf16[256,128]{1,0:T(8,128)(2,1)S(1)}, u32[]{:S(2)}, u32[]{:S(2)}) collective-permute-start(bf16[256,128]{1,0:T(8,128)(2,1)} %get-tuple-element.30), channel_id=1, source_target_pairs={{0,6},{1,7},{2,4},{3,5},{4,2},{5,3},{6,0},{7,1},{8,14},{9,15},{10,... | collective-permute-start | bytes 196616 | tf_op jit(solution)/shard_map/ppermute | solution.py:92
  147.2 10.7 %copy-start.13 = (bf16[256,128]{1,0:T(8,128)(2,1)}, bf16[256,128]{1,0:T(8,128)(2,1)S(1)}, u32[]{:S(2)}) copy-start(bf16[256,128]{1,0:T(8,128)(2,1)S(1)} %collective-permute-done.10.refs_1_) | copy-start | bytes 196612
  147.2 11.3 %collective-permute-start.15 = (bf16[256,128]{1,0:T(8,128)(2,1)}, bf16[256,128]{1,0:T(8,128)(2,1)S(1)}, u32[]{:S(2)}, u32[]{:S(2)}) collective-permute-start(bf16[256,128]{1,0:T(8,128)(2,1)} %get-tuple-element.31), channel_id=1, source_target_pairs={{0,1},{1,2},{2,3},{3,0},{4,5},{5,6},{6,7},{7,4},{8,9},{9,10},{10,1... | collective-permute-start | bytes 196616 | tf_op jit(solution)/shard_map/ppermute | solution.py:92
  148.7 9.2 %copy-start.14 = (bf16[256,128]{1,0:T(8,128)(2,1)}, bf16[256,128]{1,0:T(8,128)(2,1)S(1)}, u32[]{:S(2)}) copy-start(bf16[256,128]{1,0:T(8,128)(2,1)S(1)} %collective-permute-done.11.refs_2_) | copy-start | bytes 196612
  148.7 9.9 %collective-permute-start.16 = (bf16[256,128]{1,0:T(8,128)(2,1)}, bf16[256,128]{1,0:T(8,128)(2,1)S(1)}, u32[]{:S(2)}, u32[]{:S(2)}) collective-permute-start(bf16[256,128]{1,0:T(8,128)(2,1)} %get-tuple-element.32), channel_id=1, source_target_pairs={{0,5},{1,6},{2,7},{3,4},{4,1},{5,2},{6,3},{7,0},{8,13},{9,14},{10,... | collective-permute-start | bytes 196616 | tf_op jit(solution)/shard_map/ppermute | solution.py:92
  (11 other events, 8.4 us)

commit v3 on v2

--- a/solution.py
+++ b/solution.py
@@ -43,37 +43,61 @@
     return 2 * lax.rem(z + d + n_u, n_u) + (core if r == 0 else 1 - core)
 
 
-def stage(n_u, hp, here=None, tensors=(), slots=(), after=()):
-    n_s = 2 * n_u
-    ins = [x for x in (here,) if x is not None] + list(tensors)
-    T = tensors[0].shape[0] if tensors else here.shape[2]
-    n_split = 0 if here is None else here.shape[1]
-    nb = len(tensors)
+def pack_sides(place, tensors, slots, n_u, hp):
+    T, nb, n_out = tensors[0].shape[0], len(tensors), 2 * n_u
+
+    def body(place, *refs):
+        ins, outs, sems = refs[:nb], refs[nb:-1], refs[-1]
+        pairs = []
+        for out, (r, d) in zip(outs, sides(n_u)):
+            for i in range(nb):
+                col = (share_at(place, r, d, n_u) * hp + slots[i]) * DH
+                pairs.append((ins[i].at[:, pl.ds(pl.multiple_of(col, DH), DH)], out.at[i]))
+        copy_all(pairs, sems)
+
+    return pl.pallas_call(
+        body,
+        out_shape=[jax.ShapeDtypeStruct((nb, T, DH), jnp.bfloat16)] * n_out,
+        in_specs=[SMEM] + [ANY] * nb,
+        out_specs=[VMEM] * n_out,
+        scratch_shapes=[pltpu.SemaphoreType.DMA((n_out * nb,))],
+        compiler_params=WHOLE,
+        cost_estimate=cost(3),
+        name="pack_sides",
+    )(place, *tensors)
+
+
+def stage(place, here, tensors, slots, n_u, hp, after):
+    apart = isinstance(here, list)
+    blocks = here if apart else [here]
+    n_s, n_b, nb = 2 * n_u, len(blocks), len(tensors)
+    n_split, T = 2, blocks[0].shape[-2]
     n_copies = n_s * (n_split + nb)
-    n_in = len(ins) + len(after)
-    shapes = [(n_s * T, DH)] * n_split + [(n_s, nb, T, DH)] * (nb > 0)
-
-    def body(*refs):
+    n_in = n_b + nb + len(after)
+    shapes = [(n_s * T, DH)] * n_split + [(n_s, nb, T, DH)]
+
+    def body(place, *refs):
         outs, sems = refs[n_in:-1], refs[-1]
         pairs = []
-        for k in range(n_s):
+        for k, (r, d) in enumerate(sides(n_u)):
+            block, sender = (refs[k], share_at(place, r, -d, n_u)) if apart else (refs[0].at[k], k)
             for i in range(n_split):
-                pairs.append((refs[0].at[k, i], outs[i].at[pl.ds(k * T, T)]))
+                pairs.append((block.at[i], outs[i].at[pl.ds(pl.multiple_of(sender * T, T), T)]))
             for i in range(nb):
                 cols = pl.ds((k * hp + slots[i]) * DH, DH)
-                pairs.append((refs[len(ins) - nb + i].at[:, cols], outs[-1].at[k, i]))
+                pairs.append((refs[n_b + i].at[:, cols], outs[-1].at[k, i]))
         copy_all(pairs, sems)
 
     return pl.pallas_call(
         body,
         out_shape=[jax.ShapeDtypeStruct(shape, jnp.bfloat16) for shape in shapes],
-        in_specs=[ANY] * n_in,
+        in_specs=[SMEM] + [ANY] * n_in,
         out_specs=[VMEM] * len(shapes),
         scratch_shapes=[pltpu.SemaphoreType.DMA((n_copies,))],
         compiler_params=WHOLE,
         cost_estimate=cost(3),
         name="stage",
-    )(*ins, *after)
+    )(place, *blocks, *tensors, *after)
 
 
 def to_shares(x, n_c, n_u):
@@ -288,23 +312,23 @@
     place = jnp.stack([z, core]).astype(jnp.int32)
     table = key_table(rand_blocks, chip, n_u, n_c // 2, T // BLK)
 
-    kv, after = [], ()
-    (packed,) = stage(n_u, hp, None, [keys, values], [0, 0])
+    q_of, kv, after = [], [], (table,)
+    here = send_all(pack_sides(place, [keys, values], [0, 0], n_u, hp), n_c, n_u, 1)
     for h in range(hp):
+        if h < hp - 1:
+            tensors, slots = [keys, values, queries], [h + 1, h + 1, h]
+        else:
+            tensors, slots = [queries], [h]
+        first, second, packed = stage(place, here, tensors, slots, n_u, hp, after)
         here = to_shares(packed, n_c, n_u)
-        if h < hp - 1:
-            tensors, slots = [keys, values], [h + 1, h + 1]
-        else:
-            tensors, slots = [queries] * hp, list(range(hp))
-        first, second, packed = stage(n_u, hp, here, tensors, slots, (table, *after))
+        q_of.append((here, len(tensors) - 1))
         kv.append(gather_chips(first, second, n_c))
-        after = [side[1 << i] for side in kv[-1] for i in range((n_c // 2).bit_length() - 1)]
-    q_here = to_shares(packed, n_c, n_u)
+        after = [x for side in kv[-1] for x in side[1:]]
 
     total = None
     for h in range(hp):
         last = h == hp - 1
-        parts = attend(place, table, q_here, h, *kv[h], n_u, last, after)
+        parts = attend(place, table, *q_of[h], *kv[h], n_u, last, ())
         parts = send_all(parts, n_c, n_u, -1) if last else to_shares(parts[0], n_c, n_u)
         total = project(place, parts, h, out_weight, n_u, hp, total)
     return total

time: 169 us -> 155 us (0.917)
  waiting for transfers between devices: 77.4 us -> 56 us
  starting transfers between devices: 40.9 us -> 48.3 us
  Pallas kernels: 40.9 us -> 43.1 us
  local copies, waits for them, and re-layouts: 6.82 us -> 5.05 us
    all_to_all x4 -> x3, waiting for transfers between devices: 24.9 us -> 0.01 us  [to_shares(): lax.all_to_all(x, ('ctx', 'ulys'), split_axis=0, concat_axis=0, tiled=Tru...]
    ppermute x7 -> x14, waiting for transfers between devices: 0.61 us -> 12 us  [send(): return lax.ppermute(x, ('ctx', 'ulys'), pairs)]
    ppermute x7 -> x14, starting transfers between devices: 8.75 us -> 17.3 us  [send(): return lax.ppermute(x, ('ctx', 'ulys'), pairs)]
    ppermute x12, waiting for transfers between devices: 52 us -> 44 us  [swap_chip(): return lax.ppermute(x, 'ctx', [(i, i ^ 2 * bit) for i in range(n_c)])]
    pallas_call x0 -> x1, Pallas kernels: none -> 3.16 us  [pack_sides(): pl.pallas_call(body, out_shape=[jax.ShapeDtypeStruct((nb, T, DH), jnp.bfl...]
    all_to_all x4 -> x3, starting transfers between devices: 19.9 us -> 17.8 us  [to_shares(): lax.all_to_all(x, ('ctx', 'ulys'), split_axis=0, concat_axis=0, tiled=Tru...]
    unnamed x41 -> x59, local copies, waits for them, and re-layouts: 6.08 us -> 4.31 us
    pallas_call x3 -> x2, Pallas kernels: 8.78 us -> 7.77 us  [stage(): pl.pallas_call(body, out_shape=[jax.ShapeDtypeStruct(shape, jnp.bfloat16)...]
  transfers between devices with their start and end apart: 23 -> 29, of which waited for: 11 -> 9; matrix products, arithmetic and copies ran while one was open for 1% -> 1% of each run, Pallas kernels for 14% -> 15%
where the time goes in v3:
time: 155 us; the launch traced here: 154 us
  waiting for transfers between devices  56 us (36%)
  starting transfers between devices  48.3 us (31%)
  Pallas kernels  43.1 us (28%)
  local copies, waits for them, and re-layouts  5.05 us (3%)
    ppermute x12, waiting for transfers between devices, swap_chip(): return lax.ppermute(x, 'ctx', [(i, i ^ 2 * bit) for i in range(n_c)])  44 us
    all_to_all x3, starting transfers between devices, to_shares(): lax.all_to_all(x, ('ctx', 'ulys'), split_axis=0, concat_axis=0, tiled=Tru...  17.8 us
    ppermute x14, starting transfers between devices, send(): return lax.ppermute(x, ('ctx', 'ulys'), pairs)  17.3 us
    pallas_call x2, Pallas kernels, project(): pl.pallas_call(body, out_shape=jax.ShapeDtypeStruct((T, width), kind), in...  16.6 us
    pallas_call x2, Pallas kernels, attend(): pl.pallas_call(body, out_shape=[jax.ShapeDtypeStruct((T, DH) if apart els...  15.6 us
    ppermute x12, starting transfers between devices, swap_chip(): return lax.ppermute(x, 'ctx', [(i, i ^ 2 * bit) for i in range(n_c)])  13.2 us
    ppermute x14, waiting for transfers between devices, send(): return lax.ppermute(x, ('ctx', 'ulys'), pairs)  12 us
    pallas_call x2, Pallas kernels, stage(): pl.pallas_call(body, out_shape=[jax.ShapeDtypeStruct(shape, jnp.bfloat16)...  7.77 us
  transfers between devices with their start and end apart: 29, of which 9 were waited for; matrix products, arithmetic and copies ran while one was open for 1% of the time, Pallas kernels for 15%

profile of v3, /device:TPU:0, one launch (start us, length us, event | category | flops | bytes accessed | tf_op | source)
XLA Modules:
  0.0 154.4 jit_solution(12547468398617811445)
XLA Ops:
  0.7 3.2 %pack_sides.1 = (bf16[2,256,128]{2,1,0:T(8,128)(2,1)}, bf16[2,256,128]{2,1,0:T(8,128)(2,1)}, bf16[2,256,128]{2,1,0:T(8,128)(2,1)}, bf16[2,256,128]{2,1,0:T(8,128...) custom-call(s32[2]{0:T(128)} %pad_add_fusion.place, ...), custom_call_target="tpu_custom_call" | custom-call | flops 3449999872 | tf_op jit(solution)/shard_map/pack_sides/pallas_call | solution.py:58
  4.3 2.6 %collective-permute-start.1 = (bf16[2,256,128]{2,1,0:T(8,128)(2,1)}, bf16[2,256,128]{2,1,0:T(8,128)(2,1)S(1)}, u32[]{:S(2)}, u32[]{:S(2)}) collective-permute-start(bf16[2,256,128]{2,1,0:T(8,128)(2,1)} %get-tuple-element.29), channel_id=1, source_target_pairs={{0,1},{1,2},{2,3},{3,0},{4,5},{5,6},{6,7},{7,4},{8,9},{9,10},{10,1... | collective-permute-start | bytes 393224 | tf_op jit(solution)/shard_map/ppermute | solution.py:116
  7.0 1.3 collective-permute-start.2
  8.3 1.3 collective-permute-start.3
  9.7 1.3 collective-permute-start.4
  12.0 2.3 %collective-permute-start.5 = (bf16[2,256,128]{2,1,0:T(8,128)(2,1)}, bf16[2,256,128]{2,1,0:T(8,128)(2,1)S(1)}, u32[]{:S(2)}, u32[]{:S(2)}) collective-permute-start(bf16[2,256,128]{2,1,0:T(8,128)(2,1)} %get-tuple-element.33), channel_id=1, source_target_pairs={{0,3},{1,0},{2,1},{3,2},{4,7},{5,4},{6,5},{7,6},{8,11},{9,8},{10,9... | collective-permute-start | bytes 393224 | tf_op jit(solution)/shard_map/ppermute | solution.py:116
  16.0 8.6 %collective-permute-done.3.refs_4_ = bf16[2,256,128]{2,1,0:T(8,128)(2,1)S(1)} collective-permute-done((bf16[2,256,128]{2,1,0:T(8,128)(2,1)}, bf16[2,256,128]{2,1,0:T(8,128)(2,1)S(1)}, u32[]{:S(2)}, u32[]{:S(2)}) %collective-permute-start.3) | collective-permute-done | bytes 131104 | tf_op jit(solution)/shard_map/ppermute | solution.py:116
  24.6 2.7 %collective-permute-done.4.refs_5_ = bf16[2,256,128]{2,1,0:T(8,128)(2,1)S(1)} collective-permute-done((bf16[2,256,128]{2,1,0:T(8,128)(2,1)}, bf16[2,256,128]{2,1,0:T(8,128)(2,1)S(1)}, u32[]{:S(2)}, u32[]{:S(2)}) %collective-permute-start.4) | collective-permute-done | bytes 131104 | tf_op jit(solution)/shard_map/ppermute | solution.py:116
  28.1 4.3 %stage.2 = (bf16[2048,128]{1,0:T(8,128)(2,1)}, bf16[2048,128]{1,0:T(8,128)(2,1)}, bf16[8,3,256,128]{3,2,1,0:T(8,128)(2,1)}) custom-call(s32[2]{0:T(128)} %pad_add_fusion.place, bf16[2,256,128]{2,1,0:T(8,128)(2,1)} %get-tuple-element.27.refs_0_, bf16[2,256,128]{2,1,0:T(8,128)(2,1)} %copy-done.15, bf16[2,256,128]{2,1,0:T(8,128)(2,1)} %copy-done.16, ...), custom_call_target="tpu_custom_call" | custom-call | flops 3449999872 | tf_op jit(solution)/shard_map/stage/pallas_call | solution.py:91
  32.4 8.3 %all-to-all-start = ((bf16[8,3,256,128]{3,2,1,0:T(8,128)(2,1)}), bf16[8,3,256,128]{3,2,1,0:T(8,128)(2,1)S(1)}, u32[]{:S(2)}, u32[]{:S(2)}) async-start(bf16[8,3,256,128]{3,2,1,0:T(8,128)(2,1)} %get-tuple-element.35), calls=%async_computation | async-start | bytes 3145728 | tf_op jit(solution)/shard_map/all_to_all | solution.py:107
  40.7 1.6 %collective-permute-start.8 = (bf16[2048,128]{1,0:T(8,128)(2,1)S(1)}, bf16[2048,128]{1,0:T(8,128)(2,1)S(1)}, u32[]{:S(2)}, u32[]{:S(2)}) collective-permute-start(bf16[2048,128]{1,0:T(8,128)(2,1)S(1)} %copy-done.4), channel_id=1, source_target_pairs={{0,16},{4,20},{8,24},{12,28},{16,0},{20,4},{24,8},{28,12},{1,17},{... | collective-permute-start | bytes 1572872 | tf_op jit(solution)/shard_map/ppermute | solution.py:124
  42.3 1.5 collective-permute-start.10
  44.8 10.7 %collective-permute-done.8.refs_3_ = bf16[2048,128]{1,0:T(8,128)(2,1)S(1)} collective-permute-done((bf16[2048,128]{1,0:T(8,128)(2,1)S(1)}, bf16[2048,128]{1,0:T(8,128)(2,1)S(1)}, u32[]{:S(2)}, u32[]{:S(2)}) %collective-permute-start.8) | collective-permute-done | bytes 524320 | tf_op jit(solution)/shard_map/ppermute | solution.py:124
  55.5 1.5 collective-permute-start.9
  57.0 1.5 collective-permute-start.12
  58.5 9.8 %collective-permute-done.7.refs_2_ = bf16[2048,128]{1,0:T(8,128)(2,1)S(1)} collective-permute-done((bf16[2048,128]{1,0:T(8,128)(2,1)S(1)}, bf16[2048,128]{1,0:T(8,128)(2,1)S(1)}, u32[]{:S(2)}, u32[]{:S(2)}) %collective-permute-start.7) | collective-permute-done | bytes 524320 | tf_op jit(solution)/shard_map/ppermute | solution.py:124
  68.3 10.4 %collective-permute-done.9.refs_4_ = bf16[2048,128]{1,0:T(8,128)(2,1)S(1)} collective-permute-done((bf16[2048,128]{1,0:T(8,128)(2,1)S(1)}, bf16[2048,128]{1,0:T(8,128)(2,1)S(1)}, u32[]{:S(2)}, u32[]{:S(2)}) %collective-permute-start.9) | collective-permute-done | bytes 524320 | tf_op jit(solution)/shard_map/ppermute | solution.py:124
  80.7 3.5 %stage.3 = (bf16[2048,128]{1,0:T(8,128)(2,1)}, bf16[2048,128]{1,0:T(8,128)(2,1)}, bf16[8,1,256,128]{3,2,1,0:T(8,128)(2,1)}) custom-call(s32[2]{0:T(128)} %pad_add_fusion.place, bf16[8,3,256,128]{3,2,1,0:T(8,128)(2,1)} %copy-done, bf16[256,2048]{1,0:T(8,128)(2,1)} %refs_1_.4, bf16[2048,128]{1,0:T(8,128)(2,1)} %copy-done.8, bf16[2048,128]{1,0:T(8,128)(2,1)} %copy-done.6, ...), custom_call_target="tpu_custom_call" | custom-call | flops 3449999872 | tf_op jit(solution)/shard_map/stage/pallas_call | solution.py:91
  84.8 1.5 collective-permute-start.16
  86.3 4.7 %all-to-all-start.1 = ((bf16[8,1,256,128]{3,2,1,0:T(8,128)(2,1)}), bf16[8,1,256,128]{3,2,1,0:T(8,128)(2,1)S(1)}, u32[]{:S(2)}, u32[]{:S(2)}) async-start(bf16[8,1,256,128]{3,2,1,0:T(8,128)(2,1)} %get-tuple-element.38), calls=%async_computation.1 | async-start | bytes 1048576 | tf_op jit(solution)/shard_map/all_to_all | solution.py:107
  91.6 1.5 collective-permute-start.17
  93.1 6.3 %collective-permute-done.14.refs_3_ = bf16[2048,128]{1,0:T(8,128)(2,1)S(1)} collective-permute-done((bf16[2048,128]{1,0:T(8,128)(2,1)}, bf16[2048,128]{1,0:T(8,128)(2,1)S(1)}, u32[]{:S(2)}, u32[]{:S(2)}) %collective-permute-start.14) | collective-permute-done | bytes 524320 | tf_op jit(solution)/shard_map/ppermute | solution.py:124
  99.4 1.5 collective-permute-start.15
  101.4 7.8 %attend.3 = bf16[8,256,128]{2,1,0:T(8,128)(2,1)} custom-call(s32[2]{0:T(128)} %pad_add_fusion.place, s32[32,8]{1,0:T(8,128)} %fusion.8.refs_11_.table, bf16[8,3,256,128]{3,2,1,0:T(8,128)(2,1)} %copy-done, bf16[2048,128]{1,0:T(8,128)(2,1)} %get-tuple-element.36.refs_1_, bf16[2048,128]{1,0:T(8,128)(2,1)} %copy-done.8, bf16[2048,128]{1,0:T(8,128)(2,1)} %copy-done.6, ...), custom_call_target="tpu_custom_call" | custom-call | flops 9200000000 | tf_op jit(solution)/shard_map/attend/pallas_call | solution.py:201
  109.2 4.8 %all-to-all-start.2 = ((bf16[8,256,128]{2,1,0:T(8,128)(2,1)}), bf16[8,256,128]{2,1,0:T(8,128)(2,1)S(1)}, u32[]{:S(2)}, u32[]{:S(2)}) async-start(bf16[8,256,128]{2,1,0:T(8,128)(2,1)} %attend.3), calls=%async_computation.2 | async-start | bytes 1048576 | tf_op jit(solution)/shard_map/all_to_all | solution.py:107
  114.0 6.7 %collective-permute-done.15.refs_4_ = bf16[2048,128]{1,0:T(8,128)(2,1)} collective-permute-done((bf16[2048,128]{1,0:T(8,128)(2,1)S(1)}, bf16[2048,128]{1,0:T(8,128)(2,1)}, u32[]{:S(2)}, u32[]{:S(2)}) %collective-permute-start.15) | collective-permute-done | bytes 524320 | tf_op jit(solution)/shard_map/ppermute | solution.py:124
  120.7 7.8 %attend.2 = (bf16[256,128]{1,0:T(8,128)(2,1)}, bf16[256,128]{1,0:T(8,128)(2,1)}, bf16[256,128]{1,0:T(8,128)(2,1)}, bf16[256,128]{1,0:T(8,128)(2,1)}, bf16[256,12...) custom-call(s32[2]{0:T(128)} %pad_add_fusion.place, ...), custom_call_target="tpu_custom_call" | custom-call | flops 9200000000 | tf_op jit(solution)/shard_map/attend/pallas_call | solution.py:201
  128.6 3.0 %collective-permute-start.20 = (bf16[256,128]{1,0:T(8,128)(2,1)}, bf16[256,128]{1,0:T(8,128)(2,1)S(1)}, u32[]{:S(2)}, u32[]{:S(2)}) collective-permute-start(bf16[256,128]{1,0:T(8,128)(2,1)} %get-tuple-element.43), channel_id=1, source_target_pairs={{0,3},{1,0},{2,1},{3,2},{4,7},{5,4},{6,5},{7,6},{8,11},{9,8},{10,9... | collective-permute-start | bytes 196616 | tf_op jit(solution)/shard_map/ppermute | solution.py:116
  132.0 2.6 %collective-permute-start.23 = (bf16[256,128]{1,0:T(8,128)(2,1)}, bf16[256,128]{1,0:T(8,128)(2,1)S(1)}, u32[]{:S(2)}, u32[]{:S(2)}) collective-permute-start(bf16[256,128]{1,0:T(8,128)(2,1)} %get-tuple-element.46), channel_id=1, source_target_pairs={{0,6},{1,7},{2,4},{3,5},{4,2},{5,3},{6,0},{7,1},{8,14},{9,15},{10,... | collective-permute-start | bytes 196616 | tf_op jit(solution)/shard_map/ppermute | solution.py:116
  134.6 1.5 collective-permute-start.24
  137.0 8.2 %project.2.refs_9_ = f32[256,4096]{1,0:T(8,128)} custom-call(s32[2]{0:T(128)} %pad_add_fusion.place, bf16[8,256,128]{2,1,0:T(8,128)(2,1)} %copy-done.1, bf16[2048,4096]{1,0:T(8,128)(2,1)} %refs_8_.3), custom_call_target="tpu_custom_call" | custom-call | flops 9200000000 | tf_op jit(solution)/shard_map/project/pallas_call | solution.py:271
  145.9 8.5 %project.3 = bf16[256,4096]{1,0:T(8,128)(2,1)} custom-call(s32[2]{0:T(128)} %pad_add_fusion.place, bf16[256,128]{1,0:T(8,128)(2,1)} %get-tuple-element.41.refs_0_, bf16[256,128]{1,0:T(8,128)(2,1)} %copy-done.22, bf16[256,128]{1,0:T(8,128)(2,1)} %copy-done.23, bf16[256,128]{1,0:T(8,128)(2,1)} %copy-done.24, bf16[256,128]{1,0:T(8,128)(2,1)} %copy-done.25, ...), custom_call_target="tpu_custom_call" | custom-call | flops 9200000000 | tf_op jit(solution)/shard_map/project/pallas_call | solution.py:271
  (103 shorter events, 11.5 us)
Async XLA Ops:
  3.8 8.2 %collective-permute-start = (bf16[2,256,128]{2,1,0:T(8,128)(2,1)}, bf16[2,256,128]{2,1,0:T(8,128)(2,1)S(1)}, u32[]{:S(2)}, u32[]{:S(2)}) collective-permute-start(bf16[2,256,128]{2,1,0:T(8,128)(2,1)} %get-tuple-element.28), channel_id=1, source_target_pairs={{0,4},{1,5},{2,6},{3,7},{4,0},{5,1},{6,2},{7,3},{8,12},{9,13},{10,... | collective-permute-start | bytes 393224 | tf_op jit(solution)/shard_map/ppermute | solution.py:116
  4.3 10.0 %collective-permute-start.1 = (bf16[2,256,128]{2,1,0:T(8,128)(2,1)}, bf16[2,256,128]{2,1,0:T(8,128)(2,1)S(1)}, u32[]{:S(2)}, u32[]{:S(2)}) collective-permute-start(bf16[2,256,128]{2,1,0:T(8,128)(2,1)} %get-tuple-element.29), channel_id=1, source_target_pairs={{0,1},{1,2},{2,3},{3,0},{4,5},{5,6},{6,7},{7,4},{8,9},{9,10},{10,1... | collective-permute-start | bytes 393224 | tf_op jit(solution)/shard_map/ppermute | solution.py:116
  7.0 9.1 %collective-permute-start.2 = (bf16[2,256,128]{2,1,0:T(8,128)(2,1)}, bf16[2,256,128]{2,1,0:T(8,128)(2,1)S(1)}, u32[]{:S(2)}, u32[]{:S(2)}) collective-permute-start(bf16[2,256,128]{2,1,0:T(8,128)(2,1)} %get-tuple-element.30), channel_id=1, source_target_pairs={{0,5},{1,6},{2,7},{3,4},{4,1},{5,2},{6,3},{7,0},{8,13},{9,14},{10,... | collective-permute-start | bytes 393224 | tf_op jit(solution)/shard_map/ppermute | solution.py:116
  8.3 16.3 %collective-permute-start.3 = (bf16[2,256,128]{2,1,0:T(8,128)(2,1)}, bf16[2,256,128]{2,1,0:T(8,128)(2,1)S(1)}, u32[]{:S(2)}, u32[]{:S(2)}) collective-permute-start(bf16[2,256,128]{2,1,0:T(8,128)(2,1)} %get-tuple-element.31), channel_id=1, source_target_pairs={{0,2},{1,3},{2,0},{3,1},{4,6},{5,7},{6,4},{7,5},{8,10},{9,11},{10,... | collective-permute-start | bytes 393224 | tf_op jit(solution)/shard_map/ppermute | solution.py:116
  9.7 17.7 %collective-permute-start.4 = (bf16[2,256,128]{2,1,0:T(8,128)(2,1)}, bf16[2,256,128]{2,1,0:T(8,128)(2,1)S(1)}, u32[]{:S(2)}, u32[]{:S(2)}) collective-permute-start(bf16[2,256,128]{2,1,0:T(8,128)(2,1)} %get-tuple-element.32), channel_id=1, source_target_pairs={{0,6},{1,7},{2,4},{3,5},{4,2},{5,3},{6,0},{7,1},{8,14},{9,15},{10,... | collective-permute-start | bytes 393224 | tf_op jit(solution)/shard_map/ppermute | solution.py:116
  12.0 15.3 %copy-start.15 = (bf16[2,256,128]{2,1,0:T(8,128)(2,1)}, bf16[2,256,128]{2,1,0:T(8,128)(2,1)S(1)}, u32[]{:S(2)}) copy-start(bf16[2,256,128]{2,1,0:T(8,128)(2,1)S(1)} %collective-permute-done.refs_1_) | copy-start | bytes 393220
  12.0 15.3 %collective-permute-start.5 = (bf16[2,256,128]{2,1,0:T(8,128)(2,1)}, bf16[2,256,128]{2,1,0:T(8,128)(2,1)S(1)}, u32[]{:S(2)}, u32[]{:S(2)}) collective-permute-start(bf16[2,256,128]{2,1,0:T(8,128)(2,1)} %get-tuple-element.33), channel_id=1, source_target_pairs={{0,3},{1,0},{2,1},{3,2},{4,7},{5,4},{6,5},{7,6},{8,11},{9,8},{10,9... | collective-permute-start | bytes 393224 | tf_op jit(solution)/shard_map/ppermute | solution.py:116
  14.3 13.0 %collective-permute-start.6 = (bf16[2,256,128]{2,1,0:T(8,128)(2,1)}, bf16[2,256,128]{2,1,0:T(8,128)(2,1)S(1)}, u32[]{:S(2)}, u32[]{:S(2)}) collective-permute-start(bf16[2,256,128]{2,1,0:T(8,128)(2,1)} %get-tuple-element.34), channel_id=1, source_target_pairs={{0,7},{1,4},{2,5},{3,6},{4,3},{5,0},{6,1},{7,2},{8,15},{9,12},{10,... | collective-permute-start | bytes 393224 | tf_op jit(solution)/shard_map/ppermute | solution.py:116
  32.4 47.2 %all-to-all-start = ((bf16[8,3,256,128]{3,2,1,0:T(8,128)(2,1)}), bf16[8,3,256,128]{3,2,1,0:T(8,128)(2,1)S(1)}, u32[]{:S(2)}, u32[]{:S(2)}) async-start(bf16[8,3,256,128]{3,2,1,0:T(8,128)(2,1)} %get-tuple-element.35), calls=%async_computation | async-start | bytes 3145728 | tf_op jit(solution)/shard_map/all_to_all | solution.py:107
  40.7 14.8 %collective-permute-start.8 = (bf16[2048,128]{1,0:T(8,128)(2,1)S(1)}, bf16[2048,128]{1,0:T(8,128)(2,1)S(1)}, u32[]{:S(2)}, u32[]{:S(2)}) collective-permute-start(bf16[2048,128]{1,0:T(8,128)(2,1)S(1)} %copy-done.4), channel_id=1, source_target_pairs={{0,16},{4,20},{8,24},{12,28},{16,0},{20,4},{24,8},{28,12},{1,17},{... | collective-permute-start | bytes 1572872 | tf_op jit(solution)/shard_map/ppermute | solution.py:124
  42.3 14.8 %collective-permute-start.10 = (bf16[2048,128]{1,0:T(8,128)(2,1)S(1)}, bf16[2048,128]{1,0:T(8,128)(2,1)S(1)}, u32[]{:S(2)}, u32[]{:S(2)}) collective-permute-start(bf16[2048,128]{1,0:T(8,128)(2,1)S(1)} %copy-done.5), channel_id=1, source_target_pairs={{0,8},{4,12},{8,0},{12,4},{16,24},{20,28},{24,16},{28,20},{1,9},{5... | collective-permute-start | bytes 1572872 | tf_op jit(solution)/shard_map/ppermute | solution.py:124
  43.8 24.5 %collective-permute-start.7 = (bf16[2048,128]{1,0:T(8,128)(2,1)S(1)}, bf16[2048,128]{1,0:T(8,128)(2,1)S(1)}, u32[]{:S(2)}, u32[]{:S(2)}) collective-permute-start(bf16[2048,128]{1,0:T(8,128)(2,1)S(1)} %copy-done.4), channel_id=1, source_target_pairs={{0,8},{4,12},{8,0},{12,4},{16,24},{20,28},{24,16},{28,20},{1,9},{5... | collective-permute-start | bytes 1572872 | tf_op jit(solution)/shard_map/ppermute | solution.py:124
  44.3 24.0 %collective-permute-start.11 = (bf16[2048,128]{1,0:T(8,128)(2,1)S(1)}, bf16[2048,128]{1,0:T(8,128)(2,1)S(1)}, u32[]{:S(2)}, u32[]{:S(2)}) collective-permute-start(bf16[2048,128]{1,0:T(8,128)(2,1)S(1)} %copy-done.5), channel_id=1, source_target_pairs={{0,16},{4,20},{8,24},{12,28},{16,0},{20,4},{24,8},{28,12},{1,17},{... | collective-permute-start | bytes 1572872 | tf_op jit(solution)/shard_map/ppermute | solution.py:124
  55.5 24.1 %copy-start.6 = (bf16[2048,128]{1,0:T(8,128)(2,1)}, bf16[2048,128]{1,0:T(8,128)(2,1)S(1)}, u32[]{:S(2)}) copy-start(bf16[2048,128]{1,0:T(8,128)(2,1)S(1)} %collective-permute-done.8.refs_3_) | copy-start | bytes 1572868
  55.5 23.2 %collective-permute-start.9 = (bf16[2048,128]{1,0:T(8,128)(2,1)S(1)}, bf16[2048,128]{1,0:T(8,128)(2,1)S(1)}, u32[]{:S(2)}, u32[]{:S(2)}) collective-permute-start(bf16[2048,128]{1,0:T(8,128)(2,1)S(1)} %collective-permute-done.8.refs_3_), channel_id=1, source_target_pairs={{0,8},{4,12},{8,0},{12,4},{16,24},{20,28},{24,16},{28,20},{1,9},{5... | collective-permute-start | bytes 1572872 | tf_op jit(solution)/shard_map/ppermute | solution.py:124
  57.0 21.7 %copy-start.7 = (bf16[2048,128]{1,0:T(8,128)(2,1)}, bf16[2048,128]{1,0:T(8,128)(2,1)S(1)}, u32[]{:S(2)}) copy-start(bf16[2048,128]{1,0:T(8,128)(2,1)S(1)} %collective-permute-done.10.refs_5_.refs_6_) | copy-start | bytes 1572868
  57.0 22.5 %collective-permute-start.12 = (bf16[2048,128]{1,0:T(8,128)(2,1)S(1)}, bf16[2048,128]{1,0:T(8,128)(2,1)}, u32[]{:S(2)}, u32[]{:S(2)}) collective-permute-start(bf16[2048,128]{1,0:T(8,128)(2,1)S(1)} %collective-permute-done.10.refs_5_.refs_6_), channel_id=1, source_target_pairs={{0,16},{4,20},{8,24},{12,28},{16,0},{20,4},{24,8},{28,12},{1,17},{... | collective-permute-start | bytes 1572872 | tf_op jit(solution)/shard_map/ppermute | solution.py:124
  84.2 15.1 %collective-permute-start.14 = (bf16[2048,128]{1,0:T(8,128)(2,1)}, bf16[2048,128]{1,0:T(8,128)(2,1)S(1)}, u32[]{:S(2)}, u32[]{:S(2)}) collective-permute-start(bf16[2048,128]{1,0:T(8,128)(2,1)} %get-tuple-element.39.refs_1_), channel_id=1, source_target_pairs={{0,16},{4,20},{8,24},{12,28},{16,0},{20,4},{24,8},{28,12},{1,17},{... | collective-permute-start | bytes 1572872 | tf_op jit(solution)/shard_map/ppermute | solution.py:124
  84.8 16.1 %collective-permute-start.16 = (bf16[2048,128]{1,0:T(8,128)(2,1)}, bf16[2048,128]{1,0:T(8,128)(2,1)S(1)}, u32[]{:S(2)}, u32[]{:S(2)}) collective-permute-start(bf16[2048,128]{1,0:T(8,128)(2,1)} %get-tuple-element.40.refs_5_), channel_id=1, source_target_pairs={{0,8},{4,12},{8,0},{12,4},{16,24},{20,28},{24,16},{28,20},{1,9},{5... | collective-permute-start | bytes 1572872 | tf_op jit(solution)/shard_map/ppermute | solution.py:124
  86.3 22.9 %all-to-all-start.1 = ((bf16[8,1,256,128]{3,2,1,0:T(8,128)(2,1)}), bf16[8,1,256,128]{3,2,1,0:T(8,128)(2,1)S(1)}, u32[]{:S(2)}, u32[]{:S(2)}) async-start(bf16[8,1,256,128]{3,2,1,0:T(8,128)(2,1)} %get-tuple-element.38), calls=%async_computation.1 | async-start | bytes 1048576 | tf_op jit(solution)/shard_map/all_to_all | solution.py:107
  91.0 22.9 %collective-permute-start.13 = (bf16[2048,128]{1,0:T(8,128)(2,1)}, bf16[2048,128]{1,0:T(8,128)(2,1)S(1)}, u32[]{:S(2)}, u32[]{:S(2)}) collective-permute-start(bf16[2048,128]{1,0:T(8,128)(2,1)} %get-tuple-element.39.refs_1_), channel_id=1, source_target_pairs={{0,8},{4,12},{8,0},{12,4},{16,24},{20,28},{24,16},{28,20},{1,9},{5... | collective-permute-start | bytes 1572872 | tf_op jit(solution)/shard_map/ppermute | solution.py:124
  91.6 22.4 %collective-permute-start.17 = (bf16[2048,128]{1,0:T(8,128)(2,1)}, bf16[2048,128]{1,0:T(8,128)(2,1)S(1)}, u32[]{:S(2)}, u32[]{:S(2)}) collective-permute-start(bf16[2048,128]{1,0:T(8,128)(2,1)} %get-tuple-element.40.refs_5_), channel_id=1, source_target_pairs={{0,16},{4,20},{8,24},{12,28},{16,0},{20,4},{24,8},{28,12},{1,17},{... | collective-permute-start | bytes 1572872 | tf_op jit(solution)/shard_map/ppermute | solution.py:124
  99.4 21.4 %collective-permute-start.15 = (bf16[2048,128]{1,0:T(8,128)(2,1)S(1)}, bf16[2048,128]{1,0:T(8,128)(2,1)}, u32[]{:S(2)}, u32[]{:S(2)}) collective-permute-start(bf16[2048,128]{1,0:T(8,128)(2,1)S(1)} %collective-permute-done.14.refs_3_), channel_id=1, source_target_pairs={{0,8},{4,12},{8,0},{12,4},{16,24},{20,28},{24,16},{28,20},{1,9},{5... | collective-permute-start | bytes 1572872 | tf_op jit(solution)/shard_map/ppermute | solution.py:124
  100.9 19.9 %collective-permute-start.18 = (bf16[2048,128]{1,0:T(8,128)(2,1)S(1)}, bf16[2048,128]{1,0:T(8,128)(2,1)}, u32[]{:S(2)}, u32[]{:S(2)}) collective-permute-start(bf16[2048,128]{1,0:T(8,128)(2,1)S(1)} %collective-permute-done.16.refs_6_), channel_id=1, source_target_pairs={{0,16},{4,20},{8,24},{12,28},{16,0},{20,4},{24,8},{28,12},{1,17},{... | collective-permute-start | bytes 1572872 | tf_op jit(solution)/shard_map/ppermute | solution.py:124
  109.2 27.0 %all-to-all-start.2 = ((bf16[8,256,128]{2,1,0:T(8,128)(2,1)}), bf16[8,256,128]{2,1,0:T(8,128)(2,1)S(1)}, u32[]{:S(2)}, u32[]{:S(2)}) async-start(bf16[8,256,128]{2,1,0:T(8,128)(2,1)} %attend.3), calls=%async_computation.2 | async-start | bytes 1048576 | tf_op jit(solution)/shard_map/all_to_all | solution.py:107
  128.5 6.0 %collective-permute-start.19 = (bf16[256,128]{1,0:T(8,128)(2,1)}, bf16[256,128]{1,0:T(8,128)(2,1)S(1)}, u32[]{:S(2)}, u32[]{:S(2)}) collective-permute-start(bf16[256,128]{1,0:T(8,128)(2,1)} %get-tuple-element.42), channel_id=1, source_target_pairs={{0,4},{1,5},{2,6},{3,7},{4,0},{5,1},{6,2},{7,3},{8,12},{9,13},{10,... | collective-permute-start | bytes 196616 | tf_op jit(solution)/shard_map/ppermute | solution.py:116
  128.6 7.4 %collective-permute-start.20 = (bf16[256,128]{1,0:T(8,128)(2,1)}, bf16[256,128]{1,0:T(8,128)(2,1)S(1)}, u32[]{:S(2)}, u32[]{:S(2)}) collective-permute-start(bf16[256,128]{1,0:T(8,128)(2,1)} %get-tuple-element.43), channel_id=1, source_target_pairs={{0,3},{1,0},{2,1},{3,2},{4,7},{5,4},{6,5},{7,6},{8,11},{9,8},{10,9... | collective-permute-start | bytes 196616 | tf_op jit(solution)/shard_map/ppermute | solution.py:116
  131.7 13.5 %collective-permute-start.21 = (bf16[256,128]{1,0:T(8,128)(2,1)}, bf16[256,128]{1,0:T(8,128)(2,1)S(1)}, u32[]{:S(2)}, u32[]{:S(2)}) collective-permute-start(bf16[256,128]{1,0:T(8,128)(2,1)} %get-tuple-element.44), channel_id=1, source_target_pairs={{0,7},{1,4},{2,5},{3,6},{4,3},{5,0},{6,1},{7,2},{8,15},{9,12},{10,... | collective-permute-start | bytes 196616 | tf_op jit(solution)/shard_map/ppermute | solution.py:116
  132.0 13.2 %collective-permute-start.22 = (bf16[256,128]{1,0:T(8,128)(2,1)}, bf16[256,128]{1,0:T(8,128)(2,1)S(1)}, u32[]{:S(2)}, u32[]{:S(2)}) collective-permute-start(bf16[256,128]{1,0:T(8,128)(2,1)} %get-tuple-element.45), channel_id=1, source_target_pairs={{0,2},{1,3},{2,0},{3,1},{4,6},{5,7},{6,4},{7,5},{8,10},{9,11},{10,... | collective-permute-start | bytes 196616 | tf_op jit(solution)/shard_map/ppermute | solution.py:116
  132.0 13.2 %collective-permute-start.23 = (bf16[256,128]{1,0:T(8,128)(2,1)}, bf16[256,128]{1,0:T(8,128)(2,1)S(1)}, u32[]{:S(2)}, u32[]{:S(2)}) collective-permute-start(bf16[256,128]{1,0:T(8,128)(2,1)} %get-tuple-element.46), channel_id=1, source_target_pairs={{0,6},{1,7},{2,4},{3,5},{4,2},{5,3},{6,0},{7,1},{8,14},{9,15},{10,... | collective-permute-start | bytes 196616 | tf_op jit(solution)/shard_map/ppermute | solution.py:116
  134.6 10.7 %collective-permute-start.24 = (bf16[256,128]{1,0:T(8,128)(2,1)}, bf16[256,128]{1,0:T(8,128)(2,1)S(1)}, u32[]{:S(2)}, u32[]{:S(2)}) collective-permute-start(bf16[256,128]{1,0:T(8,128)(2,1)} %get-tuple-element.47), channel_id=1, source_target_pairs={{0,1},{1,2},{2,3},{3,0},{4,5},{5,6},{6,7},{7,4},{8,9},{9,10},{10,1... | collective-permute-start | bytes 196616 | tf_op jit(solution)/shard_map/ppermute | solution.py:116
  136.1 9.2 %collective-permute-start.25 = (bf16[256,128]{1,0:T(8,128)(2,1)}, bf16[256,128]{1,0:T(8,128)(2,1)S(1)}, u32[]{:S(2)}, u32[]{:S(2)}) collective-permute-start(bf16[256,128]{1,0:T(8,128)(2,1)} %get-tuple-element.48), channel_id=1, source_target_pairs={{0,5},{1,6},{2,7},{3,4},{4,1},{5,2},{6,3},{7,0},{8,13},{9,14},{10,... | collective-permute-start | bytes 196616 | tf_op jit(solution)/shard_map/ppermute | solution.py:116
  (26 other events, 147.6 us)

commit v4 on v3

--- a/solution.py
+++ b/solution.py
@@ -22,6 +22,10 @@
 WHOLE = pltpu.CompilerParams(vmem_limit_bytes=60 * MIB)
 
 
+def beside(n_bytes):
+    return pltpu.CompilerParams(vmem_limit_bytes=60 * MIB - n_bytes)
+
+
 def cost(us):
     return pl.CostEstimate(flops=us * 1_150_000_000, bytes_accessed=0, transcendentals=0)
 
@@ -43,7 +47,7 @@
     return 2 * lax.rem(z + d + n_u, n_u) + (core if r == 0 else 1 - core)
 
 
-def pack_sides(place, tensors, slots, n_u, hp):
+def pack_sides(place, tensors, slots, n_u):
     T, nb, n_out = tensors[0].shape[0], len(tensors), 2 * n_u
 
     def body(place, *refs):
@@ -51,7 +55,7 @@
         pairs = []
         for out, (r, d) in zip(outs, sides(n_u)):
             for i in range(nb):
-                col = (share_at(place, r, d, n_u) * hp + slots[i]) * DH
+                col = (slots[i] * n_out + share_at(place, r, d, n_u)) * DH
                 pairs.append((ins[i].at[:, pl.ds(pl.multiple_of(col, DH), DH)], out.at[i]))
         copy_all(pairs, sems)
 
@@ -67,7 +71,7 @@
     )(place, *tensors)
 
 
-def stage(place, here, tensors, slots, n_u, hp, after):
+def stage(place, here, tensors, slots, n_u, after):
     apart = isinstance(here, list)
     blocks = here if apart else [here]
     n_s, n_b, nb = 2 * n_u, len(blocks), len(tensors)
@@ -84,7 +88,7 @@
             for i in range(n_split):
                 pairs.append((block.at[i], outs[i].at[pl.ds(pl.multiple_of(sender * T, T), T)]))
             for i in range(nb):
-                cols = pl.ds((k * hp + slots[i]) * DH, DH)
+                cols = pl.ds((slots[i] * n_s + k) * DH, DH)
                 pairs.append((refs[n_b + i].at[:, cols], outs[-1].at[k, i]))
         copy_all(pairs, sems)
 
@@ -140,53 +144,56 @@
     return [a[t] for t in range(n_p)], [b[t] for t in range(n_p)]
 
 
-def attend(place, table, queries, q_index, keys, values, n_u, apart, after):
+def attend(place, table, queries, q_index, keys, values, n_u, apart):
     n_s, _, T, _ = queries.shape
     n_q = n_s * T
     span = keys[0].shape[0]
     n_k = span * len(keys)
     n_rows, n_list = table.shape
-    group = 2 * T // BLK
+    group = 4 * T // BLK
     arrays = [queries, *keys, *values]
     n_in, n_out = len(arrays), 2 * n_u if apart else 1
-    n_refs = n_in + len(after)
 
     def body(place, table, *refs):
-        ins, outs = refs[:n_in], refs[n_refs : n_refs + n_out]
-        q_vm, k_vm, v_vm, o_vm, sems, out_sems = refs[n_refs + n_out :]
+        ins, outs = refs[:n_in], refs[n_in : n_in + n_out]
+        q_vm, k_vm, v_vm, o_vm, sems, out_sems = refs[n_in + n_out :]
         pairs = []
         for k in range(n_s):
             pairs.append((ins[0].at[k, q_index], q_vm.at[pl.ds(k * T, T)]))
         for i, ref in enumerate(ins[1:]):
             vm, t = (k_vm, i) if i < len(keys) else (v_vm, i - len(keys))
             pairs.append((ref, vm.at[pl.ds(t * span, span)]))
-        copy_all(pairs, sems)
-
-        @pl.loop(0, n_rows // group)
-        def _(step):
-            rows = [step * group + g for g in range(group)]
+        copies = [pltpu.make_async_copy(a, b, sems.at[i]) for i, (a, b) in enumerate(pairs)]
+        for c in copies:
+            c.start()
+        for c in copies[: n_s + len(keys)]:
+            c.wait()
+        for step in range(n_rows // group):
+            rows = range(step * group, (step + 1) * group)
             at = [[pl.multiple_of(table[r, j] * BLK, BLK) for j in range(n_list)] for r in rows]
             s = []
             for r, listed in zip(rows, at):
-                q = q_vm[pl.ds(pl.multiple_of(r * BLK, BLK), BLK), :]
                 k = jnp.concatenate([k_vm[pl.ds(a, BLK), :] for a in listed], axis=0)
                 s.append(
                     lax.dot_general(
-                        q, k, (((1,), (1,)), ((), ())), preferred_element_type=jnp.float32
+                        q_vm[pl.ds(r * BLK, BLK), :],
+                        k,
+                        (((1,), (1,)), ((), ())),
+                        preferred_element_type=jnp.float32,
                     )
                 )
             s = jnp.concatenate(s, axis=0)
             e = jnp.exp2((s - jnp.max(s, axis=-1, keepdims=True)) * (DH**-0.5 * LOG2E))
             w = (e * (1.0 / jnp.sum(e, axis=-1, keepdims=True))).astype(jnp.bfloat16)
-            o = []
-            for g, listed in enumerate(at):
+            if step == 0:
+                for c in copies[n_s + len(keys) :]:
+                    c.wait()
+            for g, (r, listed) in enumerate(zip(rows, at)):
                 v = jnp.concatenate([v_vm[pl.ds(a, BLK), :] for a in listed], axis=0)
-                o.append(
-                    jnp.dot(
-                        w[g * BLK : (g + 1) * BLK], v, preferred_element_type=jnp.float32
-                    ).astype(jnp.bfloat16)
+                o = jnp.dot(
+                    w[g * BLK : (g + 1) * BLK], v, preferred_element_type=jnp.float32
                 )
-            o_vm[pl.ds(pl.multiple_of(step * 2 * T, 2 * T), 2 * T), :] = jnp.concatenate(o, axis=0)
+                o_vm[pl.ds(r * BLK, BLK), :] = o.astype(jnp.bfloat16)
 
         pairs = []
         if apart:
@@ -201,7 +208,7 @@
     return pl.pallas_call(
         body,
         out_shape=[jax.ShapeDtypeStruct((T, DH) if apart else (n_s, T, DH), jnp.bfloat16)] * n_out,
-        in_specs=[SMEM, SMEM] + [ANY] * n_refs,
+        in_specs=[SMEM, SMEM] + [ANY] * n_in,
         out_specs=[ANY] * n_out,
         scratch_shapes=[
             pltpu.VMEM((n_q, DH), jnp.bfloat16),
@@ -214,79 +221,74 @@
         compiler_params=WHOLE,
         cost_estimate=cost(8),
         name="attend",
-    )(place, table, *arrays, *after)
-
-
-def project(place, parts, slot, weight, n_u, hp, partial):
-    apart, last, more = isinstance(parts, list), slot == hp - 1, partial is not None
+    )(place, table, *arrays)
+
+
+def project(place, parts, weight, slot, n_u, hp, partial):
+    apart, last = isinstance(parts, list), slot == hp - 1
     arrays = parts if apart else [parts]
-    n_in = len(arrays)
     T = arrays[0].shape[-2]
     width = weight.shape[1]
     shares = 2 * n_u
     depth = shares * DH
-    tile = width // 2
-    n_tiles = width // tile
-    kind = jnp.bfloat16 if last else jnp.float32
+    n_tiles, n_chunks = 2, 1
+    tile, chunk = width // n_tiles, depth // n_chunks
+    n_in = len(arrays)
+    kept = [] if partial is None else [partial]
 
     def body(place, *refs):
-        ins, w_ref = refs[:n_in], refs[n_in]
-        out_ref, rows, w_vm, add_vm, out_vm, row_sems, w_sems, add_sems, out_sems = refs[-9:]
-        put = []
+        ins, w_ref, out_ref = refs[:n_in], refs[n_in], refs[n_in + 1 + len(kept)]
+        rows, w_vm, out_vm, row_sems, w_sems, out_sems = refs[-6:]
+        put, fetch, send = [], [], []
         for i, (r, d) in enumerate(sides(n_u)):
             src, share = (ins[i], share_at(place, r, d, n_u)) if apart else (ins[0].at[i], i)
             cols = pl.ds(pl.multiple_of(share * DH, DH), DH)
             put.append(pltpu.make_async_copy(src, rows.at[:, cols], row_sems.at[i]))
-        fetch = []
         for t in range(n_tiles):
-            cols = pl.ds(t * tile, tile)
-            fetch.append([])
-            for k in range(shares):
-                src = w_ref.at[pl.ds((k * hp + slot) * DH, DH), cols]
-                dst = w_vm.at[pl.ds(k * DH, DH), cols]
-                fetch[t].append(pltpu.make_async_copy(src, dst, w_sems.at[t, k]))
-            if more:
-                src = refs[n_in + 1].at[:, cols]
-                fetch[t].append(pltpu.make_async_copy(src, add_vm.at[:, cols], add_sems.at[t]))
-        for c in put + sum(fetch, []):
+            for k in range(n_chunks):
+                cols = pl.ds(t * tile, tile)
+                src = w_ref.at[pl.ds(slot * depth + k * chunk, chunk), cols]
+                dst = w_vm.at[pl.ds(k * chunk, chunk), cols]
+                fetch.append(pltpu.make_async_copy(src, dst, w_sems.at[t, k]))
+        for c in put + fetch:
             c.start()
         for c in put:
             c.wait()
-        send = []
         for t in range(n_tiles):
             cols = pl.ds(t * tile, tile)
-            for c in fetch[t]:
+            for c in fetch[t * n_chunks : (t + 1) * n_chunks]:
                 c.wait()
             total = jnp.dot(rows[...], w_vm[:, cols], preferred_element_type=jnp.float32)
-            if more:
-                total = total + add_vm[:, cols]
-            out_vm[:, cols] = total.astype(kind)
-            send.append(
-                pltpu.make_async_copy(out_vm.at[:, cols], out_ref.at[:, cols], out_sems.at[t])
-            )
-            send[-1].start()
+            if kept:
+                total = total + refs[n_in + 1][:, cols]
+            if last:
+                out_vm[:, cols] = total.astype(jnp.bfloat16)
+                send.append(
+                    pltpu.make_async_copy(out_vm.at[:, cols], out_ref.at[:, cols], out_sems.at[t])
+                )
+                send[-1].start()
+            else:
+                out_ref[:, cols] = total
         for c in send:
             c.wait()
 
     return pl.pallas_call(
         body,
-        out_shape=jax.ShapeDtypeStruct((T, width), kind),
-        in_specs=[SMEM] + [ANY] * (n_in + 1 + more),
-        out_specs=ANY,
+        out_shape=jax.ShapeDtypeStruct((T, width), jnp.bfloat16 if last else jnp.float32),
+        in_specs=[SMEM] + [ANY] * (n_in + 1) + [VMEM] * len(kept),
+        out_specs=ANY if last else VMEM,
         scratch_shapes=[
             pltpu.VMEM((T, depth), jnp.bfloat16),
-            pltpu.VMEM((depth, width), jnp.bfloat16),
-            pltpu.VMEM((T, width), jnp.float32),
-            pltpu.VMEM((T, width), kind),
+            pltpu.VMEM((depth, width), weight.dtype),
+            pltpu.VMEM((T, width if last else DH), jnp.bfloat16),
             pltpu.SemaphoreType.DMA((shares,)),
-            pltpu.SemaphoreType.DMA((n_tiles, shares)),
-            pltpu.SemaphoreType.DMA((n_tiles,)),
+            pltpu.SemaphoreType.DMA((n_tiles, n_chunks)),
             pltpu.SemaphoreType.DMA((n_tiles,)),
         ],
-        compiler_params=WHOLE,
-        cost_estimate=cost(8),
+        compiler_params=beside(4 * T * width + 10 * MIB),
+        cost_estimate=cost(7),
         name="project",
-    )(place, *arrays, weight, *([partial] * more))
+    )(place, *arrays, weight, *kept)
 
 
 def key_table(rand_blocks, chip, n_u, n_p, per):
@@ -313,13 +315,13 @@
     table = key_table(rand_blocks, chip, n_u, n_c // 2, T // BLK)
 
     q_of, kv, after = [], [], (table,)
-    here = send_all(pack_sides(place, [keys, values], [0, 0], n_u, hp), n_c, n_u, 1)
+    here = send_all(pack_sides(place, [keys, values], [0, 0], n_u), n_c, n_u, 1)
     for h in range(hp):
         if h < hp - 1:
             tensors, slots = [keys, values, queries], [h + 1, h + 1, h]
         else:
             tensors, slots = [queries], [h]
-        first, second, packed = stage(place, here, tensors, slots, n_u, hp, after)
+        first, second, packed = stage(place, here, tensors, slots, n_u, after)
         here = to_shares(packed, n_c, n_u)
         q_of.append((here, len(tensors) - 1))
         kv.append(gather_chips(first, second, n_c))
@@ -328,9 +330,9 @@
     total = None
     for h in range(hp):
         last = h == hp - 1
-        parts = attend(place, table, *q_of[h], *kv[h], n_u, last, ())
+        parts = attend(place, table, *q_of[h], *kv[h], n_u, last)
         parts = send_all(parts, n_c, n_u, -1) if last else to_shares(parts[0], n_c, n_u)
-        total = project(place, parts, h, out_weight, n_u, hp, total)
+        total = project(place, parts, out_weight, h, n_u, hp, total)
     return total
 
 

time: 155 us -> 150 us (0.968)
  Pallas kernels: 43.1 us -> 35.6 us
  waiting for transfers between devices: 56 us -> 59.4 us
    pallas_call x2, Pallas kernels: 16.6 us -> 12 us  [project(): pl.pallas_call(body, out_shape=jax.ShapeDtypeStruct((T, width), jnp.bfloa...]
    pallas_call x2, Pallas kernels: 15.6 us -> 12.6 us  [attend(): pl.pallas_call(body, out_shape=[jax.ShapeDtypeStruct((T, DH) if apart els...]
    ppermute x14, waiting for transfers between devices: 12 us -> 14 us  [send(): return lax.ppermute(x, ('ctx', 'ulys'), pairs)]
    unnamed x59 -> x47, local copies, waits for them, and re-layouts: 4.31 us -> 2.84 us
  transfers between devices with their start and end apart: 29 -> 29, of which waited for: 9 -> 11; matrix products, arithmetic and copies ran while one was open for 1% -> 1% of each run, Pallas kernels for 15% -> 12%
where the time goes in v4:
time: 150 us; the launch traced here: 149 us
  waiting for transfers between devices  59.4 us (40%)
  starting transfers between devices  48.5 us (32%)
  Pallas kernels  35.6 us (24%)
  local copies, waits for them, and re-layouts  3.58 us (2%)
  other arithmetic  1.54 us (1%)
    ppermute x12, waiting for transfers between devices, swap_chip(): return lax.ppermute(x, 'ctx', [(i, i ^ 2 * bit) for i in range(n_c)])  45.4 us
    all_to_all x3, starting transfers between devices, to_shares(): lax.all_to_all(x, ('ctx', 'ulys'), split_axis=0, concat_axis=0, tiled=Tru...  17.8 us
    ppermute x14, starting transfers between devices, send(): return lax.ppermute(x, ('ctx', 'ulys'), pairs)  17.5 us
    ppermute x14, waiting for transfers between devices, send(): return lax.ppermute(x, ('ctx', 'ulys'), pairs)  14 us
    ppermute x12, starting transfers between devices, swap_chip(): return lax.ppermute(x, 'ctx', [(i, i ^ 2 * bit) for i in range(n_c)])  13.2 us
    pallas_call x2, Pallas kernels, attend(): pl.pallas_call(body, out_shape=[jax.ShapeDtypeStruct((T, DH) if apart els...  12.6 us
    pallas_call x2, Pallas kernels, project(): pl.pallas_call(body, out_shape=jax.ShapeDtypeStruct((T, width), jnp.bfloa...  12 us
    pallas_call x2, Pallas kernels, stage(): pl.pallas_call(body, out_shape=[jax.ShapeDtypeStruct(shape, jnp.bfloat16)...  7.8 us
  transfers between devices with their start and end apart: 29, of which 11 were waited for; matrix products, arithmetic and copies ran while one was open for 1% of the time, Pallas kernels for 12%

profile of v4, /device:TPU:0, one launch (start us, length us, event | category | flops | bytes accessed | tf_op | source)
XLA Modules:
  0.0 149.1 jit_solution(4524730705867358838)
XLA Ops:
  0.7 3.2 %pack_sides.1 = (bf16[2,256,128]{2,1,0:T(8,128)(2,1)}, bf16[2,256,128]{2,1,0:T(8,128)(2,1)}, bf16[2,256,128]{2,1,0:T(8,128)(2,1)}, bf16[2,256,128]{2,1,0:T(8,128...) custom-call(s32[2]{0:T(128)} %pad_add_fusion.place, ...), custom_call_target="tpu_custom_call" | custom-call | flops 3449999872 | tf_op jit(solution)/shard_map/pack_sides/pallas_call | solution.py:62
  4.4 2.6 %collective-permute-start.1 = (bf16[2,256,128]{2,1,0:T(8,128)(2,1)}, bf16[2,256,128]{2,1,0:T(8,128)(2,1)S(1)}, u32[]{:S(2)}, u32[]{:S(2)}) collective-permute-start(bf16[2,256,128]{2,1,0:T(8,128)(2,1)} %get-tuple-element.29), channel_id=1, source_target_pairs={{0,1},{1,2},{2,3},{3,0},{4,5},{5,6},{6,7},{7,4},{8,9},{9,10},{10,1... | collective-permute-start | bytes 393224 | tf_op jit(solution)/shard_map/ppermute | solution.py:120
  7.0 1.3 collective-permute-start.2
  8.3 1.3 collective-permute-start.3
  12.0 2.3 %collective-permute-start.5 = (bf16[2,256,128]{2,1,0:T(8,128)(2,1)}, bf16[2,256,128]{2,1,0:T(8,128)(2,1)S(1)}, u32[]{:S(2)}, u32[]{:S(2)}) collective-permute-start(bf16[2,256,128]{2,1,0:T(8,128)(2,1)} %get-tuple-element.33), channel_id=1, source_target_pairs={{0,3},{1,0},{2,1},{3,2},{4,7},{5,4},{6,5},{7,6},{8,11},{9,8},{10,9... | collective-permute-start | bytes 393224 | tf_op jit(solution)/shard_map/ppermute | solution.py:120
  16.1 8.6 %collective-permute-done.3.refs_4_ = bf16[2,256,128]{2,1,0:T(8,128)(2,1)S(1)} collective-permute-done((bf16[2,256,128]{2,1,0:T(8,128)(2,1)}, bf16[2,256,128]{2,1,0:T(8,128)(2,1)S(1)}, u32[]{:S(2)}, u32[]{:S(2)}) %collective-permute-start.3) | collective-permute-done | bytes 131104 | tf_op jit(solution)/shard_map/ppermute | solution.py:120
  24.6 2.7 %collective-permute-done.4.refs_5_ = bf16[2,256,128]{2,1,0:T(8,128)(2,1)S(1)} collective-permute-done((bf16[2,256,128]{2,1,0:T(8,128)(2,1)}, bf16[2,256,128]{2,1,0:T(8,128)(2,1)S(1)}, u32[]{:S(2)}, u32[]{:S(2)}) %collective-permute-start.4) | collective-permute-done | bytes 131104 | tf_op jit(solution)/shard_map/ppermute | solution.py:120
  28.1 4.3 %stage.2 = (bf16[2048,128]{1,0:T(8,128)(2,1)}, bf16[2048,128]{1,0:T(8,128)(2,1)}, bf16[8,3,256,128]{3,2,1,0:T(8,128)(2,1)}) custom-call(s32[2]{0:T(128)} %pad_add_fusion.place, bf16[2,256,128]{2,1,0:T(8,128)(2,1)} %get-tuple-element.27.refs_0_, bf16[2,256,128]{2,1,0:T(8,128)(2,1)} %copy-done.16, bf16[2,256,128]{2,1,0:T(8,128)(2,1)} %copy-done.17, ...), custom_call_target="tpu_custom_call" | custom-call | flops 3449999872 | tf_op jit(solution)/shard_map/stage/pallas_call | solution.py:95
  32.4 8.3 %all-to-all-start = ((bf16[8,3,256,128]{3,2,1,0:T(8,128)(2,1)}), bf16[8,3,256,128]{3,2,1,0:T(8,128)(2,1)S(1)}, u32[]{:S(2)}, u32[]{:S(2)}) async-start(bf16[8,3,256,128]{3,2,1,0:T(8,128)(2,1)} %get-tuple-element.35), calls=%async_computation | async-start | bytes 3145728 | tf_op jit(solution)/shard_map/all_to_all | solution.py:111
  40.7 1.6 %collective-permute-start.8 = (bf16[2048,128]{1,0:T(8,128)(2,1)S(1)}, bf16[2048,128]{1,0:T(8,128)(2,1)S(1)}, u32[]{:S(2)}, u32[]{:S(2)}) collective-permute-start(bf16[2048,128]{1,0:T(8,128)(2,1)S(1)} %copy-done.5), channel_id=1, source_target_pairs={{0,16},{4,20},{8,24},{12,28},{16,0},{20,4},{24,8},{28,12},{1,17},{... | collective-permute-start | bytes 1572872 | tf_op jit(solution)/shard_map/ppermute | solution.py:128
  42.3 1.5 %collective-permute-start.10 = (bf16[2048,128]{1,0:T(8,128)(2,1)S(1)}, bf16[2048,128]{1,0:T(8,128)(2,1)S(1)}, u32[]{:S(2)}, u32[]{:S(2)}) collective-permute-start(bf16[2048,128]{1,0:T(8,128)(2,1)S(1)} %copy-done.6), channel_id=1, source_target_pairs={{0,8},{4,12},{8,0},{12,4},{16,24},{20,28},{24,16},{28,20},{1,9},{5... | collective-permute-start | bytes 1572872 | tf_op jit(solution)/shard_map/ppermute | solution.py:128
  44.8 10.7 %collective-permute-done.8.refs_3_ = bf16[2048,128]{1,0:T(8,128)(2,1)S(1)} collective-permute-done((bf16[2048,128]{1,0:T(8,128)(2,1)S(1)}, bf16[2048,128]{1,0:T(8,128)(2,1)S(1)}, u32[]{:S(2)}, u32[]{:S(2)}) %collective-permute-start.8) | collective-permute-done | bytes 524320 | tf_op jit(solution)/shard_map/ppermute | solution.py:128
  55.5 1.5 %collective-permute-start.9 = (bf16[2048,128]{1,0:T(8,128)(2,1)S(1)}, bf16[2048,128]{1,0:T(8,128)(2,1)S(1)}, u32[]{:S(2)}, u32[]{:S(2)}) collective-permute-start(bf16[2048,128]{1,0:T(8,128)(2,1)S(1)} %collective-permute-done.8.refs_3_), channel_id=1, source_target_pairs={{0,8},{4,12},{8,0},{12,4},{16,24},{20,28},{24,16},{28,20},{1,9},{5... | collective-permute-start | bytes 1572872 | tf_op jit(solution)/shard_map/ppermute | solution.py:128
  57.0 1.5 collective-permute-start.12
  58.5 9.8 %collective-permute-done.7.refs_2_ = bf16[2048,128]{1,0:T(8,128)(2,1)S(1)} collective-permute-done((bf16[2048,128]{1,0:T(8,128)(2,1)S(1)}, bf16[2048,128]{1,0:T(8,128)(2,1)S(1)}, u32[]{:S(2)}, u32[]{:S(2)}) %collective-permute-start.7) | collective-permute-done | bytes 524320 | tf_op jit(solution)/shard_map/ppermute | solution.py:128
  68.3 10.4 %collective-permute-done.9.refs_4_ = bf16[2048,128]{1,0:T(8,128)(2,1)S(1)} collective-permute-done((bf16[2048,128]{1,0:T(8,128)(2,1)S(1)}, bf16[2048,128]{1,0:T(8,128)(2,1)S(1)}, u32[]{:S(2)}, u32[]{:S(2)}) %collective-permute-start.9) | collective-permute-done | bytes 524320 | tf_op jit(solution)/shard_map/ppermute | solution.py:128
  80.7 3.5 %stage.3 = (bf16[2048,128]{1,0:T(8,128)(2,1)}, bf16[2048,128]{1,0:T(8,128)(2,1)}, bf16[8,1,256,128]{3,2,1,0:T(8,128)(2,1)}) custom-call(s32[2]{0:T(128)} %pad_add_fusion.place, bf16[8,3,256,128]{3,2,1,0:T(8,128)(2,1)} %copy-done.2, bf16[256,2048]{1,0:T(8,128)(2,1)} %refs_1_.4, bf16[2048,128]{1,0:T(8,128)(2,1)} %copy-done.9, bf16[2048,128]{1,0:T(8,128)(2,1)} %copy-done.7, ...), custom_call_target="tpu_custom_call" | custom-call | flops 3449999872 | tf_op jit(solution)/shard_map/stage/pallas_call | solution.py:95
  84.8 1.5 %collective-permute-start.16 = (bf16[2048,128]{1,0:T(8,128)(2,1)}, bf16[2048,128]{1,0:T(8,128)(2,1)S(1)}, u32[]{:S(2)}, u32[]{:S(2)}) collective-permute-start(bf16[2048,128]{1,0:T(8,128)(2,1)} %get-tuple-element.40.refs_5_), channel_id=1, source_target_pairs={{0,8},{4,12},{8,0},{12,4},{16,24},{20,28},{24,16},{28,20},{1,9},{5... | collective-permute-start | bytes 1572872 | tf_op jit(solution)/shard_map/ppermute | solution.py:128
  86.3 4.7 %all-to-all-start.1 = ((bf16[8,1,256,128]{3,2,1,0:T(8,128)(2,1)}), bf16[8,1,256,128]{3,2,1,0:T(8,128)(2,1)S(1)}, u32[]{:S(2)}, u32[]{:S(2)}) async-start(bf16[8,1,256,128]{3,2,1,0:T(8,128)(2,1)} %get-tuple-element.38), calls=%async_computation.1 | async-start | bytes 1048576 | tf_op jit(solution)/shard_map/all_to_all | solution.py:111
  91.6 1.5 %collective-permute-start.17 = (bf16[2048,128]{1,0:T(8,128)(2,1)}, bf16[2048,128]{1,0:T(8,128)(2,1)S(1)}, u32[]{:S(2)}, u32[]{:S(2)}) collective-permute-start(bf16[2048,128]{1,0:T(8,128)(2,1)} %get-tuple-element.40.refs_5_), channel_id=1, source_target_pairs={{0,16},{4,20},{8,24},{12,28},{16,0},{20,4},{24,8},{28,12},{1,17},{... | collective-permute-start | bytes 1572872 | tf_op jit(solution)/shard_map/ppermute | solution.py:128
  93.1 6.3 %collective-permute-done.14.refs_3_ = bf16[2048,128]{1,0:T(8,128)(2,1)S(1)} collective-permute-done((bf16[2048,128]{1,0:T(8,128)(2,1)}, bf16[2048,128]{1,0:T(8,128)(2,1)S(1)}, u32[]{:S(2)}, u32[]{:S(2)}) %collective-permute-start.14) | collective-permute-done | bytes 524320 | tf_op jit(solution)/shard_map/ppermute | solution.py:128
  99.4 1.5 %collective-permute-start.15 = (bf16[2048,128]{1,0:T(8,128)(2,1)S(1)}, bf16[2048,128]{1,0:T(8,128)(2,1)}, u32[]{:S(2)}, u32[]{:S(2)}) collective-permute-start(bf16[2048,128]{1,0:T(8,128)(2,1)S(1)} %collective-permute-done.14.refs_3_), channel_id=1, source_target_pairs={{0,8},{4,12},{8,0},{12,4},{16,24},{20,28},{24,16},{28,20},{1,9},{5... | collective-permute-start | bytes 1572872 | tf_op jit(solution)/shard_map/ppermute | solution.py:128
  101.4 6.3 %attend.3 = bf16[8,256,128]{2,1,0:T(8,128)(2,1)} custom-call(s32[2]{0:T(128)} %pad_add_fusion.place, s32[32,8]{1,0:T(8,128)} %fusion.8.refs_11_.table, bf16[8,3,256,128]{3,2,1,0:T(8,128)(2,1)} %copy-done.2, bf16[2048,128]{1,0:T(8,128)(2,1)} %get-tuple-element.36.refs_1_, bf16[2048,128]{1,0:T(8,128)(2,1)} %copy-done.9, bf16[2048,128]{1,0:T(8,128)(2,1)} %copy-done.7, ...), custom_call_target="tpu_custom_call" | custom-call | flops 9200000000 | tf_op jit(solution)/shard_map/attend/pallas_call | solution.py:208
  107.8 4.7 %all-to-all-start.2 = ((bf16[8,256,128]{2,1,0:T(8,128)(2,1)}), bf16[8,256,128]{2,1,0:T(8,128)(2,1)S(1)}, u32[]{:S(2)}, u32[]{:S(2)}) async-start(bf16[8,256,128]{2,1,0:T(8,128)(2,1)} %attend.3), calls=%async_computation.2 | async-start | bytes 1048576 | tf_op jit(solution)/shard_map/all_to_all | solution.py:111
  112.6 8.2 %collective-permute-done.15.refs_4_ = bf16[2048,128]{1,0:T(8,128)(2,1)} collective-permute-done((bf16[2048,128]{1,0:T(8,128)(2,1)S(1)}, bf16[2048,128]{1,0:T(8,128)(2,1)}, u32[]{:S(2)}, u32[]{:S(2)}) %collective-permute-start.15) | collective-permute-done | bytes 524320 | tf_op jit(solution)/shard_map/ppermute | solution.py:128
  120.8 6.3 %attend.2 = (bf16[256,128]{1,0:T(8,128)(2,1)}, bf16[256,128]{1,0:T(8,128)(2,1)}, bf16[256,128]{1,0:T(8,128)(2,1)}, bf16[256,128]{1,0:T(8,128)(2,1)}, bf16[256,12...) custom-call(s32[2]{0:T(128)} %pad_add_fusion.place, ...), custom_call_target="tpu_custom_call" | custom-call | flops 9200000000 | tf_op jit(solution)/shard_map/attend/pallas_call | solution.py:208
  127.2 3.0 %collective-permute-start.20 = (bf16[256,128]{1,0:T(8,128)(2,1)}, bf16[256,128]{1,0:T(8,128)(2,1)S(1)}, u32[]{:S(2)}, u32[]{:S(2)}) collective-permute-start(bf16[256,128]{1,0:T(8,128)(2,1)} %get-tuple-element.43), channel_id=1, source_target_pairs={{0,3},{1,0},{2,1},{3,2},{4,7},{5,4},{6,5},{7,6},{8,11},{9,8},{10,9... | collective-permute-start | bytes 196616 | tf_op jit(solution)/shard_map/ppermute | solution.py:120
  130.5 2.6 %collective-permute-start.23 = (bf16[256,128]{1,0:T(8,128)(2,1)}, bf16[256,128]{1,0:T(8,128)(2,1)S(1)}, u32[]{:S(2)}, u32[]{:S(2)}) collective-permute-start(bf16[256,128]{1,0:T(8,128)(2,1)} %get-tuple-element.46), channel_id=1, source_target_pairs={{0,6},{1,7},{2,4},{3,5},{4,2},{5,3},{6,0},{7,1},{8,14},{9,15},{10,... | collective-permute-start | bytes 196616 | tf_op jit(solution)/shard_map/ppermute | solution.py:120
  133.1 1.5 collective-permute-start.24
  134.9 5.5 %project.2.refs_9_ = f32[256,4096]{1,0:T(8,128)S(1)} custom-call(s32[2]{0:T(128)S(1)} %copy-done, bf16[8,256,128]{2,1,0:T(8,128)(2,1)S(1)} %all-to-all-done.2.refs_0_, bf16[2048,4096]{1,0:T(8,128)(2,1)} %refs_8_.3), custom_call_target="tpu_custom_call" | custom-call | flops 8049999872 | tf_op jit(solution)/shard_map/project/pallas_call | solution.py:275
  140.4 1.7 %collective-permute-done.22.refs_4_ = bf16[256,128]{1,0:T(8,128)(2,1)S(1)} collective-permute-done((bf16[256,128]{1,0:T(8,128)(2,1)}, bf16[256,128]{1,0:T(8,128)(2,1)S(1)}, u32[]{:S(2)}, u32[]{:S(2)}) %collective-permute-start.22) | collective-permute-done | bytes 65568 | tf_op jit(solution)/shard_map/ppermute | solution.py:120
  142.4 6.5 %project.3 = bf16[256,4096]{1,0:T(8,128)(2,1)} custom-call(s32[2]{0:T(128)S(1)} %copy-done, bf16[256,128]{1,0:T(8,128)(2,1)S(1)} %copy-done.1, bf16[256,128]{1,0:T(8,128)(2,1)S(1)} %collective-permute-done.19.refs_1_, bf16[256,128]{1,0:T(8,128)(2,1)S(1)} %collective-permute-done.20.refs_2_, bf16[256,128]{1,0:T(8,128)(2,1)S(1)} %collective-permute-done.21.refs_3_, ...), custom_call_target="tpu_custom_call" | custom-call | flops 8049999872 | tf_op jit(solution)/shard_map/project/pallas_call | solution.py:275
  (91 shorter events, 11.7 us)
Async XLA Ops:
  3.8 8.2 %collective-permute-start = (bf16[2,256,128]{2,1,0:T(8,128)(2,1)}, bf16[2,256,128]{2,1,0:T(8,128)(2,1)S(1)}, u32[]{:S(2)}, u32[]{:S(2)}) collective-permute-start(bf16[2,256,128]{2,1,0:T(8,128)(2,1)} %get-tuple-element.28), channel_id=1, source_target_pairs={{0,4},{1,5},{2,6},{3,7},{4,0},{5,1},{6,2},{7,3},{8,12},{9,13},{10,... | collective-permute-start | bytes 393224 | tf_op jit(solution)/shard_map/ppermute | solution.py:120
  4.4 10.0 %collective-permute-start.1 = (bf16[2,256,128]{2,1,0:T(8,128)(2,1)}, bf16[2,256,128]{2,1,0:T(8,128)(2,1)S(1)}, u32[]{:S(2)}, u32[]{:S(2)}) collective-permute-start(bf16[2,256,128]{2,1,0:T(8,128)(2,1)} %get-tuple-element.29), channel_id=1, source_target_pairs={{0,1},{1,2},{2,3},{3,0},{4,5},{5,6},{6,7},{7,4},{8,9},{9,10},{10,1... | collective-permute-start | bytes 393224 | tf_op jit(solution)/shard_map/ppermute | solution.py:120
  7.0 9.1 %collective-permute-start.2 = (bf16[2,256,128]{2,1,0:T(8,128)(2,1)}, bf16[2,256,128]{2,1,0:T(8,128)(2,1)S(1)}, u32[]{:S(2)}, u32[]{:S(2)}) collective-permute-start(bf16[2,256,128]{2,1,0:T(8,128)(2,1)} %get-tuple-element.30), channel_id=1, source_target_pairs={{0,5},{1,6},{2,7},{3,4},{4,1},{5,2},{6,3},{7,0},{8,13},{9,14},{10,... | collective-permute-start | bytes 393224 | tf_op jit(solution)/shard_map/ppermute | solution.py:120
  8.3 16.3 %collective-permute-start.3 = (bf16[2,256,128]{2,1,0:T(8,128)(2,1)}, bf16[2,256,128]{2,1,0:T(8,128)(2,1)S(1)}, u32[]{:S(2)}, u32[]{:S(2)}) collective-permute-start(bf16[2,256,128]{2,1,0:T(8,128)(2,1)} %get-tuple-element.31), channel_id=1, source_target_pairs={{0,2},{1,3},{2,0},{3,1},{4,6},{5,7},{6,4},{7,5},{8,10},{9,11},{10,... | collective-permute-start | bytes 393224 | tf_op jit(solution)/shard_map/ppermute | solution.py:120
  9.7 17.7 %collective-permute-start.4 = (bf16[2,256,128]{2,1,0:T(8,128)(2,1)}, bf16[2,256,128]{2,1,0:T(8,128)(2,1)S(1)}, u32[]{:S(2)}, u32[]{:S(2)}) collective-permute-start(bf16[2,256,128]{2,1,0:T(8,128)(2,1)} %get-tuple-element.32), channel_id=1, source_target_pairs={{0,6},{1,7},{2,4},{3,5},{4,2},{5,3},{6,0},{7,1},{8,14},{9,15},{10,... | collective-permute-start | bytes 393224 | tf_op jit(solution)/shard_map/ppermute | solution.py:120
  12.0 15.3 %collective-permute-start.5 = (bf16[2,256,128]{2,1,0:T(8,128)(2,1)}, bf16[2,256,128]{2,1,0:T(8,128)(2,1)S(1)}, u32[]{:S(2)}, u32[]{:S(2)}) collective-permute-start(bf16[2,256,128]{2,1,0:T(8,128)(2,1)} %get-tuple-element.33), channel_id=1, source_target_pairs={{0,3},{1,0},{2,1},{3,2},{4,7},{5,4},{6,5},{7,6},{8,11},{9,8},{10,9... | collective-permute-start | bytes 393224 | tf_op jit(solution)/shard_map/ppermute | solution.py:120
  14.3 13.0 %collective-permute-start.6 = (bf16[2,256,128]{2,1,0:T(8,128)(2,1)}, bf16[2,256,128]{2,1,0:T(8,128)(2,1)S(1)}, u32[]{:S(2)}, u32[]{:S(2)}) collective-permute-start(bf16[2,256,128]{2,1,0:T(8,128)(2,1)} %get-tuple-element.34), channel_id=1, source_target_pairs={{0,7},{1,4},{2,5},{3,6},{4,3},{5,0},{6,1},{7,2},{8,15},{9,12},{10,... | collective-permute-start | bytes 393224 | tf_op jit(solution)/shard_map/ppermute | solution.py:120
  32.4 47.1 %all-to-all-start = ((bf16[8,3,256,128]{3,2,1,0:T(8,128)(2,1)}), bf16[8,3,256,128]{3,2,1,0:T(8,128)(2,1)S(1)}, u32[]{:S(2)}, u32[]{:S(2)}) async-start(bf16[8,3,256,128]{3,2,1,0:T(8,128)(2,1)} %get-tuple-element.35), calls=%async_computation | async-start | bytes 3145728 | tf_op jit(solution)/shard_map/all_to_all | solution.py:111
  40.7 14.8 %collective-permute-start.8 = (bf16[2048,128]{1,0:T(8,128)(2,1)S(1)}, bf16[2048,128]{1,0:T(8,128)(2,1)S(1)}, u32[]{:S(2)}, u32[]{:S(2)}) collective-permute-start(bf16[2048,128]{1,0:T(8,128)(2,1)S(1)} %copy-done.5), channel_id=1, source_target_pairs={{0,16},{4,20},{8,24},{12,28},{16,0},{20,4},{24,8},{28,12},{1,17},{... | collective-permute-start | bytes 1572872 | tf_op jit(solution)/shard_map/ppermute | solution.py:128
  42.3 14.8 %collective-permute-start.10 = (bf16[2048,128]{1,0:T(8,128)(2,1)S(1)}, bf16[2048,128]{1,0:T(8,128)(2,1)S(1)}, u32[]{:S(2)}, u32[]{:S(2)}) collective-permute-start(bf16[2048,128]{1,0:T(8,128)(2,1)S(1)} %copy-done.6), channel_id=1, source_target_pairs={{0,8},{4,12},{8,0},{12,4},{16,24},{20,28},{24,16},{28,20},{1,9},{5... | collective-permute-start | bytes 1572872 | tf_op jit(solution)/shard_map/ppermute | solution.py:128
  43.8 24.5 %collective-permute-start.7 = (bf16[2048,128]{1,0:T(8,128)(2,1)S(1)}, bf16[2048,128]{1,0:T(8,128)(2,1)S(1)}, u32[]{:S(2)}, u32[]{:S(2)}) collective-permute-start(bf16[2048,128]{1,0:T(8,128)(2,1)S(1)} %copy-done.5), channel_id=1, source_target_pairs={{0,8},{4,12},{8,0},{12,4},{16,24},{20,28},{24,16},{28,20},{1,9},{5... | collective-permute-start | bytes 1572872 | tf_op jit(solution)/shard_map/ppermute | solution.py:128
  44.3 24.0 %collective-permute-start.11 = (bf16[2048,128]{1,0:T(8,128)(2,1)S(1)}, bf16[2048,128]{1,0:T(8,128)(2,1)S(1)}, u32[]{:S(2)}, u32[]{:S(2)}) collective-permute-start(bf16[2048,128]{1,0:T(8,128)(2,1)S(1)} %copy-done.6), channel_id=1, source_target_pairs={{0,16},{4,20},{8,24},{12,28},{16,0},{20,4},{24,8},{28,12},{1,17},{... | collective-permute-start | bytes 1572872 | tf_op jit(solution)/shard_map/ppermute | solution.py:128
  55.5 24.1 %copy-start.7 = (bf16[2048,128]{1,0:T(8,128)(2,1)}, bf16[2048,128]{1,0:T(8,128)(2,1)S(1)}, u32[]{:S(2)}) copy-start(bf16[2048,128]{1,0:T(8,128)(2,1)S(1)} %collective-permute-done.8.refs_3_) | copy-start | bytes 1572868
  55.5 23.2 %collective-permute-start.9 = (bf16[2048,128]{1,0:T(8,128)(2,1)S(1)}, bf16[2048,128]{1,0:T(8,128)(2,1)S(1)}, u32[]{:S(2)}, u32[]{:S(2)}) collective-permute-start(bf16[2048,128]{1,0:T(8,128)(2,1)S(1)} %collective-permute-done.8.refs_3_), channel_id=1, source_target_pairs={{0,8},{4,12},{8,0},{12,4},{16,24},{20,28},{24,16},{28,20},{1,9},{5... | collective-permute-start | bytes 1572872 | tf_op jit(solution)/shard_map/ppermute | solution.py:128
  57.0 21.7 %copy-start.8 = (bf16[2048,128]{1,0:T(8,128)(2,1)}, bf16[2048,128]{1,0:T(8,128)(2,1)S(1)}, u32[]{:S(2)}) copy-start(bf16[2048,128]{1,0:T(8,128)(2,1)S(1)} %collective-permute-done.10.refs_5_.refs_6_) | copy-start | bytes 1572868
  57.0 22.5 %collective-permute-start.12 = (bf16[2048,128]{1,0:T(8,128)(2,1)S(1)}, bf16[2048,128]{1,0:T(8,128)(2,1)}, u32[]{:S(2)}, u32[]{:S(2)}) collective-permute-start(bf16[2048,128]{1,0:T(8,128)(2,1)S(1)} %collective-permute-done.10.refs_5_.refs_6_), channel_id=1, source_target_pairs={{0,16},{4,20},{8,24},{12,28},{16,0},{20,4},{24,8},{28,12},{1,17},{... | collective-permute-start | bytes 1572872 | tf_op jit(solution)/shard_map/ppermute | solution.py:128
  84.2 15.1 %collective-permute-start.14 = (bf16[2048,128]{1,0:T(8,128)(2,1)}, bf16[2048,128]{1,0:T(8,128)(2,1)S(1)}, u32[]{:S(2)}, u32[]{:S(2)}) collective-permute-start(bf16[2048,128]{1,0:T(8,128)(2,1)} %get-tuple-element.39.refs_1_), channel_id=1, source_target_pairs={{0,16},{4,20},{8,24},{12,28},{16,0},{20,4},{24,8},{28,12},{1,17},{... | collective-permute-start | bytes 1572872 | tf_op jit(solution)/shard_map/ppermute | solution.py:128
  84.8 16.1 %collective-permute-start.16 = (bf16[2048,128]{1,0:T(8,128)(2,1)}, bf16[2048,128]{1,0:T(8,128)(2,1)S(1)}, u32[]{:S(2)}, u32[]{:S(2)}) collective-permute-start(bf16[2048,128]{1,0:T(8,128)(2,1)} %get-tuple-element.40.refs_5_), channel_id=1, source_target_pairs={{0,8},{4,12},{8,0},{12,4},{16,24},{20,28},{24,16},{28,20},{1,9},{5... | collective-permute-start | bytes 1572872 | tf_op jit(solution)/shard_map/ppermute | solution.py:128
  86.3 21.4 %all-to-all-start.1 = ((bf16[8,1,256,128]{3,2,1,0:T(8,128)(2,1)}), bf16[8,1,256,128]{3,2,1,0:T(8,128)(2,1)S(1)}, u32[]{:S(2)}, u32[]{:S(2)}) async-start(bf16[8,1,256,128]{3,2,1,0:T(8,128)(2,1)} %get-tuple-element.38), calls=%async_computation.1 | async-start | bytes 1048576 | tf_op jit(solution)/shard_map/all_to_all | solution.py:111
  91.0 21.5 %collective-permute-start.13 = (bf16[2048,128]{1,0:T(8,128)(2,1)}, bf16[2048,128]{1,0:T(8,128)(2,1)S(1)}, u32[]{:S(2)}, u32[]{:S(2)}) collective-permute-start(bf16[2048,128]{1,0:T(8,128)(2,1)} %get-tuple-element.39.refs_1_), channel_id=1, source_target_pairs={{0,8},{4,12},{8,0},{12,4},{16,24},{20,28},{24,16},{28,20},{1,9},{5... | collective-permute-start | bytes 1572872 | tf_op jit(solution)/shard_map/ppermute | solution.py:128
  91.6 21.0 %collective-permute-start.17 = (bf16[2048,128]{1,0:T(8,128)(2,1)}, bf16[2048,128]{1,0:T(8,128)(2,1)S(1)}, u32[]{:S(2)}, u32[]{:S(2)}) collective-permute-start(bf16[2048,128]{1,0:T(8,128)(2,1)} %get-tuple-element.40.refs_5_), channel_id=1, source_target_pairs={{0,16},{4,20},{8,24},{12,28},{16,0},{20,4},{24,8},{28,12},{1,17},{... | collective-permute-start | bytes 1572872 | tf_op jit(solution)/shard_map/ppermute | solution.py:128
  99.4 21.4 %collective-permute-start.15 = (bf16[2048,128]{1,0:T(8,128)(2,1)S(1)}, bf16[2048,128]{1,0:T(8,128)(2,1)}, u32[]{:S(2)}, u32[]{:S(2)}) collective-permute-start(bf16[2048,128]{1,0:T(8,128)(2,1)S(1)} %collective-permute-done.14.refs_3_), channel_id=1, source_target_pairs={{0,8},{4,12},{8,0},{12,4},{16,24},{20,28},{24,16},{28,20},{1,9},{5... | collective-permute-start | bytes 1572872 | tf_op jit(solution)/shard_map/ppermute | solution.py:128
  100.9 19.9 %collective-permute-start.18 = (bf16[2048,128]{1,0:T(8,128)(2,1)S(1)}, bf16[2048,128]{1,0:T(8,128)(2,1)}, u32[]{:S(2)}, u32[]{:S(2)}) collective-permute-start(bf16[2048,128]{1,0:T(8,128)(2,1)S(1)} %collective-permute-done.16.refs_6_), channel_id=1, source_target_pairs={{0,16},{4,20},{8,24},{12,28},{16,0},{20,4},{24,8},{28,12},{1,17},{... | collective-permute-start | bytes 1572872 | tf_op jit(solution)/shard_map/ppermute | solution.py:128
  107.8 27.1 %all-to-all-start.2 = ((bf16[8,256,128]{2,1,0:T(8,128)(2,1)}), bf16[8,256,128]{2,1,0:T(8,128)(2,1)S(1)}, u32[]{:S(2)}, u32[]{:S(2)}) async-start(bf16[8,256,128]{2,1,0:T(8,128)(2,1)} %attend.3), calls=%async_computation.2 | async-start | bytes 1048576 | tf_op jit(solution)/shard_map/all_to_all | solution.py:111
  112.5 22.4 %copy-start = (s32[2]{0:T(128)S(1)}, s32[2]{0:T(128)}, u32[]{:S(2)}) copy-start(s32[2]{0:T(128)} %pad_add_fusion.place) | copy-start | bytes 28
  127.1 6.0 %collective-permute-start.19 = (bf16[256,128]{1,0:T(8,128)(2,1)}, bf16[256,128]{1,0:T(8,128)(2,1)S(1)}, u32[]{:S(2)}, u32[]{:S(2)}) collective-permute-start(bf16[256,128]{1,0:T(8,128)(2,1)} %get-tuple-element.42), channel_id=1, source_target_pairs={{0,4},{1,5},{2,6},{3,7},{4,0},{5,1},{6,2},{7,3},{8,12},{9,13},{10,... | collective-permute-start | bytes 196616 | tf_op jit(solution)/shard_map/ppermute | solution.py:120
  127.2 7.4 %collective-permute-start.20 = (bf16[256,128]{1,0:T(8,128)(2,1)}, bf16[256,128]{1,0:T(8,128)(2,1)S(1)}, u32[]{:S(2)}, u32[]{:S(2)}) collective-permute-start(bf16[256,128]{1,0:T(8,128)(2,1)} %get-tuple-element.43), channel_id=1, source_target_pairs={{0,3},{1,0},{2,1},{3,2},{4,7},{5,4},{6,5},{7,6},{8,11},{9,8},{10,9... | collective-permute-start | bytes 196616 | tf_op jit(solution)/shard_map/ppermute | solution.py:120
  130.2 10.2 %collective-permute-start.21 = (bf16[256,128]{1,0:T(8,128)(2,1)}, bf16[256,128]{1,0:T(8,128)(2,1)S(1)}, u32[]{:S(2)}, u32[]{:S(2)}) collective-permute-start(bf16[256,128]{1,0:T(8,128)(2,1)} %get-tuple-element.44), channel_id=1, source_target_pairs={{0,7},{1,4},{2,5},{3,6},{4,3},{5,0},{6,1},{7,2},{8,15},{9,12},{10,... | collective-permute-start | bytes 196616 | tf_op jit(solution)/shard_map/ppermute | solution.py:120
  130.5 11.7 %collective-permute-start.22 = (bf16[256,128]{1,0:T(8,128)(2,1)}, bf16[256,128]{1,0:T(8,128)(2,1)S(1)}, u32[]{:S(2)}, u32[]{:S(2)}) collective-permute-start(bf16[256,128]{1,0:T(8,128)(2,1)} %get-tuple-element.45), channel_id=1, source_target_pairs={{0,2},{1,3},{2,0},{3,1},{4,6},{5,7},{6,4},{7,5},{8,10},{9,11},{10,... | collective-permute-start | bytes 196616 | tf_op jit(solution)/shard_map/ppermute | solution.py:120
  130.5 11.9 %collective-permute-start.23 = (bf16[256,128]{1,0:T(8,128)(2,1)}, bf16[256,128]{1,0:T(8,128)(2,1)S(1)}, u32[]{:S(2)}, u32[]{:S(2)}) collective-permute-start(bf16[256,128]{1,0:T(8,128)(2,1)} %get-tuple-element.46), channel_id=1, source_target_pairs={{0,6},{1,7},{2,4},{3,5},{4,2},{5,3},{6,0},{7,1},{8,14},{9,15},{10,... | collective-permute-start | bytes 196616 | tf_op jit(solution)/shard_map/ppermute | solution.py:120
  133.1 9.3 %collective-permute-start.24 = (bf16[256,128]{1,0:T(8,128)(2,1)}, bf16[256,128]{1,0:T(8,128)(2,1)S(1)}, u32[]{:S(2)}, u32[]{:S(2)}) collective-permute-start(bf16[256,128]{1,0:T(8,128)(2,1)} %get-tuple-element.47), channel_id=1, source_target_pairs={{0,1},{1,2},{2,3},{3,0},{4,5},{5,6},{6,7},{7,4},{8,9},{9,10},{10,1... | collective-permute-start | bytes 196616 | tf_op jit(solution)/shard_map/ppermute | solution.py:120
  134.6 7.8 %collective-permute-start.25 = (bf16[256,128]{1,0:T(8,128)(2,1)}, bf16[256,128]{1,0:T(8,128)(2,1)S(1)}, u32[]{:S(2)}, u32[]{:S(2)}) collective-permute-start(bf16[256,128]{1,0:T(8,128)(2,1)} %get-tuple-element.48), channel_id=1, source_target_pairs={{0,5},{1,6},{2,7},{3,4},{4,1},{5,2},{6,3},{7,0},{8,13},{9,14},{10,... | collective-permute-start | bytes 196616 | tf_op jit(solution)/shard_map/ppermute | solution.py:120
  (20 other events, 148.6 us)

commit v5 on v4

--- a/solution.py
+++ b/solution.py
@@ -15,7 +15,6 @@
 LOG2E = 1.4426950408889634
 
 ANY = pl.BlockSpec(memory_space=pl.ANY)
-SMEM = pl.BlockSpec(memory_space=pltpu.SMEM)
 VMEM = pl.BlockSpec(memory_space=pltpu.VMEM)
 
 
@@ -42,66 +41,119 @@
     return [(r, d) for d in range(n_u) for r in range(2)]
 
 
-def share_at(place, r, d, n_u):
-    z, core = place[0], place[1]
+def share_at(r, d, n_u):
+    z, core = lax.axis_index("ulys"), lax.rem(lax.axis_index("ctx"), 2)
     return 2 * lax.rem(z + d + n_u, n_u) + (core if r == 0 else 1 - core)
 
 
-def pack_sides(place, tensors, slots, n_u):
-    T, nb, n_out = tensors[0].shape[0], len(tensors), 2 * n_u
-
-    def body(place, *refs):
-        ins, outs, sems = refs[:nb], refs[nb:-1], refs[-1]
+def pack_first(tensors, n_u, early):
+    T, nb, n_s = tensors[0].shape[0], len(tensors), 2 * n_u
+    counts = [nb * (2 if early and d == 0 else 1) for _, d in sides(n_u)]
+
+    def body(*refs):
+        ins, outs = refs[:nb], refs[nb : nb + n_s]
+        held, near, in_sems, out_sems = refs[nb + n_s :]
+        pairs = [(ins[i].at[:, pl.ds(0, n_s * DH)], held.at[i]) for i in range(nb)]
+        if early:
+            cols = pl.ds(pl.multiple_of((n_s + 2 * lax.axis_index("ulys")) * DH, DH), 2 * DH)
+            pairs += [(ins[i].at[:, cols], near.at[i]) for i in range(nb)]
+        copy_all(pairs, in_sems)
         pairs = []
-        for out, (r, d) in zip(outs, sides(n_u)):
-            for i in range(nb):
-                col = (slots[i] * n_out + share_at(place, r, d, n_u)) * DH
-                pairs.append((ins[i].at[:, pl.ds(pl.multiple_of(col, DH), DH)], out.at[i]))
-        copy_all(pairs, sems)
+        for out, (r, d), count in zip(outs, sides(n_u), counts):
+            at = pl.multiple_of(share_at(r, d, n_u) * DH, DH)
+            pairs += [(held.at[i, :, pl.ds(at, DH)], out.at[i]) for i in range(nb)]
+            if count > nb:
+                at = pl.multiple_of((lax.rem(lax.axis_index("ctx"), 2) if r == 0 else 1 - lax.rem(lax.axis_index("ctx"), 2)) * DH, DH)
+                pairs += [(near.at[i, :, pl.ds(at, DH)], out.at[nb + i]) for i in range(nb)]
+        copy_all(pairs, out_sems)
 
     return pl.pallas_call(
         body,
-        out_shape=[jax.ShapeDtypeStruct((nb, T, DH), jnp.bfloat16)] * n_out,
-        in_specs=[SMEM] + [ANY] * nb,
-        out_specs=[VMEM] * n_out,
-        scratch_shapes=[pltpu.SemaphoreType.DMA((n_out * nb,))],
+        out_shape=[jax.ShapeDtypeStruct((n, T, DH), jnp.bfloat16) for n in counts],
+        in_specs=[ANY] * nb,
+        out_specs=[ANY] * n_s,
+        scratch_shapes=[
+            pltpu.VMEM((nb, T, n_s * DH), jnp.bfloat16),
+            pltpu.VMEM((nb, T, 2 * DH), jnp.bfloat16),
+            pltpu.SemaphoreType.DMA((2 * nb,)),
+            pltpu.SemaphoreType.DMA((sum(counts),)),
+        ],
         compiler_params=WHOLE,
         cost_estimate=cost(3),
-        name="pack_sides",
-    )(place, *tensors)
-
-
-def stage(place, here, tensors, slots, n_u, after):
+        name="pack_first",
+    )(*tensors)
+
+
+def pack_rest(tensors, bundles, n_u, after):
+    T, nb, n_s = tensors[0].shape[0], len(tensors), 2 * n_u
+    items = [item for bundle in bundles for item in bundle]
+
+    def body(*refs):
+        ins, outs = refs[:nb], refs[nb + 1 : nb + 1 + len(bundles)]
+        held, in_sems, out_sems = refs[nb + 1 + len(bundles) :]
+        pairs, where = [], [(b, i) for b, bundle in enumerate(bundles) for i in range(len(bundle))]
+        for n, (which, slot) in enumerate(items):
+            pairs.append((ins[which].at[:, pl.ds(slot * n_s * DH, n_s * DH)], held.at[n]))
+        copy_all(pairs, in_sems)
+        pairs = []
+        for n, (b, i) in enumerate(where):
+            for k in range(n_s):
+                pairs.append((held.at[n, :, pl.ds(k * DH, DH)], outs[b].at[k, i]))
+        copy_all(pairs, out_sems)
+
+    return pl.pallas_call(
+        body,
+        out_shape=[jax.ShapeDtypeStruct((n_s, len(b), T, DH), jnp.bfloat16) for b in bundles],
+        in_specs=[ANY] * (nb + 1),
+        out_specs=[ANY] * len(bundles),
+        scratch_shapes=[
+            pltpu.VMEM((len(items), T, n_s * DH), jnp.bfloat16),
+            pltpu.SemaphoreType.DMA((len(items),)),
+            pltpu.SemaphoreType.DMA((len(items) * n_s,)),
+        ],
+        compiler_params=WHOLE,
+        cost_estimate=cost(3),
+        name="pack_rest",
+    )(*tensors, after)
+
+
+def stage(here, packed, n_u, rest, after):
     apart = isinstance(here, list)
     blocks = here if apart else [here]
-    n_s, n_b, nb = 2 * n_u, len(blocks), len(tensors)
-    n_split, T = 2, blocks[0].shape[-2]
-    n_copies = n_s * (n_split + nb)
-    n_in = n_b + nb + len(after)
-    shapes = [(n_s * T, DH)] * n_split + [(n_s, nb, T, DH)]
-
-    def body(place, *refs):
-        outs, sems = refs[n_in:-1], refs[-1]
+    n_s, n_b, T = 2 * n_u, len(blocks), blocks[0].shape[-2]
+    n_early = blocks[0].shape[0] - 2 if apart else 0
+    shapes = [((n_s - 2 * rest) * T, DH)] * 2 + [(2 * T, DH)] * n_early
+    n_copies = sum(x.shape[0] for x in blocks) if apart else 2 * (n_s - 2 * rest)
+    n_in, n_out = n_b + 1 + len(after), len(shapes)
+
+    def body(*refs):
+        z, core = lax.axis_index("ulys"), lax.rem(lax.axis_index("ctx"), 2)
+        outs, sems = refs[n_in : n_in + n_out], refs[-1]
         pairs = []
-        for k, (r, d) in enumerate(sides(n_u)):
-            block, sender = (refs[k], share_at(place, r, -d, n_u)) if apart else (refs[0].at[k], k)
-            for i in range(n_split):
-                pairs.append((block.at[i], outs[i].at[pl.ds(pl.multiple_of(sender * T, T), T)]))
-            for i in range(nb):
-                cols = pl.ds((slots[i] * n_s + k) * DH, DH)
-                pairs.append((refs[n_b + i].at[:, cols], outs[-1].at[k, i]))
+        if apart:
+            for k, (r, d) in enumerate(sides(n_u)):
+                at = (2 * ((n_u - d) % n_u) + (core if r == 0 else 1 - core)) * T
+                for i in range(blocks[k].shape[0]):
+                    pairs.append((refs[k].at[i], outs[i].at[pl.ds(pl.multiple_of(at, T), T)]))
+        else:
+            for d in range(rest, n_u):
+                for c in range(2):
+                    src, at = 2 * lax.rem(z + d, n_u) + c, (2 * (d - rest) + c) * T
+                    for i in range(2):
+                        pairs.append((refs[0].at[src, i], outs[i].at[pl.ds(at, T)]))
         copy_all(pairs, sems)
 
     return pl.pallas_call(
         body,
-        out_shape=[jax.ShapeDtypeStruct(shape, jnp.bfloat16) for shape in shapes],
-        in_specs=[SMEM] + [ANY] * n_in,
-        out_specs=[VMEM] * len(shapes),
+        out_shape=[jax.ShapeDtypeStruct(x, jnp.bfloat16) for x in [*shapes, packed.shape]],
+        in_specs=[ANY] * n_in,
+        out_specs=[VMEM] * n_out + [ANY],
+        input_output_aliases={n_b: n_out},
         scratch_shapes=[pltpu.SemaphoreType.DMA((n_copies,))],
         compiler_params=WHOLE,
         cost_estimate=cost(3),
         name="stage",
-    )(place, *blocks, *tensors, *after)
+    )(*blocks, packed, *after)
 
 
 def to_shares(x, n_c, n_u):
@@ -144,29 +196,31 @@
     return [a[t] for t in range(n_p)], [b[t] for t in range(n_p)]
 
 
-def attend(place, table, queries, q_index, keys, values, n_u, apart):
+def attend(table, queries, q_index, keys, values, n_u, apart):
     n_s, _, T, _ = queries.shape
     n_q = n_s * T
-    span = keys[0].shape[0]
+    span = n_s * T
     n_k = span * len(keys)
+    k_parts = [(x, t * span + at) for t, parts in enumerate(keys) for x, at in parts]
+    v_parts = [(x, t * span + at) for t, parts in enumerate(values) for x, at in parts]
     n_rows, n_list = table.shape
     group = 4 * T // BLK
-    arrays = [queries, *keys, *values]
+    arrays = [queries, *(x for x, _ in k_parts + v_parts)]
     n_in, n_out = len(arrays), 2 * n_u if apart else 1
 
-    def body(place, table, *refs):
+    def body(table_ref, *refs):
         ins, outs = refs[:n_in], refs[n_in : n_in + n_out]
-        q_vm, k_vm, v_vm, o_vm, sems, out_sems = refs[n_in + n_out :]
-        pairs = []
+        table, q_vm, k_vm, v_vm, o_vm, sems, out_sems = refs[n_in + n_out :]
+        pairs = [(table_ref, table)]
         for k in range(n_s):
             pairs.append((ins[0].at[k, q_index], q_vm.at[pl.ds(k * T, T)]))
-        for i, ref in enumerate(ins[1:]):
-            vm, t = (k_vm, i) if i < len(keys) else (v_vm, i - len(keys))
-            pairs.append((ref, vm.at[pl.ds(t * span, span)]))
+        for i, (ref, (x, at)) in enumerate(zip(ins[1:], k_parts + v_parts)):
+            vm = k_vm if i < len(k_parts) else v_vm
+            pairs.append((ref, vm.at[pl.ds(at, x.shape[0])]))
         copies = [pltpu.make_async_copy(a, b, sems.at[i]) for i, (a, b) in enumerate(pairs)]
         for c in copies:
             c.start()
-        for c in copies[: n_s + len(keys)]:
+        for c in copies[: 1 + n_s + len(k_parts)]:
             c.wait()
         for step in range(n_rows // group):
             rows = range(step * group, (step + 1) * group)
@@ -186,7 +240,7 @@
             e = jnp.exp2((s - jnp.max(s, axis=-1, keepdims=True)) * (DH**-0.5 * LOG2E))
             w = (e * (1.0 / jnp.sum(e, axis=-1, keepdims=True))).astype(jnp.bfloat16)
             if step == 0:
-                for c in copies[n_s + len(keys) :]:
+                for c in copies[1 + n_s + len(k_parts) :]:
                     c.wait()
             for g, (r, listed) in enumerate(zip(rows, at)):
                 v = jnp.concatenate([v_vm[pl.ds(a, BLK), :] for a in listed], axis=0)
@@ -198,7 +252,7 @@
         pairs = []
         if apart:
             for out, (r, d) in zip(outs, sides(n_u)):
-                at = pl.multiple_of(share_at(place, r, -d, n_u) * T, T)
+                at = pl.multiple_of(share_at(r, -d, n_u) * T, T)
                 pairs.append((o_vm.at[pl.ds(at, T)], out))
         else:
             for k in range(n_s):
@@ -208,23 +262,24 @@
     return pl.pallas_call(
         body,
         out_shape=[jax.ShapeDtypeStruct((T, DH) if apart else (n_s, T, DH), jnp.bfloat16)] * n_out,
-        in_specs=[SMEM, SMEM] + [ANY] * n_in,
+        in_specs=[ANY] * (1 + n_in),
         out_specs=[ANY] * n_out,
         scratch_shapes=[
+            pltpu.SMEM(table.shape, jnp.int32),
             pltpu.VMEM((n_q, DH), jnp.bfloat16),
             pltpu.VMEM((n_k, DH), jnp.bfloat16),
             pltpu.VMEM((n_k, DH), jnp.bfloat16),
             pltpu.VMEM((n_q, DH), jnp.bfloat16),
-            pltpu.SemaphoreType.DMA((n_s + n_in - 1,)),
+            pltpu.SemaphoreType.DMA((n_s + n_in,)),
             pltpu.SemaphoreType.DMA((n_s,)),
         ],
         compiler_params=WHOLE,
         cost_estimate=cost(8),
         name="attend",
-    )(place, table, *arrays)
-
-
-def project(place, parts, weight, slot, n_u, hp, partial):
+    )(table, *arrays)
+
+
+def project(parts, weight, slot, n_u, hp, partial):
     apart, last = isinstance(parts, list), slot == hp - 1
     arrays = parts if apart else [parts]
     T = arrays[0].shape[-2]
@@ -236,12 +291,12 @@
     n_in = len(arrays)
     kept = [] if partial is None else [partial]
 
-    def body(place, *refs):
+    def body(*refs):
         ins, w_ref, out_ref = refs[:n_in], refs[n_in], refs[n_in + 1 + len(kept)]
         rows, w_vm, out_vm, row_sems, w_sems, out_sems = refs[-6:]
         put, fetch, send = [], [], []
         for i, (r, d) in enumerate(sides(n_u)):
-            src, share = (ins[i], share_at(place, r, d, n_u)) if apart else (ins[0].at[i], i)
+            src, share = (ins[i], share_at(r, d, n_u)) if apart else (ins[0].at[i], i)
             cols = pl.ds(pl.multiple_of(share * DH, DH), DH)
             put.append(pltpu.make_async_copy(src, rows.at[:, cols], row_sems.at[i]))
         for t in range(n_tiles):
@@ -275,7 +330,7 @@
     return pl.pallas_call(
         body,
         out_shape=jax.ShapeDtypeStruct((T, width), jnp.bfloat16 if last else jnp.float32),
-        in_specs=[SMEM] + [ANY] * (n_in + 1) + [VMEM] * len(kept),
+        in_specs=[ANY] * (n_in + 1) + [VMEM] * len(kept),
         out_specs=ANY if last else VMEM,
         scratch_shapes=[
             pltpu.VMEM((T, depth), jnp.bfloat16),
@@ -288,10 +343,10 @@
         compiler_params=beside(4 * T * width + 10 * MIB),
         cost_estimate=cost(7),
         name="project",
-    )(place, *arrays, weight, *kept)
-
-
-def key_table(rand_blocks, chip, n_u, n_p, per):
+    )(*arrays, weight, *kept)
+
+
+def key_table(rand_blocks, chip, here, n_u, per):
     total = rand_blocks.shape[0]
     z = jnp.arange(n_u, dtype=jnp.int32)[:, None, None]
     core = jnp.arange(2, dtype=jnp.int32)[None, :, None]
@@ -302,7 +357,7 @@
     listed = jnp.concatenate([window, leading, rand_blocks[mine]], axis=1)
     device, inner = listed // per, listed % per
     zs, cs = device % n_u, device // n_u
-    return ((((cs // 2) ^ chip) * n_u + zs) * 2 + cs % 2) * per + inner
+    return ((((cs // 2) ^ chip) * n_u + (zs - here) % n_u) * 2 + cs % 2) * per + inner
 
 
 def shards(queries, keys, values, rand_blocks, out_weight):
@@ -310,29 +365,37 @@
     T, lanes = queries.shape
     hp = lanes // DH // (2 * n_u)
     c, z = lax.axis_index("ctx"), lax.axis_index("ulys")
-    chip, core = c // 2, c % 2
-    place = jnp.stack([z, core]).astype(jnp.int32)
-    table = key_table(rand_blocks, chip, n_u, n_c // 2, T // BLK)
-
-    q_of, kv, after = [], [], (table,)
-    here = send_all(pack_sides(place, [keys, values], [0, 0], n_u), n_c, n_u, 1)
+    table = key_table(rand_blocks, c // 2, z, n_u, T // BLK)
+
+    early = False
+    bundles = [[(1, h + 1), (2, h + 1), (0, h)] for h in range(hp - 1)] + [[(0, hp - 1)]]
+    parts = pack_first([keys, values], n_u, early)
+    here = send_all(parts, n_c, n_u, 1)
+    packed = pack_rest([queries, keys, values], bundles, n_u, here[2])
+    q_of, kv, near, after = [], [], None, [table]
     for h in range(hp):
-        if h < hp - 1:
-            tensors, slots = [keys, values, queries], [h + 1, h + 1, h]
-        else:
-            tensors, slots = [queries], [h]
-        first, second, packed = stage(place, here, tensors, slots, n_u, after)
-        here = to_shares(packed, n_c, n_u)
-        q_of.append((here, len(tensors) - 1))
-        kv.append(gather_chips(first, second, n_c))
-        after = [x for side in kv[-1] for x in side[1:]]
+        rest = early and h == 1
+        *blocks, ready = stage(here, packed[h], n_u, int(rest), after)
+        here = to_shares(ready, n_c, n_u)
+        q_of.append((here, len(bundles[h]) - 1))
+        gathered = gather_chips(blocks[0], blocks[1], n_c)
+        kv.append(
+            [
+                [[(near[i][t], 0), (x, 2 * T)] if rest else [(x, 0)] for t, x in enumerate(side)]
+                for i, side in enumerate(gathered)
+            ]
+        )
+        after = [x for side in gathered for x in side[1:]]
+        if len(blocks) > 2:
+            near = gather_chips(blocks[2], blocks[3], n_c)
+            after += [x for side in near for x in side[1:]]
 
     total = None
     for h in range(hp):
         last = h == hp - 1
-        parts = attend(place, table, *q_of[h], *kv[h], n_u, last)
+        parts = attend(table, *q_of[h], *kv[h], n_u, last)
         parts = send_all(parts, n_c, n_u, -1) if last else to_shares(parts[0], n_c, n_u)
-        total = project(place, parts, out_weight, h, n_u, hp, total)
+        total = project(parts, out_weight, h, n_u, hp, total)
     return total
 
 

time: 150 us -> 144 us (0.960)
  Pallas kernels: 35.6 us -> 31.8 us
  waiting for transfers between devices: 59.4 us -> 57.5 us
    ppermute x14, waiting for transfers between devices: 14 us -> 11.1 us  [send(): return lax.ppermute(x, ('ctx', 'ulys'), pairs)]
    pallas_call x2, Pallas kernels: 12.6 us -> 10.8 us  [attend(): pl.pallas_call(body, out_shape=[jax.ShapeDtypeStruct((T, DH) if apart els...]
    pallas_call x3 -> x4, Pallas kernels: 11 us -> 10.1 us  [the longest x2 4.71 us: stage(): pl.pallas_call(body, out_shape=[jax.ShapeDtypeStruct(x, jnp.bfloat16) for...]
    unnamed x47 -> x45, local copies, waits for them, and re-layouts: 2.84 us -> 3.19 us
  transfers between devices with their start and end apart: 29 -> 29, of which waited for: 11 -> 10; matrix products, arithmetic and copies ran while one was open for 1% -> 1% of each run, Pallas kernels for 12% -> 13%
where the time goes in v5:
time: 144 us; the launch traced here: 143 us
  waiting for transfers between devices  57.5 us (40%)
  starting transfers between devices  48.4 us (34%)
  Pallas kernels  31.8 us (22%)
  local copies, waits for them, and re-layouts  3.93 us (3%)
    ppermute x12, waiting for transfers between devices, swap_chip(): return lax.ppermute(x, 'ctx', [(i, i ^ 2 * bit) for i in range(n_c)])  46.4 us
    all_to_all x3, starting transfers between devices, to_shares(): lax.all_to_all(x, ('ctx', 'ulys'), split_axis=0, concat_axis=0, tiled=Tru...  17.8 us
    ppermute x14, starting transfers between devices, send(): return lax.ppermute(x, ('ctx', 'ulys'), pairs)  17.4 us
    ppermute x12, starting transfers between devices, swap_chip(): return lax.ppermute(x, 'ctx', [(i, i ^ 2 * bit) for i in range(n_c)])  13.2 us
    ppermute x14, waiting for transfers between devices, send(): return lax.ppermute(x, ('ctx', 'ulys'), pairs)  11.1 us
    pallas_call x2, Pallas kernels, project(): pl.pallas_call(body, out_shape=jax.ShapeDtypeStruct((T, width), jnp.bfloa...  10.9 us
    pallas_call x2, Pallas kernels, attend(): pl.pallas_call(body, out_shape=[jax.ShapeDtypeStruct((T, DH) if apart els...  10.8 us
    pallas_call x2, Pallas kernels, stage(): pl.pallas_call(body, out_shape=[jax.ShapeDtypeStruct(x, jnp.bfloat16) for...  4.71 us
  transfers between devices with their start and end apart: 29, of which 10 were waited for; matrix products, arithmetic and copies ran while one was open for 1% of the time, Pallas kernels for 13%

profile of v5, /device:TPU:0, one launch (start us, length us, event | category | flops | bytes accessed | tf_op | source)
XLA Modules:
  0.0 143.0 jit_solution(15167653689047853281)
XLA Ops:
  0.0 2.3 %pack_first.1 = (bf16[2,256,128]{2,1,0:T(8,128)(2,1)}, bf16[2,256,128]{2,1,0:T(8,128)(2,1)}, bf16[2,256,128]{2,1,0:T(8,128)(2,1)}, bf16[2,256,128]{2,1,0:T(8,128...) custom-call(bf16[256,2048]{1,0:T(8,128)(2,1)} %refs_1_.4, ...), custom_call_target="tpu_custom_call" | custom-call | flops 3449999872 | tf_op jit(solution)/shard_map/pack_first/pallas_call | solution.py:70
  2.9 2.6 %collective-permute-start.1 = (bf16[2,256,128]{2,1,0:T(8,128)(2,1)}, bf16[2,256,128]{2,1,0:T(8,128)(2,1)S(1)}, u32[]{:S(2)}, u32[]{:S(2)}) collective-permute-start(bf16[2,256,128]{2,1,0:T(8,128)(2,1)} %get-tuple-element.31), channel_id=1, source_target_pairs={{0,1},{1,2},{2,3},{3,0},{4,5},{5,6},{6,7},{7,4},{8,9},{9,10},{10,1... | collective-permute-start | bytes 393224 | tf_op jit(solution)/shard_map/ppermute | solution.py:172
  5.5 1.3 collective-permute-start.2
  11.2 2.2 %collective-permute-start.5 = (bf16[2,256,128]{2,1,0:T(8,128)(2,1)}, bf16[2,256,128]{2,1,0:T(8,128)(2,1)S(1)}, u32[]{:S(2)}, u32[]{:S(2)}) collective-permute-start(bf16[2,256,128]{2,1,0:T(8,128)(2,1)} %get-tuple-element.35), channel_id=1, source_target_pairs={{0,3},{1,0},{2,1},{3,2},{4,7},{5,4},{6,5},{7,6},{8,11},{9,8},{10,9... | collective-permute-start | bytes 393224 | tf_op jit(solution)/shard_map/ppermute | solution.py:172
  14.1 3.1 %pack_rest.1 = (bf16[8,3,256,128]{3,2,1,0:T(8,128)(2,1)}, bf16[8,1,256,128]{3,2,1,0:T(8,128)(2,1)}) custom-call(bf16[256,2048]{1,0:T(8,128)(2,1)} %refs_0_.3, bf16[256,2048]{1,0:T(8,128)(2,1)} %refs_1_.4, bf16[256,2048]{1,0:T(8,128)(2,1)} %refs_2_.1, bf16[2,256,128]{2,1,0:T(8,128)(2,1)} %copy-done.16), custom_call_target="tpu_custom_call" | custom-call | flops 3449999872 | tf_op jit(solution)/shard_map/pack_rest/pallas_call | solution.py:104
  17.3 5.9 %collective-permute-done.3.refs_4_ = bf16[2,256,128]{2,1,0:T(8,128)(2,1)S(1)} collective-permute-done((bf16[2,256,128]{2,1,0:T(8,128)(2,1)}, bf16[2,256,128]{2,1,0:T(8,128)(2,1)S(1)}, u32[]{:S(2)}, u32[]{:S(2)}) %collective-permute-start.3) | collective-permute-done | bytes 131104 | tf_op jit(solution)/shard_map/ppermute | solution.py:172
  23.1 2.7 %collective-permute-done.4.refs_5_ = bf16[2,256,128]{2,1,0:T(8,128)(2,1)S(1)} collective-permute-done((bf16[2,256,128]{2,1,0:T(8,128)(2,1)}, bf16[2,256,128]{2,1,0:T(8,128)(2,1)S(1)}, u32[]{:S(2)}, u32[]{:S(2)}) %collective-permute-start.4) | collective-permute-done | bytes 131104 | tf_op jit(solution)/shard_map/ppermute | solution.py:172
  26.6 2.4 %stage.2 = (bf16[2048,128]{1,0:T(8,128)(2,1)}, bf16[2048,128]{1,0:T(8,128)(2,1)}, bf16[8,3,256,128]{3,2,1,0:T(8,128)(2,1)}) custom-call(bf16[2,256,128]{2,1,0:T(8,128)(2,1)} %get-tuple-element.29.refs_0_, bf16[2,256,128]{2,1,0:T(8,128)(2,1)} %copy-done.15, bf16[2,256,128]{2,1,0:T(8,128)(2,1)} %copy-done.16, ...), custom_call_target="tpu_custom_call", output_to_operand_aliasing={{2}: (8, {})} | custom-call | flops 3449999872 | tf_op jit(solution)/shard_map/stage/pallas_call | solution.py:146
  29.0 8.3 %all-to-all-start = ((bf16[8,3,256,128]{3,2,1,0:T(8,128)(2,1)}), bf16[8,3,256,128]{3,2,1,0:T(8,128)(2,1)S(1)}, u32[]{:S(2)}, u32[]{:S(2)}) async-start(bf16[8,3,256,128]{3,2,1,0:T(8,128)(2,1)} %get-tuple-element.38), calls=%async_computation | async-start | bytes 3145728 | tf_op jit(solution)/shard_map/all_to_all | solution.py:163
  37.3 1.6 %collective-permute-start.8 = (bf16[2048,128]{1,0:T(8,128)(2,1)S(1)}, bf16[2048,128]{1,0:T(8,128)(2,1)S(1)}, u32[]{:S(2)}, u32[]{:S(2)}) collective-permute-start(bf16[2048,128]{1,0:T(8,128)(2,1)S(1)} %copy-done.4), channel_id=1, source_target_pairs={{0,16},{4,20},{8,24},{12,28},{16,0},{20,4},{24,8},{28,12},{1,17},{... | collective-permute-start | bytes 1572872 | tf_op jit(solution)/shard_map/ppermute | solution.py:180
  38.8 1.5 %collective-permute-start.10 = (bf16[2048,128]{1,0:T(8,128)(2,1)S(1)}, bf16[2048,128]{1,0:T(8,128)(2,1)S(1)}, u32[]{:S(2)}, u32[]{:S(2)}) collective-permute-start(bf16[2048,128]{1,0:T(8,128)(2,1)S(1)} %copy-done.5), channel_id=1, source_target_pairs={{0,8},{4,12},{8,0},{12,4},{16,24},{20,28},{24,16},{28,20},{1,9},{5... | collective-permute-start | bytes 1572872 | tf_op jit(solution)/shard_map/ppermute | solution.py:180
  41.4 10.7 %collective-permute-done.8.refs_3_ = bf16[2048,128]{1,0:T(8,128)(2,1)S(1)} collective-permute-done((bf16[2048,128]{1,0:T(8,128)(2,1)S(1)}, bf16[2048,128]{1,0:T(8,128)(2,1)S(1)}, u32[]{:S(2)}, u32[]{:S(2)}) %collective-permute-start.8) | collective-permute-done | bytes 524320 | tf_op jit(solution)/shard_map/ppermute | solution.py:180
  52.1 1.5 %collective-permute-start.9 = (bf16[2048,128]{1,0:T(8,128)(2,1)S(1)}, bf16[2048,128]{1,0:T(8,128)(2,1)S(1)}, u32[]{:S(2)}, u32[]{:S(2)}) collective-permute-start(bf16[2048,128]{1,0:T(8,128)(2,1)S(1)} %collective-permute-done.8.refs_3_), channel_id=1, source_target_pairs={{0,8},{4,12},{8,0},{12,4},{16,24},{20,28},{24,16},{28,20},{1,9},{5... | collective-permute-start | bytes 1572872 | tf_op jit(solution)/shard_map/ppermute | solution.py:180
  53.6 1.5 %collective-permute-start.12 = (bf16[2048,128]{1,0:T(8,128)(2,1)S(1)}, bf16[2048,128]{1,0:T(8,128)(2,1)}, u32[]{:S(2)}, u32[]{:S(2)}) collective-permute-start(bf16[2048,128]{1,0:T(8,128)(2,1)S(1)} %collective-permute-done.10.refs_5_.refs_6_), channel_id=1, source_target_pairs={{0,16},{4,20},{8,24},{12,28},{16,0},{20,4},{24,8},{28,12},{1,17},{... | collective-permute-start | bytes 1572872 | tf_op jit(solution)/shard_map/ppermute | solution.py:180
  55.1 9.8 %collective-permute-done.7.refs_2_ = bf16[2048,128]{1,0:T(8,128)(2,1)S(1)} collective-permute-done((bf16[2048,128]{1,0:T(8,128)(2,1)S(1)}, bf16[2048,128]{1,0:T(8,128)(2,1)S(1)}, u32[]{:S(2)}, u32[]{:S(2)}) %collective-permute-start.7) | collective-permute-done | bytes 524320 | tf_op jit(solution)/shard_map/ppermute | solution.py:180
  64.9 10.4 %collective-permute-done.9.refs_4_ = bf16[2048,128]{1,0:T(8,128)(2,1)S(1)} collective-permute-done((bf16[2048,128]{1,0:T(8,128)(2,1)S(1)}, bf16[2048,128]{1,0:T(8,128)(2,1)S(1)}, u32[]{:S(2)}, u32[]{:S(2)}) %collective-permute-start.9) | collective-permute-done | bytes 524320 | tf_op jit(solution)/shard_map/ppermute | solution.py:180
  77.3 2.3 %stage.3 = (bf16[2048,128]{1,0:T(8,128)(2,1)}, bf16[2048,128]{1,0:T(8,128)(2,1)}, bf16[8,1,256,128]{3,2,1,0:T(8,128)(2,1)}) custom-call(bf16[8,3,256,128]{3,2,1,0:T(8,128)(2,1)} %copy-done.1, bf16[8,1,256,128]{3,2,1,0:T(8,128)(2,1)} %get-tuple-element.39.refs_1_, bf16[2048,128]{1,0:T(8,128)(2,1)} %copy-done.8, ...), custom_call_target="tpu_custom_call", output_to_operand_aliasing={{2}: (1, {})} | custom-call | flops 3449999872 | tf_op jit(solution)/shard_map/stage/pallas_call | solution.py:146
  80.2 1.5 %collective-permute-start.16 = (bf16[2048,128]{1,0:T(8,128)(2,1)}, bf16[2048,128]{1,0:T(8,128)(2,1)S(1)}, u32[]{:S(2)}, u32[]{:S(2)}) collective-permute-start(bf16[2048,128]{1,0:T(8,128)(2,1)} %get-tuple-element.44.refs_5_), channel_id=1, source_target_pairs={{0,8},{4,12},{8,0},{12,4},{16,24},{20,28},{24,16},{28,20},{1,9},{5... | collective-permute-start | bytes 1572872 | tf_op jit(solution)/shard_map/ppermute | solution.py:180
  81.7 4.7 %all-to-all-start.1 = ((bf16[8,1,256,128]{3,2,1,0:T(8,128)(2,1)}), bf16[8,1,256,128]{3,2,1,0:T(8,128)(2,1)S(1)}, u32[]{:S(2)}, u32[]{:S(2)}) async-start(bf16[8,1,256,128]{3,2,1,0:T(8,128)(2,1)} %get-tuple-element.42), calls=%async_computation.1 | async-start | bytes 1048576 | tf_op jit(solution)/shard_map/all_to_all | solution.py:163
  87.0 1.5 %collective-permute-start.17 = (bf16[2048,128]{1,0:T(8,128)(2,1)}, bf16[2048,128]{1,0:T(8,128)(2,1)S(1)}, u32[]{:S(2)}, u32[]{:S(2)}) collective-permute-start(bf16[2048,128]{1,0:T(8,128)(2,1)} %get-tuple-element.44.refs_5_), channel_id=1, source_target_pairs={{0,16},{4,20},{8,24},{12,28},{16,0},{20,4},{24,8},{28,12},{1,17},{... | collective-permute-start | bytes 1572872 | tf_op jit(solution)/shard_map/ppermute | solution.py:180
  88.5 6.3 %collective-permute-done.14.refs_3_ = bf16[2048,128]{1,0:T(8,128)(2,1)S(1)} collective-permute-done((bf16[2048,128]{1,0:T(8,128)(2,1)}, bf16[2048,128]{1,0:T(8,128)(2,1)S(1)}, u32[]{:S(2)}, u32[]{:S(2)}) %collective-permute-start.14) | collective-permute-done | bytes 524320 | tf_op jit(solution)/shard_map/ppermute | solution.py:180
  94.8 1.5 %collective-permute-start.15 = (bf16[2048,128]{1,0:T(8,128)(2,1)S(1)}, bf16[2048,128]{1,0:T(8,128)(2,1)}, u32[]{:S(2)}, u32[]{:S(2)}) collective-permute-start(bf16[2048,128]{1,0:T(8,128)(2,1)S(1)} %collective-permute-done.14.refs_3_), channel_id=1, source_target_pairs={{0,8},{4,12},{8,0},{12,4},{16,24},{20,28},{24,16},{28,20},{1,9},{5... | collective-permute-start | bytes 1572872 | tf_op jit(solution)/shard_map/ppermute | solution.py:180
  96.8 5.4 %attend.3 = bf16[8,256,128]{2,1,0:T(8,128)(2,1)} custom-call(s32[32,8]{1,0:T(8,128)} %fusion.8.refs_9_.table_ref, bf16[8,3,256,128]{3,2,1,0:T(8,128)(2,1)} %copy-done.1, bf16[2048,128]{1,0:T(8,128)(2,1)} %get-tuple-element.40.refs_1_, bf16[2048,128]{1,0:T(8,128)(2,1)} %copy-done.8, bf16[2048,128]{1,0:T(8,128)(2,1)} %copy-done.6, ...), custom_call_target="tpu_custom_call" | custom-call | flops 9200000000 | tf_op jit(solution)/shard_map/attend/pallas_call | solution.py:262
  102.2 4.8 %all-to-all-start.2 = ((bf16[8,256,128]{2,1,0:T(8,128)(2,1)}), bf16[8,256,128]{2,1,0:T(8,128)(2,1)S(1)}, u32[]{:S(2)}, u32[]{:S(2)}) async-start(bf16[8,256,128]{2,1,0:T(8,128)(2,1)} %attend.3), calls=%async_computation.2 | async-start | bytes 1048576 | tf_op jit(solution)/shard_map/all_to_all | solution.py:163
  107.0 9.1 %collective-permute-done.15.refs_4_ = bf16[2048,128]{1,0:T(8,128)(2,1)} collective-permute-done((bf16[2048,128]{1,0:T(8,128)(2,1)S(1)}, bf16[2048,128]{1,0:T(8,128)(2,1)}, u32[]{:S(2)}, u32[]{:S(2)}) %collective-permute-start.15) | collective-permute-done | bytes 524320 | tf_op jit(solution)/shard_map/ppermute | solution.py:180
  116.2 5.4 %attend.2 = (bf16[256,128]{1,0:T(8,128)(2,1)}, bf16[256,128]{1,0:T(8,128)(2,1)}, bf16[256,128]{1,0:T(8,128)(2,1)}, bf16[256,128]{1,0:T(8,128)(2,1)}, bf16[256,12...) custom-call(s32[32,8]{1,0:T(8,128)} %fusion.8.refs_9_.table_ref, ...), custom_call_target="tpu_custom_call" | custom-call | flops 9200000000 | tf_op jit(solution)/shard_map/attend/pallas_call | solution.py:262
  121.6 3.0 %collective-permute-start.20 = (bf16[256,128]{1,0:T(8,128)(2,1)}, bf16[256,128]{1,0:T(8,128)(2,1)S(1)}, u32[]{:S(2)}, u32[]{:S(2)}) collective-permute-start(bf16[256,128]{1,0:T(8,128)(2,1)} %get-tuple-element.47), channel_id=1, source_target_pairs={{0,3},{1,0},{2,1},{3,2},{4,7},{5,4},{6,5},{7,6},{8,11},{9,8},{10,9... | collective-permute-start | bytes 196616 | tf_op jit(solution)/shard_map/ppermute | solution.py:172
  125.0 2.6 %collective-permute-start.23 = (bf16[256,128]{1,0:T(8,128)(2,1)}, bf16[256,128]{1,0:T(8,128)(2,1)S(1)}, u32[]{:S(2)}, u32[]{:S(2)}) collective-permute-start(bf16[256,128]{1,0:T(8,128)(2,1)} %get-tuple-element.50), channel_id=1, source_target_pairs={{0,6},{1,7},{2,4},{3,5},{4,2},{5,3},{6,0},{7,1},{8,14},{9,15},{10,... | collective-permute-start | bytes 196616 | tf_op jit(solution)/shard_map/ppermute | solution.py:172
  127.6 1.5 %collective-permute-start.24 = (bf16[256,128]{1,0:T(8,128)(2,1)}, bf16[256,128]{1,0:T(8,128)(2,1)S(1)}, u32[]{:S(2)}, u32[]{:S(2)}) collective-permute-start(bf16[256,128]{1,0:T(8,128)(2,1)} %get-tuple-element.51), channel_id=1, source_target_pairs={{0,1},{1,2},{2,3},{3,0},{4,5},{5,6},{6,7},{7,4},{8,9},{9,10},{10,1... | collective-permute-start | bytes 196616 | tf_op jit(solution)/shard_map/ppermute | solution.py:172
  129.4 5.0 %project.2.refs_9_ = f32[256,4096]{1,0:T(8,128)S(1)} custom-call(bf16[8,256,128]{2,1,0:T(8,128)(2,1)S(1)} %all-to-all-done.2.refs_0_, bf16[2048,4096]{1,0:T(8,128)(2,1)} %refs_8_.1), custom_call_target="tpu_custom_call" | custom-call | flops 8049999872 | tf_op jit(solution)/shard_map/project/pallas_call | solution.py:330
  134.4 2.3 %collective-permute-done.22.refs_4_ = bf16[256,128]{1,0:T(8,128)(2,1)S(1)} collective-permute-done((bf16[256,128]{1,0:T(8,128)(2,1)}, bf16[256,128]{1,0:T(8,128)(2,1)S(1)}, u32[]{:S(2)}, u32[]{:S(2)}) %collective-permute-start.22) | collective-permute-done | bytes 65568 | tf_op jit(solution)/shard_map/ppermute | solution.py:172
  136.9 6.0 %project.3 = bf16[256,4096]{1,0:T(8,128)(2,1)} custom-call(bf16[256,128]{1,0:T(8,128)(2,1)S(1)} %copy-done, bf16[256,128]{1,0:T(8,128)(2,1)S(1)} %collective-permute-done.19.refs_1_, bf16[256,128]{1,0:T(8,128)(2,1)S(1)} %collective-permute-done.20.refs_2_, bf16[256,128]{1,0:T(8,128)(2,1)S(1)} %collective-permute-done.21.refs_3_, ...), custom_call_target="tpu_custom_call" | custom-call | flops 8049999872 | tf_op jit(solution)/shard_map/project/pallas_call | solution.py:330
  (89 shorter events, 12.0 us)
Async XLA Ops:
  2.3 8.9 %collective-permute-start = (bf16[2,256,128]{2,1,0:T(8,128)(2,1)}, bf16[2,256,128]{2,1,0:T(8,128)(2,1)S(1)}, u32[]{:S(2)}, u32[]{:S(2)}) collective-permute-start(bf16[2,256,128]{2,1,0:T(8,128)(2,1)} %get-tuple-element.30), channel_id=1, source_target_pairs={{0,4},{1,5},{2,6},{3,7},{4,0},{5,1},{6,2},{7,3},{8,12},{9,13},{10,... | collective-permute-start | bytes 393224 | tf_op jit(solution)/shard_map/ppermute | solution.py:172
  2.9 10.6 %collective-permute-start.1 = (bf16[2,256,128]{2,1,0:T(8,128)(2,1)}, bf16[2,256,128]{2,1,0:T(8,128)(2,1)S(1)}, u32[]{:S(2)}, u32[]{:S(2)}) collective-permute-start(bf16[2,256,128]{2,1,0:T(8,128)(2,1)} %get-tuple-element.31), channel_id=1, source_target_pairs={{0,1},{1,2},{2,3},{3,0},{4,5},{5,6},{6,7},{7,4},{8,9},{9,10},{10,1... | collective-permute-start | bytes 393224 | tf_op jit(solution)/shard_map/ppermute | solution.py:172
  5.5 11.7 %collective-permute-start.2 = (bf16[2,256,128]{2,1,0:T(8,128)(2,1)}, bf16[2,256,128]{2,1,0:T(8,128)(2,1)S(1)}, u32[]{:S(2)}, u32[]{:S(2)}) collective-permute-start(bf16[2,256,128]{2,1,0:T(8,128)(2,1)} %get-tuple-element.32), channel_id=1, source_target_pairs={{0,5},{1,6},{2,7},{3,4},{4,1},{5,2},{6,3},{7,0},{8,13},{9,14},{10,... | collective-permute-start | bytes 393224 | tf_op jit(solution)/shard_map/ppermute | solution.py:172
  6.8 16.3 %collective-permute-start.3 = (bf16[2,256,128]{2,1,0:T(8,128)(2,1)}, bf16[2,256,128]{2,1,0:T(8,128)(2,1)S(1)}, u32[]{:S(2)}, u32[]{:S(2)}) collective-permute-start(bf16[2,256,128]{2,1,0:T(8,128)(2,1)} %get-tuple-element.33), channel_id=1, source_target_pairs={{0,2},{1,3},{2,0},{3,1},{4,6},{5,7},{6,4},{7,5},{8,10},{9,11},{10,... | collective-permute-start | bytes 393224 | tf_op jit(solution)/shard_map/ppermute | solution.py:172
  8.2 17.7 %collective-permute-start.4 = (bf16[2,256,128]{2,1,0:T(8,128)(2,1)}, bf16[2,256,128]{2,1,0:T(8,128)(2,1)S(1)}, u32[]{:S(2)}, u32[]{:S(2)}) collective-permute-start(bf16[2,256,128]{2,1,0:T(8,128)(2,1)} %get-tuple-element.34), channel_id=1, source_target_pairs={{0,6},{1,7},{2,4},{3,5},{4,2},{5,3},{6,0},{7,1},{8,14},{9,15},{10,... | collective-permute-start | bytes 393224 | tf_op jit(solution)/shard_map/ppermute | solution.py:172
  11.2 14.6 %collective-permute-start.5 = (bf16[2,256,128]{2,1,0:T(8,128)(2,1)}, bf16[2,256,128]{2,1,0:T(8,128)(2,1)S(1)}, u32[]{:S(2)}, u32[]{:S(2)}) collective-permute-start(bf16[2,256,128]{2,1,0:T(8,128)(2,1)} %get-tuple-element.35), channel_id=1, source_target_pairs={{0,3},{1,0},{2,1},{3,2},{4,7},{5,4},{6,5},{7,6},{8,11},{9,8},{10,9... | collective-permute-start | bytes 393224 | tf_op jit(solution)/shard_map/ppermute | solution.py:172
  13.5 12.4 %collective-permute-start.6 = (bf16[2,256,128]{2,1,0:T(8,128)(2,1)}, bf16[2,256,128]{2,1,0:T(8,128)(2,1)S(1)}, u32[]{:S(2)}, u32[]{:S(2)}) collective-permute-start(bf16[2,256,128]{2,1,0:T(8,128)(2,1)} %get-tuple-element.36), channel_id=1, source_target_pairs={{0,7},{1,4},{2,5},{3,6},{4,3},{5,0},{6,1},{7,2},{8,15},{9,12},{10,... | collective-permute-start | bytes 393224 | tf_op jit(solution)/shard_map/ppermute | solution.py:172
  29.0 47.1 %all-to-all-start = ((bf16[8,3,256,128]{3,2,1,0:T(8,128)(2,1)}), bf16[8,3,256,128]{3,2,1,0:T(8,128)(2,1)S(1)}, u32[]{:S(2)}, u32[]{:S(2)}) async-start(bf16[8,3,256,128]{3,2,1,0:T(8,128)(2,1)} %get-tuple-element.38), calls=%async_computation | async-start | bytes 3145728 | tf_op jit(solution)/shard_map/all_to_all | solution.py:163
  37.3 14.8 %collective-permute-start.8 = (bf16[2048,128]{1,0:T(8,128)(2,1)S(1)}, bf16[2048,128]{1,0:T(8,128)(2,1)S(1)}, u32[]{:S(2)}, u32[]{:S(2)}) collective-permute-start(bf16[2048,128]{1,0:T(8,128)(2,1)S(1)} %copy-done.4), channel_id=1, source_target_pairs={{0,16},{4,20},{8,24},{12,28},{16,0},{20,4},{24,8},{28,12},{1,17},{... | collective-permute-start | bytes 1572872 | tf_op jit(solution)/shard_map/ppermute | solution.py:180
  38.8 14.8 %collective-permute-start.10 = (bf16[2048,128]{1,0:T(8,128)(2,1)S(1)}, bf16[2048,128]{1,0:T(8,128)(2,1)S(1)}, u32[]{:S(2)}, u32[]{:S(2)}) collective-permute-start(bf16[2048,128]{1,0:T(8,128)(2,1)S(1)} %copy-done.5), channel_id=1, source_target_pairs={{0,8},{4,12},{8,0},{12,4},{16,24},{20,28},{24,16},{28,20},{1,9},{5... | collective-permute-start | bytes 1572872 | tf_op jit(solution)/shard_map/ppermute | solution.py:180
  40.3 24.5 %collective-permute-start.7 = (bf16[2048,128]{1,0:T(8,128)(2,1)S(1)}, bf16[2048,128]{1,0:T(8,128)(2,1)S(1)}, u32[]{:S(2)}, u32[]{:S(2)}) collective-permute-start(bf16[2048,128]{1,0:T(8,128)(2,1)S(1)} %copy-done.4), channel_id=1, source_target_pairs={{0,8},{4,12},{8,0},{12,4},{16,24},{20,28},{24,16},{28,20},{1,9},{5... | collective-permute-start | bytes 1572872 | tf_op jit(solution)/shard_map/ppermute | solution.py:180
  40.9 24.0 %collective-permute-start.11 = (bf16[2048,128]{1,0:T(8,128)(2,1)S(1)}, bf16[2048,128]{1,0:T(8,128)(2,1)S(1)}, u32[]{:S(2)}, u32[]{:S(2)}) collective-permute-start(bf16[2048,128]{1,0:T(8,128)(2,1)S(1)} %copy-done.5), channel_id=1, source_target_pairs={{0,16},{4,20},{8,24},{12,28},{16,0},{20,4},{24,8},{28,12},{1,17},{... | collective-permute-start | bytes 1572872 | tf_op jit(solution)/shard_map/ppermute | solution.py:180
  52.1 24.1 %copy-start.6 = (bf16[2048,128]{1,0:T(8,128)(2,1)}, bf16[2048,128]{1,0:T(8,128)(2,1)S(1)}, u32[]{:S(2)}) copy-start(bf16[2048,128]{1,0:T(8,128)(2,1)S(1)} %collective-permute-done.8.refs_3_) | copy-start | bytes 1572868
  52.1 23.2 %collective-permute-start.9 = (bf16[2048,128]{1,0:T(8,128)(2,1)S(1)}, bf16[2048,128]{1,0:T(8,128)(2,1)S(1)}, u32[]{:S(2)}, u32[]{:S(2)}) collective-permute-start(bf16[2048,128]{1,0:T(8,128)(2,1)S(1)} %collective-permute-done.8.refs_3_), channel_id=1, source_target_pairs={{0,8},{4,12},{8,0},{12,4},{16,24},{20,28},{24,16},{28,20},{1,9},{5... | collective-permute-start | bytes 1572872 | tf_op jit(solution)/shard_map/ppermute | solution.py:180
  53.6 21.7 %copy-start.7 = (bf16[2048,128]{1,0:T(8,128)(2,1)}, bf16[2048,128]{1,0:T(8,128)(2,1)S(1)}, u32[]{:S(2)}) copy-start(bf16[2048,128]{1,0:T(8,128)(2,1)S(1)} %collective-permute-done.10.refs_5_.refs_6_) | copy-start | bytes 1572868
  53.6 22.5 %collective-permute-start.12 = (bf16[2048,128]{1,0:T(8,128)(2,1)S(1)}, bf16[2048,128]{1,0:T(8,128)(2,1)}, u32[]{:S(2)}, u32[]{:S(2)}) collective-permute-start(bf16[2048,128]{1,0:T(8,128)(2,1)S(1)} %collective-permute-done.10.refs_5_.refs_6_), channel_id=1, source_target_pairs={{0,16},{4,20},{8,24},{12,28},{16,0},{20,4},{24,8},{28,12},{1,17},{... | collective-permute-start | bytes 1572872 | tf_op jit(solution)/shard_map/ppermute | solution.py:180
  79.6 15.1 %collective-permute-start.14 = (bf16[2048,128]{1,0:T(8,128)(2,1)}, bf16[2048,128]{1,0:T(8,128)(2,1)S(1)}, u32[]{:S(2)}, u32[]{:S(2)}) collective-permute-start(bf16[2048,128]{1,0:T(8,128)(2,1)} %get-tuple-element.43.refs_1_), channel_id=1, source_target_pairs={{0,16},{4,20},{8,24},{12,28},{16,0},{20,4},{24,8},{28,12},{1,17},{... | collective-permute-start | bytes 1572872 | tf_op jit(solution)/shard_map/ppermute | solution.py:180
  80.2 16.1 %collective-permute-start.16 = (bf16[2048,128]{1,0:T(8,128)(2,1)}, bf16[2048,128]{1,0:T(8,128)(2,1)S(1)}, u32[]{:S(2)}, u32[]{:S(2)}) collective-permute-start(bf16[2048,128]{1,0:T(8,128)(2,1)} %get-tuple-element.44.refs_5_), channel_id=1, source_target_pairs={{0,8},{4,12},{8,0},{12,4},{16,24},{20,28},{24,16},{28,20},{1,9},{5... | collective-permute-start | bytes 1572872 | tf_op jit(solution)/shard_map/ppermute | solution.py:180
  81.7 20.5 %all-to-all-start.1 = ((bf16[8,1,256,128]{3,2,1,0:T(8,128)(2,1)}), bf16[8,1,256,128]{3,2,1,0:T(8,128)(2,1)S(1)}, u32[]{:S(2)}, u32[]{:S(2)}) async-start(bf16[8,1,256,128]{3,2,1,0:T(8,128)(2,1)} %get-tuple-element.42), calls=%async_computation.1 | async-start | bytes 1048576 | tf_op jit(solution)/shard_map/all_to_all | solution.py:163
  86.4 20.5 %collective-permute-start.13 = (bf16[2048,128]{1,0:T(8,128)(2,1)}, bf16[2048,128]{1,0:T(8,128)(2,1)S(1)}, u32[]{:S(2)}, u32[]{:S(2)}) collective-permute-start(bf16[2048,128]{1,0:T(8,128)(2,1)} %get-tuple-element.43.refs_1_), channel_id=1, source_target_pairs={{0,8},{4,12},{8,0},{12,4},{16,24},{20,28},{24,16},{28,20},{1,9},{5... | collective-permute-start | bytes 1572872 | tf_op jit(solution)/shard_map/ppermute | solution.py:180
  87.0 20.0 %collective-permute-start.17 = (bf16[2048,128]{1,0:T(8,128)(2,1)}, bf16[2048,128]{1,0:T(8,128)(2,1)S(1)}, u32[]{:S(2)}, u32[]{:S(2)}) collective-permute-start(bf16[2048,128]{1,0:T(8,128)(2,1)} %get-tuple-element.44.refs_5_), channel_id=1, source_target_pairs={{0,16},{4,20},{8,24},{12,28},{16,0},{20,4},{24,8},{28,12},{1,17},{... | collective-permute-start | bytes 1572872 | tf_op jit(solution)/shard_map/ppermute | solution.py:180
  94.8 21.4 %collective-permute-start.15 = (bf16[2048,128]{1,0:T(8,128)(2,1)S(1)}, bf16[2048,128]{1,0:T(8,128)(2,1)}, u32[]{:S(2)}, u32[]{:S(2)}) collective-permute-start(bf16[2048,128]{1,0:T(8,128)(2,1)S(1)} %collective-permute-done.14.refs_3_), channel_id=1, source_target_pairs={{0,8},{4,12},{8,0},{12,4},{16,24},{20,28},{24,16},{28,20},{1,9},{5... | collective-permute-start | bytes 1572872 | tf_op jit(solution)/shard_map/ppermute | solution.py:180
  96.3 19.9 %collective-permute-start.18 = (bf16[2048,128]{1,0:T(8,128)(2,1)S(1)}, bf16[2048,128]{1,0:T(8,128)(2,1)}, u32[]{:S(2)}, u32[]{:S(2)}) collective-permute-start(bf16[2048,128]{1,0:T(8,128)(2,1)S(1)} %collective-permute-done.16.refs_6_), channel_id=1, source_target_pairs={{0,16},{4,20},{8,24},{12,28},{16,0},{20,4},{24,8},{28,12},{1,17},{... | collective-permute-start | bytes 1572872 | tf_op jit(solution)/shard_map/ppermute | solution.py:180
  102.2 14.0 %copy-start.2 = (bf16[8,1,256,128]{3,2,1,0:T(8,128)(2,1)}, bf16[8,1,256,128]{3,2,1,0:T(8,128)(2,1)S(1)}, u32[]{:S(2)}) copy-start(bf16[8,1,256,128]{3,2,1,0:T(8,128)(2,1)S(1)} %all-to-all-done.1.refs_0_) | copy-start | bytes 1572868
  102.2 27.2 %all-to-all-start.2 = ((bf16[8,256,128]{2,1,0:T(8,128)(2,1)}), bf16[8,256,128]{2,1,0:T(8,128)(2,1)S(1)}, u32[]{:S(2)}, u32[]{:S(2)}) async-start(bf16[8,256,128]{2,1,0:T(8,128)(2,1)} %attend.3), calls=%async_computation.2 | async-start | bytes 1048576 | tf_op jit(solution)/shard_map/all_to_all | solution.py:163
  121.6 6.0 %collective-permute-start.19 = (bf16[256,128]{1,0:T(8,128)(2,1)}, bf16[256,128]{1,0:T(8,128)(2,1)S(1)}, u32[]{:S(2)}, u32[]{:S(2)}) collective-permute-start(bf16[256,128]{1,0:T(8,128)(2,1)} %get-tuple-element.46), channel_id=1, source_target_pairs={{0,4},{1,5},{2,6},{3,7},{4,0},{5,1},{6,2},{7,3},{8,12},{9,13},{10,... | collective-permute-start | bytes 196616 | tf_op jit(solution)/shard_map/ppermute | solution.py:172
  121.6 7.4 %collective-permute-start.20 = (bf16[256,128]{1,0:T(8,128)(2,1)}, bf16[256,128]{1,0:T(8,128)(2,1)S(1)}, u32[]{:S(2)}, u32[]{:S(2)}) collective-permute-start(bf16[256,128]{1,0:T(8,128)(2,1)} %get-tuple-element.47), channel_id=1, source_target_pairs={{0,3},{1,0},{2,1},{3,2},{4,7},{5,4},{6,5},{7,6},{8,11},{9,8},{10,9... | collective-permute-start | bytes 196616 | tf_op jit(solution)/shard_map/ppermute | solution.py:172
  124.6 9.7 %collective-permute-start.21 = (bf16[256,128]{1,0:T(8,128)(2,1)}, bf16[256,128]{1,0:T(8,128)(2,1)S(1)}, u32[]{:S(2)}, u32[]{:S(2)}) collective-permute-start(bf16[256,128]{1,0:T(8,128)(2,1)} %get-tuple-element.48), channel_id=1, source_target_pairs={{0,7},{1,4},{2,5},{3,6},{4,3},{5,0},{6,1},{7,2},{8,15},{9,12},{10,... | collective-permute-start | bytes 196616 | tf_op jit(solution)/shard_map/ppermute | solution.py:172
  125.0 11.7 %collective-permute-start.22 = (bf16[256,128]{1,0:T(8,128)(2,1)}, bf16[256,128]{1,0:T(8,128)(2,1)S(1)}, u32[]{:S(2)}, u32[]{:S(2)}) collective-permute-start(bf16[256,128]{1,0:T(8,128)(2,1)} %get-tuple-element.49), channel_id=1, source_target_pairs={{0,2},{1,3},{2,0},{3,1},{4,6},{5,7},{6,4},{7,5},{8,10},{9,11},{10,... | collective-permute-start | bytes 196616 | tf_op jit(solution)/shard_map/ppermute | solution.py:172
  125.0 11.9 %collective-permute-start.23 = (bf16[256,128]{1,0:T(8,128)(2,1)}, bf16[256,128]{1,0:T(8,128)(2,1)S(1)}, u32[]{:S(2)}, u32[]{:S(2)}) collective-permute-start(bf16[256,128]{1,0:T(8,128)(2,1)} %get-tuple-element.50), channel_id=1, source_target_pairs={{0,6},{1,7},{2,4},{3,5},{4,2},{5,3},{6,0},{7,1},{8,14},{9,15},{10,... | collective-permute-start | bytes 196616 | tf_op jit(solution)/shard_map/ppermute | solution.py:172
  127.6 9.3 %collective-permute-start.24 = (bf16[256,128]{1,0:T(8,128)(2,1)}, bf16[256,128]{1,0:T(8,128)(2,1)S(1)}, u32[]{:S(2)}, u32[]{:S(2)}) collective-permute-start(bf16[256,128]{1,0:T(8,128)(2,1)} %get-tuple-element.51), channel_id=1, source_target_pairs={{0,1},{1,2},{2,3},{3,0},{4,5},{5,6},{6,7},{7,4},{8,9},{9,10},{10,1... | collective-permute-start | bytes 196616 | tf_op jit(solution)/shard_map/ppermute | solution.py:172
  129.1 7.8 %collective-permute-start.25 = (bf16[256,128]{1,0:T(8,128)(2,1)}, bf16[256,128]{1,0:T(8,128)(2,1)S(1)}, u32[]{:S(2)}, u32[]{:S(2)}) collective-permute-start(bf16[256,128]{1,0:T(8,128)(2,1)} %get-tuple-element.52), channel_id=1, source_target_pairs={{0,5},{1,6},{2,7},{3,4},{4,1},{5,2},{6,3},{7,0},{8,13},{9,14},{10,... | collective-permute-start | bytes 196616 | tf_op jit(solution)/shard_map/ppermute | solution.py:172
  (19 other events, 110.4 us)

commit v6 on v5

--- a/solution.py
+++ b/solution.py
@@ -78,7 +78,7 @@
             pltpu.SemaphoreType.DMA((2 * nb,)),
             pltpu.SemaphoreType.DMA((sum(counts),)),
         ],
-        compiler_params=WHOLE,
+        compiler_params=beside(8 * MIB),
         cost_estimate=cost(3),
         name="pack_first",
     )(*tensors)
@@ -111,7 +111,7 @@
             pltpu.SemaphoreType.DMA((len(items),)),
             pltpu.SemaphoreType.DMA((len(items) * n_s,)),
         ],
-        compiler_params=WHOLE,
+        compiler_params=beside(8 * MIB),
         cost_estimate=cost(3),
         name="pack_rest",
     )(*tensors, after)
@@ -150,7 +150,7 @@
         out_specs=[VMEM] * n_out + [ANY],
         input_output_aliases={n_b: n_out},
         scratch_shapes=[pltpu.SemaphoreType.DMA((n_copies,))],
-        compiler_params=WHOLE,
+        compiler_params=beside(8 * MIB),
         cost_estimate=cost(3),
         name="stage",
     )(*blocks, packed, *after)

time: 144 us -> 141 us (0.979)
  Pallas kernels: 31.8 us -> 30 us
    unnamed x45 -> x35, local copies, waits for them, and re-layouts: 3.19 us -> 2.11 us
where the time goes in v6:
time: 141 us; the launch traced here: 140 us
  waiting for transfers between devices  58.4 us (41%)
  starting transfers between devices  48.4 us (34%)
  Pallas kernels  30 us (21%)
  local copies, waits for them, and re-layouts  2.85 us (2%)
    ppermute x12, waiting for transfers between devices, swap_chip(): return lax.ppermute(x, 'ctx', [(i, i ^ 2 * bit) for i in range(n_c)])  46.3 us
    all_to_all x3, starting transfers between devices, to_shares(): lax.all_to_all(x, ('ctx', 'ulys'), split_axis=0, concat_axis=0, tiled=Tru...  17.8 us
    ppermute x14, starting transfers between devices, send(): return lax.ppermute(x, ('ctx', 'ulys'), pairs)  17.5 us
    ppermute x12, starting transfers between devices, swap_chip(): return lax.ppermute(x, 'ctx', [(i, i ^ 2 * bit) for i in range(n_c)])  13.1 us
    ppermute x14, waiting for transfers between devices, send(): return lax.ppermute(x, ('ctx', 'ulys'), pairs)  12.1 us
    pallas_call x2, Pallas kernels, project(): pl.pallas_call(body, out_shape=jax.ShapeDtypeStruct((T, width), jnp.bfloa...  10.9 us
    pallas_call x2, Pallas kernels, attend(): pl.pallas_call(body, out_shape=[jax.ShapeDtypeStruct((T, DH) if apart els...  10.8 us
    pallas_call x2, Pallas kernels, stage(): pl.pallas_call(body, out_shape=[jax.ShapeDtypeStruct(x, jnp.bfloat16) for...  3.73 us
  transfers between devices with their start and end apart: 29, of which 10 were waited for; matrix products, arithmetic and copies ran while one was open for 1% of the time, Pallas kernels for 13%

profile of v6, /device:TPU:0, one launch (start us, length us, event | category | flops | bytes accessed | tf_op | source)
XLA Modules:
  0.0 140.3 jit_solution(3777663993396178315)
XLA Ops:
  0.0 1.8 %pack_first.1 = (bf16[2,256,128]{2,1,0:T(8,128)(2,1)S(1)}, bf16[2,256,128]{2,1,0:T(8,128)(2,1)S(1)}, bf16[2,256,128]{2,1,0:T(8,128)(2,1)S(1)}, bf16[2,256,128]{2...) custom-call(bf16[256,2048]{1,0:T(8,128)(2,1)} %refs_1_.4, ...), custom_call_target="tpu_custom_call" | custom-call | flops 3449999872 | tf_op jit(solution)/shard_map/pack_first/pallas_call | solution.py:70
  2.3 2.6 %collective-permute-start.1 = (bf16[2,256,128]{2,1,0:T(8,128)(2,1)S(1)}, bf16[2,256,128]{2,1,0:T(8,128)(2,1)S(1)}, u32[]{:S(2)}, u32[]{:S(2)}) collective-permute-start(bf16[2,256,128]{2,1,0:T(8,128)(2,1)S(1)} %get-tuple-element.31), channel_id=1, source_target_pairs={{0,1},{1,2},{2,3},{3,0},{4,5},{5,6},{6,7},{7,4},{8,9},{9,10},{10,1... | collective-permute-start | bytes 393224 | tf_op jit(solution)/shard_map/ppermute | solution.py:172
  4.9 1.3 collective-permute-start.2
  10.1 2.3 %collective-permute-start.5 = (bf16[2,256,128]{2,1,0:T(8,128)(2,1)S(1)}, bf16[2,256,128]{2,1,0:T(8,128)(2,1)S(1)}, u32[]{:S(2)}, u32[]{:S(2)}) collective-permute-start(bf16[2,256,128]{2,1,0:T(8,128)(2,1)S(1)} %get-tuple-element.35), channel_id=1, source_target_pairs={{0,3},{1,0},{2,1},{3,2},{4,7},{5,4},{6,5},{7,6},{8,11},{9,8},{10,9... | collective-permute-start | bytes 393224 | tf_op jit(solution)/shard_map/ppermute | solution.py:172
  12.7 2.8 %pack_rest.1 = (bf16[8,3,256,128]{3,2,1,0:T(8,128)(2,1)}, bf16[8,1,256,128]{3,2,1,0:T(8,128)(2,1)}) custom-call(bf16[256,2048]{1,0:T(8,128)(2,1)S(1)} %copy-done.1, bf16[256,2048]{1,0:T(8,128)(2,1)} %refs_1_.4, bf16[256,2048]{1,0:T(8,128)(2,1)} %refs_2_.1, bf16[2,256,128]{2,1,0:T(8,128)(2,1)S(1)} %collective-permute-done.1.refs_3_.refs_2_), custom_call_target="tpu_custom_call" | custom-call | flops 3449999872 | tf_op jit(solution)/shard_map/pack_rest/pallas_call | solution.py:104
  15.5 6.9 %collective-permute-done.3.refs_4_ = bf16[2,256,128]{2,1,0:T(8,128)(2,1)S(1)} collective-permute-done((bf16[2,256,128]{2,1,0:T(8,128)(2,1)S(1)}, bf16[2,256,128]{2,1,0:T(8,128)(2,1)S(1)}, u32[]{:S(2)}, u32[]{:S(2)}) %collective-permute-start.3) | collective-permute-done | bytes 131104 | tf_op jit(solution)/shard_map/ppermute | solution.py:172
  22.4 2.7 %collective-permute-done.4.refs_5_ = bf16[2,256,128]{2,1,0:T(8,128)(2,1)S(1)} collective-permute-done((bf16[2,256,128]{2,1,0:T(8,128)(2,1)S(1)}, bf16[2,256,128]{2,1,0:T(8,128)(2,1)S(1)}, u32[]{:S(2)}, u32[]{:S(2)}) %collective-permute-start.4) | collective-permute-done | bytes 131104 | tf_op jit(solution)/shard_map/ppermute | solution.py:172
  25.1 2.4 %stage.2 = (bf16[2048,128]{1,0:T(8,128)(2,1)S(1)}, bf16[2048,128]{1,0:T(8,128)(2,1)}, bf16[8,3,256,128]{3,2,1,0:T(8,128)(2,1)}) custom-call(bf16[2,256,128]{2,1,0:T(8,128)(2,1)S(1)} %get-tuple-element.29.refs_0_, bf16[2,256,128]{2,1,0:T(8,128)(2,1)S(1)} %collective-permute-done.refs_1_, ...), custom_call_target="tpu_custom_call", output_to_operand_aliasing={{2}: (8, {})} | custom-call | flops 3449999872 | tf_op jit(solution)/shard_map/stage/pallas_call | solution.py:146
  27.5 8.3 %all-to-all-start = ((bf16[8,3,256,128]{3,2,1,0:T(8,128)(2,1)}), bf16[8,3,256,128]{3,2,1,0:T(8,128)(2,1)S(1)}, u32[]{:S(2)}, u32[]{:S(2)}) async-start(bf16[8,3,256,128]{3,2,1,0:T(8,128)(2,1)} %get-tuple-element.38), calls=%async_computation | async-start | bytes 3145728 | tf_op jit(solution)/shard_map/all_to_all | solution.py:163
  35.7 1.5 %collective-permute-start.8 = (bf16[2048,128]{1,0:T(8,128)(2,1)S(1)}, bf16[2048,128]{1,0:T(8,128)(2,1)S(1)}, u32[]{:S(2)}, u32[]{:S(2)}) collective-permute-start(bf16[2048,128]{1,0:T(8,128)(2,1)S(1)} %get-tuple-element.40.refs_1_), channel_id=1, source_target_pairs={{0,16},{4,20},{8,24},{12,28},{16,0},{20,4},{24,8},{28,12},{1,17},{... | collective-permute-start | bytes 1572872 | tf_op jit(solution)/shard_map/ppermute | solution.py:180
  37.3 1.5 %collective-permute-start.10 = (bf16[2048,128]{1,0:T(8,128)(2,1)S(1)}, bf16[2048,128]{1,0:T(8,128)(2,1)S(1)}, u32[]{:S(2)}, u32[]{:S(2)}) collective-permute-start(bf16[2048,128]{1,0:T(8,128)(2,1)S(1)} %copy-done.9), channel_id=1, source_target_pairs={{0,8},{4,12},{8,0},{12,4},{16,24},{20,28},{24,16},{28,20},{1,9},{5... | collective-permute-start | bytes 1572872 | tf_op jit(solution)/shard_map/ppermute | solution.py:180
  39.8 10.7 %collective-permute-done.8.refs_3_ = bf16[2048,128]{1,0:T(8,128)(2,1)S(1)} collective-permute-done((bf16[2048,128]{1,0:T(8,128)(2,1)S(1)}, bf16[2048,128]{1,0:T(8,128)(2,1)S(1)}, u32[]{:S(2)}, u32[]{:S(2)}) %collective-permute-start.8) | collective-permute-done | bytes 524320 | tf_op jit(solution)/shard_map/ppermute | solution.py:180
  50.5 1.5 %collective-permute-start.9 = (bf16[2048,128]{1,0:T(8,128)(2,1)S(1)}, bf16[2048,128]{1,0:T(8,128)(2,1)S(1)}, u32[]{:S(2)}, u32[]{:S(2)}) collective-permute-start(bf16[2048,128]{1,0:T(8,128)(2,1)S(1)} %collective-permute-done.8.refs_3_), channel_id=1, source_target_pairs={{0,8},{4,12},{8,0},{12,4},{16,24},{20,28},{24,16},{28,20},{1,9},{5... | collective-permute-start | bytes 1572872 | tf_op jit(solution)/shard_map/ppermute | solution.py:180
  52.0 1.5 %collective-permute-start.12 = (bf16[2048,128]{1,0:T(8,128)(2,1)S(1)}, bf16[2048,128]{1,0:T(8,128)(2,1)}, u32[]{:S(2)}, u32[]{:S(2)}) collective-permute-start(bf16[2048,128]{1,0:T(8,128)(2,1)S(1)} %collective-permute-done.10.refs_5_.refs_6_), channel_id=1, source_target_pairs={{0,16},{4,20},{8,24},{12,28},{16,0},{20,4},{24,8},{28,12},{1,17},{... | collective-permute-start | bytes 1572872 | tf_op jit(solution)/shard_map/ppermute | solution.py:180
  53.5 9.8 %collective-permute-done.7.refs_2_ = bf16[2048,128]{1,0:T(8,128)(2,1)S(1)} collective-permute-done((bf16[2048,128]{1,0:T(8,128)(2,1)S(1)}, bf16[2048,128]{1,0:T(8,128)(2,1)S(1)}, u32[]{:S(2)}, u32[]{:S(2)}) %collective-permute-start.7) | collective-permute-done | bytes 524320 | tf_op jit(solution)/shard_map/ppermute | solution.py:180
  63.3 10.5 %collective-permute-done.9.refs_4_ = bf16[2048,128]{1,0:T(8,128)(2,1)S(1)} collective-permute-done((bf16[2048,128]{1,0:T(8,128)(2,1)S(1)}, bf16[2048,128]{1,0:T(8,128)(2,1)S(1)}, u32[]{:S(2)}, u32[]{:S(2)}) %collective-permute-start.9) | collective-permute-done | bytes 524320 | tf_op jit(solution)/shard_map/ppermute | solution.py:180
  75.8 1.4 stage.3
  77.7 1.5 %collective-permute-start.16 = (bf16[2048,128]{1,0:T(8,128)(2,1)S(1)}, bf16[2048,128]{1,0:T(8,128)(2,1)S(1)}, u32[]{:S(2)}, u32[]{:S(2)}) collective-permute-start(bf16[2048,128]{1,0:T(8,128)(2,1)S(1)} %get-tuple-element.44.refs_5_), channel_id=1, source_target_pairs={{0,8},{4,12},{8,0},{12,4},{16,24},{20,28},{24,16},{28,20},{1,9},{5... | collective-permute-start | bytes 1572872 | tf_op jit(solution)/shard_map/ppermute | solution.py:180
  79.2 4.7 %all-to-all-start.1 = ((bf16[8,1,256,128]{3,2,1,0:T(8,128)(2,1)}), bf16[8,1,256,128]{3,2,1,0:T(8,128)(2,1)S(1)}, u32[]{:S(2)}, u32[]{:S(2)}) async-start(bf16[8,1,256,128]{3,2,1,0:T(8,128)(2,1)} %get-tuple-element.42), calls=%async_computation.1 | async-start | bytes 1048576 | tf_op jit(solution)/shard_map/all_to_all | solution.py:163
  84.5 1.5 %collective-permute-start.17 = (bf16[2048,128]{1,0:T(8,128)(2,1)S(1)}, bf16[2048,128]{1,0:T(8,128)(2,1)}, u32[]{:S(2)}, u32[]{:S(2)}) collective-permute-start(bf16[2048,128]{1,0:T(8,128)(2,1)S(1)} %get-tuple-element.44.refs_5_), channel_id=1, source_target_pairs={{0,16},{4,20},{8,24},{12,28},{16,0},{20,4},{24,8},{28,12},{1,17},{... | collective-permute-start | bytes 1572872 | tf_op jit(solution)/shard_map/ppermute | solution.py:180
  86.0 6.1 %collective-permute-done.14.refs_3_ = bf16[2048,128]{1,0:T(8,128)(2,1)S(1)} collective-permute-done((bf16[2048,128]{1,0:T(8,128)(2,1)S(1)}, bf16[2048,128]{1,0:T(8,128)(2,1)S(1)}, u32[]{:S(2)}, u32[]{:S(2)}) %collective-permute-start.14) | collective-permute-done | bytes 524320 | tf_op jit(solution)/shard_map/ppermute | solution.py:180
  92.1 1.5 %collective-permute-start.15 = (bf16[2048,128]{1,0:T(8,128)(2,1)S(1)}, bf16[2048,128]{1,0:T(8,128)(2,1)}, u32[]{:S(2)}, u32[]{:S(2)}) collective-permute-start(bf16[2048,128]{1,0:T(8,128)(2,1)S(1)} %collective-permute-done.14.refs_3_), channel_id=1, source_target_pairs={{0,8},{4,12},{8,0},{12,4},{16,24},{20,28},{24,16},{28,20},{1,9},{5... | collective-permute-start | bytes 1572872 | tf_op jit(solution)/shard_map/ppermute | solution.py:180
  94.1 5.4 %attend.3 = bf16[8,256,128]{2,1,0:T(8,128)(2,1)} custom-call(s32[32,8]{1,0:T(8,128)} %copy-done, bf16[8,3,256,128]{3,2,1,0:T(8,128)(2,1)} %copy-done.6, bf16[2048,128]{1,0:T(8,128)(2,1)} %copy-done.2, bf16[2048,128]{1,0:T(8,128)(2,1)} %copy-done.12, bf16[2048,128]{1,0:T(8,128)(2,1)} %copy-done.10, bf16[2048,128]{1,0:T(8,128)(2,1)} %copy-done.15, ...), custom_call_target="tpu_custom_call" | custom-call | flops 9200000000 | tf_op jit(solution)/shard_map/attend/pallas_call | solution.py:262
  99.6 4.8 %all-to-all-start.2 = ((bf16[8,256,128]{2,1,0:T(8,128)(2,1)}), bf16[8,256,128]{2,1,0:T(8,128)(2,1)S(1)}, u32[]{:S(2)}, u32[]{:S(2)}) async-start(bf16[8,256,128]{2,1,0:T(8,128)(2,1)} %attend.3), calls=%async_computation.2 | async-start | bytes 1048576 | tf_op jit(solution)/shard_map/all_to_all | solution.py:163
  104.3 9.1 %collective-permute-done.15.refs_4_ = bf16[2048,128]{1,0:T(8,128)(2,1)} collective-permute-done((bf16[2048,128]{1,0:T(8,128)(2,1)S(1)}, bf16[2048,128]{1,0:T(8,128)(2,1)}, u32[]{:S(2)}, u32[]{:S(2)}) %collective-permute-start.15) | collective-permute-done | bytes 524320 | tf_op jit(solution)/shard_map/ppermute | solution.py:180
  113.5 5.4 %attend.2 = (bf16[256,128]{1,0:T(8,128)(2,1)}, bf16[256,128]{1,0:T(8,128)(2,1)}, bf16[256,128]{1,0:T(8,128)(2,1)}, bf16[256,128]{1,0:T(8,128)(2,1)}, bf16[256,12...) custom-call(s32[32,8]{1,0:T(8,128)} %copy-done, ...), custom_call_target="tpu_custom_call" | custom-call | flops 9200000000 | tf_op jit(solution)/shard_map/attend/pallas_call | solution.py:262
  118.9 3.0 %collective-permute-start.20 = (bf16[256,128]{1,0:T(8,128)(2,1)}, bf16[256,128]{1,0:T(8,128)(2,1)S(1)}, u32[]{:S(2)}, u32[]{:S(2)}) collective-permute-start(bf16[256,128]{1,0:T(8,128)(2,1)} %get-tuple-element.47), channel_id=1, source_target_pairs={{0,3},{1,0},{2,1},{3,2},{4,7},{5,4},{6,5},{7,6},{8,11},{9,8},{10,9... | collective-permute-start | bytes 196616 | tf_op jit(solution)/shard_map/ppermute | solution.py:172
  122.3 2.6 %collective-permute-start.23 = (bf16[256,128]{1,0:T(8,128)(2,1)}, bf16[256,128]{1,0:T(8,128)(2,1)S(1)}, u32[]{:S(2)}, u32[]{:S(2)}) collective-permute-start(bf16[256,128]{1,0:T(8,128)(2,1)} %get-tuple-element.50), channel_id=1, source_target_pairs={{0,6},{1,7},{2,4},{3,5},{4,2},{5,3},{6,0},{7,1},{8,14},{9,15},{10,... | collective-permute-start | bytes 196616 | tf_op jit(solution)/shard_map/ppermute | solution.py:172
  124.9 1.5 %collective-permute-start.24 = (bf16[256,128]{1,0:T(8,128)(2,1)}, bf16[256,128]{1,0:T(8,128)(2,1)S(1)}, u32[]{:S(2)}, u32[]{:S(2)}) collective-permute-start(bf16[256,128]{1,0:T(8,128)(2,1)} %get-tuple-element.51), channel_id=1, source_target_pairs={{0,1},{1,2},{2,3},{3,0},{4,5},{5,6},{6,7},{7,4},{8,9},{9,10},{10,1... | collective-permute-start | bytes 196616 | tf_op jit(solution)/shard_map/ppermute | solution.py:172
  126.7 5.0 %project.2.refs_9_ = f32[256,4096]{1,0:T(8,128)S(1)} custom-call(bf16[8,256,128]{2,1,0:T(8,128)(2,1)S(1)} %all-to-all-done.2.refs_0_, bf16[2048,4096]{1,0:T(8,128)(2,1)} %refs_8_.1), custom_call_target="tpu_custom_call" | custom-call | flops 8049999872 | tf_op jit(solution)/shard_map/project/pallas_call | solution.py:330
  131.7 2.3 %collective-permute-done.22.refs_4_ = bf16[256,128]{1,0:T(8,128)(2,1)S(1)} collective-permute-done((bf16[256,128]{1,0:T(8,128)(2,1)}, bf16[256,128]{1,0:T(8,128)(2,1)S(1)}, u32[]{:S(2)}, u32[]{:S(2)}) %collective-permute-start.22) | collective-permute-done | bytes 65568 | tf_op jit(solution)/shard_map/ppermute | solution.py:172
  134.2 6.0 %project.3 = bf16[256,4096]{1,0:T(8,128)(2,1)} custom-call(bf16[256,128]{1,0:T(8,128)(2,1)S(1)} %copy-done.5, bf16[256,128]{1,0:T(8,128)(2,1)S(1)} %collective-permute-done.19.refs_1_, bf16[256,128]{1,0:T(8,128)(2,1)S(1)} %collective-permute-done.20.refs_2_, bf16[256,128]{1,0:T(8,128)(2,1)S(1)} %collective-permute-done.21.refs_3_, ...), custom_call_target="tpu_custom_call" | custom-call | flops 8049999872 | tf_op jit(solution)/shard_map/project/pallas_call | solution.py:330
  (79 shorter events, 10.3 us)
Async XLA Ops:
  1.8 8.3 %collective-permute-start = (bf16[2,256,128]{2,1,0:T(8,128)(2,1)S(1)}, bf16[2,256,128]{2,1,0:T(8,128)(2,1)S(1)}, u32[]{:S(2)}, u32[]{:S(2)}) collective-permute-start(bf16[2,256,128]{2,1,0:T(8,128)(2,1)S(1)} %get-tuple-element.30), channel_id=1, source_target_pairs={{0,4},{1,5},{2,6},{3,7},{4,0},{5,1},{6,2},{7,3},{8,12},{9,13},{10,... | collective-permute-start | bytes 393224 | tf_op jit(solution)/shard_map/ppermute | solution.py:172
  2.3 10.1 %collective-permute-start.1 = (bf16[2,256,128]{2,1,0:T(8,128)(2,1)S(1)}, bf16[2,256,128]{2,1,0:T(8,128)(2,1)S(1)}, u32[]{:S(2)}, u32[]{:S(2)}) collective-permute-start(bf16[2,256,128]{2,1,0:T(8,128)(2,1)S(1)} %get-tuple-element.31), channel_id=1, source_target_pairs={{0,1},{1,2},{2,3},{3,0},{4,5},{5,6},{6,7},{7,4},{8,9},{9,10},{10,1... | collective-permute-start | bytes 393224 | tf_op jit(solution)/shard_map/ppermute | solution.py:172
  4.9 10.6 %collective-permute-start.2 = (bf16[2,256,128]{2,1,0:T(8,128)(2,1)S(1)}, bf16[2,256,128]{2,1,0:T(8,128)(2,1)S(1)}, u32[]{:S(2)}, u32[]{:S(2)}) collective-permute-start(bf16[2,256,128]{2,1,0:T(8,128)(2,1)S(1)} %get-tuple-element.32), channel_id=1, source_target_pairs={{0,5},{1,6},{2,7},{3,4},{4,1},{5,2},{6,3},{7,0},{8,13},{9,14},{10,... | collective-permute-start | bytes 393224 | tf_op jit(solution)/shard_map/ppermute | solution.py:172
  6.3 16.1 %collective-permute-start.3 = (bf16[2,256,128]{2,1,0:T(8,128)(2,1)S(1)}, bf16[2,256,128]{2,1,0:T(8,128)(2,1)S(1)}, u32[]{:S(2)}, u32[]{:S(2)}) collective-permute-start(bf16[2,256,128]{2,1,0:T(8,128)(2,1)S(1)} %get-tuple-element.33), channel_id=1, source_target_pairs={{0,2},{1,3},{2,0},{3,1},{4,6},{5,7},{6,4},{7,5},{8,10},{9,11},{10,... | collective-permute-start | bytes 393224 | tf_op jit(solution)/shard_map/ppermute | solution.py:172
  7.6 17.4 %collective-permute-start.4 = (bf16[2,256,128]{2,1,0:T(8,128)(2,1)S(1)}, bf16[2,256,128]{2,1,0:T(8,128)(2,1)S(1)}, u32[]{:S(2)}, u32[]{:S(2)}) collective-permute-start(bf16[2,256,128]{2,1,0:T(8,128)(2,1)S(1)} %get-tuple-element.34), channel_id=1, source_target_pairs={{0,6},{1,7},{2,4},{3,5},{4,2},{5,3},{6,0},{7,1},{8,14},{9,15},{10,... | collective-permute-start | bytes 393224 | tf_op jit(solution)/shard_map/ppermute | solution.py:172
  10.1 15.0 %collective-permute-start.5 = (bf16[2,256,128]{2,1,0:T(8,128)(2,1)S(1)}, bf16[2,256,128]{2,1,0:T(8,128)(2,1)S(1)}, u32[]{:S(2)}, u32[]{:S(2)}) collective-permute-start(bf16[2,256,128]{2,1,0:T(8,128)(2,1)S(1)} %get-tuple-element.35), channel_id=1, source_target_pairs={{0,3},{1,0},{2,1},{3,2},{4,7},{5,4},{6,5},{7,6},{8,11},{9,8},{10,9... | collective-permute-start | bytes 393224 | tf_op jit(solution)/shard_map/ppermute | solution.py:172
  12.4 12.7 %collective-permute-start.6 = (bf16[2,256,128]{2,1,0:T(8,128)(2,1)S(1)}, bf16[2,256,128]{2,1,0:T(8,128)(2,1)S(1)}, u32[]{:S(2)}, u32[]{:S(2)}) collective-permute-start(bf16[2,256,128]{2,1,0:T(8,128)(2,1)S(1)} %get-tuple-element.36), channel_id=1, source_target_pairs={{0,7},{1,4},{2,5},{3,6},{4,3},{5,0},{6,1},{7,2},{8,15},{9,12},{10,... | collective-permute-start | bytes 393224 | tf_op jit(solution)/shard_map/ppermute | solution.py:172
  27.4 49.7 %copy-start.2 = (bf16[2048,128]{1,0:T(8,128)(2,1)}, bf16[2048,128]{1,0:T(8,128)(2,1)S(1)}, u32[]{:S(2)}) copy-start(bf16[2048,128]{1,0:T(8,128)(2,1)S(1)} %get-tuple-element.40.refs_1_) | copy-start | bytes 1572868
  27.5 47.1 %all-to-all-start = ((bf16[8,3,256,128]{3,2,1,0:T(8,128)(2,1)}), bf16[8,3,256,128]{3,2,1,0:T(8,128)(2,1)S(1)}, u32[]{:S(2)}, u32[]{:S(2)}) async-start(bf16[8,3,256,128]{3,2,1,0:T(8,128)(2,1)} %get-tuple-element.38), calls=%async_computation | async-start | bytes 3145728 | tf_op jit(solution)/shard_map/all_to_all | solution.py:163
  35.7 14.7 %collective-permute-start.8 = (bf16[2048,128]{1,0:T(8,128)(2,1)S(1)}, bf16[2048,128]{1,0:T(8,128)(2,1)S(1)}, u32[]{:S(2)}, u32[]{:S(2)}) collective-permute-start(bf16[2048,128]{1,0:T(8,128)(2,1)S(1)} %get-tuple-element.40.refs_1_), channel_id=1, source_target_pairs={{0,16},{4,20},{8,24},{12,28},{16,0},{20,4},{24,8},{28,12},{1,17},{... | collective-permute-start | bytes 1572872 | tf_op jit(solution)/shard_map/ppermute | solution.py:180
  37.3 14.8 %collective-permute-start.10 = (bf16[2048,128]{1,0:T(8,128)(2,1)S(1)}, bf16[2048,128]{1,0:T(8,128)(2,1)S(1)}, u32[]{:S(2)}, u32[]{:S(2)}) collective-permute-start(bf16[2048,128]{1,0:T(8,128)(2,1)S(1)} %copy-done.9), channel_id=1, source_target_pairs={{0,8},{4,12},{8,0},{12,4},{16,24},{20,28},{24,16},{28,20},{1,9},{5... | collective-permute-start | bytes 1572872 | tf_op jit(solution)/shard_map/ppermute | solution.py:180
  38.7 24.5 %collective-permute-start.7 = (bf16[2048,128]{1,0:T(8,128)(2,1)S(1)}, bf16[2048,128]{1,0:T(8,128)(2,1)S(1)}, u32[]{:S(2)}, u32[]{:S(2)}) collective-permute-start(bf16[2048,128]{1,0:T(8,128)(2,1)S(1)} %get-tuple-element.40.refs_1_), channel_id=1, source_target_pairs={{0,8},{4,12},{8,0},{12,4},{16,24},{20,28},{24,16},{28,20},{1,9},{5... | collective-permute-start | bytes 1572872 | tf_op jit(solution)/shard_map/ppermute | solution.py:180
  39.3 24.0 %collective-permute-start.11 = (bf16[2048,128]{1,0:T(8,128)(2,1)S(1)}, bf16[2048,128]{1,0:T(8,128)(2,1)S(1)}, u32[]{:S(2)}, u32[]{:S(2)}) collective-permute-start(bf16[2048,128]{1,0:T(8,128)(2,1)S(1)} %copy-done.9), channel_id=1, source_target_pairs={{0,16},{4,20},{8,24},{12,28},{16,0},{20,4},{24,8},{28,12},{1,17},{... | collective-permute-start | bytes 1572872 | tf_op jit(solution)/shard_map/ppermute | solution.py:180
  50.4 24.2 %copy-start.10 = (bf16[2048,128]{1,0:T(8,128)(2,1)}, bf16[2048,128]{1,0:T(8,128)(2,1)S(1)}, u32[]{:S(2)}) copy-start(bf16[2048,128]{1,0:T(8,128)(2,1)S(1)} %collective-permute-done.8.refs_3_) | copy-start | bytes 1572868
  50.5 23.3 %collective-permute-start.9 = (bf16[2048,128]{1,0:T(8,128)(2,1)S(1)}, bf16[2048,128]{1,0:T(8,128)(2,1)S(1)}, u32[]{:S(2)}, u32[]{:S(2)}) collective-permute-start(bf16[2048,128]{1,0:T(8,128)(2,1)S(1)} %collective-permute-done.8.refs_3_), channel_id=1, source_target_pairs={{0,8},{4,12},{8,0},{12,4},{16,24},{20,28},{24,16},{28,20},{1,9},{5... | collective-permute-start | bytes 1572872 | tf_op jit(solution)/shard_map/ppermute | solution.py:180
  52.0 22.6 %collective-permute-start.12 = (bf16[2048,128]{1,0:T(8,128)(2,1)S(1)}, bf16[2048,128]{1,0:T(8,128)(2,1)}, u32[]{:S(2)}, u32[]{:S(2)}) collective-permute-start(bf16[2048,128]{1,0:T(8,128)(2,1)S(1)} %collective-permute-done.10.refs_5_.refs_6_), channel_id=1, source_target_pairs={{0,16},{4,20},{8,24},{12,28},{16,0},{20,4},{24,8},{28,12},{1,17},{... | collective-permute-start | bytes 1572872 | tf_op jit(solution)/shard_map/ppermute | solution.py:180
  77.1 22.4 %copy-start.3 = (bf16[2048,128]{1,0:T(8,128)(2,1)}, bf16[2048,128]{1,0:T(8,128)(2,1)S(1)}, u32[]{:S(2)}) copy-start(bf16[2048,128]{1,0:T(8,128)(2,1)S(1)} %get-tuple-element.43.refs_1_) | copy-start | bytes 1572868
  77.2 14.9 %collective-permute-start.14 = (bf16[2048,128]{1,0:T(8,128)(2,1)S(1)}, bf16[2048,128]{1,0:T(8,128)(2,1)S(1)}, u32[]{:S(2)}, u32[]{:S(2)}) collective-permute-start(bf16[2048,128]{1,0:T(8,128)(2,1)S(1)} %get-tuple-element.43.refs_1_), channel_id=1, source_target_pairs={{0,16},{4,20},{8,24},{12,28},{16,0},{20,4},{24,8},{28,12},{1,17},{... | collective-permute-start | bytes 1572872 | tf_op jit(solution)/shard_map/ppermute | solution.py:180
  77.7 15.9 %collective-permute-start.16 = (bf16[2048,128]{1,0:T(8,128)(2,1)S(1)}, bf16[2048,128]{1,0:T(8,128)(2,1)S(1)}, u32[]{:S(2)}, u32[]{:S(2)}) collective-permute-start(bf16[2048,128]{1,0:T(8,128)(2,1)S(1)} %get-tuple-element.44.refs_5_), channel_id=1, source_target_pairs={{0,8},{4,12},{8,0},{12,4},{16,24},{20,28},{24,16},{28,20},{1,9},{5... | collective-permute-start | bytes 1572872 | tf_op jit(solution)/shard_map/ppermute | solution.py:180
  79.2 20.3 %all-to-all-start.1 = ((bf16[8,1,256,128]{3,2,1,0:T(8,128)(2,1)}), bf16[8,1,256,128]{3,2,1,0:T(8,128)(2,1)S(1)}, u32[]{:S(2)}, u32[]{:S(2)}) async-start(bf16[8,1,256,128]{3,2,1,0:T(8,128)(2,1)} %get-tuple-element.42), calls=%async_computation.1 | async-start | bytes 1048576 | tf_op jit(solution)/shard_map/all_to_all | solution.py:163
  84.0 20.3 %collective-permute-start.13 = (bf16[2048,128]{1,0:T(8,128)(2,1)S(1)}, bf16[2048,128]{1,0:T(8,128)(2,1)}, u32[]{:S(2)}, u32[]{:S(2)}) collective-permute-start(bf16[2048,128]{1,0:T(8,128)(2,1)S(1)} %get-tuple-element.43.refs_1_), channel_id=1, source_target_pairs={{0,8},{4,12},{8,0},{12,4},{16,24},{20,28},{24,16},{28,20},{1,9},{5... | collective-permute-start | bytes 1572872 | tf_op jit(solution)/shard_map/ppermute | solution.py:180
  84.5 19.8 %collective-permute-start.17 = (bf16[2048,128]{1,0:T(8,128)(2,1)S(1)}, bf16[2048,128]{1,0:T(8,128)(2,1)}, u32[]{:S(2)}, u32[]{:S(2)}) collective-permute-start(bf16[2048,128]{1,0:T(8,128)(2,1)S(1)} %get-tuple-element.44.refs_5_), channel_id=1, source_target_pairs={{0,16},{4,20},{8,24},{12,28},{16,0},{20,4},{24,8},{28,12},{1,17},{... | collective-permute-start | bytes 1572872 | tf_op jit(solution)/shard_map/ppermute | solution.py:180
  92.1 21.4 %collective-permute-start.15 = (bf16[2048,128]{1,0:T(8,128)(2,1)S(1)}, bf16[2048,128]{1,0:T(8,128)(2,1)}, u32[]{:S(2)}, u32[]{:S(2)}) collective-permute-start(bf16[2048,128]{1,0:T(8,128)(2,1)S(1)} %collective-permute-done.14.refs_3_), channel_id=1, source_target_pairs={{0,8},{4,12},{8,0},{12,4},{16,24},{20,28},{24,16},{28,20},{1,9},{5... | collective-permute-start | bytes 1572872 | tf_op jit(solution)/shard_map/ppermute | solution.py:180
  93.6 19.9 %collective-permute-start.18 = (bf16[2048,128]{1,0:T(8,128)(2,1)S(1)}, bf16[2048,128]{1,0:T(8,128)(2,1)}, u32[]{:S(2)}, u32[]{:S(2)}) collective-permute-start(bf16[2048,128]{1,0:T(8,128)(2,1)S(1)} %collective-permute-done.16.refs_6_), channel_id=1, source_target_pairs={{0,16},{4,20},{8,24},{12,28},{16,0},{20,4},{24,8},{28,12},{1,17},{... | collective-permute-start | bytes 1572872 | tf_op jit(solution)/shard_map/ppermute | solution.py:180
  99.6 27.1 %all-to-all-start.2 = ((bf16[8,256,128]{2,1,0:T(8,128)(2,1)}), bf16[8,256,128]{2,1,0:T(8,128)(2,1)S(1)}, u32[]{:S(2)}, u32[]{:S(2)}) async-start(bf16[8,256,128]{2,1,0:T(8,128)(2,1)} %attend.3), calls=%async_computation.2 | async-start | bytes 1048576 | tf_op jit(solution)/shard_map/all_to_all | solution.py:163
  118.9 6.0 %collective-permute-start.19 = (bf16[256,128]{1,0:T(8,128)(2,1)}, bf16[256,128]{1,0:T(8,128)(2,1)S(1)}, u32[]{:S(2)}, u32[]{:S(2)}) collective-permute-start(bf16[256,128]{1,0:T(8,128)(2,1)} %get-tuple-element.46), channel_id=1, source_target_pairs={{0,4},{1,5},{2,6},{3,7},{4,0},{5,1},{6,2},{7,3},{8,12},{9,13},{10,... | collective-permute-start | bytes 196616 | tf_op jit(solution)/shard_map/ppermute | solution.py:172
  118.9 7.4 %collective-permute-start.20 = (bf16[256,128]{1,0:T(8,128)(2,1)}, bf16[256,128]{1,0:T(8,128)(2,1)S(1)}, u32[]{:S(2)}, u32[]{:S(2)}) collective-permute-start(bf16[256,128]{1,0:T(8,128)(2,1)} %get-tuple-element.47), channel_id=1, source_target_pairs={{0,3},{1,0},{2,1},{3,2},{4,7},{5,4},{6,5},{7,6},{8,11},{9,8},{10,9... | collective-permute-start | bytes 196616 | tf_op jit(solution)/shard_map/ppermute | solution.py:172
  122.0 9.7 %collective-permute-start.21 = (bf16[256,128]{1,0:T(8,128)(2,1)}, bf16[256,128]{1,0:T(8,128)(2,1)S(1)}, u32[]{:S(2)}, u32[]{:S(2)}) collective-permute-start(bf16[256,128]{1,0:T(8,128)(2,1)} %get-tuple-element.48), channel_id=1, source_target_pairs={{0,7},{1,4},{2,5},{3,6},{4,3},{5,0},{6,1},{7,2},{8,15},{9,12},{10,... | collective-permute-start | bytes 196616 | tf_op jit(solution)/shard_map/ppermute | solution.py:172
  122.3 11.7 %collective-permute-start.22 = (bf16[256,128]{1,0:T(8,128)(2,1)}, bf16[256,128]{1,0:T(8,128)(2,1)S(1)}, u32[]{:S(2)}, u32[]{:S(2)}) collective-permute-start(bf16[256,128]{1,0:T(8,128)(2,1)} %get-tuple-element.49), channel_id=1, source_target_pairs={{0,2},{1,3},{2,0},{3,1},{4,6},{5,7},{6,4},{7,5},{8,10},{9,11},{10,... | collective-permute-start | bytes 196616 | tf_op jit(solution)/shard_map/ppermute | solution.py:172
  122.3 11.9 %collective-permute-start.23 = (bf16[256,128]{1,0:T(8,128)(2,1)}, bf16[256,128]{1,0:T(8,128)(2,1)S(1)}, u32[]{:S(2)}, u32[]{:S(2)}) collective-permute-start(bf16[256,128]{1,0:T(8,128)(2,1)} %get-tuple-element.50), channel_id=1, source_target_pairs={{0,6},{1,7},{2,4},{3,5},{4,2},{5,3},{6,0},{7,1},{8,14},{9,15},{10,... | collective-permute-start | bytes 196616 | tf_op jit(solution)/shard_map/ppermute | solution.py:172
  124.9 9.3 %collective-permute-start.24 = (bf16[256,128]{1,0:T(8,128)(2,1)}, bf16[256,128]{1,0:T(8,128)(2,1)S(1)}, u32[]{:S(2)}, u32[]{:S(2)}) collective-permute-start(bf16[256,128]{1,0:T(8,128)(2,1)} %get-tuple-element.51), channel_id=1, source_target_pairs={{0,1},{1,2},{2,3},{3,0},{4,5},{5,6},{6,7},{7,4},{8,9},{9,10},{10,1... | collective-permute-start | bytes 196616 | tf_op jit(solution)/shard_map/ppermute | solution.py:172
  126.4 7.8 %collective-permute-start.25 = (bf16[256,128]{1,0:T(8,128)(2,1)}, bf16[256,128]{1,0:T(8,128)(2,1)S(1)}, u32[]{:S(2)}, u32[]{:S(2)}) collective-permute-start(bf16[256,128]{1,0:T(8,128)(2,1)} %get-tuple-element.52), channel_id=1, source_target_pairs={{0,5},{1,6},{2,7},{3,4},{4,1},{5,2},{6,3},{7,0},{8,13},{9,14},{10,... | collective-permute-start | bytes 196616 | tf_op jit(solution)/shard_map/ppermute | solution.py:172
  (14 other events, 149.0 us)

commit v7 on v6

--- a/solution.py
+++ b/solution.py
@@ -46,42 +46,103 @@
     return 2 * lax.rem(z + d + n_u, n_u) + (core if r == 0 else 1 - core)
 
 
-def pack_first(tensors, n_u, early):
+def pack_first(tensors, n_u, hp):
     T, nb, n_s = tensors[0].shape[0], len(tensors), 2 * n_u
-    counts = [nb * (2 if early and d == 0 else 1) for _, d in sides(n_u)]
-
-    def body(*refs):
-        ins, outs = refs[:nb], refs[nb : nb + n_s]
-        held, near, in_sems, out_sems = refs[nb + n_s :]
+
+    def body(*refs):
+        ins, outs = refs[:nb], refs[nb : nb + n_u + 1]
+        held, near, in_sems, out_sems = refs[nb + n_u + 1 :]
+        z, core = lax.axis_index("ulys"), lax.rem(lax.axis_index("ctx"), 2)
         pairs = [(ins[i].at[:, pl.ds(0, n_s * DH)], held.at[i]) for i in range(nb)]
-        if early:
-            cols = pl.ds(pl.multiple_of((n_s + 2 * lax.axis_index("ulys")) * DH, DH), 2 * DH)
-            pairs += [(ins[i].at[:, cols], near.at[i]) for i in range(nb)]
+        for h in range(hp):
+            cols = pl.ds(pl.multiple_of((h * n_s + 2 * z) * DH, DH), 2 * DH)
+            pairs += [(ins[i].at[:, cols], near.at[h * nb + i]) for i in range(nb)]
         copy_all(pairs, in_sems)
         pairs = []
-        for out, (r, d), count in zip(outs, sides(n_u), counts):
-            at = pl.multiple_of(share_at(r, d, n_u) * DH, DH)
-            pairs += [(held.at[i, :, pl.ds(at, DH)], out.at[i]) for i in range(nb)]
-            if count > nb:
-                at = pl.multiple_of((lax.rem(lax.axis_index("ctx"), 2) if r == 0 else 1 - lax.rem(lax.axis_index("ctx"), 2)) * DH, DH)
-                pairs += [(near.at[i, :, pl.ds(at, DH)], out.at[nb + i]) for i in range(nb)]
+        for r in range(2):
+            for d in range(1, n_u):
+                cols = pl.ds(pl.multiple_of(share_at(r, d, n_u) * DH, DH), DH)
+                pairs += [(held.at[i, :, cols], outs[d - 1].at[r, i]) for i in range(nb)]
+            cols = pl.ds(pl.multiple_of((core if r == 0 else 1 - core) * DH, DH), DH)
+            pairs += [(near.at[i, :, cols], outs[n_u - 1 + r].at[i]) for i in range(hp * nb)]
         copy_all(pairs, out_sems)
 
-    return pl.pallas_call(
-        body,
-        out_shape=[jax.ShapeDtypeStruct((n, T, DH), jnp.bfloat16) for n in counts],
+    shapes = [(2, nb, T, DH)] * (n_u - 1) + [(hp * nb, T, DH)] * 2
+    return pl.pallas_call(
+        body,
+        out_shape=[jax.ShapeDtypeStruct(x, jnp.bfloat16) for x in shapes],
         in_specs=[ANY] * nb,
-        out_specs=[ANY] * n_s,
+        out_specs=[ANY] * (n_u + 1),
         scratch_shapes=[
             pltpu.VMEM((nb, T, n_s * DH), jnp.bfloat16),
-            pltpu.VMEM((nb, T, 2 * DH), jnp.bfloat16),
-            pltpu.SemaphoreType.DMA((2 * nb,)),
-            pltpu.SemaphoreType.DMA((sum(counts),)),
+            pltpu.VMEM((hp * nb, T, 2 * DH), jnp.bfloat16),
+            pltpu.SemaphoreType.DMA(((1 + hp) * nb,)),
+            pltpu.SemaphoreType.DMA(((n_s - 2 + 2 * hp) * nb,)),
         ],
         compiler_params=beside(8 * MIB),
-        cost_estimate=cost(3),
+        cost_estimate=cost(2),
         name="pack_first",
     )(*tensors)
+
+
+def for_other(parts):
+    n = len(parts)
+
+    def body(*refs):
+        copy_all([(refs[i].at[1], refs[n].at[i]) for i in range(n)], refs[n + 1])
+
+    return pl.pallas_call(
+        body,
+        out_shape=jax.ShapeDtypeStruct((n, *parts[0].shape[1:]), jnp.bfloat16),
+        in_specs=[ANY] * n,
+        out_specs=VMEM,
+        scratch_shapes=[pltpu.SemaphoreType.DMA((n,))],
+        compiler_params=beside(8 * MIB),
+        cost_estimate=cost(1),
+        name="for_other",
+    )(*parts)
+
+
+def release(packed, after):
+    def body(*refs):
+        pass
+
+    return pl.pallas_call(
+        body,
+        out_shape=jax.ShapeDtypeStruct(packed.shape, packed.dtype),
+        in_specs=[ANY] * (1 + len(after)),
+        out_specs=ANY,
+        input_output_aliases={0: 0},
+        compiler_params=WHOLE,
+        cost_estimate=cost(1),
+        name="release",
+    )(packed, *after)
+
+
+def join(mine, other, hp):
+    n, T, _ = mine.shape
+    nb = n // hp
+
+    def body(mine_ref, other_ref, out, sems):
+        core = lax.rem(lax.axis_index("ctx"), 2)
+        pairs = []
+        for r, ref in enumerate((mine_ref, other_ref)):
+            for h in range(hp):
+                for i in range(nb):
+                    at = (2 * (i * hp + h) + (core if r == 0 else 1 - core)) * T
+                    pairs.append((ref.at[h * nb + i], out.at[pl.ds(pl.multiple_of(at, T), T)]))
+        copy_all(pairs, sems)
+
+    return pl.pallas_call(
+        body,
+        out_shape=jax.ShapeDtypeStruct((2 * n * T, DH), jnp.bfloat16),
+        in_specs=[ANY] * 2,
+        out_specs=VMEM,
+        scratch_shapes=[pltpu.SemaphoreType.DMA((2 * hp * nb,))],
+        compiler_params=beside(8 * MIB),
+        cost_estimate=cost(2),
+        name="join",
+    )(mine, other)
 
 
 def pack_rest(tensors, bundles, n_u, after):
@@ -117,43 +178,37 @@
     )(*tensors, after)
 
 
-def stage(here, packed, n_u, rest, after):
-    apart = isinstance(here, list)
-    blocks = here if apart else [here]
-    n_s, n_b, T = 2 * n_u, len(blocks), blocks[0].shape[-2]
-    n_early = blocks[0].shape[0] - 2 if apart else 0
-    shapes = [((n_s - 2 * rest) * T, DH)] * 2 + [(2 * T, DH)] * n_early
-    n_copies = sum(x.shape[0] for x in blocks) if apart else 2 * (n_s - 2 * rest)
-    n_in, n_out = n_b + 1 + len(after), len(shapes)
+def stage(blocks, packed, n_u, after):
+    n_s, n_b, T = 2 * n_u, len(blocks), blocks[0].shape[2]
+    last = [] if packed is None else [packed]
+    n_in = n_b + len(last) + len(after)
 
     def body(*refs):
         z, core = lax.axis_index("ulys"), lax.rem(lax.axis_index("ctx"), 2)
-        outs, sems = refs[n_in : n_in + n_out], refs[-1]
+        outs, sems = refs[n_in : n_in + 2], refs[-1]
         pairs = []
-        if apart:
-            for k, (r, d) in enumerate(sides(n_u)):
-                at = (2 * ((n_u - d) % n_u) + (core if r == 0 else 1 - core)) * T
-                for i in range(blocks[k].shape[0]):
-                    pairs.append((refs[k].at[i], outs[i].at[pl.ds(pl.multiple_of(at, T), T)]))
-        else:
-            for d in range(rest, n_u):
-                for c in range(2):
-                    src, at = 2 * lax.rem(z + d, n_u) + c, (2 * (d - rest) + c) * T
-                    for i in range(2):
-                        pairs.append((refs[0].at[src, i], outs[i].at[pl.ds(at, T)]))
+        for k in range(2, n_s):
+            d, c = k // 2, k % 2
+            if n_b == 1:
+                block, at = refs[0].at[2 * lax.rem(z + d, n_u) + c], (k - 2) * T
+            else:
+                block = refs[n_u - d - 1].at[0] if c == 0 else refs[n_b - 1].at[n_u - d - 1]
+                at = (2 * (d - 1) + (core if c == 0 else 1 - core)) * T
+            pairs += [(block.at[i], outs[i].at[pl.ds(pl.multiple_of(at, T), T)]) for i in range(2)]
         copy_all(pairs, sems)
 
-    return pl.pallas_call(
-        body,
-        out_shape=[jax.ShapeDtypeStruct(x, jnp.bfloat16) for x in [*shapes, packed.shape]],
+    shapes = [((n_s - 2) * T, DH)] * 2 + [x.shape for x in last]
+    return pl.pallas_call(
+        body,
+        out_shape=[jax.ShapeDtypeStruct(x, jnp.bfloat16) for x in shapes],
         in_specs=[ANY] * n_in,
-        out_specs=[VMEM] * n_out + [ANY],
-        input_output_aliases={n_b: n_out},
-        scratch_shapes=[pltpu.SemaphoreType.DMA((n_copies,))],
+        out_specs=[VMEM] * 2 + [ANY] * len(last),
+        input_output_aliases={n_b: 2} if last else {},
+        scratch_shapes=[pltpu.SemaphoreType.DMA((2 * (n_s - 2),))],
         compiler_params=beside(8 * MIB),
         cost_estimate=cost(3),
         name="stage",
-    )(*blocks, packed, *after)
+    )(*blocks, *last, *after)
 
 
 def to_shares(x, n_c, n_u):
@@ -176,8 +231,32 @@
     return [send(x, r, (sign * d) % n_u, n_c, n_u) for x, (r, d) in zip(parts, sides(n_u))]
 
 
+def swap_core(x, n_c):
+    return lax.ppermute(x, "ctx", [(i, i ^ 1) for i in range(n_c)])
+
+
 def swap_chip(x, bit, n_c):
     return lax.ppermute(x, "ctx", [(i, i ^ (2 * bit)) for i in range(n_c)])
+
+
+def gather_whole(x, n_c):
+    n_p, half = n_c // 2, x.shape[0] // 2
+    got, halves = [], {0: [(x, 0), (x, half)]}
+
+    def again(part, bit):
+        y, at = part
+        got.append(swap_chip(y if y.shape[0] == half else y[at : at + half], bit, n_c))
+        return (got[-1], 0)
+
+    for t in range(1, n_p):
+        if t & (t - 1) == 0:
+            got.append(swap_chip(x, t, n_c))
+            halves[t] = [(got[-1], 0), (got[-1], half)]
+    for t in range(1, n_p):
+        if t & (t - 1) != 0:
+            low, high = t & -t, 1 << (t.bit_length() - 1)
+            halves[t] = [again(halves[t ^ low][0], low), again(halves[t ^ high][1], high)]
+    return [[halves[t][i] for t in range(n_p)] for i in range(2)], got
 
 
 def gather_chips(first, second, n_c):
@@ -196,16 +275,20 @@
     return [a[t] for t in range(n_p)], [b[t] for t in range(n_p)]
 
 
-def attend(table, queries, q_index, keys, values, n_u, apart):
+def attend(table, queries, q_index, slot, near, far, n_u, apart):
     n_s, _, T, _ = queries.shape
     n_q = n_s * T
     span = n_s * T
-    n_k = span * len(keys)
-    k_parts = [(x, t * span + at) for t, parts in enumerate(keys) for x, at in parts]
-    v_parts = [(x, t * span + at) for t, parts in enumerate(values) for x, at in parts]
+    n_k = span * len(far[0])
+    parts = []
+    for nears, fars in zip(near, far):
+        for t, ((x, at), y) in enumerate(zip(nears, fars)):
+            parts.append((x, at + slot * 2 * T, t * span, 2 * T))
+            parts.append((y, 0, t * span + 2 * T, span - 2 * T))
+    n_half = len(parts) // 2
     n_rows, n_list = table.shape
     group = 4 * T // BLK
-    arrays = [queries, *(x for x, _ in k_parts + v_parts)]
+    arrays = [queries, *(x for x, _, _, _ in parts)]
     n_in, n_out = len(arrays), 2 * n_u if apart else 1
 
     def body(table_ref, *refs):
@@ -214,13 +297,13 @@
         pairs = [(table_ref, table)]
         for k in range(n_s):
             pairs.append((ins[0].at[k, q_index], q_vm.at[pl.ds(k * T, T)]))
-        for i, (ref, (x, at)) in enumerate(zip(ins[1:], k_parts + v_parts)):
-            vm = k_vm if i < len(k_parts) else v_vm
-            pairs.append((ref, vm.at[pl.ds(at, x.shape[0])]))
+        for i, (ref, (_, src, dst, n)) in enumerate(zip(ins[1:], parts)):
+            vm = k_vm if i < n_half else v_vm
+            pairs.append((ref.at[pl.ds(src, n)], vm.at[pl.ds(dst, n)]))
         copies = [pltpu.make_async_copy(a, b, sems.at[i]) for i, (a, b) in enumerate(pairs)]
         for c in copies:
             c.start()
-        for c in copies[: 1 + n_s + len(k_parts)]:
+        for c in copies[: 1 + n_s + n_half]:
             c.wait()
         for step in range(n_rows // group):
             rows = range(step * group, (step + 1) * group)
@@ -240,7 +323,7 @@
             e = jnp.exp2((s - jnp.max(s, axis=-1, keepdims=True)) * (DH**-0.5 * LOG2E))
             w = (e * (1.0 / jnp.sum(e, axis=-1, keepdims=True))).astype(jnp.bfloat16)
             if step == 0:
-                for c in copies[1 + n_s + len(k_parts) :]:
+                for c in copies[1 + n_s + n_half :]:
                     c.wait()
             for g, (r, listed) in enumerate(zip(rows, at)):
                 v = jnp.concatenate([v_vm[pl.ds(a, BLK), :] for a in listed], axis=0)
@@ -367,33 +450,29 @@
     c, z = lax.axis_index("ctx"), lax.axis_index("ulys")
     table = key_table(rand_blocks, c // 2, z, n_u, T // BLK)
 
-    early = False
     bundles = [[(1, h + 1), (2, h + 1), (0, h)] for h in range(hp - 1)] + [[(0, hp - 1)]]
-    parts = pack_first([keys, values], n_u, early)
-    here = send_all(parts, n_c, n_u, 1)
-    packed = pack_rest([queries, keys, values], bundles, n_u, here[2])
-    q_of, kv, near, after = [], [], None, [table]
+    *parts, mine, others = pack_first([keys, values], n_u, hp)
+    along = [lax.ppermute(x, "ulys", [(i, (i + d) % n_u) for i in range(n_u)]) for d, x in enumerate(parts, 1)]
+    joined = join(mine, swap_core(others, n_c), hp)
+    packed = pack_rest([queries, keys, values], bundles, n_u, joined)
+    near, rounds = gather_whole(joined, n_c)
+    blocks = [*along, swap_core(for_other(along), n_c)]
+    q_of, far, after = [], [], [table]
     for h in range(hp):
-        rest = early and h == 1
-        *blocks, ready = stage(here, packed[h], n_u, int(rest), after)
+        if h == 0:
+            first, second = stage(blocks, None, n_u, after)
+            ready = release(packed[0], [*along, *rounds])
+        else:
+            first, second, ready = stage([here], packed[h], n_u, after)
         here = to_shares(ready, n_c, n_u)
         q_of.append((here, len(bundles[h]) - 1))
-        gathered = gather_chips(blocks[0], blocks[1], n_c)
-        kv.append(
-            [
-                [[(near[i][t], 0), (x, 2 * T)] if rest else [(x, 0)] for t, x in enumerate(side)]
-                for i, side in enumerate(gathered)
-            ]
-        )
-        after = [x for side in gathered for x in side[1:]]
-        if len(blocks) > 2:
-            near = gather_chips(blocks[2], blocks[3], n_c)
-            after += [x for side in near for x in side[1:]]
+        far.append(gather_chips(first, second, n_c))
+        after = [x for side in far[-1] for x in side[1:]]
 
     total = None
     for h in range(hp):
         last = h == hp - 1
-        parts = attend(table, *q_of[h], *kv[h], n_u, last)
+        parts = attend(table, *q_of[h], h, near, far[h], n_u, last)
         parts = send_all(parts, n_c, n_u, -1) if last else to_shares(parts[0], n_c, n_u)
         total = project(parts, out_weight, h, n_u, hp, total)
     return total

time: 141 us -> 136 us (0.965)
  waiting for transfers between devices: 58.4 us -> 51.7 us
    ppermute x14 -> x7, starting transfers between devices: 17.5 us -> 6.2 us  [send(): return lax.ppermute(x, ('ctx', 'ulys'), pairs)]
    ppermute x12 -> x16, waiting for transfers between devices: 46.3 us -> 36.5 us  [swap_chip(): return lax.ppermute(x, 'ctx', [(i, i ^ 2 * bit) for i in range(n_c)])]
    ppermute x14 -> x7, waiting for transfers between devices: 12.1 us -> 4.87 us  [send(): return lax.ppermute(x, ('ctx', 'ulys'), pairs)]
    ppermute x12 -> x16, starting transfers between devices: 13.1 us -> 20.2 us  [swap_chip(): return lax.ppermute(x, 'ctx', [(i, i ^ 2 * bit) for i in range(n_c)])]
    ppermute x0 -> x5, starting transfers between devices: none -> 6.61 us  [the longest x3 5.53 us: shards(): lax.ppermute(x, 'ulys', [(i, (i + d) % n_u) for i in range(n_u)])]
    all_to_all x3, waiting for transfers between devices: 0.01 us -> 5.83 us  [to_shares(): lax.all_to_all(x, ('ctx', 'ulys'), split_axis=0, concat_axis=0, tiled=Tru...]
    ppermute x0 -> x5, waiting for transfers between devices: none -> 4.58 us  [the longest x3 3.06 us: shards(): lax.ppermute(x, 'ulys', [(i, (i + d) % n_u) for i in range(n_u)])]
    all_to_all x3, starting transfers between devices: 17.8 us -> 15.5 us  [to_shares(): lax.all_to_all(x, ('ctx', 'ulys'), split_axis=0, concat_axis=0, tiled=Tru...]
  transfers between devices with their start and end apart: 29 -> 31, of which waited for: 10 -> 14; matrix products, arithmetic and copies ran while one was open for 1% -> 1% of each run, Pallas kernels for 13% -> 15%
where the time goes in v7:
time: 136 us; the launch traced here: 134 us
  waiting for transfers between devices  51.7 us (38%)
  starting transfers between devices  48.5 us (36%)
  Pallas kernels  30.4 us (22%)
  local copies, waits for them, and re-layouts  2.72 us (2%)
    ppermute x16, waiting for transfers between devices, swap_chip(): return lax.ppermute(x, 'ctx', [(i, i ^ 2 * bit) for i in range(n_c)])  36.5 us
    ppermute x16, starting transfers between devices, swap_chip(): return lax.ppermute(x, 'ctx', [(i, i ^ 2 * bit) for i in range(n_c)])  20.2 us
    all_to_all x3, starting transfers between devices, to_shares(): lax.all_to_all(x, ('ctx', 'ulys'), split_axis=0, concat_axis=0, tiled=Tru...  15.5 us
    pallas_call x2, Pallas kernels, project(): pl.pallas_call(body, out_shape=jax.ShapeDtypeStruct((T, width), jnp.bfloa...  10.9 us
    pallas_call x2, Pallas kernels, attend(): pl.pallas_call(body, out_shape=[jax.ShapeDtypeStruct((T, DH) if apart els...  10.9 us
    ppermute x7, starting transfers between devices, send(): return lax.ppermute(x, ('ctx', 'ulys'), pairs)  6.2 us
    all_to_all x3, waiting for transfers between devices, to_shares(): lax.all_to_all(x, ('ctx', 'ulys'), split_axis=0, concat_axis=0, tiled=Tru...  5.83 us
    ppermute x3, starting transfers between devices, shards(): lax.ppermute(x, 'ulys', [(i, (i + d) % n_u) for i in range(n_u)])  5.53 us
  transfers between devices with their start and end apart: 31, of which 14 were waited for; matrix products, arithmetic and copies ran while one was open for 1% of the time, Pallas kernels for 15%

profile of v7, /device:TPU:0, one launch (start us, length us, event | category | flops | bytes accessed | tf_op | source)
XLA Modules:
  0.0 134.2 jit_solution(3658477323477014417)
XLA Ops:
  0.0 1.9 %pack_first.1 = (bf16[2,2,256,128]{3,2,1,0:T(8,128)(2,1)S(1)}, bf16[2,2,256,128]{3,2,1,0:T(8,128)(2,1)S(1)}, bf16[2,2,256,128]{3,2,1,0:T(8,128)(2,1)S(1)}, bf16[...) custom-call(bf16[256,2048]{1,0:T(8,128)(2,1)} %refs_1_.4, bf16[256,2048]{1,0:T(8,128)(2,1)} %refs_2_.1), custom_call_target="tpu_custom_call" | custom-call | flops 2300000000 | tf_op jit(solution)/shard_map/pack_first/pallas_call | solution.py:71
  4.4 3.0 %collective-permute-start.5 = (bf16[2048,128]{1,0:T(8,128)(2,1)S(1)}, bf16[2048,128]{1,0:T(8,128)(2,1)S(1)}, u32[]{:S(2)}, u32[]{:S(2)}) collective-permute-start(bf16[2048,128]{1,0:T(8,128)(2,1)S(1)} %join.1.refs_3_.refs_1_.refs_9_), channel_id=1, source_target_pairs={{0,16},{4,20},{8,24},{12,28},{16,0},{20,4},{24,8},{28,12},{1,17},{... | collective-permute-start | bytes 1572872 | tf_op jit(solution)/shard_map/ppermute | solution.py:239
  7.3 1.5 %collective-permute-start.4 = (bf16[2048,128]{1,0:T(8,128)(2,1)S(1)}, bf16[2048,128]{1,0:T(8,128)(2,1)S(1)}, u32[]{:S(2)}, u32[]{:S(2)}) collective-permute-start(bf16[2048,128]{1,0:T(8,128)(2,1)S(1)} %join.1.refs_3_.refs_1_.refs_9_), channel_id=1, source_target_pairs={{0,8},{4,12},{8,0},{12,4},{16,24},{20,28},{24,16},{28,20},{1,9},{5... | collective-permute-start | bytes 1572872 | tf_op jit(solution)/shard_map/ppermute | solution.py:239
  8.8 1.6 %collective-permute-start.1 = (bf16[2,2,256,128]{3,2,1,0:T(8,128)(2,1)S(1)}, bf16[2,2,256,128]{3,2,1,0:T(8,128)(2,1)S(1)}, u32[]{:S(2)}, u32[]{:S(2)}) collective-permute-start(bf16[2,2,256,128]{3,2,1,0:T(8,128)(2,1)S(1)} %get-tuple-element.28), channel_id=1, source_target_pairs={{0,1},{1,2},{2,3},{3,0},{4,5},{5,6},{6,7},{7,4},{8,9},{9,10},{10,1... | collective-permute-start | bytes 786440 | tf_op jit(solution)/shard_map/ppermute | solution.py:455
  10.4 2.6 %collective-permute-start.2 = (bf16[2,2,256,128]{3,2,1,0:T(8,128)(2,1)S(1)}, bf16[2,2,256,128]{3,2,1,0:T(8,128)(2,1)S(1)}, u32[]{:S(2)}, u32[]{:S(2)}) collective-permute-start(bf16[2,2,256,128]{3,2,1,0:T(8,128)(2,1)S(1)} %get-tuple-element.29), channel_id=1, source_target_pairs={{0,2},{1,3},{2,0},{3,1},{4,6},{5,7},{6,4},{7,5},{8,10},{9,11},{10,... | collective-permute-start | bytes 786440 | tf_op jit(solution)/shard_map/ppermute | solution.py:455
  14.3 5.2 %collective-permute-done.5.refs_5_.refs_13_ = bf16[2048,128]{1,0:T(8,128)(2,1)S(1)} collective-permute-done((bf16[2048,128]{1,0:T(8,128)(2,1)S(1)}, bf16[2048,128]{1,0:T(8,128)(2,1)S(1)}, u32[]{:S(2)}, u32[]{:S(2)}) %collective-permute-start.5) | collective-permute-done | bytes 524320 | tf_op jit(solution)/shard_map/ppermute | solution.py:239
  19.6 1.8 %collective-permute-start.6 = (bf16[1024,128]{1,0:T(8,128)(2,1)S(1)}, bf16[1024,128]{1,0:T(8,128)(2,1)S(1)}, u32[]{:S(2)}, u32[]{:S(2)}) collective-permute-start(bf16[1024,128]{1,0:T(8,128)(2,1)S(1)} %slice.10), channel_id=1, source_target_pairs={{0,8},{4,12},{8,0},{12,4},{16,24},{20,28},{24,16},{28,20},{1,9},{5... | collective-permute-start | bytes 786440 | tf_op jit(solution)/shard_map/ppermute | solution.py:239
  21.4 1.6 %collective-permute-start.7 = (bf16[1024,128]{1,0:T(8,128)(2,1)S(1)}, bf16[1024,128]{1,0:T(8,128)(2,1)S(1)}, u32[]{:S(2)}, u32[]{:S(2)}) collective-permute-start(bf16[1024,128]{1,0:T(8,128)(2,1)S(1)} %slice.11), channel_id=1, source_target_pairs={{0,16},{4,20},{8,24},{12,28},{16,0},{20,4},{24,8},{28,12},{1,17},{... | collective-permute-start | bytes 786440 | tf_op jit(solution)/shard_map/ppermute | solution.py:239
  23.0 3.0 %pack_rest.1 = (bf16[8,3,256,128]{3,2,1,0:T(8,128)(2,1)}, bf16[8,1,256,128]{3,2,1,0:T(8,128)(2,1)S(1)}) custom-call(bf16[256,2048]{1,0:T(8,128)(2,1)} %refs_0_.3, bf16[256,2048]{1,0:T(8,128)(2,1)} %refs_1_.4, bf16[256,2048]{1,0:T(8,128)(2,1)} %refs_2_.1, bf16[2048,128]{1,0:T(8,128)(2,1)S(1)} %join.1.refs_3_.refs_1_.refs_9_), custom_call_target="tpu_custom_call" | custom-call | flops 3449999872 | tf_op jit(solution)/shard_map/pack_rest/pallas_call | solution.py:165
  26.8 3.1 %collective-permute-done.2.refs_2_.refs_1_ = bf16[2,2,256,128]{3,2,1,0:T(8,128)(2,1)S(1)} collective-permute-done((bf16[2,2,256,128]{3,2,1,0:T(8,128)(2,1)S(1)}, bf16[2,2,256,128]{3,2,1,0:T(8,128)(2,1)S(1)}, u32[]{:S(2)}, u32[]{:S(2)}) %collective-permute-start.2) | collective-permute-done | bytes 262176 | tf_op jit(solution)/shard_map/ppermute | solution.py:455
  30.8 8.5 %all-to-all-start = ((bf16[8,3,256,128]{3,2,1,0:T(8,128)(2,1)}), bf16[8,3,256,128]{3,2,1,0:T(8,128)(2,1)}, u32[]{:S(2)}, u32[]{:S(2)}) async-start(bf16[8,3,256,128]{3,2,1,0:T(8,128)(2,1)} %release.1), calls=%async_computation | async-start | bytes 3145728 | tf_op jit(solution)/shard_map/all_to_all | solution.py:218
  44.3 1.5 %collective-permute-start.9 = (bf16[1536,128]{1,0:T(8,128)(2,1)S(1)}, bf16[1536,128]{1,0:T(8,128)(2,1)S(1)}, u32[]{:S(2)}, u32[]{:S(2)}) collective-permute-start(bf16[1536,128]{1,0:T(8,128)(2,1)S(1)} %get-tuple-element.32.refs_2_), channel_id=1, source_target_pairs={{0,8},{4,12},{8,0},{12,4},{16,24},{20,28},{24,16},{28,20},{1,9},{5... | collective-permute-start | bytes 1179656 | tf_op jit(solution)/shard_map/ppermute | solution.py:239
  45.8 1.5 %collective-permute-start.13 = (bf16[1536,128]{1,0:T(8,128)(2,1)S(1)}, bf16[1536,128]{1,0:T(8,128)(2,1)S(1)}, u32[]{:S(2)}, u32[]{:S(2)}) collective-permute-start(bf16[1536,128]{1,0:T(8,128)(2,1)S(1)} %get-tuple-element.33.refs_10_), channel_id=1, source_target_pairs={{0,16},{4,20},{8,24},{12,28},{16,0},{20,4},{24,8},{28,12},{1,17},{... | collective-permute-start | bytes 1179656 | tf_op jit(solution)/shard_map/ppermute | solution.py:239
  47.3 7.9 %collective-permute-done.10.refs_3_.refs_6_ = bf16[1536,128]{1,0:T(8,128)(2,1)S(1)} collective-permute-done((bf16[1536,128]{1,0:T(8,128)(2,1)S(1)}, bf16[1536,128]{1,0:T(8,128)(2,1)S(1)}, u32[]{:S(2)}, u32[]{:S(2)}) %collective-permute-start.10) | collective-permute-done | bytes 393248 | tf_op jit(solution)/shard_map/ppermute | solution.py:239
  55.7 1.5 %collective-permute-start.14 = (bf16[1536,128]{1,0:T(8,128)(2,1)S(1)}, bf16[1536,128]{1,0:T(8,128)(2,1)S(1)}, u32[]{:S(2)}, u32[]{:S(2)}) collective-permute-start(bf16[1536,128]{1,0:T(8,128)(2,1)S(1)} %collective-permute-done.12.refs_5_.refs_12_), channel_id=1, source_target_pairs={{0,16},{4,20},{8,24},{12,28},{16,0},{20,4},{24,8},{28,12},{1,17},{... | collective-permute-start | bytes 1179656 | tf_op jit(solution)/shard_map/ppermute | solution.py:239
  57.2 6.9 %collective-permute-done.9.refs_2_.refs_4_ = bf16[1536,128]{1,0:T(8,128)(2,1)S(1)} collective-permute-done((bf16[1536,128]{1,0:T(8,128)(2,1)S(1)}, bf16[1536,128]{1,0:T(8,128)(2,1)S(1)}, u32[]{:S(2)}, u32[]{:S(2)}) %collective-permute-start.9) | collective-permute-done | bytes 393248 | tf_op jit(solution)/shard_map/ppermute | solution.py:239
  64.1 7.6 %collective-permute-done.11.refs_4_.refs_8_ = bf16[1536,128]{1,0:T(8,128)(2,1)S(1)} collective-permute-done((bf16[1536,128]{1,0:T(8,128)(2,1)S(1)}, bf16[1536,128]{1,0:T(8,128)(2,1)S(1)}, u32[]{:S(2)}, u32[]{:S(2)}) %collective-permute-start.11) | collective-permute-done | bytes 393248 | tf_op jit(solution)/shard_map/ppermute | solution.py:239
  71.7 5.6 %all-to-all-done.refs_0_ = bf16[8,3,256,128]{3,2,1,0:T(8,128)(2,1)} async-done(((bf16[8,3,256,128]{3,2,1,0:T(8,128)(2,1)}), bf16[8,3,256,128]{3,2,1,0:T(8,128)(2,1)}, u32[]{:S(2)}, u32[]{:S(2)}) %all-to-all-start) | async-done | bytes 1572896 | tf_op jit(solution)/shard_map/all_to_all | solution.py:218
  79.7 3.5 %all-to-all-start.1 = ((bf16[8,1,256,128]{3,2,1,0:T(8,128)(2,1)}), bf16[8,1,256,128]{3,2,1,0:T(8,128)(2,1)S(1)}, u32[]{:S(2)}, u32[]{:S(2)}) async-start(bf16[8,1,256,128]{3,2,1,0:T(8,128)(2,1)} %get-tuple-element.34), calls=%async_computation.1 | async-start | bytes 1048576 | tf_op jit(solution)/shard_map/all_to_all | solution.py:218
  83.2 1.6 %collective-permute-start.15 = (bf16[1536,128]{1,0:T(8,128)(2,1)S(1)}, bf16[1536,128]{1,0:T(8,128)(2,1)S(1)}, u32[]{:S(2)}, u32[]{:S(2)}) collective-permute-start(bf16[1536,128]{1,0:T(8,128)(2,1)S(1)} %get-tuple-element.35.refs_2_), channel_id=1, source_target_pairs={{0,8},{4,12},{8,0},{12,4},{16,24},{20,28},{24,16},{28,20},{1,9},{5... | collective-permute-start | bytes 1179656 | tf_op jit(solution)/shard_map/ppermute | solution.py:239
  84.8 1.5 %collective-permute-start.19 = (bf16[1536,128]{1,0:T(8,128)(2,1)S(1)}, bf16[1536,128]{1,0:T(8,128)(2,1)S(1)}, u32[]{:S(2)}, u32[]{:S(2)}) collective-permute-start(bf16[1536,128]{1,0:T(8,128)(2,1)S(1)} %get-tuple-element.36.refs_10_), channel_id=1, source_target_pairs={{0,16},{4,20},{8,24},{12,28},{16,0},{20,4},{24,8},{28,12},{1,17},{... | collective-permute-start | bytes 1179656 | tf_op jit(solution)/shard_map/ppermute | solution.py:239
  86.3 4.4 %collective-permute-done.16.refs_6_ = bf16[1536,128]{1,0:T(8,128)(2,1)S(1)} collective-permute-done((bf16[1536,128]{1,0:T(8,128)(2,1)S(1)}, bf16[1536,128]{1,0:T(8,128)(2,1)S(1)}, u32[]{:S(2)}, u32[]{:S(2)}) %collective-permute-start.16) | collective-permute-done | bytes 393248 | tf_op jit(solution)/shard_map/ppermute | solution.py:239
  91.3 1.5 %collective-permute-start.20 = (bf16[1536,128]{1,0:T(8,128)(2,1)S(1)}, bf16[1536,128]{1,0:T(8,128)(2,1)}, u32[]{:S(2)}, u32[]{:S(2)}) collective-permute-start(bf16[1536,128]{1,0:T(8,128)(2,1)S(1)} %collective-permute-done.18.refs_12_), channel_id=1, source_target_pairs={{0,16},{4,20},{8,24},{12,28},{16,0},{20,4},{24,8},{28,12},{1,17},{... | collective-permute-start | bytes 1179656 | tf_op jit(solution)/shard_map/ppermute | solution.py:239
  92.8 5.4 %attend.3 = bf16[8,256,128]{2,1,0:T(8,128)(2,1)} custom-call(s32[32,8]{1,0:T(8,128)} %copy-done.7, bf16[8,3,256,128]{3,2,1,0:T(8,128)(2,1)} %all-to-all-done.refs_0_, bf16[2048,128]{1,0:T(8,128)(2,1)} %copy-done.8, bf16[1536,128]{1,0:T(8,128)(2,1)} %copy-done.9, bf16[2048,128]{1,0:T(8,128)(2,1)} %copy-done.18, bf16[1536,128]{1,0:T(8,128)(2,1)} %copy-done.14, ...), custom_call_target="tpu_custom_call" | custom-call | flops 9200000000 | tf_op jit(solution)/shard_map/attend/pallas_call | solution.py:345
  98.5 3.5 %all-to-all-start.2 = ((bf16[8,256,128]{2,1,0:T(8,128)(2,1)}), bf16[8,256,128]{2,1,0:T(8,128)(2,1)S(1)}, u32[]{:S(2)}, u32[]{:S(2)}) async-start(bf16[8,256,128]{2,1,0:T(8,128)(2,1)} %attend.3), calls=%async_computation.2 | async-start | bytes 1048576 | tf_op jit(solution)/shard_map/all_to_all | solution.py:218
  102.1 4.5 %collective-permute-done.17.refs_8_ = bf16[1536,128]{1,0:T(8,128)(2,1)} collective-permute-done((bf16[1536,128]{1,0:T(8,128)(2,1)S(1)}, bf16[1536,128]{1,0:T(8,128)(2,1)}, u32[]{:S(2)}, u32[]{:S(2)}) %collective-permute-start.17) | collective-permute-done | bytes 393248 | tf_op jit(solution)/shard_map/ppermute | solution.py:239
  106.6 5.5 %attend.2 = (bf16[256,128]{1,0:T(8,128)(2,1)}, bf16[256,128]{1,0:T(8,128)(2,1)}, bf16[256,128]{1,0:T(8,128)(2,1)}, bf16[256,128]{1,0:T(8,128)(2,1)}, bf16[256,12...) custom-call(s32[32,8]{1,0:T(8,128)} %copy-done.7, ...), custom_call_target="tpu_custom_call" | custom-call | flops 9200000000 | tf_op jit(solution)/shard_map/attend/pallas_call | solution.py:345
  112.1 1.7 %collective-permute-start.22 = (bf16[256,128]{1,0:T(8,128)(2,1)}, bf16[256,128]{1,0:T(8,128)(2,1)S(1)}, u32[]{:S(2)}, u32[]{:S(2)}) collective-permute-start(bf16[256,128]{1,0:T(8,128)(2,1)} %get-tuple-element.39), channel_id=1, source_target_pairs={{0,3},{1,0},{2,1},{3,2},{4,7},{5,4},{6,5},{7,6},{8,11},{9,8},{10,9... | collective-permute-start | bytes 196616 | tf_op jit(solution)/shard_map/ppermute | solution.py:227
  116.4 1.8 %collective-permute-start.26 = (bf16[256,128]{1,0:T(8,128)(2,1)}, bf16[256,128]{1,0:T(8,128)(2,1)S(1)}, u32[]{:S(2)}, u32[]{:S(2)}) collective-permute-start(bf16[256,128]{1,0:T(8,128)(2,1)} %get-tuple-element.43), channel_id=1, source_target_pairs={{0,1},{1,2},{2,3},{3,0},{4,5},{5,6},{6,7},{7,4},{8,9},{9,10},{10,1... | collective-permute-start | bytes 196616 | tf_op jit(solution)/shard_map/ppermute | solution.py:227
  118.8 5.0 %project.2.refs_9_ = f32[256,4096]{1,0:T(8,128)S(1)} custom-call(bf16[8,256,128]{2,1,0:T(8,128)(2,1)S(1)} %all-to-all-done.2.refs_0_, bf16[2048,4096]{1,0:T(8,128)(2,1)} %refs_8_.1), custom_call_target="tpu_custom_call" | custom-call | flops 8049999872 | tf_op jit(solution)/shard_map/project/pallas_call | solution.py:413
  123.8 3.8 %collective-permute-done.24.refs_4_ = bf16[256,128]{1,0:T(8,128)(2,1)S(1)} collective-permute-done((bf16[256,128]{1,0:T(8,128)(2,1)}, bf16[256,128]{1,0:T(8,128)(2,1)S(1)}, u32[]{:S(2)}, u32[]{:S(2)}) %collective-permute-start.24) | collective-permute-done | bytes 65568 | tf_op jit(solution)/shard_map/ppermute | solution.py:227
  128.1 6.0 %project.3 = bf16[256,4096]{1,0:T(8,128)(2,1)} custom-call(bf16[256,128]{1,0:T(8,128)(2,1)S(1)} %copy-done.16, bf16[256,128]{1,0:T(8,128)(2,1)S(1)} %collective-permute-done.21.refs_1_, bf16[256,128]{1,0:T(8,128)(2,1)S(1)} %collective-permute-done.22.refs_2_, bf16[256,128]{1,0:T(8,128)(2,1)S(1)} %collective-permute-done.23.refs_3_, ...), custom_call_target="tpu_custom_call" | custom-call | flops 8049999872 | tf_op jit(solution)/shard_map/project/pallas_call | solution.py:413
  (114 shorter events, 17.9 us)
Async XLA Ops:
  1.9 1.7 %collective-permute-start = (bf16[4,256,128]{2,1,0:T(8,128)(2,1)S(1)}, bf16[4,256,128]{2,1,0:T(8,128)(2,1)S(1)}, u32[]{:S(2)}, u32[]{:S(2)}) collective-permute-start(bf16[4,256,128]{2,1,0:T(8,128)(2,1)S(1)} %get-tuple-element.26), channel_id=1, source_target_pairs={{0,4},{4,0},{8,12},{12,8},{16,20},{20,16},{24,28},{28,24},{1,5},{5... | collective-permute-start | bytes 786440 | tf_op jit(solution)/shard_map/ppermute | solution.py:235
  4.4 15.2 %collective-permute-start.5 = (bf16[2048,128]{1,0:T(8,128)(2,1)S(1)}, bf16[2048,128]{1,0:T(8,128)(2,1)S(1)}, u32[]{:S(2)}, u32[]{:S(2)}) collective-permute-start(bf16[2048,128]{1,0:T(8,128)(2,1)S(1)} %join.1.refs_3_.refs_1_.refs_9_), channel_id=1, source_target_pairs={{0,16},{4,20},{8,24},{12,28},{16,0},{20,4},{24,8},{28,12},{1,17},{... | collective-permute-start | bytes 1572872 | tf_op jit(solution)/shard_map/ppermute | solution.py:239
  7.3 14.0 %collective-permute-start.4 = (bf16[2048,128]{1,0:T(8,128)(2,1)S(1)}, bf16[2048,128]{1,0:T(8,128)(2,1)S(1)}, u32[]{:S(2)}, u32[]{:S(2)}) collective-permute-start(bf16[2048,128]{1,0:T(8,128)(2,1)S(1)} %join.1.refs_3_.refs_1_.refs_9_), channel_id=1, source_target_pairs={{0,8},{4,12},{8,0},{12,4},{16,24},{20,28},{24,16},{28,20},{1,9},{5... | collective-permute-start | bytes 1572872 | tf_op jit(solution)/shard_map/ppermute | solution.py:239
  8.8 18.0 %collective-permute-start.1 = (bf16[2,2,256,128]{3,2,1,0:T(8,128)(2,1)S(1)}, bf16[2,2,256,128]{3,2,1,0:T(8,128)(2,1)S(1)}, u32[]{:S(2)}, u32[]{:S(2)}) collective-permute-start(bf16[2,2,256,128]{3,2,1,0:T(8,128)(2,1)S(1)} %get-tuple-element.28), channel_id=1, source_target_pairs={{0,1},{1,2},{2,3},{3,0},{4,5},{5,6},{6,7},{7,4},{8,9},{9,10},{10,1... | collective-permute-start | bytes 786440 | tf_op jit(solution)/shard_map/ppermute | solution.py:455
  10.4 19.4 %collective-permute-start.2 = (bf16[2,2,256,128]{3,2,1,0:T(8,128)(2,1)S(1)}, bf16[2,2,256,128]{3,2,1,0:T(8,128)(2,1)S(1)}, u32[]{:S(2)}, u32[]{:S(2)}) collective-permute-start(bf16[2,2,256,128]{3,2,1,0:T(8,128)(2,1)S(1)} %get-tuple-element.29), channel_id=1, source_target_pairs={{0,2},{1,3},{2,0},{3,1},{4,6},{5,7},{6,4},{7,5},{8,10},{9,11},{10,... | collective-permute-start | bytes 786440 | tf_op jit(solution)/shard_map/ppermute | solution.py:455
  13.0 16.9 %collective-permute-start.3 = (bf16[2,2,256,128]{3,2,1,0:T(8,128)(2,1)S(1)}, bf16[2,2,256,128]{3,2,1,0:T(8,128)(2,1)S(1)}, u32[]{:S(2)}, u32[]{:S(2)}) collective-permute-start(bf16[2,2,256,128]{3,2,1,0:T(8,128)(2,1)S(1)} %get-tuple-element.30), channel_id=1, source_target_pairs={{0,3},{1,0},{2,1},{3,2},{4,7},{5,4},{6,5},{7,6},{8,11},{9,8},{10,9... | collective-permute-start | bytes 786440 | tf_op jit(solution)/shard_map/ppermute | solution.py:455
  19.6 10.3 %collective-permute-start.6 = (bf16[1024,128]{1,0:T(8,128)(2,1)S(1)}, bf16[1024,128]{1,0:T(8,128)(2,1)S(1)}, u32[]{:S(2)}, u32[]{:S(2)}) collective-permute-start(bf16[1024,128]{1,0:T(8,128)(2,1)S(1)} %slice.10), channel_id=1, source_target_pairs={{0,8},{4,12},{8,0},{12,4},{16,24},{20,28},{24,16},{28,20},{1,9},{5... | collective-permute-start | bytes 786440 | tf_op jit(solution)/shard_map/ppermute | solution.py:239
  21.4 8.5 %collective-permute-start.7 = (bf16[1024,128]{1,0:T(8,128)(2,1)S(1)}, bf16[1024,128]{1,0:T(8,128)(2,1)S(1)}, u32[]{:S(2)}, u32[]{:S(2)}) collective-permute-start(bf16[1024,128]{1,0:T(8,128)(2,1)S(1)} %slice.11), channel_id=1, source_target_pairs={{0,16},{4,20},{8,24},{12,28},{16,0},{20,4},{24,8},{28,12},{1,17},{... | collective-permute-start | bytes 786440 | tf_op jit(solution)/shard_map/ppermute | solution.py:239
  30.8 46.5 %all-to-all-start = ((bf16[8,3,256,128]{3,2,1,0:T(8,128)(2,1)}), bf16[8,3,256,128]{3,2,1,0:T(8,128)(2,1)}, u32[]{:S(2)}, u32[]{:S(2)}) async-start(bf16[8,3,256,128]{3,2,1,0:T(8,128)(2,1)} %release.1), calls=%async_computation | async-start | bytes 3145728 | tf_op jit(solution)/shard_map/all_to_all | solution.py:218
  40.1 1.9 %collective-permute-start.8 = (bf16[3,2,256,128]{3,2,1,0:T(8,128)(2,1)S(1)}, bf16[3,2,256,128]{3,2,1,0:T(8,128)(2,1)S(1)}, u32[]{:S(2)}, u32[]{:S(2)}) collective-permute-start(bf16[3,2,256,128]{3,2,1,0:T(8,128)(2,1)S(1)} %for_other.1), channel_id=1, source_target_pairs={{0,4},{4,0},{8,12},{12,8},{16,20},{20,16},{24,28},{28,24},{1,5},{5... | collective-permute-start | bytes 1179656 | tf_op jit(solution)/shard_map/ppermute | solution.py:235
  43.1 35.4 %copy-start.9 = (bf16[1536,128]{1,0:T(8,128)(2,1)}, bf16[1536,128]{1,0:T(8,128)(2,1)S(1)}, u32[]{:S(2)}) copy-start(bf16[1536,128]{1,0:T(8,128)(2,1)S(1)} %get-tuple-element.32.refs_2_) | copy-start | bytes 1179652
  43.1 12.0 %collective-permute-start.10 = (bf16[1536,128]{1,0:T(8,128)(2,1)S(1)}, bf16[1536,128]{1,0:T(8,128)(2,1)S(1)}, u32[]{:S(2)}, u32[]{:S(2)}) collective-permute-start(bf16[1536,128]{1,0:T(8,128)(2,1)S(1)} %get-tuple-element.32.refs_2_), channel_id=1, source_target_pairs={{0,16},{4,20},{8,24},{12,28},{16,0},{20,4},{24,8},{28,12},{1,17},{... | collective-permute-start | bytes 1179656 | tf_op jit(solution)/shard_map/ppermute | solution.py:239
  43.7 12.0 %collective-permute-start.12 = (bf16[1536,128]{1,0:T(8,128)(2,1)S(1)}, bf16[1536,128]{1,0:T(8,128)(2,1)S(1)}, u32[]{:S(2)}, u32[]{:S(2)}) collective-permute-start(bf16[1536,128]{1,0:T(8,128)(2,1)S(1)} %get-tuple-element.33.refs_10_), channel_id=1, source_target_pairs={{0,8},{4,12},{8,0},{12,4},{16,24},{20,28},{24,16},{28,20},{1,9},{5... | collective-permute-start | bytes 1179656 | tf_op jit(solution)/shard_map/ppermute | solution.py:239
  44.3 19.9 %collective-permute-start.9 = (bf16[1536,128]{1,0:T(8,128)(2,1)S(1)}, bf16[1536,128]{1,0:T(8,128)(2,1)S(1)}, u32[]{:S(2)}, u32[]{:S(2)}) collective-permute-start(bf16[1536,128]{1,0:T(8,128)(2,1)S(1)} %get-tuple-element.32.refs_2_), channel_id=1, source_target_pairs={{0,8},{4,12},{8,0},{12,4},{16,24},{20,28},{24,16},{28,20},{1,9},{5... | collective-permute-start | bytes 1179656 | tf_op jit(solution)/shard_map/ppermute | solution.py:239
  45.8 18.4 %collective-permute-start.13 = (bf16[1536,128]{1,0:T(8,128)(2,1)S(1)}, bf16[1536,128]{1,0:T(8,128)(2,1)S(1)}, u32[]{:S(2)}, u32[]{:S(2)}) collective-permute-start(bf16[1536,128]{1,0:T(8,128)(2,1)S(1)} %get-tuple-element.33.refs_10_), channel_id=1, source_target_pairs={{0,16},{4,20},{8,24},{12,28},{16,0},{20,4},{24,8},{28,12},{1,17},{... | collective-permute-start | bytes 1179656 | tf_op jit(solution)/shard_map/ppermute | solution.py:239
  55.2 16.5 %collective-permute-start.11 = (bf16[1536,128]{1,0:T(8,128)(2,1)S(1)}, bf16[1536,128]{1,0:T(8,128)(2,1)S(1)}, u32[]{:S(2)}, u32[]{:S(2)}) collective-permute-start(bf16[1536,128]{1,0:T(8,128)(2,1)S(1)} %collective-permute-done.10.refs_3_.refs_6_), channel_id=1, source_target_pairs={{0,8},{4,12},{8,0},{12,4},{16,24},{20,28},{24,16},{28,20},{1,9},{5... | collective-permute-start | bytes 1179656 | tf_op jit(solution)/shard_map/ppermute | solution.py:239
  55.7 16.0 %collective-permute-start.14 = (bf16[1536,128]{1,0:T(8,128)(2,1)S(1)}, bf16[1536,128]{1,0:T(8,128)(2,1)S(1)}, u32[]{:S(2)}, u32[]{:S(2)}) collective-permute-start(bf16[1536,128]{1,0:T(8,128)(2,1)S(1)} %collective-permute-done.12.refs_5_.refs_12_), channel_id=1, source_target_pairs={{0,16},{4,20},{8,24},{12,28},{16,0},{20,4},{24,8},{28,12},{1,17},{... | collective-permute-start | bytes 1179656 | tf_op jit(solution)/shard_map/ppermute | solution.py:239
  78.6 12.1 %collective-permute-start.16 = (bf16[1536,128]{1,0:T(8,128)(2,1)S(1)}, bf16[1536,128]{1,0:T(8,128)(2,1)S(1)}, u32[]{:S(2)}, u32[]{:S(2)}) collective-permute-start(bf16[1536,128]{1,0:T(8,128)(2,1)S(1)} %get-tuple-element.35.refs_2_), channel_id=1, source_target_pairs={{0,16},{4,20},{8,24},{12,28},{16,0},{20,4},{24,8},{28,12},{1,17},{... | collective-permute-start | bytes 1179656 | tf_op jit(solution)/shard_map/ppermute | solution.py:239
  79.2 12.1 %collective-permute-start.18 = (bf16[1536,128]{1,0:T(8,128)(2,1)S(1)}, bf16[1536,128]{1,0:T(8,128)(2,1)S(1)}, u32[]{:S(2)}, u32[]{:S(2)}) collective-permute-start(bf16[1536,128]{1,0:T(8,128)(2,1)S(1)} %get-tuple-element.36.refs_10_), channel_id=1, source_target_pairs={{0,8},{4,12},{8,0},{12,4},{16,24},{20,28},{24,16},{28,20},{1,9},{5... | collective-permute-start | bytes 1179656 | tf_op jit(solution)/shard_map/ppermute | solution.py:239
  79.7 18.8 %all-to-all-start.1 = ((bf16[8,1,256,128]{3,2,1,0:T(8,128)(2,1)}), bf16[8,1,256,128]{3,2,1,0:T(8,128)(2,1)S(1)}, u32[]{:S(2)}, u32[]{:S(2)}) async-start(bf16[8,1,256,128]{3,2,1,0:T(8,128)(2,1)} %get-tuple-element.34), calls=%async_computation.1 | async-start | bytes 1048576 | tf_op jit(solution)/shard_map/all_to_all | solution.py:218
  83.2 18.8 %collective-permute-start.15 = (bf16[1536,128]{1,0:T(8,128)(2,1)S(1)}, bf16[1536,128]{1,0:T(8,128)(2,1)S(1)}, u32[]{:S(2)}, u32[]{:S(2)}) collective-permute-start(bf16[1536,128]{1,0:T(8,128)(2,1)S(1)} %get-tuple-element.35.refs_2_), channel_id=1, source_target_pairs={{0,8},{4,12},{8,0},{12,4},{16,24},{20,28},{24,16},{28,20},{1,9},{5... | collective-permute-start | bytes 1179656 | tf_op jit(solution)/shard_map/ppermute | solution.py:239
  84.8 17.2 %collective-permute-start.19 = (bf16[1536,128]{1,0:T(8,128)(2,1)S(1)}, bf16[1536,128]{1,0:T(8,128)(2,1)S(1)}, u32[]{:S(2)}, u32[]{:S(2)}) collective-permute-start(bf16[1536,128]{1,0:T(8,128)(2,1)S(1)} %get-tuple-element.36.refs_10_), channel_id=1, source_target_pairs={{0,16},{4,20},{8,24},{12,28},{16,0},{20,4},{24,8},{28,12},{1,17},{... | collective-permute-start | bytes 1179656 | tf_op jit(solution)/shard_map/ppermute | solution.py:239
  90.7 15.8 %collective-permute-start.17 = (bf16[1536,128]{1,0:T(8,128)(2,1)S(1)}, bf16[1536,128]{1,0:T(8,128)(2,1)}, u32[]{:S(2)}, u32[]{:S(2)}) collective-permute-start(bf16[1536,128]{1,0:T(8,128)(2,1)S(1)} %collective-permute-done.16.refs_6_), channel_id=1, source_target_pairs={{0,8},{4,12},{8,0},{12,4},{16,24},{20,28},{24,16},{28,20},{1,9},{5... | collective-permute-start | bytes 1179656 | tf_op jit(solution)/shard_map/ppermute | solution.py:239
  91.3 15.3 %collective-permute-start.20 = (bf16[1536,128]{1,0:T(8,128)(2,1)S(1)}, bf16[1536,128]{1,0:T(8,128)(2,1)}, u32[]{:S(2)}, u32[]{:S(2)}) collective-permute-start(bf16[1536,128]{1,0:T(8,128)(2,1)S(1)} %collective-permute-done.18.refs_12_), channel_id=1, source_target_pairs={{0,16},{4,20},{8,24},{12,28},{16,0},{20,4},{24,8},{28,12},{1,17},{... | collective-permute-start | bytes 1179656 | tf_op jit(solution)/shard_map/ppermute | solution.py:239
  98.5 20.3 %all-to-all-start.2 = ((bf16[8,256,128]{2,1,0:T(8,128)(2,1)}), bf16[8,256,128]{2,1,0:T(8,128)(2,1)S(1)}, u32[]{:S(2)}, u32[]{:S(2)}) async-start(bf16[8,256,128]{2,1,0:T(8,128)(2,1)} %attend.3), calls=%async_computation.2 | async-start | bytes 1048576 | tf_op jit(solution)/shard_map/all_to_all | solution.py:218
  112.0 4.4 %collective-permute-start.21 = (bf16[256,128]{1,0:T(8,128)(2,1)}, bf16[256,128]{1,0:T(8,128)(2,1)S(1)}, u32[]{:S(2)}, u32[]{:S(2)}) collective-permute-start(bf16[256,128]{1,0:T(8,128)(2,1)} %get-tuple-element.38), channel_id=1, source_target_pairs={{0,4},{1,5},{2,6},{3,7},{4,0},{5,1},{6,2},{7,3},{8,12},{9,13},{10,... | collective-permute-start | bytes 196616 | tf_op jit(solution)/shard_map/ppermute | solution.py:227
  112.1 6.7 %collective-permute-start.22 = (bf16[256,128]{1,0:T(8,128)(2,1)}, bf16[256,128]{1,0:T(8,128)(2,1)S(1)}, u32[]{:S(2)}, u32[]{:S(2)}) collective-permute-start(bf16[256,128]{1,0:T(8,128)(2,1)} %get-tuple-element.39), channel_id=1, source_target_pairs={{0,3},{1,0},{2,1},{3,2},{4,7},{5,4},{6,5},{7,6},{8,11},{9,8},{10,9... | collective-permute-start | bytes 196616 | tf_op jit(solution)/shard_map/ppermute | solution.py:227
  113.8 9.9 %collective-permute-start.23 = (bf16[256,128]{1,0:T(8,128)(2,1)}, bf16[256,128]{1,0:T(8,128)(2,1)S(1)}, u32[]{:S(2)}, u32[]{:S(2)}) collective-permute-start(bf16[256,128]{1,0:T(8,128)(2,1)} %get-tuple-element.40), channel_id=1, source_target_pairs={{0,7},{1,4},{2,5},{3,6},{4,3},{5,0},{6,1},{7,2},{8,15},{9,12},{10,... | collective-permute-start | bytes 196616 | tf_op jit(solution)/shard_map/ppermute | solution.py:227
  113.9 13.7 %collective-permute-start.24 = (bf16[256,128]{1,0:T(8,128)(2,1)}, bf16[256,128]{1,0:T(8,128)(2,1)S(1)}, u32[]{:S(2)}, u32[]{:S(2)}) collective-permute-start(bf16[256,128]{1,0:T(8,128)(2,1)} %get-tuple-element.41), channel_id=1, source_target_pairs={{0,2},{1,3},{2,0},{3,1},{4,6},{5,7},{6,4},{7,5},{8,10},{9,11},{10,... | collective-permute-start | bytes 196616 | tf_op jit(solution)/shard_map/ppermute | solution.py:227
  115.4 12.7 %collective-permute-start.25 = (bf16[256,128]{1,0:T(8,128)(2,1)}, bf16[256,128]{1,0:T(8,128)(2,1)S(1)}, u32[]{:S(2)}, u32[]{:S(2)}) collective-permute-start(bf16[256,128]{1,0:T(8,128)(2,1)} %get-tuple-element.42), channel_id=1, source_target_pairs={{0,6},{1,7},{2,4},{3,5},{4,2},{5,3},{6,0},{7,1},{8,14},{9,15},{10,... | collective-permute-start | bytes 196616 | tf_op jit(solution)/shard_map/ppermute | solution.py:227
  116.4 11.7 %collective-permute-start.26 = (bf16[256,128]{1,0:T(8,128)(2,1)}, bf16[256,128]{1,0:T(8,128)(2,1)S(1)}, u32[]{:S(2)}, u32[]{:S(2)}) collective-permute-start(bf16[256,128]{1,0:T(8,128)(2,1)} %get-tuple-element.43), channel_id=1, source_target_pairs={{0,1},{1,2},{2,3},{3,0},{4,5},{5,6},{6,7},{7,4},{8,9},{9,10},{10,1... | collective-permute-start | bytes 196616 | tf_op jit(solution)/shard_map/ppermute | solution.py:227
  118.8 9.3 %collective-permute-start.27 = (bf16[256,128]{1,0:T(8,128)(2,1)}, bf16[256,128]{1,0:T(8,128)(2,1)S(1)}, u32[]{:S(2)}, u32[]{:S(2)}) collective-permute-start(bf16[256,128]{1,0:T(8,128)(2,1)} %get-tuple-element.44), channel_id=1, source_target_pairs={{0,5},{1,6},{2,7},{3,4},{4,1},{5,2},{6,3},{7,0},{8,13},{9,14},{10,... | collective-permute-start | bytes 196616 | tf_op jit(solution)/shard_map/ppermute | solution.py:227
  (29 other events, 269.3 us)

commit v8 on v7

--- a/solution.py
+++ b/solution.py
@@ -98,7 +98,7 @@
         out_specs=VMEM,
         scratch_shapes=[pltpu.SemaphoreType.DMA((n,))],
         compiler_params=beside(8 * MIB),
-        cost_estimate=cost(1),
+        cost_estimate=cost(4),
         name="for_other",
     )(*parts)
 
@@ -113,7 +113,7 @@
         in_specs=[ANY] * (1 + len(after)),
         out_specs=ANY,
         input_output_aliases={0: 0},
-        compiler_params=WHOLE,
+        compiler_params=beside(8 * MIB),
         cost_estimate=cost(1),
         name="release",
     )(packed, *after)
@@ -456,18 +456,21 @@
     joined = join(mine, swap_core(others, n_c), hp)
     packed = pack_rest([queries, keys, values], bundles, n_u, joined)
     near, rounds = gather_whole(joined, n_c)
-    blocks = [*along, swap_core(for_other(along), n_c)]
+    meant = for_other(along)
+    blocks = [*along, swap_core(meant, n_c)]
     q_of, far, after = [], [], [table]
+    direct = (n_c // 2).bit_length() - 1
     for h in range(hp):
         if h == 0:
             first, second = stage(blocks, None, n_u, after)
-            ready = release(packed[0], [*along, *rounds])
+            ready = release(packed[0], [meant, *rounds[:direct]])
         else:
             first, second, ready = stage([here], packed[h], n_u, after)
         here = to_shares(ready, n_c, n_u)
         q_of.append((here, len(bundles[h]) - 1))
         far.append(gather_chips(first, second, n_c))
-        after = [x for side in far[-1] for x in side[1:]]
+        after = [x for side in far[-1] for x in side[1:]] + rounds[direct:]
+        rounds = rounds[:direct]
 
     total = None
     for h in range(hp):

time: 136 us -> 135 us (level)
  waiting for transfers between devices: 51.7 us -> 48.1 us
  starting transfers between devices: 48.5 us -> 51 us
    ppermute x16, waiting for transfers between devices: 36.5 us -> 30.7 us  [swap_chip(): return lax.ppermute(x, 'ctx', [(i, i ^ 2 * bit) for i in range(n_c)])]
    ppermute x3, waiting for transfers between devices: 3.06 us -> 8.71 us  [shards(): lax.ppermute(x, 'ulys', [(i, (i + d) % n_u) for i in range(n_u)])]
    ppermute x7, starting transfers between devices: 6.2 us -> 9.02 us  [send(): return lax.ppermute(x, ('ctx', 'ulys'), pairs)]
    ppermute x16, starting transfers between devices: 20.2 us -> 17.6 us  [swap_chip(): return lax.ppermute(x, 'ctx', [(i, i ^ 2 * bit) for i in range(n_c)])]
    all_to_all x3, waiting for transfers between devices: 5.83 us -> 3.83 us  [to_shares(): lax.all_to_all(x, ('ctx', 'ulys'), split_axis=0, concat_axis=0, tiled=Tru...]
  transfers between devices with their start and end apart: 31 -> 31, of which waited for: 14 -> 11; matrix products, arithmetic and copies ran while one was open for 1% -> 1% of each run, Pallas kernels for 15% -> 16%
where the time goes in v8:
time: 135 us; the launch traced here: 133 us
  starting transfers between devices  51 us (38%)
  waiting for transfers between devices  48.1 us (36%)
  Pallas kernels  30.4 us (23%)
  local copies, waits for them, and re-layouts  2.59 us (2%)
    ppermute x16, waiting for transfers between devices, swap_chip(): return lax.ppermute(x, 'ctx', [(i, i ^ 2 * bit) for i in range(n_c)])  30.7 us
    ppermute x16, starting transfers between devices, swap_chip(): return lax.ppermute(x, 'ctx', [(i, i ^ 2 * bit) for i in range(n_c)])  17.6 us
    all_to_all x3, starting transfers between devices, to_shares(): lax.all_to_all(x, ('ctx', 'ulys'), split_axis=0, concat_axis=0, tiled=Tru...  16.8 us
    pallas_call x2, Pallas kernels, project(): pl.pallas_call(body, out_shape=jax.ShapeDtypeStruct((T, width), jnp.bfloa...  10.9 us
    pallas_call x2, Pallas kernels, attend(): pl.pallas_call(body, out_shape=[jax.ShapeDtypeStruct((T, DH) if apart els...  10.9 us
    ppermute x7, starting transfers between devices, send(): return lax.ppermute(x, ('ctx', 'ulys'), pairs)  9.02 us
    ppermute x3, waiting for transfers between devices, shards(): lax.ppermute(x, 'ulys', [(i, (i + d) % n_u) for i in range(n_u)])  8.71 us
    ppermute x3, starting transfers between devices, shards(): lax.ppermute(x, 'ulys', [(i, (i + d) % n_u) for i in range(n_u)])  6.59 us
  transfers between devices with their start and end apart: 31, of which 11 were waited for; matrix products, arithmetic and copies ran while one was open for 1% of the time, Pallas kernels for 16%

profile of v8, /device:TPU:0, one launch (start us, length us, event | category | flops | bytes accessed | tf_op | source)
XLA Modules:
  0.0 133.0 jit_solution(7622306137090516510)
XLA Ops:
  0.0 1.9 %pack_first.1 = (bf16[2,2,256,128]{3,2,1,0:T(8,128)(2,1)S(1)}, bf16[2,2,256,128]{3,2,1,0:T(8,128)(2,1)S(1)}, bf16[2,2,256,128]{3,2,1,0:T(8,128)(2,1)S(1)}, bf16[...) custom-call(bf16[256,2048]{1,0:T(8,128)(2,1)} %refs_1_.4, bf16[256,2048]{1,0:T(8,128)(2,1)} %refs_2_.1), custom_call_target="tpu_custom_call" | custom-call | flops 2300000000 | tf_op jit(solution)/shard_map/pack_first/pallas_call | solution.py:71
  2.5 2.6 %collective-permute-start.1 = (bf16[2,2,256,128]{3,2,1,0:T(8,128)(2,1)S(1)}, bf16[2,2,256,128]{3,2,1,0:T(8,128)(2,1)S(1)}, u32[]{:S(2)}, u32[]{:S(2)}) collective-permute-start(bf16[2,2,256,128]{3,2,1,0:T(8,128)(2,1)S(1)} %get-tuple-element.28), channel_id=1, source_target_pairs={{0,1},{1,2},{2,3},{3,0},{4,5},{5,6},{6,7},{7,4},{8,9},{9,10},{10,1... | collective-permute-start | bytes 786440 | tf_op jit(solution)/shard_map/ppermute | solution.py:455
  5.1 2.6 %collective-permute-start.2 = (bf16[2,2,256,128]{3,2,1,0:T(8,128)(2,1)S(1)}, bf16[2,2,256,128]{3,2,1,0:T(8,128)(2,1)S(1)}, u32[]{:S(2)}, u32[]{:S(2)}) collective-permute-start(bf16[2,2,256,128]{3,2,1,0:T(8,128)(2,1)S(1)} %get-tuple-element.29), channel_id=1, source_target_pairs={{0,2},{1,3},{2,0},{3,1},{4,6},{5,7},{6,4},{7,5},{8,10},{9,11},{10,... | collective-permute-start | bytes 786440 | tf_op jit(solution)/shard_map/ppermute | solution.py:455
  9.8 1.6 %collective-permute-start.5 = (bf16[2048,128]{1,0:T(8,128)(2,1)S(1)}, bf16[2048,128]{1,0:T(8,128)(2,1)S(1)}, u32[]{:S(2)}, u32[]{:S(2)}) collective-permute-start(bf16[2048,128]{1,0:T(8,128)(2,1)S(1)} %join.1.refs_3_.refs_1_.refs_9_), channel_id=1, source_target_pairs={{0,16},{4,20},{8,24},{12,28},{16,0},{20,4},{24,8},{28,12},{1,17},{... | collective-permute-start | bytes 1572872 | tf_op jit(solution)/shard_map/ppermute | solution.py:239
  11.4 1.5 %collective-permute-start.4 = (bf16[2048,128]{1,0:T(8,128)(2,1)S(1)}, bf16[2048,128]{1,0:T(8,128)(2,1)S(1)}, u32[]{:S(2)}, u32[]{:S(2)}) collective-permute-start(bf16[2048,128]{1,0:T(8,128)(2,1)S(1)} %join.1.refs_3_.refs_1_.refs_9_), channel_id=1, source_target_pairs={{0,8},{4,12},{8,0},{12,4},{16,24},{20,28},{24,16},{28,20},{1,9},{5... | collective-permute-start | bytes 1572872 | tf_op jit(solution)/shard_map/ppermute | solution.py:239
  12.9 3.0 %pack_rest.1 = (bf16[8,3,256,128]{3,2,1,0:T(8,128)(2,1)}, bf16[8,1,256,128]{3,2,1,0:T(8,128)(2,1)S(1)}) custom-call(bf16[256,2048]{1,0:T(8,128)(2,1)} %refs_0_.3, bf16[256,2048]{1,0:T(8,128)(2,1)} %refs_1_.4, bf16[256,2048]{1,0:T(8,128)(2,1)} %refs_2_.1, bf16[2048,128]{1,0:T(8,128)(2,1)S(1)} %join.1.refs_3_.refs_1_.refs_9_), custom_call_target="tpu_custom_call" | custom-call | flops 3449999872 | tf_op jit(solution)/shard_map/pack_rest/pallas_call | solution.py:165
  16.7 8.7 %collective-permute-done.2.refs_1_ = bf16[2,2,256,128]{3,2,1,0:T(8,128)(2,1)S(1)} collective-permute-done((bf16[2,2,256,128]{3,2,1,0:T(8,128)(2,1)S(1)}, bf16[2,2,256,128]{3,2,1,0:T(8,128)(2,1)S(1)}, u32[]{:S(2)}, u32[]{:S(2)}) %collective-permute-start.2) | collective-permute-done | bytes 262176 | tf_op jit(solution)/shard_map/ppermute | solution.py:455
  26.0 8.6 %all-to-all-start = ((bf16[8,3,256,128]{3,2,1,0:T(8,128)(2,1)}), bf16[8,3,256,128]{3,2,1,0:T(8,128)(2,1)}, u32[]{:S(2)}, u32[]{:S(2)}) async-start(bf16[8,3,256,128]{3,2,1,0:T(8,128)(2,1)} %release.1), calls=%async_computation | async-start | bytes 3145728 | tf_op jit(solution)/shard_map/all_to_all | solution.py:218
  37.7 1.6 %collective-permute-start.8 = (bf16[1536,128]{1,0:T(8,128)(2,1)S(1)}, bf16[1536,128]{1,0:T(8,128)(2,1)S(1)}, u32[]{:S(2)}, u32[]{:S(2)}) collective-permute-start(bf16[1536,128]{1,0:T(8,128)(2,1)S(1)} %get-tuple-element.32.refs_2_), channel_id=1, source_target_pairs={{0,16},{4,20},{8,24},{12,28},{16,0},{20,4},{24,8},{28,12},{1,17},{... | collective-permute-start | bytes 1179656 | tf_op jit(solution)/shard_map/ppermute | solution.py:239
  39.3 1.5 %collective-permute-start.10 = (bf16[1536,128]{1,0:T(8,128)(2,1)S(1)}, bf16[1536,128]{1,0:T(8,128)(2,1)S(1)}, u32[]{:S(2)}, u32[]{:S(2)}) collective-permute-start(bf16[1536,128]{1,0:T(8,128)(2,1)S(1)} %get-tuple-element.33.refs_10_), channel_id=1, source_target_pairs={{0,8},{4,12},{8,0},{12,4},{16,24},{20,28},{24,16},{28,20},{1,9},{5... | collective-permute-start | bytes 1179656 | tf_op jit(solution)/shard_map/ppermute | solution.py:239
  41.9 7.9 %collective-permute-done.8.refs_3_.refs_6_ = bf16[1536,128]{1,0:T(8,128)(2,1)S(1)} collective-permute-done((bf16[1536,128]{1,0:T(8,128)(2,1)S(1)}, bf16[1536,128]{1,0:T(8,128)(2,1)S(1)}, u32[]{:S(2)}, u32[]{:S(2)}) %collective-permute-start.8) | collective-permute-done | bytes 393248 | tf_op jit(solution)/shard_map/ppermute | solution.py:239
  49.7 1.5 %collective-permute-start.9 = (bf16[1536,128]{1,0:T(8,128)(2,1)S(1)}, bf16[1536,128]{1,0:T(8,128)(2,1)S(1)}, u32[]{:S(2)}, u32[]{:S(2)}) collective-permute-start(bf16[1536,128]{1,0:T(8,128)(2,1)S(1)} %collective-permute-done.8.refs_3_.refs_6_), channel_id=1, source_target_pairs={{0,8},{4,12},{8,0},{12,4},{16,24},{20,28},{24,16},{28,20},{1,9},{5... | collective-permute-start | bytes 1179656 | tf_op jit(solution)/shard_map/ppermute | solution.py:239
  51.3 1.5 %collective-permute-start.12 = (bf16[1536,128]{1,0:T(8,128)(2,1)S(1)}, bf16[1536,128]{1,0:T(8,128)(2,1)}, u32[]{:S(2)}, u32[]{:S(2)}) collective-permute-start(bf16[1536,128]{1,0:T(8,128)(2,1)S(1)} %collective-permute-done.10.refs_5_.refs_12_), channel_id=1, source_target_pairs={{0,16},{4,20},{8,24},{12,28},{16,0},{20,4},{24,8},{28,12},{1,17},{... | collective-permute-start | bytes 1179656 | tf_op jit(solution)/shard_map/ppermute | solution.py:239
  53.4 6.3 %collective-permute-done.7.refs_2_.refs_4_ = bf16[1536,128]{1,0:T(8,128)(2,1)S(1)} collective-permute-done((bf16[1536,128]{1,0:T(8,128)(2,1)S(1)}, bf16[1536,128]{1,0:T(8,128)(2,1)S(1)}, u32[]{:S(2)}, u32[]{:S(2)}) %collective-permute-start.7) | collective-permute-done | bytes 393248 | tf_op jit(solution)/shard_map/ppermute | solution.py:239
  60.2 12.7 %collective-permute-done.13.refs_8_.refs_7_ = bf16[1024,128]{1,0:T(8,128)(2,1)S(1)} collective-permute-done((bf16[1024,128]{1,0:T(8,128)(2,1)S(1)}, bf16[1024,128]{1,0:T(8,128)(2,1)S(1)}, u32[]{:S(2)}, u32[]{:S(2)}) %collective-permute-start.13) | collective-permute-done | bytes 262176 | tf_op jit(solution)/shard_map/ppermute | solution.py:239
  75.7 1.5 %collective-permute-start.18 = (bf16[1536,128]{1,0:T(8,128)(2,1)S(1)}, bf16[1536,128]{1,0:T(8,128)(2,1)S(1)}, u32[]{:S(2)}, u32[]{:S(2)}) collective-permute-start(bf16[1536,128]{1,0:T(8,128)(2,1)S(1)} %get-tuple-element.36.refs_10_), channel_id=1, source_target_pairs={{0,8},{4,12},{8,0},{12,4},{16,24},{20,28},{24,16},{28,20},{1,9},{5... | collective-permute-start | bytes 1179656 | tf_op jit(solution)/shard_map/ppermute | solution.py:239
  77.2 4.7 %all-to-all-start.1 = ((bf16[8,1,256,128]{3,2,1,0:T(8,128)(2,1)}), bf16[8,1,256,128]{3,2,1,0:T(8,128)(2,1)S(1)}, u32[]{:S(2)}, u32[]{:S(2)}) async-start(bf16[8,1,256,128]{3,2,1,0:T(8,128)(2,1)} %get-tuple-element.34), calls=%async_computation.1 | async-start | bytes 1048576 | tf_op jit(solution)/shard_map/all_to_all | solution.py:218
  82.4 1.5 %collective-permute-start.19 = (bf16[1536,128]{1,0:T(8,128)(2,1)S(1)}, bf16[1536,128]{1,0:T(8,128)(2,1)S(1)}, u32[]{:S(2)}, u32[]{:S(2)}) collective-permute-start(bf16[1536,128]{1,0:T(8,128)(2,1)S(1)} %get-tuple-element.36.refs_10_), channel_id=1, source_target_pairs={{0,16},{4,20},{8,24},{12,28},{16,0},{20,4},{24,8},{28,12},{1,17},{... | collective-permute-start | bytes 1179656 | tf_op jit(solution)/shard_map/ppermute | solution.py:239
  84.0 1.8 %collective-permute-done.16.refs_6_ = bf16[1536,128]{1,0:T(8,128)(2,1)S(1)} collective-permute-done((bf16[1536,128]{1,0:T(8,128)(2,1)S(1)}, bf16[1536,128]{1,0:T(8,128)(2,1)S(1)}, u32[]{:S(2)}, u32[]{:S(2)}) %collective-permute-start.16) | collective-permute-done | bytes 393248 | tf_op jit(solution)/shard_map/ppermute | solution.py:239
  85.7 1.5 %collective-permute-start.17 = (bf16[1536,128]{1,0:T(8,128)(2,1)S(1)}, bf16[1536,128]{1,0:T(8,128)(2,1)}, u32[]{:S(2)}, u32[]{:S(2)}) collective-permute-start(bf16[1536,128]{1,0:T(8,128)(2,1)S(1)} %collective-permute-done.16.refs_6_), channel_id=1, source_target_pairs={{0,8},{4,12},{8,0},{12,4},{16,24},{20,28},{24,16},{28,20},{1,9},{5... | collective-permute-start | bytes 1179656 | tf_op jit(solution)/shard_map/ppermute | solution.py:239
  88.0 5.4 %attend.3 = bf16[8,256,128]{2,1,0:T(8,128)(2,1)} custom-call(s32[32,8]{1,0:T(8,128)} %copy-done.3, bf16[8,3,256,128]{3,2,1,0:T(8,128)(2,1)} %all-to-all-done.refs_0_, bf16[2048,128]{1,0:T(8,128)(2,1)} %copy-done.4, bf16[1536,128]{1,0:T(8,128)(2,1)} %copy-done.5, bf16[2048,128]{1,0:T(8,128)(2,1)} %copy-done.1, bf16[1536,128]{1,0:T(8,128)(2,1)} %copy-done.7, ...), custom_call_target="tpu_custom_call" | custom-call | flops 9200000000 | tf_op jit(solution)/shard_map/attend/pallas_call | solution.py:345
  93.4 3.8 %all-to-all-done.1.refs_0_ = bf16[8,1,256,128]{3,2,1,0:T(8,128)(2,1)S(1)} async-done(((bf16[8,1,256,128]{3,2,1,0:T(8,128)(2,1)}), bf16[8,1,256,128]{3,2,1,0:T(8,128)(2,1)S(1)}, u32[]{:S(2)}, u32[]{:S(2)}) %all-to-all-start.1) | async-done | bytes 524320 | tf_op jit(solution)/shard_map/all_to_all | solution.py:218
  97.3 3.5 %all-to-all-start.2 = ((bf16[8,256,128]{2,1,0:T(8,128)(2,1)}), bf16[8,256,128]{2,1,0:T(8,128)(2,1)S(1)}, u32[]{:S(2)}, u32[]{:S(2)}) async-start(bf16[8,256,128]{2,1,0:T(8,128)(2,1)} %attend.3), calls=%async_computation.2 | async-start | bytes 1048576 | tf_op jit(solution)/shard_map/all_to_all | solution.py:218
  100.8 2.0 %collective-permute-done.17.refs_8_ = bf16[1536,128]{1,0:T(8,128)(2,1)} collective-permute-done((bf16[1536,128]{1,0:T(8,128)(2,1)S(1)}, bf16[1536,128]{1,0:T(8,128)(2,1)}, u32[]{:S(2)}, u32[]{:S(2)}) %collective-permute-start.17) | collective-permute-done | bytes 393248 | tf_op jit(solution)/shard_map/ppermute | solution.py:239
  102.8 5.5 %attend.2 = (bf16[256,128]{1,0:T(8,128)(2,1)}, bf16[256,128]{1,0:T(8,128)(2,1)}, bf16[256,128]{1,0:T(8,128)(2,1)}, bf16[256,128]{1,0:T(8,128)(2,1)}, bf16[256,12...) custom-call(s32[32,8]{1,0:T(8,128)} %copy-done.3, ...), custom_call_target="tpu_custom_call" | custom-call | flops 9200000000 | tf_op jit(solution)/shard_map/attend/pallas_call | solution.py:345
  108.4 3.2 %collective-permute-start.22 = (bf16[256,128]{1,0:T(8,128)(2,1)}, bf16[256,128]{1,0:T(8,128)(2,1)S(1)}, u32[]{:S(2)}, u32[]{:S(2)}) collective-permute-start(bf16[256,128]{1,0:T(8,128)(2,1)} %get-tuple-element.39), channel_id=1, source_target_pairs={{0,3},{1,0},{2,1},{3,2},{4,7},{5,4},{6,5},{7,6},{8,11},{9,8},{10,9... | collective-permute-start | bytes 196616 | tf_op jit(solution)/shard_map/ppermute | solution.py:227
  111.9 2.6 %collective-permute-start.25 = (bf16[256,128]{1,0:T(8,128)(2,1)}, bf16[256,128]{1,0:T(8,128)(2,1)S(1)}, u32[]{:S(2)}, u32[]{:S(2)}) collective-permute-start(bf16[256,128]{1,0:T(8,128)(2,1)} %get-tuple-element.42), channel_id=1, source_target_pairs={{0,6},{1,7},{2,4},{3,5},{4,2},{5,3},{6,0},{7,1},{8,14},{9,15},{10,... | collective-permute-start | bytes 196616 | tf_op jit(solution)/shard_map/ppermute | solution.py:227
  114.5 1.5 %collective-permute-start.26 = (bf16[256,128]{1,0:T(8,128)(2,1)}, bf16[256,128]{1,0:T(8,128)(2,1)S(1)}, u32[]{:S(2)}, u32[]{:S(2)}) collective-permute-start(bf16[256,128]{1,0:T(8,128)(2,1)} %get-tuple-element.43), channel_id=1, source_target_pairs={{0,1},{1,2},{2,3},{3,0},{4,5},{5,6},{6,7},{7,4},{8,9},{9,10},{10,1... | collective-permute-start | bytes 196616 | tf_op jit(solution)/shard_map/ppermute | solution.py:227
  116.0 1.4 %collective-permute-start.27 = (bf16[256,128]{1,0:T(8,128)(2,1)}, bf16[256,128]{1,0:T(8,128)(2,1)S(1)}, u32[]{:S(2)}, u32[]{:S(2)}) collective-permute-start(bf16[256,128]{1,0:T(8,128)(2,1)} %get-tuple-element.44), channel_id=1, source_target_pairs={{0,5},{1,6},{2,7},{3,4},{4,1},{5,2},{6,3},{7,0},{8,13},{9,14},{10,... | collective-permute-start | bytes 196616 | tf_op jit(solution)/shard_map/ppermute | solution.py:227
  117.3 5.0 %project.2.refs_9_ = f32[256,4096]{1,0:T(8,128)S(1)} custom-call(bf16[8,256,128]{2,1,0:T(8,128)(2,1)S(1)} %all-to-all-done.2.refs_0_, bf16[2048,4096]{1,0:T(8,128)(2,1)} %refs_8_.1), custom_call_target="tpu_custom_call" | custom-call | flops 8049999872 | tf_op jit(solution)/shard_map/project/pallas_call | solution.py:413
  122.3 4.0 %collective-permute-done.24.refs_4_ = bf16[256,128]{1,0:T(8,128)(2,1)S(1)} collective-permute-done((bf16[256,128]{1,0:T(8,128)(2,1)}, bf16[256,128]{1,0:T(8,128)(2,1)S(1)}, u32[]{:S(2)}, u32[]{:S(2)}) %collective-permute-start.24) | collective-permute-done | bytes 65568 | tf_op jit(solution)/shard_map/ppermute | solution.py:227
  126.8 6.0 %project.3 = bf16[256,4096]{1,0:T(8,128)(2,1)} custom-call(bf16[256,128]{1,0:T(8,128)(2,1)S(1)} %copy-done.12, bf16[256,128]{1,0:T(8,128)(2,1)S(1)} %collective-permute-done.21.refs_1_, bf16[256,128]{1,0:T(8,128)(2,1)S(1)} %collective-permute-done.22.refs_2_, bf16[256,128]{1,0:T(8,128)(2,1)S(1)} %collective-permute-done.23.refs_3_, ...), custom_call_target="tpu_custom_call" | custom-call | flops 8049999872 | tf_op jit(solution)/shard_map/project/pallas_call | solution.py:413
  (100 shorter events, 14.2 us)
Async XLA Ops:
  1.9 7.1 %collective-permute-start = (bf16[4,256,128]{2,1,0:T(8,128)(2,1)S(1)}, bf16[4,256,128]{2,1,0:T(8,128)(2,1)S(1)}, u32[]{:S(2)}, u32[]{:S(2)}) collective-permute-start(bf16[4,256,128]{2,1,0:T(8,128)(2,1)S(1)} %get-tuple-element.26), channel_id=1, source_target_pairs={{0,4},{4,0},{8,12},{12,8},{16,20},{20,16},{24,28},{28,24},{1,5},{5... | collective-permute-start | bytes 786440 | tf_op jit(solution)/shard_map/ppermute | solution.py:235
  2.5 14.2 %collective-permute-start.1 = (bf16[2,2,256,128]{3,2,1,0:T(8,128)(2,1)S(1)}, bf16[2,2,256,128]{3,2,1,0:T(8,128)(2,1)S(1)}, u32[]{:S(2)}, u32[]{:S(2)}) collective-permute-start(bf16[2,2,256,128]{3,2,1,0:T(8,128)(2,1)S(1)} %get-tuple-element.28), channel_id=1, source_target_pairs={{0,1},{1,2},{2,3},{3,0},{4,5},{5,6},{6,7},{7,4},{8,9},{9,10},{10,1... | collective-permute-start | bytes 786440 | tf_op jit(solution)/shard_map/ppermute | solution.py:455
  5.1 20.3 %collective-permute-start.2 = (bf16[2,2,256,128]{3,2,1,0:T(8,128)(2,1)S(1)}, bf16[2,2,256,128]{3,2,1,0:T(8,128)(2,1)S(1)}, u32[]{:S(2)}, u32[]{:S(2)}) collective-permute-start(bf16[2,2,256,128]{3,2,1,0:T(8,128)(2,1)S(1)} %get-tuple-element.29), channel_id=1, source_target_pairs={{0,2},{1,3},{2,0},{3,1},{4,6},{5,7},{6,4},{7,5},{8,10},{9,11},{10,... | collective-permute-start | bytes 786440 | tf_op jit(solution)/shard_map/ppermute | solution.py:455
  7.7 17.7 %collective-permute-start.3 = (bf16[2,2,256,128]{3,2,1,0:T(8,128)(2,1)S(1)}, bf16[2,2,256,128]{3,2,1,0:T(8,128)(2,1)S(1)}, u32[]{:S(2)}, u32[]{:S(2)}) collective-permute-start(bf16[2,2,256,128]{3,2,1,0:T(8,128)(2,1)S(1)} %get-tuple-element.30), channel_id=1, source_target_pairs={{0,3},{1,0},{2,1},{3,2},{4,7},{5,4},{6,5},{7,6},{8,11},{9,8},{10,9... | collective-permute-start | bytes 786440 | tf_op jit(solution)/shard_map/ppermute | solution.py:455
  9.8 16.1 %collective-permute-start.5 = (bf16[2048,128]{1,0:T(8,128)(2,1)S(1)}, bf16[2048,128]{1,0:T(8,128)(2,1)S(1)}, u32[]{:S(2)}, u32[]{:S(2)}) collective-permute-start(bf16[2048,128]{1,0:T(8,128)(2,1)S(1)} %join.1.refs_3_.refs_1_.refs_9_), channel_id=1, source_target_pairs={{0,16},{4,20},{8,24},{12,28},{16,0},{20,4},{24,8},{28,12},{1,17},{... | collective-permute-start | bytes 1572872 | tf_op jit(solution)/shard_map/ppermute | solution.py:239
  11.4 14.5 %collective-permute-start.4 = (bf16[2048,128]{1,0:T(8,128)(2,1)S(1)}, bf16[2048,128]{1,0:T(8,128)(2,1)S(1)}, u32[]{:S(2)}, u32[]{:S(2)}) collective-permute-start(bf16[2048,128]{1,0:T(8,128)(2,1)S(1)} %join.1.refs_3_.refs_1_.refs_9_), channel_id=1, source_target_pairs={{0,8},{4,12},{8,0},{12,4},{16,24},{20,28},{24,16},{28,20},{1,9},{5... | collective-permute-start | bytes 1572872 | tf_op jit(solution)/shard_map/ppermute | solution.py:239
  26.0 47.8 %all-to-all-start = ((bf16[8,3,256,128]{3,2,1,0:T(8,128)(2,1)}), bf16[8,3,256,128]{3,2,1,0:T(8,128)(2,1)}, u32[]{:S(2)}, u32[]{:S(2)}) async-start(bf16[8,3,256,128]{3,2,1,0:T(8,128)(2,1)} %release.1), calls=%async_computation | async-start | bytes 3145728 | tf_op jit(solution)/shard_map/all_to_all | solution.py:218
  34.7 1.9 %collective-permute-start.6 = (bf16[3,2,256,128]{3,2,1,0:T(8,128)(2,1)S(1)}, bf16[3,2,256,128]{3,2,1,0:T(8,128)(2,1)S(1)}, u32[]{:S(2)}, u32[]{:S(2)}) collective-permute-start(bf16[3,2,256,128]{3,2,1,0:T(8,128)(2,1)S(1)} %for_other.1.refs_1_), channel_id=1, source_target_pairs={{0,4},{4,0},{8,12},{12,8},{16,20},{20,16},{24,28},{28,24},{1,5},{5... | collective-permute-start | bytes 1179656 | tf_op jit(solution)/shard_map/ppermute | solution.py:235
  37.7 37.3 %copy-start.5 = (bf16[1536,128]{1,0:T(8,128)(2,1)}, bf16[1536,128]{1,0:T(8,128)(2,1)S(1)}, u32[]{:S(2)}) copy-start(bf16[1536,128]{1,0:T(8,128)(2,1)S(1)} %get-tuple-element.32.refs_2_) | copy-start | bytes 1179652
  37.7 12.0 %collective-permute-start.8 = (bf16[1536,128]{1,0:T(8,128)(2,1)S(1)}, bf16[1536,128]{1,0:T(8,128)(2,1)S(1)}, u32[]{:S(2)}, u32[]{:S(2)}) collective-permute-start(bf16[1536,128]{1,0:T(8,128)(2,1)S(1)} %get-tuple-element.32.refs_2_), channel_id=1, source_target_pairs={{0,16},{4,20},{8,24},{12,28},{16,0},{20,4},{24,8},{28,12},{1,17},{... | collective-permute-start | bytes 1179656 | tf_op jit(solution)/shard_map/ppermute | solution.py:239
  39.3 12.0 %collective-permute-start.10 = (bf16[1536,128]{1,0:T(8,128)(2,1)S(1)}, bf16[1536,128]{1,0:T(8,128)(2,1)S(1)}, u32[]{:S(2)}, u32[]{:S(2)}) collective-permute-start(bf16[1536,128]{1,0:T(8,128)(2,1)S(1)} %get-tuple-element.33.refs_10_), channel_id=1, source_target_pairs={{0,8},{4,12},{8,0},{12,4},{16,24},{20,28},{24,16},{28,20},{1,9},{5... | collective-permute-start | bytes 1179656 | tf_op jit(solution)/shard_map/ppermute | solution.py:239
  40.8 18.9 %collective-permute-start.7 = (bf16[1536,128]{1,0:T(8,128)(2,1)S(1)}, bf16[1536,128]{1,0:T(8,128)(2,1)S(1)}, u32[]{:S(2)}, u32[]{:S(2)}) collective-permute-start(bf16[1536,128]{1,0:T(8,128)(2,1)S(1)} %get-tuple-element.32.refs_2_), channel_id=1, source_target_pairs={{0,8},{4,12},{8,0},{12,4},{16,24},{20,28},{24,16},{28,20},{1,9},{5... | collective-permute-start | bytes 1179656 | tf_op jit(solution)/shard_map/ppermute | solution.py:239
  41.3 18.9 %collective-permute-start.11 = (bf16[1536,128]{1,0:T(8,128)(2,1)S(1)}, bf16[1536,128]{1,0:T(8,128)(2,1)S(1)}, u32[]{:S(2)}, u32[]{:S(2)}) collective-permute-start(bf16[1536,128]{1,0:T(8,128)(2,1)S(1)} %get-tuple-element.33.refs_10_), channel_id=1, source_target_pairs={{0,16},{4,20},{8,24},{12,28},{16,0},{20,4},{24,8},{28,12},{1,17},{... | collective-permute-start | bytes 1179656 | tf_op jit(solution)/shard_map/ppermute | solution.py:239
  49.7 23.2 %collective-permute-start.9 = (bf16[1536,128]{1,0:T(8,128)(2,1)S(1)}, bf16[1536,128]{1,0:T(8,128)(2,1)S(1)}, u32[]{:S(2)}, u32[]{:S(2)}) collective-permute-start(bf16[1536,128]{1,0:T(8,128)(2,1)S(1)} %collective-permute-done.8.refs_3_.refs_6_), channel_id=1, source_target_pairs={{0,8},{4,12},{8,0},{12,4},{16,24},{20,28},{24,16},{28,20},{1,9},{5... | collective-permute-start | bytes 1179656 | tf_op jit(solution)/shard_map/ppermute | solution.py:239
  51.3 22.5 %collective-permute-start.12 = (bf16[1536,128]{1,0:T(8,128)(2,1)S(1)}, bf16[1536,128]{1,0:T(8,128)(2,1)}, u32[]{:S(2)}, u32[]{:S(2)}) collective-permute-start(bf16[1536,128]{1,0:T(8,128)(2,1)S(1)} %collective-permute-done.10.refs_5_.refs_12_), channel_id=1, source_target_pairs={{0,16},{4,20},{8,24},{12,28},{16,0},{20,4},{24,8},{28,12},{1,17},{... | collective-permute-start | bytes 1179656 | tf_op jit(solution)/shard_map/ppermute | solution.py:239
  52.8 20.1 %collective-permute-start.13 = (bf16[1024,128]{1,0:T(8,128)(2,1)S(1)}, bf16[1024,128]{1,0:T(8,128)(2,1)S(1)}, u32[]{:S(2)}, u32[]{:S(2)}) collective-permute-start(bf16[1024,128]{1,0:T(8,128)(2,1)S(1)} %slice.10), channel_id=1, source_target_pairs={{0,8},{4,12},{8,0},{12,4},{16,24},{20,28},{24,16},{28,20},{1,9},{5... | collective-permute-start | bytes 786440 | tf_op jit(solution)/shard_map/ppermute | solution.py:239
  59.7 13.2 %collective-permute-start.14 = (bf16[1024,128]{1,0:T(8,128)(2,1)S(1)}, bf16[1024,128]{1,0:T(8,128)(2,1)S(1)}, u32[]{:S(2)}, u32[]{:S(2)}) collective-permute-start(bf16[1024,128]{1,0:T(8,128)(2,1)S(1)} %slice.11), channel_id=1, source_target_pairs={{0,16},{4,20},{8,24},{12,28},{16,0},{20,4},{24,8},{28,12},{1,17},{... | collective-permute-start | bytes 786440 | tf_op jit(solution)/shard_map/ppermute | solution.py:239
  75.1 10.6 %collective-permute-start.16 = (bf16[1536,128]{1,0:T(8,128)(2,1)S(1)}, bf16[1536,128]{1,0:T(8,128)(2,1)S(1)}, u32[]{:S(2)}, u32[]{:S(2)}) collective-permute-start(bf16[1536,128]{1,0:T(8,128)(2,1)S(1)} %get-tuple-element.35.refs_2_), channel_id=1, source_target_pairs={{0,16},{4,20},{8,24},{12,28},{16,0},{20,4},{24,8},{28,12},{1,17},{... | collective-permute-start | bytes 1179656 | tf_op jit(solution)/shard_map/ppermute | solution.py:239
  75.7 11.6 %collective-permute-start.18 = (bf16[1536,128]{1,0:T(8,128)(2,1)S(1)}, bf16[1536,128]{1,0:T(8,128)(2,1)S(1)}, u32[]{:S(2)}, u32[]{:S(2)}) collective-permute-start(bf16[1536,128]{1,0:T(8,128)(2,1)S(1)} %get-tuple-element.36.refs_10_), channel_id=1, source_target_pairs={{0,8},{4,12},{8,0},{12,4},{16,24},{20,28},{24,16},{28,20},{1,9},{5... | collective-permute-start | bytes 1179656 | tf_op jit(solution)/shard_map/ppermute | solution.py:239
  77.2 20.1 %all-to-all-start.1 = ((bf16[8,1,256,128]{3,2,1,0:T(8,128)(2,1)}), bf16[8,1,256,128]{3,2,1,0:T(8,128)(2,1)S(1)}, u32[]{:S(2)}, u32[]{:S(2)}) async-start(bf16[8,1,256,128]{3,2,1,0:T(8,128)(2,1)} %get-tuple-element.34), calls=%async_computation.1 | async-start | bytes 1048576 | tf_op jit(solution)/shard_map/all_to_all | solution.py:218
  81.9 18.9 %collective-permute-start.15 = (bf16[1536,128]{1,0:T(8,128)(2,1)S(1)}, bf16[1536,128]{1,0:T(8,128)(2,1)S(1)}, u32[]{:S(2)}, u32[]{:S(2)}) collective-permute-start(bf16[1536,128]{1,0:T(8,128)(2,1)S(1)} %get-tuple-element.35.refs_2_), channel_id=1, source_target_pairs={{0,8},{4,12},{8,0},{12,4},{16,24},{20,28},{24,16},{28,20},{1,9},{5... | collective-permute-start | bytes 1179656 | tf_op jit(solution)/shard_map/ppermute | solution.py:239
  82.4 18.4 %collective-permute-start.19 = (bf16[1536,128]{1,0:T(8,128)(2,1)S(1)}, bf16[1536,128]{1,0:T(8,128)(2,1)S(1)}, u32[]{:S(2)}, u32[]{:S(2)}) collective-permute-start(bf16[1536,128]{1,0:T(8,128)(2,1)S(1)} %get-tuple-element.36.refs_10_), channel_id=1, source_target_pairs={{0,16},{4,20},{8,24},{12,28},{16,0},{20,4},{24,8},{28,12},{1,17},{... | collective-permute-start | bytes 1179656 | tf_op jit(solution)/shard_map/ppermute | solution.py:239
  85.7 17.0 %collective-permute-start.17 = (bf16[1536,128]{1,0:T(8,128)(2,1)S(1)}, bf16[1536,128]{1,0:T(8,128)(2,1)}, u32[]{:S(2)}, u32[]{:S(2)}) collective-permute-start(bf16[1536,128]{1,0:T(8,128)(2,1)S(1)} %collective-permute-done.16.refs_6_), channel_id=1, source_target_pairs={{0,8},{4,12},{8,0},{12,4},{16,24},{20,28},{24,16},{28,20},{1,9},{5... | collective-permute-start | bytes 1179656 | tf_op jit(solution)/shard_map/ppermute | solution.py:239
  87.2 15.6 %collective-permute-start.20 = (bf16[1536,128]{1,0:T(8,128)(2,1)S(1)}, bf16[1536,128]{1,0:T(8,128)(2,1)}, u32[]{:S(2)}, u32[]{:S(2)}) collective-permute-start(bf16[1536,128]{1,0:T(8,128)(2,1)S(1)} %collective-permute-done.18.refs_12_), channel_id=1, source_target_pairs={{0,16},{4,20},{8,24},{12,28},{16,0},{20,4},{24,8},{28,12},{1,17},{... | collective-permute-start | bytes 1179656 | tf_op jit(solution)/shard_map/ppermute | solution.py:239
  97.3 20.1 %all-to-all-start.2 = ((bf16[8,256,128]{2,1,0:T(8,128)(2,1)}), bf16[8,256,128]{2,1,0:T(8,128)(2,1)S(1)}, u32[]{:S(2)}, u32[]{:S(2)}) async-start(bf16[8,256,128]{2,1,0:T(8,128)(2,1)} %attend.3), calls=%async_computation.2 | async-start | bytes 1048576 | tf_op jit(solution)/shard_map/all_to_all | solution.py:218
  108.3 6.2 %collective-permute-start.21 = (bf16[256,128]{1,0:T(8,128)(2,1)}, bf16[256,128]{1,0:T(8,128)(2,1)S(1)}, u32[]{:S(2)}, u32[]{:S(2)}) collective-permute-start(bf16[256,128]{1,0:T(8,128)(2,1)} %get-tuple-element.38), channel_id=1, source_target_pairs={{0,4},{1,5},{2,6},{3,7},{4,0},{5,1},{6,2},{7,3},{8,12},{9,13},{10,... | collective-permute-start | bytes 196616 | tf_op jit(solution)/shard_map/ppermute | solution.py:227
  108.4 7.6 %collective-permute-start.22 = (bf16[256,128]{1,0:T(8,128)(2,1)}, bf16[256,128]{1,0:T(8,128)(2,1)S(1)}, u32[]{:S(2)}, u32[]{:S(2)}) collective-permute-start(bf16[256,128]{1,0:T(8,128)(2,1)} %get-tuple-element.39), channel_id=1, source_target_pairs={{0,3},{1,0},{2,1},{3,2},{4,7},{5,4},{6,5},{7,6},{8,11},{9,8},{10,9... | collective-permute-start | bytes 196616 | tf_op jit(solution)/shard_map/ppermute | solution.py:227
  111.6 10.8 %collective-permute-start.23 = (bf16[256,128]{1,0:T(8,128)(2,1)}, bf16[256,128]{1,0:T(8,128)(2,1)S(1)}, u32[]{:S(2)}, u32[]{:S(2)}) collective-permute-start(bf16[256,128]{1,0:T(8,128)(2,1)} %get-tuple-element.40), channel_id=1, source_target_pairs={{0,7},{1,4},{2,5},{3,6},{4,3},{5,0},{6,1},{7,2},{8,15},{9,12},{10,... | collective-permute-start | bytes 196616 | tf_op jit(solution)/shard_map/ppermute | solution.py:227
  111.9 14.5 %collective-permute-start.24 = (bf16[256,128]{1,0:T(8,128)(2,1)}, bf16[256,128]{1,0:T(8,128)(2,1)S(1)}, u32[]{:S(2)}, u32[]{:S(2)}) collective-permute-start(bf16[256,128]{1,0:T(8,128)(2,1)} %get-tuple-element.41), channel_id=1, source_target_pairs={{0,2},{1,3},{2,0},{3,1},{4,6},{5,7},{6,4},{7,5},{8,10},{9,11},{10,... | collective-permute-start | bytes 196616 | tf_op jit(solution)/shard_map/ppermute | solution.py:227
  111.9 14.9 %collective-permute-start.25 = (bf16[256,128]{1,0:T(8,128)(2,1)}, bf16[256,128]{1,0:T(8,128)(2,1)S(1)}, u32[]{:S(2)}, u32[]{:S(2)}) collective-permute-start(bf16[256,128]{1,0:T(8,128)(2,1)} %get-tuple-element.42), channel_id=1, source_target_pairs={{0,6},{1,7},{2,4},{3,5},{4,2},{5,3},{6,0},{7,1},{8,14},{9,15},{10,... | collective-permute-start | bytes 196616 | tf_op jit(solution)/shard_map/ppermute | solution.py:227
  114.5 12.3 %collective-permute-start.26 = (bf16[256,128]{1,0:T(8,128)(2,1)}, bf16[256,128]{1,0:T(8,128)(2,1)S(1)}, u32[]{:S(2)}, u32[]{:S(2)}) collective-permute-start(bf16[256,128]{1,0:T(8,128)(2,1)} %get-tuple-element.43), channel_id=1, source_target_pairs={{0,1},{1,2},{2,3},{3,0},{4,5},{5,6},{6,7},{7,4},{8,9},{9,10},{10,1... | collective-permute-start | bytes 196616 | tf_op jit(solution)/shard_map/ppermute | solution.py:227
  116.0 10.9 %collective-permute-start.27 = (bf16[256,128]{1,0:T(8,128)(2,1)}, bf16[256,128]{1,0:T(8,128)(2,1)S(1)}, u32[]{:S(2)}, u32[]{:S(2)}) collective-permute-start(bf16[256,128]{1,0:T(8,128)(2,1)} %get-tuple-element.44), channel_id=1, source_target_pairs={{0,5},{1,6},{2,7},{3,4},{4,1},{5,2},{6,3},{7,0},{8,13},{9,14},{10,... | collective-permute-start | bytes 196616 | tf_op jit(solution)/shard_map/ppermute | solution.py:227
  (22 other events, 259.1 us)

commit v9 on v8

--- a/solution.py
+++ b/solution.py
@@ -150,8 +150,8 @@
     items = [item for bundle in bundles for item in bundle]
 
     def body(*refs):
-        ins, outs = refs[:nb], refs[nb + 1 : nb + 1 + len(bundles)]
-        held, in_sems, out_sems = refs[nb + 1 + len(bundles) :]
+        ins, outs = refs[:nb], refs[nb + len(after) : nb + len(after) + len(bundles)]
+        held, in_sems, out_sems = refs[nb + len(after) + len(bundles) :]
         pairs, where = [], [(b, i) for b, bundle in enumerate(bundles) for i in range(len(bundle))]
         for n, (which, slot) in enumerate(items):
             pairs.append((ins[which].at[:, pl.ds(slot * n_s * DH, n_s * DH)], held.at[n]))
@@ -165,7 +165,7 @@
     return pl.pallas_call(
         body,
         out_shape=[jax.ShapeDtypeStruct((n_s, len(b), T, DH), jnp.bfloat16) for b in bundles],
-        in_specs=[ANY] * (nb + 1),
+        in_specs=[ANY] * (nb + len(after)),
         out_specs=[ANY] * len(bundles),
         scratch_shapes=[
             pltpu.VMEM((len(items), T, n_s * DH), jnp.bfloat16),
@@ -175,7 +175,7 @@
         compiler_params=beside(8 * MIB),
         cost_estimate=cost(3),
         name="pack_rest",
-    )(*tensors, after)
+    )(*tensors, *after)
 
 
 def stage(blocks, packed, n_u, after):
@@ -454,11 +454,11 @@
     *parts, mine, others = pack_first([keys, values], n_u, hp)
     along = [lax.ppermute(x, "ulys", [(i, (i + d) % n_u) for i in range(n_u)]) for d, x in enumerate(parts, 1)]
     joined = join(mine, swap_core(others, n_c), hp)
-    packed = pack_rest([queries, keys, values], bundles, n_u, joined)
+    packed = pack_rest([queries, keys, values], bundles, n_u, [joined, table])
     near, rounds = gather_whole(joined, n_c)
     meant = for_other(along)
     blocks = [*along, swap_core(meant, n_c)]
-    q_of, far, after = [], [], [table]
+    q_of, far, after = [], [], []
     direct = (n_c // 2).bit_length() - 1
     for h in range(hp):
         if h == 0:

time: 135 us -> 135 us (level)
  no operation moved by 1% of the time
where the time goes in v9:
time: 135 us; the launch traced here: 133 us
  starting transfers between devices  51.1 us (38%)
  waiting for transfers between devices  47.8 us (35%)
  Pallas kernels  30.4 us (23%)
  local copies, waits for them, and re-layouts  2.57 us (2%)
    ppermute x16, waiting for transfers between devices, swap_chip(): return lax.ppermute(x, 'ctx', [(i, i ^ 2 * bit) for i in range(n_c)])  30.1 us
    ppermute x16, starting transfers between devices, swap_chip(): return lax.ppermute(x, 'ctx', [(i, i ^ 2 * bit) for i in range(n_c)])  17.7 us
    all_to_all x3, starting transfers between devices, to_shares(): lax.all_to_all(x, ('ctx', 'ulys'), split_axis=0, concat_axis=0, tiled=Tru...  16.8 us
    pallas_call x2, Pallas kernels, project(): pl.pallas_call(body, out_shape=jax.ShapeDtypeStruct((T, width), jnp.bfloa...  10.9 us
    pallas_call x2, Pallas kernels, attend(): pl.pallas_call(body, out_shape=[jax.ShapeDtypeStruct((T, DH) if apart els...  10.9 us
    ppermute x7, starting transfers between devices, send(): return lax.ppermute(x, ('ctx', 'ulys'), pairs)  8.93 us
    ppermute x3, waiting for transfers between devices, shards(): lax.ppermute(x, 'ulys', [(i, (i + d) % n_u) for i in range(n_u)])  7.49 us
    ppermute x3, starting transfers between devices, shards(): lax.ppermute(x, 'ulys', [(i, (i + d) % n_u) for i in range(n_u)])  6.59 us
  transfers between devices with their start and end apart: 31, of which 11 were waited for; matrix products, arithmetic and copies ran while one was open for 1% of the time, Pallas kernels for 16%

profile of v9, /device:TPU:0, one launch (start us, length us, event | category | flops | bytes accessed | tf_op | source)
XLA Modules:
  0.0 132.7 jit_solution(5848618403094956214)
XLA Ops:
  0.0 1.9 %pack_first.1 = (bf16[2,2,256,128]{3,2,1,0:T(8,128)(2,1)S(1)}, bf16[2,2,256,128]{3,2,1,0:T(8,128)(2,1)S(1)}, bf16[2,2,256,128]{3,2,1,0:T(8,128)(2,1)S(1)}, bf16[...) custom-call(bf16[256,2048]{1,0:T(8,128)(2,1)} %refs_1_.4, bf16[256,2048]{1,0:T(8,128)(2,1)} %refs_2_.1), custom_call_target="tpu_custom_call" | custom-call | flops 2300000000 | tf_op jit(solution)/shard_map/pack_first/pallas_call | solution.py:71
  2.5 2.6 %collective-permute-start.1 = (bf16[2,2,256,128]{3,2,1,0:T(8,128)(2,1)S(1)}, bf16[2,2,256,128]{3,2,1,0:T(8,128)(2,1)S(1)}, u32[]{:S(2)}, u32[]{:S(2)}) collective-permute-start(bf16[2,2,256,128]{3,2,1,0:T(8,128)(2,1)S(1)} %get-tuple-element.28), channel_id=1, source_target_pairs={{0,1},{1,2},{2,3},{3,0},{4,5},{5,6},{6,7},{7,4},{8,9},{9,10},{10,1... | collective-permute-start | bytes 786440 | tf_op jit(solution)/shard_map/ppermute | solution.py:455
  5.1 2.6 %collective-permute-start.2 = (bf16[2,2,256,128]{3,2,1,0:T(8,128)(2,1)S(1)}, bf16[2,2,256,128]{3,2,1,0:T(8,128)(2,1)S(1)}, u32[]{:S(2)}, u32[]{:S(2)}) collective-permute-start(bf16[2,2,256,128]{3,2,1,0:T(8,128)(2,1)S(1)} %get-tuple-element.29), channel_id=1, source_target_pairs={{0,2},{1,3},{2,0},{3,1},{4,6},{5,7},{6,4},{7,5},{8,10},{9,11},{10,... | collective-permute-start | bytes 786440 | tf_op jit(solution)/shard_map/ppermute | solution.py:455
  7.7 1.4 %collective-permute-start.3 = (bf16[2,2,256,128]{3,2,1,0:T(8,128)(2,1)S(1)}, bf16[2,2,256,128]{3,2,1,0:T(8,128)(2,1)S(1)}, u32[]{:S(2)}, u32[]{:S(2)}) collective-permute-start(bf16[2,2,256,128]{3,2,1,0:T(8,128)(2,1)S(1)} %get-tuple-element.30), channel_id=1, source_target_pairs={{0,3},{1,0},{2,1},{3,2},{4,7},{5,4},{6,5},{7,6},{8,11},{9,8},{10,9... | collective-permute-start | bytes 786440 | tf_op jit(solution)/shard_map/ppermute | solution.py:455
  11.0 1.6 %collective-permute-start.5 = (bf16[2048,128]{1,0:T(8,128)(2,1)S(1)}, bf16[2048,128]{1,0:T(8,128)(2,1)S(1)}, u32[]{:S(2)}, u32[]{:S(2)}) collective-permute-start(bf16[2048,128]{1,0:T(8,128)(2,1)S(1)} %join.1.refs_3_.refs_1_.refs_9_), channel_id=1, source_target_pairs={{0,16},{4,20},{8,24},{12,28},{16,0},{20,4},{24,8},{28,12},{1,17},{... | collective-permute-start | bytes 1572872 | tf_op jit(solution)/shard_map/ppermute | solution.py:239
  12.6 1.5 %collective-permute-start.4 = (bf16[2048,128]{1,0:T(8,128)(2,1)S(1)}, bf16[2048,128]{1,0:T(8,128)(2,1)S(1)}, u32[]{:S(2)}, u32[]{:S(2)}) collective-permute-start(bf16[2048,128]{1,0:T(8,128)(2,1)S(1)} %join.1.refs_3_.refs_1_.refs_9_), channel_id=1, source_target_pairs={{0,8},{4,12},{8,0},{12,4},{16,24},{20,28},{24,16},{28,20},{1,9},{5... | collective-permute-start | bytes 1572872 | tf_op jit(solution)/shard_map/ppermute | solution.py:239
  14.1 3.0 %pack_rest.1 = (bf16[8,3,256,128]{3,2,1,0:T(8,128)(2,1)}, bf16[8,1,256,128]{3,2,1,0:T(8,128)(2,1)S(1)}) custom-call(bf16[256,2048]{1,0:T(8,128)(2,1)} %refs_0_.3, bf16[256,2048]{1,0:T(8,128)(2,1)} %refs_1_.4, bf16[256,2048]{1,0:T(8,128)(2,1)} %refs_2_.1, bf16[2048,128]{1,0:T(8,128)(2,1)S(1)} %join.1.refs_3_.refs_1_.refs_9_, s32[32,8]{1,0:T(8,128)S(1)} %fusion.8.refs_4_.table_ref), custom_call_target="tpu_custom_call" | custom-call | flops 3449999872 | tf_op jit(solution)/shard_map/pack_rest/pallas_call | solution.py:165
  17.9 7.5 %collective-permute-done.2.refs_1_ = bf16[2,2,256,128]{3,2,1,0:T(8,128)(2,1)S(1)} collective-permute-done((bf16[2,2,256,128]{3,2,1,0:T(8,128)(2,1)S(1)}, bf16[2,2,256,128]{3,2,1,0:T(8,128)(2,1)S(1)}, u32[]{:S(2)}, u32[]{:S(2)}) %collective-permute-start.2) | collective-permute-done | bytes 262176 | tf_op jit(solution)/shard_map/ppermute | solution.py:455
  26.0 8.4 %all-to-all-start = ((bf16[8,3,256,128]{3,2,1,0:T(8,128)(2,1)}), bf16[8,3,256,128]{3,2,1,0:T(8,128)(2,1)}, u32[]{:S(2)}, u32[]{:S(2)}) async-start(bf16[8,3,256,128]{3,2,1,0:T(8,128)(2,1)} %release.1), calls=%async_computation | async-start | bytes 3145728 | tf_op jit(solution)/shard_map/all_to_all | solution.py:218
  34.9 1.5 %collective-permute-done.6.refs_3_ = bf16[3,2,256,128]{3,2,1,0:T(8,128)(2,1)S(1)} collective-permute-done((bf16[3,2,256,128]{3,2,1,0:T(8,128)(2,1)S(1)}, bf16[3,2,256,128]{3,2,1,0:T(8,128)(2,1)S(1)}, u32[]{:S(2)}, u32[]{:S(2)}) %collective-permute-start.6) | collective-permute-done | bytes 393248 | tf_op jit(solution)/shard_map/ppermute | solution.py:235
  37.5 1.6 %collective-permute-start.8 = (bf16[1536,128]{1,0:T(8,128)(2,1)S(1)}, bf16[1536,128]{1,0:T(8,128)(2,1)S(1)}, u32[]{:S(2)}, u32[]{:S(2)}) collective-permute-start(bf16[1536,128]{1,0:T(8,128)(2,1)S(1)} %get-tuple-element.32.refs_2_), channel_id=1, source_target_pairs={{0,16},{4,20},{8,24},{12,28},{16,0},{20,4},{24,8},{28,12},{1,17},{... | collective-permute-start | bytes 1179656 | tf_op jit(solution)/shard_map/ppermute | solution.py:239
  39.1 1.5 %collective-permute-start.10 = (bf16[1536,128]{1,0:T(8,128)(2,1)S(1)}, bf16[1536,128]{1,0:T(8,128)(2,1)S(1)}, u32[]{:S(2)}, u32[]{:S(2)}) collective-permute-start(bf16[1536,128]{1,0:T(8,128)(2,1)S(1)} %get-tuple-element.33.refs_10_), channel_id=1, source_target_pairs={{0,8},{4,12},{8,0},{12,4},{16,24},{20,28},{24,16},{28,20},{1,9},{5... | collective-permute-start | bytes 1179656 | tf_op jit(solution)/shard_map/ppermute | solution.py:239
  41.7 7.9 %collective-permute-done.8.refs_3_.refs_6_ = bf16[1536,128]{1,0:T(8,128)(2,1)S(1)} collective-permute-done((bf16[1536,128]{1,0:T(8,128)(2,1)S(1)}, bf16[1536,128]{1,0:T(8,128)(2,1)S(1)}, u32[]{:S(2)}, u32[]{:S(2)}) %collective-permute-start.8) | collective-permute-done | bytes 393248 | tf_op jit(solution)/shard_map/ppermute | solution.py:239
  49.6 1.5 %collective-permute-start.9 = (bf16[1536,128]{1,0:T(8,128)(2,1)S(1)}, bf16[1536,128]{1,0:T(8,128)(2,1)S(1)}, u32[]{:S(2)}, u32[]{:S(2)}) collective-permute-start(bf16[1536,128]{1,0:T(8,128)(2,1)S(1)} %collective-permute-done.8.refs_3_.refs_6_), channel_id=1, source_target_pairs={{0,8},{4,12},{8,0},{12,4},{16,24},{20,28},{24,16},{28,20},{1,9},{5... | collective-permute-start | bytes 1179656 | tf_op jit(solution)/shard_map/ppermute | solution.py:239
  51.1 1.5 %collective-permute-start.12 = (bf16[1536,128]{1,0:T(8,128)(2,1)S(1)}, bf16[1536,128]{1,0:T(8,128)(2,1)}, u32[]{:S(2)}, u32[]{:S(2)}) collective-permute-start(bf16[1536,128]{1,0:T(8,128)(2,1)S(1)} %collective-permute-done.10.refs_5_.refs_12_), channel_id=1, source_target_pairs={{0,16},{4,20},{8,24},{12,28},{16,0},{20,4},{24,8},{28,12},{1,17},{... | collective-permute-start | bytes 1179656 | tf_op jit(solution)/shard_map/ppermute | solution.py:239
  53.2 6.3 %collective-permute-done.7.refs_2_.refs_4_ = bf16[1536,128]{1,0:T(8,128)(2,1)S(1)} collective-permute-done((bf16[1536,128]{1,0:T(8,128)(2,1)S(1)}, bf16[1536,128]{1,0:T(8,128)(2,1)S(1)}, u32[]{:S(2)}, u32[]{:S(2)}) %collective-permute-start.7) | collective-permute-done | bytes 393248 | tf_op jit(solution)/shard_map/ppermute | solution.py:239
  60.1 12.5 %collective-permute-done.13.refs_8_.refs_7_ = bf16[1024,128]{1,0:T(8,128)(2,1)S(1)} collective-permute-done((bf16[1024,128]{1,0:T(8,128)(2,1)S(1)}, bf16[1024,128]{1,0:T(8,128)(2,1)S(1)}, u32[]{:S(2)}, u32[]{:S(2)}) %collective-permute-start.13) | collective-permute-done | bytes 262176 | tf_op jit(solution)/shard_map/ppermute | solution.py:239
  75.3 1.5 %collective-permute-start.18 = (bf16[1536,128]{1,0:T(8,128)(2,1)S(1)}, bf16[1536,128]{1,0:T(8,128)(2,1)S(1)}, u32[]{:S(2)}, u32[]{:S(2)}) collective-permute-start(bf16[1536,128]{1,0:T(8,128)(2,1)S(1)} %get-tuple-element.36.refs_10_), channel_id=1, source_target_pairs={{0,8},{4,12},{8,0},{12,4},{16,24},{20,28},{24,16},{28,20},{1,9},{5... | collective-permute-start | bytes 1179656 | tf_op jit(solution)/shard_map/ppermute | solution.py:239
  76.8 4.9 %all-to-all-start.1 = ((bf16[8,1,256,128]{3,2,1,0:T(8,128)(2,1)}), bf16[8,1,256,128]{3,2,1,0:T(8,128)(2,1)S(1)}, u32[]{:S(2)}, u32[]{:S(2)}) async-start(bf16[8,1,256,128]{3,2,1,0:T(8,128)(2,1)} %get-tuple-element.34), calls=%async_computation.1 | async-start | bytes 1048576 | tf_op jit(solution)/shard_map/all_to_all | solution.py:218
  82.2 1.5 %collective-permute-start.19 = (bf16[1536,128]{1,0:T(8,128)(2,1)S(1)}, bf16[1536,128]{1,0:T(8,128)(2,1)S(1)}, u32[]{:S(2)}, u32[]{:S(2)}) collective-permute-start(bf16[1536,128]{1,0:T(8,128)(2,1)S(1)} %get-tuple-element.36.refs_10_), channel_id=1, source_target_pairs={{0,16},{4,20},{8,24},{12,28},{16,0},{20,4},{24,8},{28,12},{1,17},{... | collective-permute-start | bytes 1179656 | tf_op jit(solution)/shard_map/ppermute | solution.py:239
  85.1 1.5 %collective-permute-start.17 = (bf16[1536,128]{1,0:T(8,128)(2,1)S(1)}, bf16[1536,128]{1,0:T(8,128)(2,1)}, u32[]{:S(2)}, u32[]{:S(2)}) collective-permute-start(bf16[1536,128]{1,0:T(8,128)(2,1)S(1)} %collective-permute-done.16.refs_6_), channel_id=1, source_target_pairs={{0,8},{4,12},{8,0},{12,4},{16,24},{20,28},{24,16},{28,20},{1,9},{5... | collective-permute-start | bytes 1179656 | tf_op jit(solution)/shard_map/ppermute | solution.py:239
  87.4 5.4 %attend.3 = bf16[8,256,128]{2,1,0:T(8,128)(2,1)} custom-call(s32[32,8]{1,0:T(8,128)} %copy-done.3, bf16[8,3,256,128]{3,2,1,0:T(8,128)(2,1)} %all-to-all-done.refs_0_, bf16[2048,128]{1,0:T(8,128)(2,1)} %copy-done.4, bf16[1536,128]{1,0:T(8,128)(2,1)} %copy-done.5, bf16[2048,128]{1,0:T(8,128)(2,1)} %copy-done.1, bf16[1536,128]{1,0:T(8,128)(2,1)} %copy-done.7, ...), custom_call_target="tpu_custom_call" | custom-call | flops 9200000000 | tf_op jit(solution)/shard_map/attend/pallas_call | solution.py:345
  92.9 4.2 %all-to-all-done.1.refs_0_ = bf16[8,1,256,128]{3,2,1,0:T(8,128)(2,1)S(1)} async-done(((bf16[8,1,256,128]{3,2,1,0:T(8,128)(2,1)}), bf16[8,1,256,128]{3,2,1,0:T(8,128)(2,1)S(1)}, u32[]{:S(2)}, u32[]{:S(2)}) %all-to-all-start.1) | async-done | bytes 524320 | tf_op jit(solution)/shard_map/all_to_all | solution.py:218
  97.1 3.5 %all-to-all-start.2 = ((bf16[8,256,128]{2,1,0:T(8,128)(2,1)}), bf16[8,256,128]{2,1,0:T(8,128)(2,1)S(1)}, u32[]{:S(2)}, u32[]{:S(2)}) async-start(bf16[8,256,128]{2,1,0:T(8,128)(2,1)} %attend.3), calls=%async_computation.2 | async-start | bytes 1048576 | tf_op jit(solution)/shard_map/all_to_all | solution.py:218
  100.6 2.0 %collective-permute-done.17.refs_8_ = bf16[1536,128]{1,0:T(8,128)(2,1)} collective-permute-done((bf16[1536,128]{1,0:T(8,128)(2,1)S(1)}, bf16[1536,128]{1,0:T(8,128)(2,1)}, u32[]{:S(2)}, u32[]{:S(2)}) %collective-permute-start.17) | collective-permute-done | bytes 393248 | tf_op jit(solution)/shard_map/ppermute | solution.py:239
  102.6 5.5 %attend.2 = (bf16[256,128]{1,0:T(8,128)(2,1)}, bf16[256,128]{1,0:T(8,128)(2,1)}, bf16[256,128]{1,0:T(8,128)(2,1)}, bf16[256,128]{1,0:T(8,128)(2,1)}, bf16[256,12...) custom-call(s32[32,8]{1,0:T(8,128)} %copy-done.3, ...), custom_call_target="tpu_custom_call" | custom-call | flops 9200000000 | tf_op jit(solution)/shard_map/attend/pallas_call | solution.py:345
  108.2 3.3 %collective-permute-start.22 = (bf16[256,128]{1,0:T(8,128)(2,1)}, bf16[256,128]{1,0:T(8,128)(2,1)S(1)}, u32[]{:S(2)}, u32[]{:S(2)}) collective-permute-start(bf16[256,128]{1,0:T(8,128)(2,1)} %get-tuple-element.39), channel_id=1, source_target_pairs={{0,3},{1,0},{2,1},{3,2},{4,7},{5,4},{6,5},{7,6},{8,11},{9,8},{10,9... | collective-permute-start | bytes 196616 | tf_op jit(solution)/shard_map/ppermute | solution.py:227
  111.8 2.6 %collective-permute-start.25 = (bf16[256,128]{1,0:T(8,128)(2,1)}, bf16[256,128]{1,0:T(8,128)(2,1)S(1)}, u32[]{:S(2)}, u32[]{:S(2)}) collective-permute-start(bf16[256,128]{1,0:T(8,128)(2,1)} %get-tuple-element.42), channel_id=1, source_target_pairs={{0,6},{1,7},{2,4},{3,5},{4,2},{5,3},{6,0},{7,1},{8,14},{9,15},{10,... | collective-permute-start | bytes 196616 | tf_op jit(solution)/shard_map/ppermute | solution.py:227
  114.4 1.5 %collective-permute-start.26 = (bf16[256,128]{1,0:T(8,128)(2,1)}, bf16[256,128]{1,0:T(8,128)(2,1)S(1)}, u32[]{:S(2)}, u32[]{:S(2)}) collective-permute-start(bf16[256,128]{1,0:T(8,128)(2,1)} %get-tuple-element.43), channel_id=1, source_target_pairs={{0,1},{1,2},{2,3},{3,0},{4,5},{5,6},{6,7},{7,4},{8,9},{9,10},{10,1... | collective-permute-start | bytes 196616 | tf_op jit(solution)/shard_map/ppermute | solution.py:227
  117.1 5.0 %project.2.refs_9_ = f32[256,4096]{1,0:T(8,128)S(1)} custom-call(bf16[8,256,128]{2,1,0:T(8,128)(2,1)S(1)} %all-to-all-done.2.refs_0_, bf16[2048,4096]{1,0:T(8,128)(2,1)} %refs_8_.1), custom_call_target="tpu_custom_call" | custom-call | flops 8049999872 | tf_op jit(solution)/shard_map/project/pallas_call | solution.py:413
  122.1 4.1 %collective-permute-done.24.refs_4_ = bf16[256,128]{1,0:T(8,128)(2,1)S(1)} collective-permute-done((bf16[256,128]{1,0:T(8,128)(2,1)}, bf16[256,128]{1,0:T(8,128)(2,1)S(1)}, u32[]{:S(2)}, u32[]{:S(2)}) %collective-permute-start.24) | collective-permute-done | bytes 65568 | tf_op jit(solution)/shard_map/ppermute | solution.py:227
  126.6 6.0 %project.3 = bf16[256,4096]{1,0:T(8,128)(2,1)} custom-call(bf16[256,128]{1,0:T(8,128)(2,1)S(1)} %copy-done.12, bf16[256,128]{1,0:T(8,128)(2,1)S(1)} %collective-permute-done.21.refs_1_, bf16[256,128]{1,0:T(8,128)(2,1)S(1)} %collective-permute-done.22.refs_2_, bf16[256,128]{1,0:T(8,128)(2,1)S(1)} %collective-permute-done.23.refs_3_, ...), custom_call_target="tpu_custom_call" | custom-call | flops 8049999872 | tf_op jit(solution)/shard_map/project/pallas_call | solution.py:413
  (100 shorter events, 15.1 us)
Async XLA Ops:
  1.9 8.3 %collective-permute-start = (bf16[4,256,128]{2,1,0:T(8,128)(2,1)S(1)}, bf16[4,256,128]{2,1,0:T(8,128)(2,1)S(1)}, u32[]{:S(2)}, u32[]{:S(2)}) collective-permute-start(bf16[4,256,128]{2,1,0:T(8,128)(2,1)S(1)} %get-tuple-element.26), channel_id=1, source_target_pairs={{0,4},{4,0},{8,12},{12,8},{16,20},{20,16},{24,28},{28,24},{1,5},{5... | collective-permute-start | bytes 786440 | tf_op jit(solution)/shard_map/ppermute | solution.py:235
  2.5 15.4 %collective-permute-start.1 = (bf16[2,2,256,128]{3,2,1,0:T(8,128)(2,1)S(1)}, bf16[2,2,256,128]{3,2,1,0:T(8,128)(2,1)S(1)}, u32[]{:S(2)}, u32[]{:S(2)}) collective-permute-start(bf16[2,2,256,128]{3,2,1,0:T(8,128)(2,1)S(1)} %get-tuple-element.28), channel_id=1, source_target_pairs={{0,1},{1,2},{2,3},{3,0},{4,5},{5,6},{6,7},{7,4},{8,9},{9,10},{10,1... | collective-permute-start | bytes 786440 | tf_op jit(solution)/shard_map/ppermute | solution.py:455
  5.1 20.3 %collective-permute-start.2 = (bf16[2,2,256,128]{3,2,1,0:T(8,128)(2,1)S(1)}, bf16[2,2,256,128]{3,2,1,0:T(8,128)(2,1)S(1)}, u32[]{:S(2)}, u32[]{:S(2)}) collective-permute-start(bf16[2,2,256,128]{3,2,1,0:T(8,128)(2,1)S(1)} %get-tuple-element.29), channel_id=1, source_target_pairs={{0,2},{1,3},{2,0},{3,1},{4,6},{5,7},{6,4},{7,5},{8,10},{9,11},{10,... | collective-permute-start | bytes 786440 | tf_op jit(solution)/shard_map/ppermute | solution.py:455
  7.7 17.7 %collective-permute-start.3 = (bf16[2,2,256,128]{3,2,1,0:T(8,128)(2,1)S(1)}, bf16[2,2,256,128]{3,2,1,0:T(8,128)(2,1)S(1)}, u32[]{:S(2)}, u32[]{:S(2)}) collective-permute-start(bf16[2,2,256,128]{3,2,1,0:T(8,128)(2,1)S(1)} %get-tuple-element.30), channel_id=1, source_target_pairs={{0,3},{1,0},{2,1},{3,2},{4,7},{5,4},{6,5},{7,6},{8,11},{9,8},{10,9... | collective-permute-start | bytes 786440 | tf_op jit(solution)/shard_map/ppermute | solution.py:455
  11.0 14.9 %collective-permute-start.5 = (bf16[2048,128]{1,0:T(8,128)(2,1)S(1)}, bf16[2048,128]{1,0:T(8,128)(2,1)S(1)}, u32[]{:S(2)}, u32[]{:S(2)}) collective-permute-start(bf16[2048,128]{1,0:T(8,128)(2,1)S(1)} %join.1.refs_3_.refs_1_.refs_9_), channel_id=1, source_target_pairs={{0,16},{4,20},{8,24},{12,28},{16,0},{20,4},{24,8},{28,12},{1,17},{... | collective-permute-start | bytes 1572872 | tf_op jit(solution)/shard_map/ppermute | solution.py:239
  12.6 13.3 %collective-permute-start.4 = (bf16[2048,128]{1,0:T(8,128)(2,1)S(1)}, bf16[2048,128]{1,0:T(8,128)(2,1)S(1)}, u32[]{:S(2)}, u32[]{:S(2)}) collective-permute-start(bf16[2048,128]{1,0:T(8,128)(2,1)S(1)} %join.1.refs_3_.refs_1_.refs_9_), channel_id=1, source_target_pairs={{0,8},{4,12},{8,0},{12,4},{16,24},{20,28},{24,16},{28,20},{1,9},{5... | collective-permute-start | bytes 1572872 | tf_op jit(solution)/shard_map/ppermute | solution.py:239
  26.0 47.4 %all-to-all-start = ((bf16[8,3,256,128]{3,2,1,0:T(8,128)(2,1)}), bf16[8,3,256,128]{3,2,1,0:T(8,128)(2,1)}, u32[]{:S(2)}, u32[]{:S(2)}) async-start(bf16[8,3,256,128]{3,2,1,0:T(8,128)(2,1)} %release.1), calls=%async_computation | async-start | bytes 3145728 | tf_op jit(solution)/shard_map/all_to_all | solution.py:218
  34.4 2.0 %collective-permute-start.6 = (bf16[3,2,256,128]{3,2,1,0:T(8,128)(2,1)S(1)}, bf16[3,2,256,128]{3,2,1,0:T(8,128)(2,1)S(1)}, u32[]{:S(2)}, u32[]{:S(2)}) collective-permute-start(bf16[3,2,256,128]{3,2,1,0:T(8,128)(2,1)S(1)} %for_other.1.refs_1_), channel_id=1, source_target_pairs={{0,4},{4,0},{8,12},{12,8},{16,20},{20,16},{24,28},{28,24},{1,5},{5... | collective-permute-start | bytes 1179656 | tf_op jit(solution)/shard_map/ppermute | solution.py:235
  37.5 37.2 %copy-start.5 = (bf16[1536,128]{1,0:T(8,128)(2,1)}, bf16[1536,128]{1,0:T(8,128)(2,1)S(1)}, u32[]{:S(2)}) copy-start(bf16[1536,128]{1,0:T(8,128)(2,1)S(1)} %get-tuple-element.32.refs_2_) | copy-start | bytes 1179652
  37.5 12.0 %collective-permute-start.8 = (bf16[1536,128]{1,0:T(8,128)(2,1)S(1)}, bf16[1536,128]{1,0:T(8,128)(2,1)S(1)}, u32[]{:S(2)}, u32[]{:S(2)}) collective-permute-start(bf16[1536,128]{1,0:T(8,128)(2,1)S(1)} %get-tuple-element.32.refs_2_), channel_id=1, source_target_pairs={{0,16},{4,20},{8,24},{12,28},{16,0},{20,4},{24,8},{28,12},{1,17},{... | collective-permute-start | bytes 1179656 | tf_op jit(solution)/shard_map/ppermute | solution.py:239
  39.1 12.0 %collective-permute-start.10 = (bf16[1536,128]{1,0:T(8,128)(2,1)S(1)}, bf16[1536,128]{1,0:T(8,128)(2,1)S(1)}, u32[]{:S(2)}, u32[]{:S(2)}) collective-permute-start(bf16[1536,128]{1,0:T(8,128)(2,1)S(1)} %get-tuple-element.33.refs_10_), channel_id=1, source_target_pairs={{0,8},{4,12},{8,0},{12,4},{16,24},{20,28},{24,16},{28,20},{1,9},{5... | collective-permute-start | bytes 1179656 | tf_op jit(solution)/shard_map/ppermute | solution.py:239
  40.6 18.9 %collective-permute-start.7 = (bf16[1536,128]{1,0:T(8,128)(2,1)S(1)}, bf16[1536,128]{1,0:T(8,128)(2,1)S(1)}, u32[]{:S(2)}, u32[]{:S(2)}) collective-permute-start(bf16[1536,128]{1,0:T(8,128)(2,1)S(1)} %get-tuple-element.32.refs_2_), channel_id=1, source_target_pairs={{0,8},{4,12},{8,0},{12,4},{16,24},{20,28},{24,16},{28,20},{1,9},{5... | collective-permute-start | bytes 1179656 | tf_op jit(solution)/shard_map/ppermute | solution.py:239
  41.2 18.9 %collective-permute-start.11 = (bf16[1536,128]{1,0:T(8,128)(2,1)S(1)}, bf16[1536,128]{1,0:T(8,128)(2,1)S(1)}, u32[]{:S(2)}, u32[]{:S(2)}) collective-permute-start(bf16[1536,128]{1,0:T(8,128)(2,1)S(1)} %get-tuple-element.33.refs_10_), channel_id=1, source_target_pairs={{0,16},{4,20},{8,24},{12,28},{16,0},{20,4},{24,8},{28,12},{1,17},{... | collective-permute-start | bytes 1179656 | tf_op jit(solution)/shard_map/ppermute | solution.py:239
  49.6 23.0 %collective-permute-start.9 = (bf16[1536,128]{1,0:T(8,128)(2,1)S(1)}, bf16[1536,128]{1,0:T(8,128)(2,1)S(1)}, u32[]{:S(2)}, u32[]{:S(2)}) collective-permute-start(bf16[1536,128]{1,0:T(8,128)(2,1)S(1)} %collective-permute-done.8.refs_3_.refs_6_), channel_id=1, source_target_pairs={{0,8},{4,12},{8,0},{12,4},{16,24},{20,28},{24,16},{28,20},{1,9},{5... | collective-permute-start | bytes 1179656 | tf_op jit(solution)/shard_map/ppermute | solution.py:239
  51.1 22.3 %collective-permute-start.12 = (bf16[1536,128]{1,0:T(8,128)(2,1)S(1)}, bf16[1536,128]{1,0:T(8,128)(2,1)}, u32[]{:S(2)}, u32[]{:S(2)}) collective-permute-start(bf16[1536,128]{1,0:T(8,128)(2,1)S(1)} %collective-permute-done.10.refs_5_.refs_12_), channel_id=1, source_target_pairs={{0,16},{4,20},{8,24},{12,28},{16,0},{20,4},{24,8},{28,12},{1,17},{... | collective-permute-start | bytes 1179656 | tf_op jit(solution)/shard_map/ppermute | solution.py:239
  52.6 20.0 %collective-permute-start.13 = (bf16[1024,128]{1,0:T(8,128)(2,1)S(1)}, bf16[1024,128]{1,0:T(8,128)(2,1)S(1)}, u32[]{:S(2)}, u32[]{:S(2)}) collective-permute-start(bf16[1024,128]{1,0:T(8,128)(2,1)S(1)} %slice.10), channel_id=1, source_target_pairs={{0,8},{4,12},{8,0},{12,4},{16,24},{20,28},{24,16},{28,20},{1,9},{5... | collective-permute-start | bytes 786440 | tf_op jit(solution)/shard_map/ppermute | solution.py:239
  59.5 13.0 %collective-permute-start.14 = (bf16[1024,128]{1,0:T(8,128)(2,1)S(1)}, bf16[1024,128]{1,0:T(8,128)(2,1)S(1)}, u32[]{:S(2)}, u32[]{:S(2)}) collective-permute-start(bf16[1024,128]{1,0:T(8,128)(2,1)S(1)} %slice.11), channel_id=1, source_target_pairs={{0,16},{4,20},{8,24},{12,28},{16,0},{20,4},{24,8},{28,12},{1,17},{... | collective-permute-start | bytes 786440 | tf_op jit(solution)/shard_map/ppermute | solution.py:239
  74.8 10.3 %collective-permute-start.16 = (bf16[1536,128]{1,0:T(8,128)(2,1)S(1)}, bf16[1536,128]{1,0:T(8,128)(2,1)S(1)}, u32[]{:S(2)}, u32[]{:S(2)}) collective-permute-start(bf16[1536,128]{1,0:T(8,128)(2,1)S(1)} %get-tuple-element.35.refs_2_), channel_id=1, source_target_pairs={{0,16},{4,20},{8,24},{12,28},{16,0},{20,4},{24,8},{28,12},{1,17},{... | collective-permute-start | bytes 1179656 | tf_op jit(solution)/shard_map/ppermute | solution.py:239
  75.3 11.2 %collective-permute-start.18 = (bf16[1536,128]{1,0:T(8,128)(2,1)S(1)}, bf16[1536,128]{1,0:T(8,128)(2,1)S(1)}, u32[]{:S(2)}, u32[]{:S(2)}) collective-permute-start(bf16[1536,128]{1,0:T(8,128)(2,1)S(1)} %get-tuple-element.36.refs_10_), channel_id=1, source_target_pairs={{0,8},{4,12},{8,0},{12,4},{16,24},{20,28},{24,16},{28,20},{1,9},{5... | collective-permute-start | bytes 1179656 | tf_op jit(solution)/shard_map/ppermute | solution.py:239
  76.8 20.2 %all-to-all-start.1 = ((bf16[8,1,256,128]{3,2,1,0:T(8,128)(2,1)}), bf16[8,1,256,128]{3,2,1,0:T(8,128)(2,1)S(1)}, u32[]{:S(2)}, u32[]{:S(2)}) async-start(bf16[8,1,256,128]{3,2,1,0:T(8,128)(2,1)} %get-tuple-element.34), calls=%async_computation.1 | async-start | bytes 1048576 | tf_op jit(solution)/shard_map/all_to_all | solution.py:218
  81.7 18.9 %collective-permute-start.15 = (bf16[1536,128]{1,0:T(8,128)(2,1)S(1)}, bf16[1536,128]{1,0:T(8,128)(2,1)S(1)}, u32[]{:S(2)}, u32[]{:S(2)}) collective-permute-start(bf16[1536,128]{1,0:T(8,128)(2,1)S(1)} %get-tuple-element.35.refs_2_), channel_id=1, source_target_pairs={{0,8},{4,12},{8,0},{12,4},{16,24},{20,28},{24,16},{28,20},{1,9},{5... | collective-permute-start | bytes 1179656 | tf_op jit(solution)/shard_map/ppermute | solution.py:239
  82.2 18.4 %collective-permute-start.19 = (bf16[1536,128]{1,0:T(8,128)(2,1)S(1)}, bf16[1536,128]{1,0:T(8,128)(2,1)S(1)}, u32[]{:S(2)}, u32[]{:S(2)}) collective-permute-start(bf16[1536,128]{1,0:T(8,128)(2,1)S(1)} %get-tuple-element.36.refs_10_), channel_id=1, source_target_pairs={{0,16},{4,20},{8,24},{12,28},{16,0},{20,4},{24,8},{28,12},{1,17},{... | collective-permute-start | bytes 1179656 | tf_op jit(solution)/shard_map/ppermute | solution.py:239
  85.1 17.5 %collective-permute-start.17 = (bf16[1536,128]{1,0:T(8,128)(2,1)S(1)}, bf16[1536,128]{1,0:T(8,128)(2,1)}, u32[]{:S(2)}, u32[]{:S(2)}) collective-permute-start(bf16[1536,128]{1,0:T(8,128)(2,1)S(1)} %collective-permute-done.16.refs_6_), channel_id=1, source_target_pairs={{0,8},{4,12},{8,0},{12,4},{16,24},{20,28},{24,16},{28,20},{1,9},{5... | collective-permute-start | bytes 1179656 | tf_op jit(solution)/shard_map/ppermute | solution.py:239
  86.6 16.1 %collective-permute-start.20 = (bf16[1536,128]{1,0:T(8,128)(2,1)S(1)}, bf16[1536,128]{1,0:T(8,128)(2,1)}, u32[]{:S(2)}, u32[]{:S(2)}) collective-permute-start(bf16[1536,128]{1,0:T(8,128)(2,1)S(1)} %collective-permute-done.18.refs_12_), channel_id=1, source_target_pairs={{0,16},{4,20},{8,24},{12,28},{16,0},{20,4},{24,8},{28,12},{1,17},{... | collective-permute-start | bytes 1179656 | tf_op jit(solution)/shard_map/ppermute | solution.py:239
  97.1 20.0 %all-to-all-start.2 = ((bf16[8,256,128]{2,1,0:T(8,128)(2,1)}), bf16[8,256,128]{2,1,0:T(8,128)(2,1)S(1)}, u32[]{:S(2)}, u32[]{:S(2)}) async-start(bf16[8,256,128]{2,1,0:T(8,128)(2,1)} %attend.3), calls=%async_computation.2 | async-start | bytes 1048576 | tf_op jit(solution)/shard_map/all_to_all | solution.py:218
  108.1 6.3 %collective-permute-start.21 = (bf16[256,128]{1,0:T(8,128)(2,1)}, bf16[256,128]{1,0:T(8,128)(2,1)S(1)}, u32[]{:S(2)}, u32[]{:S(2)}) collective-permute-start(bf16[256,128]{1,0:T(8,128)(2,1)} %get-tuple-element.38), channel_id=1, source_target_pairs={{0,4},{1,5},{2,6},{3,7},{4,0},{5,1},{6,2},{7,3},{8,12},{9,13},{10,... | collective-permute-start | bytes 196616 | tf_op jit(solution)/shard_map/ppermute | solution.py:227
  108.2 7.7 %collective-permute-start.22 = (bf16[256,128]{1,0:T(8,128)(2,1)}, bf16[256,128]{1,0:T(8,128)(2,1)S(1)}, u32[]{:S(2)}, u32[]{:S(2)}) collective-permute-start(bf16[256,128]{1,0:T(8,128)(2,1)} %get-tuple-element.39), channel_id=1, source_target_pairs={{0,3},{1,0},{2,1},{3,2},{4,7},{5,4},{6,5},{7,6},{8,11},{9,8},{10,9... | collective-permute-start | bytes 196616 | tf_op jit(solution)/shard_map/ppermute | solution.py:227
  111.5 10.5 %collective-permute-start.23 = (bf16[256,128]{1,0:T(8,128)(2,1)}, bf16[256,128]{1,0:T(8,128)(2,1)S(1)}, u32[]{:S(2)}, u32[]{:S(2)}) collective-permute-start(bf16[256,128]{1,0:T(8,128)(2,1)} %get-tuple-element.40), channel_id=1, source_target_pairs={{0,7},{1,4},{2,5},{3,6},{4,3},{5,0},{6,1},{7,2},{8,15},{9,12},{10,... | collective-permute-start | bytes 196616 | tf_op jit(solution)/shard_map/ppermute | solution.py:227
  111.8 14.3 %collective-permute-start.24 = (bf16[256,128]{1,0:T(8,128)(2,1)}, bf16[256,128]{1,0:T(8,128)(2,1)S(1)}, u32[]{:S(2)}, u32[]{:S(2)}) collective-permute-start(bf16[256,128]{1,0:T(8,128)(2,1)} %get-tuple-element.41), channel_id=1, source_target_pairs={{0,2},{1,3},{2,0},{3,1},{4,6},{5,7},{6,4},{7,5},{8,10},{9,11},{10,... | collective-permute-start | bytes 196616 | tf_op jit(solution)/shard_map/ppermute | solution.py:227
  111.8 14.8 %collective-permute-start.25 = (bf16[256,128]{1,0:T(8,128)(2,1)}, bf16[256,128]{1,0:T(8,128)(2,1)S(1)}, u32[]{:S(2)}, u32[]{:S(2)}) collective-permute-start(bf16[256,128]{1,0:T(8,128)(2,1)} %get-tuple-element.42), channel_id=1, source_target_pairs={{0,6},{1,7},{2,4},{3,5},{4,2},{5,3},{6,0},{7,1},{8,14},{9,15},{10,... | collective-permute-start | bytes 196616 | tf_op jit(solution)/shard_map/ppermute | solution.py:227
  114.4 12.2 %collective-permute-start.26 = (bf16[256,128]{1,0:T(8,128)(2,1)}, bf16[256,128]{1,0:T(8,128)(2,1)S(1)}, u32[]{:S(2)}, u32[]{:S(2)}) collective-permute-start(bf16[256,128]{1,0:T(8,128)(2,1)} %get-tuple-element.43), channel_id=1, source_target_pairs={{0,1},{1,2},{2,3},{3,0},{4,5},{5,6},{6,7},{7,4},{8,9},{9,10},{10,1... | collective-permute-start | bytes 196616 | tf_op jit(solution)/shard_map/ppermute | solution.py:227
  115.9 10.7 %collective-permute-start.27 = (bf16[256,128]{1,0:T(8,128)(2,1)}, bf16[256,128]{1,0:T(8,128)(2,1)S(1)}, u32[]{:S(2)}, u32[]{:S(2)}) collective-permute-start(bf16[256,128]{1,0:T(8,128)(2,1)} %get-tuple-element.44), channel_id=1, source_target_pairs={{0,5},{1,6},{2,7},{3,4},{4,1},{5,2},{6,3},{7,0},{8,13},{9,14},{10,... | collective-permute-start | bytes 196616 | tf_op jit(solution)/shard_map/ppermute | solution.py:227
  (22 other events, 260.9 us)
